TPU v7x, 32 devices: a whole 2x2x4 slice. The times are simulated.
32 devices in a mesh: ens: 8 (over z, core), tile: 4 (over y, x).
Axes of the slice: x: 2, y: 2, z: 4, core: 2. Of those that a mesh axis runs over, the one named last changes fastest.
Arguments:
- coords: float32 [64, 3, 3200], P('ens', None, 'tile'), may hold values from -6 to 6
- counts: int32 [3200, 3200], P('tile'), may hold values from 0 to 63, as said below
- segments: int32 [3200], replicated, may hold values from 0 to 7, never falling along the last dimension, each value on 1 to 800 neighbouring positions
Outputs:
- gradient: float32 [64, 3, 3200], P('ens', None, 'tile')
Inputs may be any that keep to these rules, and one draw needn't show every extreme that they name: counts is symmetric: counts[i, j] == counts[j, i].
All inputs are finite; a program needn't handle non-finite values.
Results may differ from a plain program's by a relative error of at most 0.00011.
Values sent between devices are 32-bit elements; how exact they have to be, the bound alone decides.
No kernel may reach another device: no remote copies, remote signals or barrier semaphores. Data moves between devices by JAX's collectives and lax.ppermute only.
A program may use at most 64 MiB of HBM per device.

v0:
```python
import functools

import jax
import jax.numpy as jnp
from jax import lax
from jax.experimental import pallas as pl
from jax.experimental.pallas import tpu as pltpu
from jax.sharding import PartitionSpec as P

LANES = 128
WIDE = 256


def split3(v):
    hi = v.astype(jnp.bfloat16).astype(jnp.float32)
    rest = v - hi
    mid = rest.astype(jnp.bfloat16).astype(jnp.float32)
    return hi, mid, rest - mid


def augment(v, norm_row, one_row):
    n = v.shape[1]
    norm = 1.5 - 0.5 * jnp.sum(v * v, axis=0, keepdims=True)
    v8 = jnp.concatenate([v, jnp.zeros((5, n), jnp.float32)], axis=0)
    row = lax.broadcasted_iota(jnp.int32, (8, n), 0)
    return jnp.where(row == norm_row, norm, jnp.where(row == one_row, 1.0, v8))


def pair_kernel(structs, tiles, row_base_ref, rows_ref, seg_rows_ref, seg_cols_ref, col_ids_ref, counts_ref, *rest):
    cols_refs = rest[:tiles]
    out_ref, lhs_ref, rhs_ref, weight_ref = rest[tiles:]
    n_rows = rows_ref.shape[2]
    n_cols = counts_ref.shape[1]
    wide = weight_ref.shape[1]
    starts = [(a, min(WIDE, wide - a)) for a in range(0, wide, WIDE)]

    def features(s, carry):
        rows = augment(rows_ref[s], 3, 4)
        hi, mid, lo = split3(rows)
        left = jnp.concatenate([hi, hi, mid, mid, hi, lo], axis=0)
        lhs_ref[s] = left.T.astype(jnp.bfloat16)
        cols = [ref[s] for ref in cols_refs]
        if wide > n_cols:
            cols.append(jnp.zeros((3, wide - n_cols), jnp.float32))
        hi, mid, lo = split3(augment(jnp.concatenate(cols, axis=1), 4, 3))
        rhs_ref[s] = jnp.concatenate([hi, mid, hi, mid, lo, hi], axis=0).astype(jnp.bfloat16)
        return carry

    lax.fori_loop(0, structs, features, 0)
    weight_ref[...] = jnp.zeros_like(weight_ref)

    def tanh_block(s, start, size):
        half = jnp.dot(lhs_ref[s], rhs_ref[s, :, pl.ds(start, size)], preferred_element_type=jnp.float32)
        return jnp.tanh(half)

    def add_one(s, carry):
        for start, size in starts:
            weight_ref[:, pl.ds(start, size)] += tanh_block(s, start, size)
        return carry

    lax.fori_loop(0, structs, add_one, 0)

    count = counts_ref[...].astype(jnp.float32)
    target = count / (count + 8.0)
    pbar = 0.5 + (0.5 / structs) * weight_ref[:, pl.ds(0, n_cols)]
    row_ids = row_base_ref[0] + lax.broadcasted_iota(jnp.int32, (n_rows, n_cols), 0)
    weight = jnp.where(seg_rows_ref[...] == seg_cols_ref[...], 1.0, 0.3)
    weight = jnp.where(row_ids == col_ids_ref[...], 0.0, weight)
    weight_ref[:, pl.ds(0, n_cols)] = weight * (pbar - target)
    if wide > n_cols:
        weight_ref[:, pl.ds(n_cols, wide - n_cols)] = jnp.zeros((n_rows, wide - n_cols), jnp.float32)

    def grad_one(s, carry):
        total = jnp.zeros((16, n_rows), jnp.float32)
        for start, size in starts:
            t = tanh_block(s, start, size)
            g = weight_ref[:, pl.ds(start, size)] * (1.0 - t * t)
            hi = g.astype(jnp.bfloat16)
            lo = (g - hi.astype(jnp.float32)).astype(jnp.bfloat16)
            part = rhs_ref[s, pl.ds(0, 16), pl.ds(start, size)]
            dims = (((1,), (1,)), ((), ()))
            total += lax.dot_general(part, hi, dims, preferred_element_type=jnp.float32)
            total += lax.dot_general(part, lo, dims, preferred_element_type=jnp.float32)
        mixed = total[0:3] + total[8:11]
        out_ref[s] = (0.25 / 16) * (mixed - total[3:4] * rows_ref[s])
        return carry

    lax.fori_loop(0, structs, grad_one, 0)


def split_ens(n_ens, beads, tiles):
    best = None
    for parts in range(1, n_ens + 1):
        if n_ens % parts or beads % parts or beads % (n_ens // parts):
            continue
        cost = 2 * (beads // parts) + tiles * (beads // (n_ens // parts))
        if best is None or cost < best[0]:
            best = (cost, parts)
    return best[1]


def on_device(coords, counts, segments):
    local_n, _, beads = coords.shape
    n_tile = lax.axis_size("tile")
    n_ens = lax.axis_size("ens")
    structs = local_n * n_ens
    n_p = split_ens(n_ens, beads, n_tile)
    n_q = n_ens // n_p
    n_rows, piece = beads // n_p, beads // n_q
    n_cols = piece * n_tile
    tile, ens = lax.axis_index("tile"), lax.axis_index("ens")
    p, q = lax.rem(ens, n_p), lax.div(ens, n_p)

    col_send = jnp.moveaxis(coords.reshape(local_n, 3, n_q, piece), 2, 0)
    col_send = jnp.broadcast_to(col_send[:, None], (n_q, n_p, local_n, 3, piece)).reshape(n_ens, local_n, 3, piece)
    row_send = jnp.moveaxis(coords.reshape(local_n, 3, n_p, n_rows), 2, 0)
    row_send = jnp.broadcast_to(row_send[None], (n_q, n_p, local_n, 3, n_rows)).reshape(n_ens, local_n, 3, n_rows)
    own = lax.all_to_all(col_send, "ens", 0, 0, tiled=True).reshape(structs, 3, piece)
    cols = [own]
    for k in range(1, n_tile):
        cols.append(lax.ppermute(own, "tile", [(t, (t - k) % n_tile) for t in range(n_tile)]))
    rows = lax.all_to_all(row_send, "ens", 0, 0, tiled=True).reshape(structs, 3, n_rows)

    row_base = tile * beads + p * n_rows
    col_bases = [lax.rem(tile + k, n_tile) * beads + q * piece for k in range(n_tile)]
    own_counts = lax.dynamic_slice_in_dim(counts, p * n_rows, n_rows, 0)
    block = jnp.concatenate([lax.dynamic_slice_in_dim(own_counts, b, piece, 1) for b in col_bases], axis=1)
    seg_cols = jnp.concatenate([lax.dynamic_slice_in_dim(segments, b, piece) for b in col_bases])[None, :]
    col_ids = jnp.concatenate([b + jnp.arange(piece, dtype=jnp.int32) for b in col_bases])[None, :]
    seg_rows = lax.dynamic_slice_in_dim(segments, row_base, n_rows)[:, None]

    wide = -(-n_cols // LANES) * LANES
    vmem = pl.BlockSpec(memory_space=pltpu.VMEM)
    grad = pl.pallas_call(
        functools.partial(pair_kernel, structs, n_tile),
        out_shape=jax.ShapeDtypeStruct((structs, 3, n_rows), jnp.float32),
        in_specs=[pl.BlockSpec(memory_space=pltpu.SMEM)] + [vmem] * (5 + n_tile),
        out_specs=vmem,
        scratch_shapes=[
            pltpu.VMEM((structs, n_rows, 48), jnp.bfloat16),
            pltpu.VMEM((structs, 48, wide), jnp.bfloat16),
            pltpu.VMEM((n_rows, wide), jnp.float32),
        ],
        compiler_params=pltpu.CompilerParams(vmem_limit_bytes=48 << 20),
        name="pairs",
    )(row_base[None], rows, seg_rows, seg_cols, col_ids, block, *cols)

    back = lax.all_to_all(grad.reshape(n_ens, local_n, 3, n_rows), "ens", 0, 0, tiled=True)
    back = jnp.sum(back.reshape(n_q, n_p, local_n, 3, n_rows), axis=0)
    return jnp.moveaxis(back, 0, 2).reshape(local_n, 3, beads)


def solution(mesh):
    return jax.shard_map(
        on_device,
        mesh=mesh,
        in_specs=(P("ens", None, "tile"), P("tile", None), P()),
        out_specs=P("ens", None, "tile"),
        check_vma=False,
    )
```

profile of v0, /device:TPU:0, one launch (start us, length us, event | category | flops | bytes accessed | tf_op | source)
XLA Modules:
  0.0 162.8 jit_solution(12581466771646170612)
XLA Ops:
  0.0 1.0 reshape.32
  1.0 0.7 broadcast_in_dim.29
  1.7 6.3 %all-to-all-start.1 = ((f32[8,8,3,200]{3,1,2,0:T(8,128)}), f32[8,8,3,200]{3,1,2,0:T(8,128)S(1)}, u32[]{:S(2)}, u32[]{:S(2)}) async-start(f32[8,8,3,200]{3,1,2,0:T(8,128)} %bitcast.6), calls=%async_computation.1 | async-start | bytes 393216 | tf_op jit(solution)/shard_map/all_to_all | solution.py:118
  8.1 1.0 reshape.29
  9.1 0.9 fusion.1
  10.1 6.3 %all-to-all-done.1 = f32[8,8,3,200]{3,1,2,0:T(8,128)S(1)} async-done(((f32[8,8,3,200]{3,1,2,0:T(8,128)}), f32[8,8,3,200]{3,1,2,0:T(8,128)S(1)}, u32[]{:S(2)}, u32[]{:S(2)}) %all-to-all-start.1) | async-done | bytes 153632 | tf_op jit(solution)/shard_map/all_to_all | solution.py:118
  16.4 0.8 broadcast_in_dim.25
  17.2 4.1 %all-to-all-start = ((f32[8,8,3,400]{3,1,2,0:T(8,128)}), f32[8,8,3,400]{3,1,2,0:T(8,128)}, u32[]{:S(2)}, u32[]{:S(2)}) async-start(f32[8,8,3,400]{3,1,2,0:T(8,128)} %bitcast.2), calls=%async_computation | async-start | bytes 786432 | tf_op jit(solution)/shard_map/all_to_all | solution.py:122
  21.4 0.1 pad_add_fusion.1
  21.5 3.0 %fusion = (s32[400,200]{1,0:T(8,128)S(1)}, s32[400,200]{1,0:T(8,128)S(1)}, s32[400,200]{1,0:T(8,128)}, s32[400,200]{1,0:T(8,128)}) fusion(s32[800,3200]{1,0:T(8,128)} %param.4, s32[]{:T(128)S(6)} %select_n.38, s32[]{:T(128)S(6)} %select_n.39, s32[]{:T(128)S(6)} %select_n.40, s32[]{:T(128)S(6)} %select_n.42, s32[]{:T(128)S(6)} %select_n.41), kind=kLoop, calls=%fused_computation.8 | loop fusion | bytes 2560020 | tf_op jit(solution)/shard_map/dynamic_slice | solution.py:127
  24.5 0.1 copy.19
  24.6 2.5 %collective-permute-start = (f32[64,3,200]{2,1,0:T(4,128)S(1)}, f32[64,3,200]{2,1,0:T(4,128)S(1)}, u32[]{:S(2)}, u32[]{:S(2)}) collective-permute-start(f32[64,3,200]{2,1,0:T(4,128)S(1)} %bitcast.21), channel_id=1, source_target_pairs={{0,3},{1,0},{2,1},{3,2},{4,7},{5,4},{6,5},{7,6},{8,11},{9,8},{10,9... | collective-permute-start | bytes 460808 | tf_op jit(solution)/shard_map/ppermute | solution.py:121
  27.1 0.5 collective-permute-start.1
  27.6 0.6 collective-permute-start.2
  28.2 0.1 pad_add_fusion.2
  28.3 0.8 dynamic_slice.28
  29.1 0.1 copy.20.seg_rows_ref
  29.2 1.7 %pad_add_fusion.counts_ref = s32[400,800]{1,0:T(8,128)S(1)} fusion(s32[400,200]{1,0:T(8,128)} %get-tuple-element.7, s32[400,200]{1,0:T(8,128)} %get-tuple-element.8, s32[400,200]{1,0:T(8,128)S(1)} %get-tuple-element.6, s32[400,200]{1,0:T(8,128)S(1)} %get-tuple-element.5), kind=kLoop, calls=%fused_computation | loop fusion | flops 960000 | bytes 2560000 | tf_op jit(solution)/shard_map/concatenate | solution.py:127
  30.9 3.0 %all-to-all-done = f32[8,8,3,400]{3,1,2,0:T(8,128)} async-done(((f32[8,8,3,400]{3,1,2,0:T(8,128)}), f32[8,8,3,400]{3,1,2,0:T(8,128)}, u32[]{:S(2)}, u32[]{:S(2)}) %all-to-all-start) | async-done | bytes 307232 | tf_op jit(solution)/shard_map/all_to_all | solution.py:122
  33.9 1.3 copy.17
  35.2 0.0 collective-permute-done.rest_1_
  35.2 5.8 %collective-permute-done.1.rest_2_ = f32[64,3,200]{2,1,0:T(4,128)S(1)} collective-permute-done((f32[64,3,200]{2,1,0:T(4,128)S(1)}, f32[64,3,200]{2,1,0:T(4,128)S(1)}, u32[]{:S(2)}, u32[]{:S(2)}) %collective-permute-start.1) | collective-permute-done | bytes 153632 | tf_op jit(solution)/shard_map/ppermute | solution.py:121
  41.0 0.0 collective-permute-done.2.rest_3_
  41.0 103.6 %pairs.1 = f32[64,3,400]{2,1,0:T(4,128)S(1)} custom-call(s32[1]{0:T(128)} %bitcast.row_base_ref, f32[64,3,400]{2,1,0:T(4,128)S(1)} %bitcast.19, s32[400,1]{1,0:T(8,128)S(1)} %copy.20.seg_rows_ref, s32[1,800]{1,0:T(1,128)S(1)} %broadcast_in_dim.27.seg_cols_ref, s32[1,800]{1,0:T(1,128)S(1)} %broadcast_in_dim.28.col_ids_ref, ...), custom_call_target="tpu_custom_call" | custom-call | tf_op jit(solution)/shard_map/pairs/pallas_call | solution.py:134
  144.6 0.1 copy.21
  144.8 17.1 %all_to_all.15 = f32[8,8,3,400]{3,1,2,0:T(8,128)S(1)} all-to-all(f32[8,8,3,400]{3,1,2,0:T(8,128)S(1)} %copy.21), channel_id=1, replica_groups=mesh['ens'=8,'tile'=4] {'ens'}, dimensions={0} | all-to-all | bytes 614400 | tf_op jit(solution)/shard_map/all_to_all | solution.py:148
  161.9 0.1 copy.26
  161.9 0.1 copy.23
  162.0 0.8 reshape.37
  (7 shorter events, 0.1 us)
Async XLA Ops:
  1.7 14.7 %all-to-all-start.1 = ((f32[8,8,3,200]{3,1,2,0:T(8,128)}), f32[8,8,3,200]{3,1,2,0:T(8,128)S(1)}, u32[]{:S(2)}, u32[]{:S(2)}) async-start(f32[8,8,3,200]{3,1,2,0:T(8,128)} %bitcast.6), calls=%async_computation.1 | async-start | bytes 393216 | tf_op jit(solution)/shard_map/all_to_all | solution.py:118
  17.2 16.7 %all-to-all-start = ((f32[8,8,3,400]{3,1,2,0:T(8,128)}), f32[8,8,3,400]{3,1,2,0:T(8,128)}, u32[]{:S(2)}, u32[]{:S(2)}) async-start(f32[8,8,3,400]{3,1,2,0:T(8,128)} %bitcast.2), calls=%async_computation | async-start | bytes 786432 | tf_op jit(solution)/shard_map/all_to_all | solution.py:122
  24.6 10.5 %collective-permute-start = (f32[64,3,200]{2,1,0:T(4,128)S(1)}, f32[64,3,200]{2,1,0:T(4,128)S(1)}, u32[]{:S(2)}, u32[]{:S(2)}) collective-permute-start(f32[64,3,200]{2,1,0:T(4,128)S(1)} %bitcast.21), channel_id=1, source_target_pairs={{0,3},{1,0},{2,1},{3,2},{4,7},{5,4},{6,5},{7,6},{8,11},{9,8},{10,9... | collective-permute-start | bytes 460808 | tf_op jit(solution)/shard_map/ppermute | solution.py:121
  27.1 13.8 %collective-permute-start.1 = (f32[64,3,200]{2,1,0:T(4,128)S(1)}, f32[64,3,200]{2,1,0:T(4,128)S(1)}, u32[]{:S(2)}, u32[]{:S(2)}) collective-permute-start(f32[64,3,200]{2,1,0:T(4,128)S(1)} %bitcast.22), channel_id=1, source_target_pairs={{0,2},{1,3},{2,0},{3,1},{4,6},{5,7},{6,4},{7,5},{8,10},{9,11},{10,... | collective-permute-start | bytes 460808 | tf_op jit(solution)/shard_map/ppermute | solution.py:121
  27.6 13.3 %collective-permute-start.2 = (f32[64,3,200]{2,1,0:T(4,128)S(1)}, f32[64,3,200]{2,1,0:T(4,128)S(1)}, u32[]{:S(2)}, u32[]{:S(2)}) collective-permute-start(f32[64,3,200]{2,1,0:T(4,128)S(1)} %bitcast.23), channel_id=1, source_target_pairs={{0,1},{1,2},{2,3},{3,0},{4,5},{5,6},{6,7},{7,4},{8,9},{9,10},{10,1... | collective-permute-start | bytes 460808 | tf_op jit(solution)/shard_map/ppermute | solution.py:121
where the time goes:
time: 163 us
  Pallas kernels  104 us (64%)
  blocking collectives  17.1 us (10%)
  waiting for transfers between devices  15.1 us (9%)
  starting transfers between devices  14 us (9%)
  local copies, waits for them, and re-layouts  10.9 us (7%)
  other arithmetic  1.87 us (1%)
    pallas_call x1, Pallas kernels, on_device(): pl.pallas_call(functools.partial(pair_kernel, structs, n_tile), out_shape...  104 us
    all_to_all x1, blocking collectives, on_device(): lax.all_to_all(grad.reshape(n_ens, local_n, 3, n_rows), 'ens', 0, 0, tile...  17.1 us
    all_to_all x1, waiting for transfers between devices, on_device(): lax.all_to_all(col_send, 'ens', 0, 0, tiled=True).reshape(structs, 3, piece)  6.34 us
    all_to_all x1, starting transfers between devices, on_device(): lax.all_to_all(col_send, 'ens', 0, 0, tiled=True).reshape(structs, 3, piece)  6.33 us
    ppermute x3, waiting for transfers between devices, on_device(): lax.ppermute(own, 'tile', [(t, (t - k) % n_tile) for t in range(n_tile)])  5.8 us
    all_to_all x1, starting transfers between devices, on_device(): lax.all_to_all(row_send, 'ens', 0, 0, tiled=True)  4.11 us
    ppermute x3, starting transfers between devices, on_device(): lax.ppermute(own, 'tile', [(t, (t - k) % n_tile) for t in range(n_tile)])  3.6 us
  transfers between devices with their start and end apart: 5, of which 3 were waited for; matrix products, arithmetic and copies ran while one was open for 6% of the time, Pallas kernels for 0%

commit v1 on v0

v1 whole, which is shorter than its diff:
```python
import functools

import jax
import jax.numpy as jnp
from jax import lax
from jax.experimental import pallas as pl
from jax.experimental.pallas import tpu as pltpu
from jax.sharding import PartitionSpec as P

LANES = 128
WIDE = 256


def split3(v):
    hi = v.astype(jnp.bfloat16).astype(jnp.float32)
    rest = v - hi
    mid = rest.astype(jnp.bfloat16).astype(jnp.float32)
    return hi, mid, rest - mid


def augment(v, norm_row, one_row):
    n = v.shape[1]
    norm = 1.5 - 0.5 * jnp.sum(v * v, axis=0, keepdims=True)
    v8 = jnp.concatenate([v, jnp.zeros((5, n), jnp.float32)], axis=0)
    row = lax.broadcasted_iota(jnp.int32, (8, n), 0)
    return jnp.where(row == norm_row, norm, jnp.where(row == one_row, 1.0, v8))


def pair_kernel(structs, tiles, base_ref, out_xyz_ref, seg_out_ref, seg_par_ref, par_ids_ref, counts_ref, *rest):
    par_refs = rest[:tiles]
    grad_ref, lhs_ref, rhs_ref, terms_ref, weight_ref = rest[tiles:]
    n_out = out_xyz_ref.shape[2]
    n_par = counts_ref.shape[0]
    wide = weight_ref.shape[1]
    deep = terms_ref.shape[2]
    starts = [(a, min(WIDE, n_par - a)) for a in range(0, n_par, WIDE)]

    def features(s, carry):
        par = [ref[s] for ref in par_refs]
        if deep > n_par:
            par.append(jnp.zeros((3, deep - n_par), jnp.float32))
        hi, mid, lo = split3(augment(jnp.concatenate(par, axis=1), 4, 3))
        left = jnp.concatenate([hi, mid, hi, mid, lo, hi], axis=0)
        lhs_ref[s] = left.T[:n_par].astype(jnp.bfloat16)
        terms_ref[s] = left[0:16].astype(jnp.bfloat16)
        out = out_xyz_ref[s]
        if wide > n_out:
            out = jnp.concatenate([out, jnp.zeros((3, wide - n_out), jnp.float32)], axis=1)
        hi, mid, lo = split3(augment(out, 3, 4))
        rhs_ref[s] = jnp.concatenate([hi, hi, mid, mid, hi, lo], axis=0).astype(jnp.bfloat16)
        return carry

    lax.fori_loop(0, structs, features, 0)
    weight_ref[...] = jnp.zeros_like(weight_ref)

    def tanh_block(s, start, size):
        half = jnp.dot(lhs_ref[s, pl.ds(start, size)], rhs_ref[s], preferred_element_type=jnp.float32)
        return jnp.tanh(half)

    def add_one(s, carry):
        for start, size in starts:
            weight_ref[pl.ds(start, size)] += tanh_block(s, start, size)
        return carry

    lax.fori_loop(0, structs, add_one, 0)

    count = counts_ref[...].astype(jnp.float32)
    target = count / (count + 8.0)
    pbar = 0.5 + (0.5 / structs) * weight_ref[:, pl.ds(0, n_out)]
    out_ids = base_ref[0] + lax.broadcasted_iota(jnp.int32, (n_par, n_out), 1)
    weight = jnp.where(seg_par_ref[...] == seg_out_ref[...], 1.0, 0.3)
    weight = jnp.where(out_ids == par_ids_ref[...], 0.0, weight)
    weight_ref[:, pl.ds(0, n_out)] = weight * (pbar - target)
    if wide > n_out:
        weight_ref[:, pl.ds(n_out, wide - n_out)] = jnp.zeros((n_par, wide - n_out), jnp.float32)

    def grad_one(s, carry):
        total = jnp.zeros((16, wide), jnp.float32)
        for start, size in starts:
            t = tanh_block(s, start, size)
            g = weight_ref[pl.ds(start, size)] * (1.0 - t * t)
            hi = g.astype(jnp.bfloat16)
            lo = (g - hi.astype(jnp.float32)).astype(jnp.bfloat16)
            terms = terms_ref[s, :, pl.ds(start, size)]
            total += jnp.dot(terms, hi, preferred_element_type=jnp.float32)
            total += jnp.dot(terms, lo, preferred_element_type=jnp.float32)
        total = total[:, :n_out]
        mixed = total[0:3] + total[8:11]
        grad_ref[s] = (0.25 / 16) * (mixed - total[3:4] * out_xyz_ref[s])
        return carry

    lax.fori_loop(0, structs, grad_one, 0)


def split_ens(n_ens, beads, tiles):
    best = None
    for parts in range(1, n_ens + 1):
        if n_ens % parts or beads % parts or beads % (n_ens // parts):
            continue
        cost = 2 * (beads // parts) + tiles * (beads // (n_ens // parts))
        if best is None or cost < best[0]:
            best = (cost, parts)
    return best[1]


def on_device(coords, counts, segments):
    local_n, _, beads = coords.shape
    n_tile = lax.axis_size("tile")
    n_ens = lax.axis_size("ens")
    structs = local_n * n_ens
    n_p = split_ens(n_ens, beads, n_tile)
    n_q = n_ens // n_p
    n_rows, piece = beads // n_p, beads // n_q
    n_cols = piece * n_tile
    tile, ens = lax.axis_index("tile"), lax.axis_index("ens")
    p, q = lax.rem(ens, n_p), lax.div(ens, n_p)

    col_send = jnp.moveaxis(coords.reshape(local_n, 3, n_q, piece), 2, 0)
    col_send = jnp.broadcast_to(col_send[:, None], (n_q, n_p, local_n, 3, piece)).reshape(n_ens, local_n, 3, piece)
    row_send = jnp.moveaxis(coords.reshape(local_n, 3, n_p, n_rows), 2, 0)
    row_send = jnp.broadcast_to(row_send[None], (n_q, n_p, local_n, 3, n_rows)).reshape(n_ens, local_n, 3, n_rows)
    own = lax.all_to_all(col_send, "ens", 0, 0, tiled=True).reshape(structs, 3, piece)
    cols = [own]
    for k in range(1, n_tile):
        cols.append(lax.ppermute(own, "tile", [(t, (t - k) % n_tile) for t in range(n_tile)]))
    rows = lax.all_to_all(row_send, "ens", 0, 0, tiled=True).reshape(structs, 3, n_rows)

    row_base = tile * beads + p * n_rows
    col_bases = [lax.rem(tile + k, n_tile) * beads + q * piece for k in range(n_tile)]
    own_counts = lax.dynamic_slice_in_dim(counts, p * n_rows, n_rows, 0)
    block = jnp.concatenate([lax.dynamic_slice_in_dim(own_counts, b, piece, 1) for b in col_bases], axis=1).T
    seg_cols = jnp.concatenate([lax.dynamic_slice_in_dim(segments, b, piece) for b in col_bases])[:, None]
    col_ids = jnp.concatenate([b + jnp.arange(piece, dtype=jnp.int32) for b in col_bases])[:, None]
    seg_rows = lax.dynamic_slice_in_dim(segments, row_base, n_rows)[None, :]

    wide = -(-n_rows // LANES) * LANES
    deep = -(-n_cols // LANES) * LANES
    vmem = pl.BlockSpec(memory_space=pltpu.VMEM)
    grad = pl.pallas_call(
        functools.partial(pair_kernel, structs, n_tile),
        out_shape=jax.ShapeDtypeStruct((structs, 3, n_rows), jnp.float32),
        in_specs=[pl.BlockSpec(memory_space=pltpu.SMEM)] + [vmem] * (5 + n_tile),
        out_specs=vmem,
        scratch_shapes=[
            pltpu.VMEM((structs, n_cols, 48), jnp.bfloat16),
            pltpu.VMEM((structs, 48, wide), jnp.bfloat16),
            pltpu.VMEM((structs, 16, deep), jnp.bfloat16),
            pltpu.VMEM((n_cols, wide), jnp.float32),
        ],
        compiler_params=pltpu.CompilerParams(vmem_limit_bytes=48 << 20),
        name="pairs",
    )(row_base[None], rows, seg_rows, seg_cols, col_ids, block, *cols)

    back = lax.all_to_all(grad.reshape(n_ens, local_n, 3, n_rows), "ens", 0, 0, tiled=True)
    back = jnp.sum(back.reshape(n_q, n_p, local_n, 3, n_rows), axis=0)
    return jnp.moveaxis(back, 0, 2).reshape(local_n, 3, beads)


def solution(mesh):
    return jax.shard_map(
        on_device,
        mesh=mesh,
        in_specs=(P("ens", None, "tile"), P("tile", None), P()),
        out_specs=P("ens", None, "tile"),
        check_vma=False,
    )
```

time: 163 us -> 169 us (1.037)
  Pallas kernels: 104 us -> 107 us
  local copies, waits for them, and re-layouts: 10.9 us -> 13.9 us
    unnamed x1 -> x5, local copies, waits for them, and re-layouts: 0.07 us -> 3.83 us
    pallas_call x1, Pallas kernels: 104 us -> 107 us  [on_device(): pl.pallas_call(functools.partial(pair_kernel, structs, n_tile), out_shape...]
    all_to_all x1, waiting for transfers between devices: 6.34 us -> 4.16 us  [on_device(): lax.all_to_all(col_send, 'ens', 0, 0, tiled=True).reshape(structs, 3, piece)]
    ppermute x3, waiting for transfers between devices: 5.8 us -> 7.77 us  [on_device(): lax.ppermute(own, 'tile', [(t, (t - k) % n_tile) for t in range(n_tile)])]
  transfers between devices with their start and end apart: 5 -> 5, of which waited for: 3 -> 4; matrix products, arithmetic and copies ran while one was open for 6% -> 7% of each run, Pallas kernels for 0% -> 0%
where the time goes in v1:
time: 169 us; the launch traced here: 168 us
  Pallas kernels  107 us (63%)
  blocking collectives  17.1 us (10%)
  waiting for transfers between devices  14.2 us (8%)
  starting transfers between devices  14 us (8%)
  local copies, waits for them, and re-layouts  13.9 us (8%)
  other arithmetic  1.7 us (1%)
    pallas_call x1, Pallas kernels, on_device(): pl.pallas_call(functools.partial(pair_kernel, structs, n_tile), out_shape...  107 us
    all_to_all x1, blocking collectives, on_device(): lax.all_to_all(grad.reshape(n_ens, local_n, 3, n_rows), 'ens', 0, 0, tile...  17.1 us
    ppermute x3, waiting for transfers between devices, on_device(): lax.ppermute(own, 'tile', [(t, (t - k) % n_tile) for t in range(n_tile)])  7.77 us
    all_to_all x1, starting transfers between devices, on_device(): lax.all_to_all(col_send, 'ens', 0, 0, tiled=True).reshape(structs, 3, piece)  6.33 us
    all_to_all x1, waiting for transfers between devices, on_device(): lax.all_to_all(col_send, 'ens', 0, 0, tiled=True).reshape(structs, 3, piece)  4.16 us
    all_to_all x1, starting transfers between devices, on_device(): lax.all_to_all(row_send, 'ens', 0, 0, tiled=True)  4.09 us
    unnamed x5, local copies, waits for them, and re-layouts  3.83 us
    ppermute x3, starting transfers between devices, on_device(): lax.ppermute(own, 'tile', [(t, (t - k) % n_tile) for t in range(n_tile)])  3.61 us
  transfers between devices with their start and end apart: 5, of which 4 were waited for; matrix products, arithmetic and copies ran while one was open for 7% of the time, Pallas kernels for 0%

profile of v1, /device:TPU:0, one launch (start us, length us, event | category | flops | bytes accessed | tf_op | source)
XLA Modules:
  0.0 168.0 jit_solution(17313774027574933043)
XLA Ops:
  0.0 1.0 reshape.32
  1.0 0.7 broadcast_in_dim.29
  1.7 6.3 %all-to-all-start.1 = ((f32[8,8,3,200]{3,1,2,0:T(8,128)}), f32[8,8,3,200]{3,1,2,0:T(8,128)S(1)}, u32[]{:S(2)}, u32[]{:S(2)}) async-start(f32[8,8,3,200]{3,1,2,0:T(8,128)} %bitcast.7), calls=%async_computation.1 | async-start | bytes 393216 | tf_op jit(solution)/shard_map/all_to_all | solution.py:122
  8.1 1.0 reshape.29
  9.2 0.9 fusion.1
  10.1 2.2 %fusion = (s32[400,200]{1,0:T(8,128)S(1)}, s32[400,200]{1,0:T(8,128)S(1)}, s32[400,200]{1,0:T(8,128)S(1)}, s32[400,200]{1,0:T(8,128)S(1)}) fusion(s32[800,3200]{1,0:T(8,128)} %param.4, s32[]{:T(128)S(6)} %select_n.38, s32[]{:T(128)S(6)} %select_n.39, s32[]{:T(128)S(6)} %select_n.41, s32[]{:T(128)S(6)} %select_n.40, s32[]{:T(128)S(6)} %select_n.42), kind=kLoop, calls=%fused_computation.8 | loop fusion | bytes 2560020 | tf_op jit(solution)/shard_map/dynamic_slice | solution.py:131
  12.2 4.2 %all-to-all-done.1 = f32[8,8,3,200]{3,1,2,0:T(8,128)S(1)} async-done(((f32[8,8,3,200]{3,1,2,0:T(8,128)}), f32[8,8,3,200]{3,1,2,0:T(8,128)S(1)}, u32[]{:S(2)}, u32[]{:S(2)}) %all-to-all-start.1) | async-done | bytes 153632 | tf_op jit(solution)/shard_map/all_to_all | solution.py:122
  16.4 0.8 broadcast_in_dim.25
  17.2 4.1 %all-to-all-start = ((f32[8,8,3,400]{3,1,2,0:T(8,128)}), f32[8,8,3,400]{3,1,2,0:T(8,128)}, u32[]{:S(2)}, u32[]{:S(2)}) async-start(f32[8,8,3,400]{3,1,2,0:T(8,128)} %bitcast.2), calls=%async_computation | async-start | bytes 786432 | tf_op jit(solution)/shard_map/all_to_all | solution.py:126
  21.3 0.1 pad_add_fusion
  21.4 1.0 copy.44
  22.3 0.9 copy.45
  23.3 0.9 copy.46
  24.2 0.9 copy.47
  25.1 0.2 broadcast_in_dim.30.seg_par_ref
  25.3 0.1 pad_add_fusion.1
  25.4 0.2 broadcast_in_dim.31.par_ids_ref
  25.6 0.8 dynamic_slice.28
  26.3 0.1 copy.37
  26.4 2.5 %collective-permute-start = (f32[64,3,200]{2,1,0:T(4,128)S(1)}, f32[64,3,200]{2,1,0:T(4,128)S(1)}, u32[]{:S(2)}, u32[]{:S(2)}) collective-permute-start(f32[64,3,200]{2,1,0:T(4,128)S(1)} %bitcast.23), channel_id=1, source_target_pairs={{0,3},{1,0},{2,1},{3,2},{4,7},{5,4},{6,5},{7,6},{8,11},{9,8},{10,9... | collective-permute-start | bytes 460808 | tf_op jit(solution)/shard_map/ppermute | solution.py:125
  29.0 0.5 collective-permute-start.1
  29.5 0.6 collective-permute-start.2
  30.1 1.5 add_bitcast_fusion.counts_ref
  31.6 2.3 %all-to-all-done = f32[8,8,3,400]{3,1,2,0:T(8,128)} async-done(((f32[8,8,3,400]{3,1,2,0:T(8,128)}), f32[8,8,3,400]{3,1,2,0:T(8,128)}, u32[]{:S(2)}, u32[]{:S(2)}) %all-to-all-start) | async-done | bytes 307232 | tf_op jit(solution)/shard_map/all_to_all | solution.py:126
  33.8 1.3 copy.31
  35.1 0.5 collective-permute-done.rest_1_
  35.6 7.2 %collective-permute-done.1.rest_2_ = f32[64,3,200]{2,1,0:T(4,128)S(1)} collective-permute-done((f32[64,3,200]{2,1,0:T(4,128)S(1)}, f32[64,3,200]{2,1,0:T(4,128)S(1)}, u32[]{:S(2)}, u32[]{:S(2)}) %collective-permute-start.1) | collective-permute-done | bytes 153632 | tf_op jit(solution)/shard_map/ppermute | solution.py:125
  42.9 106.9 %pairs.1 = f32[64,3,400]{2,1,0:T(4,128)S(1)} custom-call(s32[1]{0:T(128)} %bitcast.base_ref, f32[64,3,400]{2,1,0:T(4,128)S(1)} %bitcast.21, s32[1,400]{1,0:T(1,128)S(1)} %bitcast.27, s32[800,1]{1,0:T(8,128)S(1)} %broadcast_in_dim.30.seg_par_ref, s32[800,1]{1,0:T(8,128)S(1)} %broadcast_in_dim.31.par_ids_ref, s32[800,400]{1,0:T(8,128)S(1)} %add_bitcast_fusion.counts_ref, ...), custom_call_target="tpu_custom_call" | custom-call | tf_op jit(solution)/shard_map/pairs/pallas_call | solution.py:139
  149.8 0.1 copy.40
  149.9 17.1 %all_to_all.15 = f32[8,8,3,400]{3,1,2,0:T(8,128)S(1)} all-to-all(f32[8,8,3,400]{3,1,2,0:T(8,128)S(1)} %copy.40), channel_id=1, replica_groups=mesh['ens'=8,'tile'=4] {'ens'}, dimensions={0} | all-to-all | bytes 614400 | tf_op jit(solution)/shard_map/all_to_all | solution.py:154
  167.1 0.1 copy.42
  167.2 0.8 reshape.37
  (7 shorter events, 0.2 us)
Async XLA Ops:
  1.7 14.7 %all-to-all-start.1 = ((f32[8,8,3,200]{3,1,2,0:T(8,128)}), f32[8,8,3,200]{3,1,2,0:T(8,128)S(1)}, u32[]{:S(2)}, u32[]{:S(2)}) async-start(f32[8,8,3,200]{3,1,2,0:T(8,128)} %bitcast.7), calls=%async_computation.1 | async-start | bytes 393216 | tf_op jit(solution)/shard_map/all_to_all | solution.py:122
  17.2 16.7 %all-to-all-start = ((f32[8,8,3,400]{3,1,2,0:T(8,128)}), f32[8,8,3,400]{3,1,2,0:T(8,128)}, u32[]{:S(2)}, u32[]{:S(2)}) async-start(f32[8,8,3,400]{3,1,2,0:T(8,128)} %bitcast.2), calls=%async_computation | async-start | bytes 786432 | tf_op jit(solution)/shard_map/all_to_all | solution.py:126
  26.4 9.2 %collective-permute-start = (f32[64,3,200]{2,1,0:T(4,128)S(1)}, f32[64,3,200]{2,1,0:T(4,128)S(1)}, u32[]{:S(2)}, u32[]{:S(2)}) collective-permute-start(f32[64,3,200]{2,1,0:T(4,128)S(1)} %bitcast.23), channel_id=1, source_target_pairs={{0,3},{1,0},{2,1},{3,2},{4,7},{5,4},{6,5},{7,6},{8,11},{9,8},{10,9... | collective-permute-start | bytes 460808 | tf_op jit(solution)/shard_map/ppermute | solution.py:125
  29.0 13.9 %collective-permute-start.1 = (f32[64,3,200]{2,1,0:T(4,128)S(1)}, f32[64,3,200]{2,1,0:T(4,128)S(1)}, u32[]{:S(2)}, u32[]{:S(2)}) collective-permute-start(f32[64,3,200]{2,1,0:T(4,128)S(1)} %bitcast.24), channel_id=1, source_target_pairs={{0,2},{1,3},{2,0},{3,1},{4,6},{5,7},{6,4},{7,5},{8,10},{9,11},{10,... | collective-permute-start | bytes 460808 | tf_op jit(solution)/shard_map/ppermute | solution.py:125
  29.5 13.4 %collective-permute-start.2 = (f32[64,3,200]{2,1,0:T(4,128)S(1)}, f32[64,3,200]{2,1,0:T(4,128)S(1)}, u32[]{:S(2)}, u32[]{:S(2)}) collective-permute-start(f32[64,3,200]{2,1,0:T(4,128)S(1)} %bitcast.25), channel_id=1, source_target_pairs={{0,1},{1,2},{2,3},{3,0},{4,5},{5,6},{6,7},{7,4},{8,9},{9,10},{10,1... | collective-permute-start | bytes 460808 | tf_op jit(solution)/shard_map/ppermute | solution.py:125

commit v2 on v1

--- a/solution.py
+++ b/solution.py
@@ -50,7 +50,7 @@
         rhs_ref[s] = jnp.concatenate([hi, hi, mid, mid, hi, lo], axis=0).astype(jnp.bfloat16)
         return carry
 
-    lax.fori_loop(0, structs, features, 0)
+    lax.fori_loop(0, structs, features, 0, unroll=4)
     weight_ref[...] = jnp.zeros_like(weight_ref)
 
     def tanh_block(s, start, size):
@@ -62,7 +62,7 @@
             weight_ref[pl.ds(start, size)] += tanh_block(s, start, size)
         return carry
 
-    lax.fori_loop(0, structs, add_one, 0)
+    lax.fori_loop(0, structs, add_one, 0, unroll=4)
 
     count = counts_ref[...].astype(jnp.float32)
     target = count / (count + 8.0)
@@ -89,7 +89,7 @@
         grad_ref[s] = (0.25 / 16) * (mixed - total[3:4] * out_xyz_ref[s])
         return carry
 
-    lax.fori_loop(0, structs, grad_one, 0)
+    lax.fori_loop(0, structs, grad_one, 0, unroll=2)
 
 
 def split_ens(n_ens, beads, tiles):

time: 169 us -> 150 us (0.89)
  Pallas kernels: 107 us -> 88.5 us
    pallas_call x1, Pallas kernels: 107 us -> 88.5 us  [on_device(): pl.pallas_call(functools.partial(pair_kernel, structs, n_tile), out_shape...]
  transfers between devices with their start and end apart: 5 -> 5, of which waited for: 4 -> 4; matrix products, arithmetic and copies ran while one was open for 7% -> 8% of each run, Pallas kernels for 0% -> 0%
where the time goes in v2:
time: 150 us
  Pallas kernels  88.5 us (59%)
  blocking collectives  17.1 us (11%)
  waiting for transfers between devices  14.2 us (9%)
  starting transfers between devices  14 us (9%)
  local copies, waits for them, and re-layouts  13.9 us (9%)
  other arithmetic  1.7 us (1%)
    pallas_call x1, Pallas kernels, on_device(): pl.pallas_call(functools.partial(pair_kernel, structs, n_tile), out_shape...  88.5 us
    all_to_all x1, blocking collectives, on_device(): lax.all_to_all(grad.reshape(n_ens, local_n, 3, n_rows), 'ens', 0, 0, tile...  17.1 us
    ppermute x3, waiting for transfers between devices, on_device(): lax.ppermute(own, 'tile', [(t, (t - k) % n_tile) for t in range(n_tile)])  7.77 us
    all_to_all x1, starting transfers between devices, on_device(): lax.all_to_all(col_send, 'ens', 0, 0, tiled=True).reshape(structs, 3, piece)  6.33 us
    all_to_all x1, waiting for transfers between devices, on_device(): lax.all_to_all(col_send, 'ens', 0, 0, tiled=True).reshape(structs, 3, piece)  4.16 us
    all_to_all x1, starting transfers between devices, on_device(): lax.all_to_all(row_send, 'ens', 0, 0, tiled=True)  4.09 us
    unnamed x5, local copies, waits for them, and re-layouts  3.83 us
    ppermute x3, starting transfers between devices, on_device(): lax.ppermute(own, 'tile', [(t, (t - k) % n_tile) for t in range(n_tile)])  3.61 us
  transfers between devices with their start and end apart: 5, of which 4 were waited for; matrix products, arithmetic and copies ran while one was open for 8% of the time, Pallas kernels for 0%

profile of v2, /device:TPU:0, one launch (start us, length us, event | category | flops | bytes accessed | tf_op | source)
XLA Modules:
  0.0 149.7 jit_solution(1289077552662463341)
XLA Ops:
  0.0 1.0 reshape.32
  1.0 0.7 broadcast_in_dim.29
  1.7 6.3 %all-to-all-start.1 = ((f32[8,8,3,200]{3,1,2,0:T(8,128)}), f32[8,8,3,200]{3,1,2,0:T(8,128)S(1)}, u32[]{:S(2)}, u32[]{:S(2)}) async-start(f32[8,8,3,200]{3,1,2,0:T(8,128)} %bitcast.7), calls=%async_computation.1 | async-start | bytes 393216 | tf_op jit(solution)/shard_map/all_to_all | solution.py:122
  8.1 1.0 reshape.29
  9.2 0.9 fusion.1
  10.1 2.2 %fusion = (s32[400,200]{1,0:T(8,128)S(1)}, s32[400,200]{1,0:T(8,128)S(1)}, s32[400,200]{1,0:T(8,128)S(1)}, s32[400,200]{1,0:T(8,128)S(1)}) fusion(s32[800,3200]{1,0:T(8,128)} %param.4, s32[]{:T(128)S(6)} %select_n.38, s32[]{:T(128)S(6)} %select_n.39, s32[]{:T(128)S(6)} %select_n.41, s32[]{:T(128)S(6)} %select_n.40, s32[]{:T(128)S(6)} %select_n.42), kind=kLoop, calls=%fused_computation.8 | loop fusion | bytes 2560020 | tf_op jit(solution)/shard_map/dynamic_slice | solution.py:131
  12.2 4.2 %all-to-all-done.1 = f32[8,8,3,200]{3,1,2,0:T(8,128)S(1)} async-done(((f32[8,8,3,200]{3,1,2,0:T(8,128)}), f32[8,8,3,200]{3,1,2,0:T(8,128)S(1)}, u32[]{:S(2)}, u32[]{:S(2)}) %all-to-all-start.1) | async-done | bytes 153632 | tf_op jit(solution)/shard_map/all_to_all | solution.py:122
  16.4 0.8 broadcast_in_dim.25
  17.2 4.1 %all-to-all-start = ((f32[8,8,3,400]{3,1,2,0:T(8,128)}), f32[8,8,3,400]{3,1,2,0:T(8,128)}, u32[]{:S(2)}, u32[]{:S(2)}) async-start(f32[8,8,3,400]{3,1,2,0:T(8,128)} %bitcast.2), calls=%async_computation | async-start | bytes 786432 | tf_op jit(solution)/shard_map/all_to_all | solution.py:126
  21.3 0.1 pad_add_fusion
  21.4 1.0 copy.44
  22.3 0.9 copy.45
  23.3 0.9 copy.46
  24.2 0.9 copy.47
  25.1 0.2 broadcast_in_dim.30.seg_par_ref
  25.3 0.1 pad_add_fusion.1
  25.4 0.2 broadcast_in_dim.31.par_ids_ref
  25.6 0.8 dynamic_slice.28
  26.3 0.1 copy.37
  26.4 2.5 %collective-permute-start = (f32[64,3,200]{2,1,0:T(4,128)S(1)}, f32[64,3,200]{2,1,0:T(4,128)S(1)}, u32[]{:S(2)}, u32[]{:S(2)}) collective-permute-start(f32[64,3,200]{2,1,0:T(4,128)S(1)} %bitcast.23), channel_id=1, source_target_pairs={{0,3},{1,0},{2,1},{3,2},{4,7},{5,4},{6,5},{7,6},{8,11},{9,8},{10,9... | collective-permute-start | bytes 460808 | tf_op jit(solution)/shard_map/ppermute | solution.py:125
  29.0 0.5 collective-permute-start.1
  29.5 0.6 collective-permute-start.2
  30.1 1.5 %add_bitcast_fusion.counts_ref = s32[800,400]{1,0:T(8,128)S(1)} fusion(s32[400,200]{0,1:T(8,128)} %copy.47, s32[400,200]{0,1:T(8,128)} %copy.46, s32[400,200]{0,1:T(8,128)} %copy.45, s32[400,200]{0,1:T(8,128)} %copy.44), kind=kLoop, calls=%fused_computation | loop fusion | flops 960000 | bytes 2560000 | tf_op jit(solution)/shard_map/transpose | solution.py:131
  31.6 2.3 %all-to-all-done = f32[8,8,3,400]{3,1,2,0:T(8,128)} async-done(((f32[8,8,3,400]{3,1,2,0:T(8,128)}), f32[8,8,3,400]{3,1,2,0:T(8,128)}, u32[]{:S(2)}, u32[]{:S(2)}) %all-to-all-start) | async-done | bytes 307232 | tf_op jit(solution)/shard_map/all_to_all | solution.py:126
  33.8 1.3 copy.31
  35.1 0.5 collective-permute-done.rest_1_
  35.6 7.2 %collective-permute-done.1.rest_2_ = f32[64,3,200]{2,1,0:T(4,128)S(1)} collective-permute-done((f32[64,3,200]{2,1,0:T(4,128)S(1)}, f32[64,3,200]{2,1,0:T(4,128)S(1)}, u32[]{:S(2)}, u32[]{:S(2)}) %collective-permute-start.1) | collective-permute-done | bytes 153632 | tf_op jit(solution)/shard_map/ppermute | solution.py:125
  42.9 88.5 %pairs.1 = f32[64,3,400]{2,1,0:T(4,128)S(1)} custom-call(s32[1]{0:T(128)} %bitcast.base_ref, f32[64,3,400]{2,1,0:T(4,128)S(1)} %bitcast.21, s32[1,400]{1,0:T(1,128)S(1)} %bitcast.27, s32[800,1]{1,0:T(8,128)S(1)} %broadcast_in_dim.30.seg_par_ref, s32[800,1]{1,0:T(8,128)S(1)} %broadcast_in_dim.31.par_ids_ref, s32[800,400]{1,0:T(8,128)S(1)} %add_bitcast_fusion.counts_ref, ...), custom_call_target="tpu_custom_call" | custom-call | tf_op jit(solution)/shard_map/pairs/pallas_call | solution.py:139
  131.4 0.1 copy.40
  131.5 17.1 %all_to_all.15 = f32[8,8,3,400]{3,1,2,0:T(8,128)S(1)} all-to-all(f32[8,8,3,400]{3,1,2,0:T(8,128)S(1)} %copy.40), channel_id=1, replica_groups=mesh['ens'=8,'tile'=4] {'ens'}, dimensions={0} | all-to-all | bytes 614400 | tf_op jit(solution)/shard_map/all_to_all | solution.py:154
  148.8 0.1 copy.42
  148.9 0.8 reshape.37
  (7 shorter events, 0.2 us)
Async XLA Ops:
  1.7 14.7 %all-to-all-start.1 = ((f32[8,8,3,200]{3,1,2,0:T(8,128)}), f32[8,8,3,200]{3,1,2,0:T(8,128)S(1)}, u32[]{:S(2)}, u32[]{:S(2)}) async-start(f32[8,8,3,200]{3,1,2,0:T(8,128)} %bitcast.7), calls=%async_computation.1 | async-start | bytes 393216 | tf_op jit(solution)/shard_map/all_to_all | solution.py:122
  17.2 16.7 %all-to-all-start = ((f32[8,8,3,400]{3,1,2,0:T(8,128)}), f32[8,8,3,400]{3,1,2,0:T(8,128)}, u32[]{:S(2)}, u32[]{:S(2)}) async-start(f32[8,8,3,400]{3,1,2,0:T(8,128)} %bitcast.2), calls=%async_computation | async-start | bytes 786432 | tf_op jit(solution)/shard_map/all_to_all | solution.py:126
  26.4 9.2 %collective-permute-start = (f32[64,3,200]{2,1,0:T(4,128)S(1)}, f32[64,3,200]{2,1,0:T(4,128)S(1)}, u32[]{:S(2)}, u32[]{:S(2)}) collective-permute-start(f32[64,3,200]{2,1,0:T(4,128)S(1)} %bitcast.23), channel_id=1, source_target_pairs={{0,3},{1,0},{2,1},{3,2},{4,7},{5,4},{6,5},{7,6},{8,11},{9,8},{10,9... | collective-permute-start | bytes 460808 | tf_op jit(solution)/shard_map/ppermute | solution.py:125
  29.0 13.9 %collective-permute-start.1 = (f32[64,3,200]{2,1,0:T(4,128)S(1)}, f32[64,3,200]{2,1,0:T(4,128)S(1)}, u32[]{:S(2)}, u32[]{:S(2)}) collective-permute-start(f32[64,3,200]{2,1,0:T(4,128)S(1)} %bitcast.24), channel_id=1, source_target_pairs={{0,2},{1,3},{2,0},{3,1},{4,6},{5,7},{6,4},{7,5},{8,10},{9,11},{10,... | collective-permute-start | bytes 460808 | tf_op jit(solution)/shard_map/ppermute | solution.py:125
  29.5 13.4 %collective-permute-start.2 = (f32[64,3,200]{2,1,0:T(4,128)S(1)}, f32[64,3,200]{2,1,0:T(4,128)S(1)}, u32[]{:S(2)}, u32[]{:S(2)}) collective-permute-start(f32[64,3,200]{2,1,0:T(4,128)S(1)} %bitcast.25), channel_id=1, source_target_pairs={{0,1},{1,2},{2,3},{3,0},{4,5},{5,6},{6,7},{7,4},{8,9},{9,10},{10,1... | collective-permute-start | bytes 460808 | tf_op jit(solution)/shard_map/ppermute | solution.py:125

commit v3 on v2

v3 whole, which is shorter than its diff:
```python
import functools

import jax
import jax.numpy as jnp
from jax import lax
from jax.experimental import pallas as pl
from jax.experimental.pallas import tpu as pltpu
from jax.sharding import PartitionSpec as P

LANES = 128
WIDE = 256


def split3(v):
    hi = v.astype(jnp.bfloat16).astype(jnp.float32)
    rest = v - hi
    mid = rest.astype(jnp.bfloat16).astype(jnp.float32)
    return hi, mid, rest - mid


def augment(v, norm_row, one_row):
    n = v.shape[1]
    norm = 1.5 - 0.5 * jnp.sum(v * v, axis=0, keepdims=True)
    v8 = jnp.concatenate([v, jnp.zeros((5, n), jnp.float32)], axis=0)
    row = lax.broadcasted_iota(jnp.int32, (8, n), 0)
    return jnp.where(row == norm_row, norm, jnp.where(row == one_row, 1.0, v8))


def pair_kernel(n_groups, n_mix, n_out_refs, base_ref, seg_out_ref, seg_par_ref, par_ids_ref, counts_ref, *rest):
    n_par_refs = len(rest) - 2 * n_out_refs - 6
    out_refs, rest = rest[:n_out_refs], rest[n_out_refs:]
    par_refs, rest = rest[:n_par_refs], rest[n_par_refs:]
    grad_refs, (xyz_ref, grad_ref, lhs_ref, rhs_ref, terms_ref, weight_ref) = rest[:n_out_refs], rest[n_out_refs:]
    structs, _, n_out = xyz_ref.shape
    per = structs // n_groups
    block = structs // n_out_refs
    n_par = counts_ref.shape[0]
    wide = weight_ref.shape[1]
    deep = terms_ref.shape[2]
    starts = [(a, min(WIDE, n_par - a)) for a in range(0, n_par, WIDE)]

    for r, ref in enumerate(out_refs):
        xyz_ref[pl.ds(r * block, block)] = ref[...]

    def features(s, carry):
        group, inside = lax.div(s, per), lax.rem(s, per)
        par = [ref[(group ^ (j % n_mix)) * per + inside] for j, ref in enumerate(par_refs)]
        if deep > n_par:
            par.append(jnp.zeros((3, deep - n_par), jnp.float32))
        hi, mid, lo = split3(augment(jnp.concatenate(par, axis=1), 4, 3))
        left = jnp.concatenate([hi, mid, hi, mid, lo, hi], axis=0)
        lhs_ref[s] = left.T[:n_par].astype(jnp.bfloat16)
        terms_ref[s] = left[0:16].astype(jnp.bfloat16)
        out = xyz_ref[s]
        if wide > n_out:
            out = jnp.concatenate([out, jnp.zeros((3, wide - n_out), jnp.float32)], axis=1)
        hi, mid, lo = split3(augment(out, 3, 4))
        rhs_ref[s] = jnp.concatenate([hi, hi, mid, mid, hi, lo], axis=0).astype(jnp.bfloat16)
        return carry

    lax.fori_loop(0, structs, features, 0, unroll=4)
    weight_ref[...] = jnp.zeros_like(weight_ref)

    def tanh_block(s, start, size):
        half = jnp.dot(lhs_ref[s, pl.ds(start, size)], rhs_ref[s], preferred_element_type=jnp.float32)
        return jnp.tanh(half)

    def add_one(s, carry):
        for start, size in starts:
            weight_ref[pl.ds(start, size)] += tanh_block(s, start, size)
        return carry

    lax.fori_loop(0, structs, add_one, 0, unroll=4)

    count = counts_ref[...].astype(jnp.float32)
    target = count / (count + 8.0)
    pbar = 0.5 + (0.5 / structs) * weight_ref[:, pl.ds(0, n_out)]
    out_ids = base_ref[0] + lax.broadcasted_iota(jnp.int32, (n_par, n_out), 1)
    weight = jnp.where(seg_par_ref[...] == seg_out_ref[...], 1.0, 0.3)
    weight = jnp.where(out_ids == par_ids_ref[...], 0.0, weight)
    weight_ref[:, pl.ds(0, n_out)] = weight * (pbar - target)
    if wide > n_out:
        weight_ref[:, pl.ds(n_out, wide - n_out)] = jnp.zeros((n_par, wide - n_out), jnp.float32)

    def grad_one(s, carry):
        total = jnp.zeros((16, wide), jnp.float32)
        for start, size in starts:
            t = tanh_block(s, start, size)
            g = weight_ref[pl.ds(start, size)] * (1.0 - t * t)
            hi = g.astype(jnp.bfloat16)
            lo = (g - hi.astype(jnp.float32)).astype(jnp.bfloat16)
            terms = terms_ref[s, :, pl.ds(start, size)]
            total += jnp.dot(terms, hi, preferred_element_type=jnp.float32)
            total += jnp.dot(terms, lo, preferred_element_type=jnp.float32)
        total = total[:, :n_out]
        grad_ref[s] = (0.25 / 16) * (total[0:3] + total[8:11] - total[3:4] * xyz_ref[s])
        return carry

    lax.fori_loop(0, structs, grad_one, 0, unroll=2)
    for r, ref in enumerate(grad_refs):
        ref[...] = grad_ref[pl.ds(r * block, block)]


def split_ens(n_ens, beads, tiles):
    best = None
    for parts in range(1, n_ens + 1):
        if n_ens % parts or beads % parts or beads % (n_ens // parts):
            continue
        cost = 2 * (beads // parts) + tiles * (beads // (n_ens // parts))
        if best is None or cost < best[0]:
            best = (cost, parts)
    return best[1]


def pair_gradients(out_list, par_list, par_bases, out_base, counts, segments, p, n_groups, n_mix):
    n_out, chunk = out_list[0].shape[2], par_list[0].shape[2]
    n_par = chunk * len(par_list)
    structs = par_list[0].shape[0]
    own_counts = lax.dynamic_slice_in_dim(counts, p * n_out, n_out, 0)
    block = jnp.concatenate([lax.dynamic_slice_in_dim(own_counts, b, chunk, 1) for b in par_bases], axis=1).T
    seg_par = jnp.concatenate([lax.dynamic_slice_in_dim(segments, b, chunk) for b in par_bases])[:, None]
    par_ids = jnp.concatenate([b + jnp.arange(chunk, dtype=jnp.int32) for b in par_bases])[:, None]
    seg_out = lax.dynamic_slice_in_dim(segments, out_base, n_out)[None, :]
    wide = -(-n_out // LANES) * LANES
    deep = -(-n_par // LANES) * LANES
    vmem = pl.BlockSpec(memory_space=pltpu.VMEM)
    return pl.pallas_call(
        functools.partial(pair_kernel, n_groups, n_mix, len(out_list)),
        out_shape=[jax.ShapeDtypeStruct(x.shape, jnp.float32) for x in out_list],
        in_specs=[pl.BlockSpec(memory_space=pltpu.SMEM)] + [vmem] * (4 + len(out_list) + len(par_list)),
        out_specs=[vmem] * len(out_list),
        scratch_shapes=[
            pltpu.VMEM((structs, 3, n_out), jnp.float32),
            pltpu.VMEM((structs, 3, n_out), jnp.float32),
            pltpu.VMEM((structs, n_par, 48), jnp.bfloat16),
            pltpu.VMEM((structs, 48, wide), jnp.bfloat16),
            pltpu.VMEM((structs, 16, deep), jnp.bfloat16),
            pltpu.VMEM((n_par, wide), jnp.float32),
        ],
        compiler_params=pltpu.CompilerParams(vmem_limit_bytes=48 << 20),
        name="pairs",
    )(out_base[None], seg_out, seg_par, par_ids, block, *out_list, *par_list)


def swap(x, axes, size, flip):
    return lax.ppermute(x, axes, [(i, flip(i)) for i in range(size)])


def by_permutes(coords, counts, segments, n_p, n_q, n_tile):
    local_n, _, beads = coords.shape
    n_ens, n_layer = n_p * n_q, n_p * n_tile
    n_out, chunk = beads // n_p, beads // n_ens
    tile, ens = lax.axis_index("tile"), lax.axis_index("ens")
    p, q = lax.rem(ens, n_p), lax.div(ens, n_p)
    halves = [lax.dynamic_slice_in_dim(coords, (p ^ h) * n_out, n_out, 2) for h in range(n_p)]
    out_list = [halves[0]] + [None] * (n_ens - 1)
    for k in reversed(range(1, n_ens)):
        out_list[k] = swap(halves[k % n_p], "ens", n_ens, lambda e, k=k: e ^ k)
    own = jnp.concatenate([lax.dynamic_slice_in_dim(x, q * chunk, chunk, 2) for x in out_list], axis=0)

    def layer_flip(r):
        dt, dp = divmod(r, n_p)

        def flip(i):
            e, t = divmod(i, n_tile)
            return (e ^ dp) * n_tile + (t ^ dt)

        return flip

    par_list = [own] + [None] * (n_layer - 1)
    par_bases = []
    for r in range(n_layer):
        par_bases.append((tile ^ (r // n_p)) * beads + (p ^ (r % n_p)) * n_out + q * chunk)
    for r in reversed(range(1, n_layer)):
        par_list[r] = swap(own, ("ens", "tile"), n_ens * n_tile, layer_flip(r))

    out_base = tile * beads + p * n_out
    grads = pair_gradients(out_list, par_list, par_bases, out_base, counts, segments, p, n_ens, n_p)
    back = [grads[0]] + [None] * (n_ens - 1)
    for k in reversed(range(1, n_ens)):
        back[k] = swap(grads[k], "ens", n_ens, lambda e, k=k: e ^ k)
    sums = [functools.reduce(jnp.add, back[h::n_p]) for h in range(n_p)]
    if n_p == 1:
        return sums[0]
    if n_p == 2:
        parts = [jnp.where(p == h, sums[0], sums[1]) for h in range(2)]
    else:
        stacked = jnp.stack(sums)
        parts = [lax.dynamic_index_in_dim(stacked, p ^ h, 0, keepdims=False) for h in range(n_p)]
    return jnp.concatenate(parts, axis=2)


def by_all_to_all(coords, counts, segments, n_p, n_q, n_tile):
    local_n, _, beads = coords.shape
    n_ens = n_p * n_q
    structs = local_n * n_ens
    n_out, piece = beads // n_p, beads // n_q
    tile, ens = lax.axis_index("tile"), lax.axis_index("ens")
    p, q = lax.rem(ens, n_p), lax.div(ens, n_p)
    par_send = jnp.moveaxis(coords.reshape(local_n, 3, n_q, piece), 2, 0)
    par_send = jnp.broadcast_to(par_send[:, None], (n_q, n_p, local_n, 3, piece)).reshape(n_ens, local_n, 3, piece)
    out_send = jnp.moveaxis(coords.reshape(local_n, 3, n_p, n_out), 2, 0)
    out_send = jnp.broadcast_to(out_send[None], (n_q, n_p, local_n, 3, n_out)).reshape(n_ens, local_n, 3, n_out)
    own = lax.all_to_all(par_send, "ens", 0, 0, tiled=True).reshape(structs, 3, piece)
    par_list = [own]
    for k in range(1, n_tile):
        par_list.append(lax.ppermute(own, "tile", [(t, (t - k) % n_tile) for t in range(n_tile)]))
    par_bases = [lax.rem(tile + k, n_tile) * beads + q * piece for k in range(n_tile)]
    out = lax.all_to_all(out_send, "ens", 0, 0, tiled=True).reshape(structs, 3, n_out)
    out_base = tile * beads + p * n_out
    (grad,) = pair_gradients([out], par_list, par_bases, out_base, counts, segments, p, n_ens, 1)
    back = lax.all_to_all(grad.reshape(n_ens, local_n, 3, n_out), "ens", 0, 0, tiled=True)
    back = jnp.sum(back.reshape(n_q, n_p, local_n, 3, n_out), axis=0)
    return jnp.moveaxis(back, 0, 2).reshape(local_n, 3, beads)


def power_of_two(n):
    return n & (n - 1) == 0


def on_device(coords, counts, segments):
    beads = coords.shape[2]
    n_tile, n_ens = lax.axis_size("tile"), lax.axis_size("ens")
    n_p = split_ens(n_ens, beads, n_tile)
    n_q = n_ens // n_p
    few = n_ens * n_tile <= 64 and beads % n_ens == 0 and power_of_two(n_ens) and power_of_two(n_tile)
    return (by_permutes if few else by_all_to_all)(coords, counts, segments, n_p, n_q, n_tile)


def solution(mesh):
    return jax.shard_map(
        on_device,
        mesh=mesh,
        in_specs=(P("ens", None, "tile"), P("tile", None), P()),
        out_specs=P("ens", None, "tile"),
        check_vma=False,
    )
```

time: 150 us -> 165 us (1.10)
  blocking collectives: 17.1 us -> 0 us
  local copies, waits for them, and re-layouts: 13.9 us -> 29.9 us
  starting transfers between devices: 14 us -> 23.7 us
  waiting for transfers between devices: 14.2 us -> 19.3 us
    ppermute x3 -> x21, starting transfers between devices: 3.61 us -> 23.7 us  [swap(): return lax.ppermute(x, axes, [(i, flip(i)) for i in range(size)])]
    all_to_all x1 -> x0, blocking collectives: 17.1 us -> none  [on_device(): lax.all_to_all(grad.reshape(n_ens, local_n, 3, n_rows), 'ens', 0, 0, tile...]
    ppermute x3 -> x21, waiting for transfers between devices: 7.77 us -> 19.3 us  [swap(): return lax.ppermute(x, axes, [(i, flip(i)) for i in range(size)])]
    unnamed x5 -> x43, local copies, waits for them, and re-layouts: 3.83 us -> 14.8 us
    all_to_all x2 -> x0, starting transfers between devices: 10.4 us -> none  [the longest x1 6.33 us: on_device(): lax.all_to_all(col_send, 'ens', 0, 0, tiled=True).reshape(structs, 3, piece)]
    concatenate x0 -> x5, local copies, waits for them, and re-layouts: none -> 8.82 us  [the longest x1 7.92 us: pair_gradients(): jnp.concatenate([lax.dynamic_slice_in_dim(own_counts, b, chunk, 1) for b...]
    all_to_all x2 -> x0, waiting for transfers between devices: 6.42 us -> none  [the longest x1 4.16 us: on_device(): lax.all_to_all(col_send, 'ens', 0, 0, tiled=True).reshape(structs, 3, piece)]
    reshape x4 -> x0, local copies, waits for them, and re-layouts: 2.95 us -> none  [the longest x1 1.02 us: on_device(): row_send = jnp.moveaxis(coords.reshape(local_n, 3, n_p, n_rows), 2, 0)]
  transfers between devices with their start and end apart: 5 -> 21, of which waited for: 4 -> 9; matrix products, arithmetic and copies ran while one was open for 8% -> 13% of each run, Pallas kernels for 0% -> 0%
where the time goes in v3:
time: 165 us; the launch traced here: 164 us
  Pallas kernels  90.1 us (55%)
  local copies, waits for them, and re-layouts  29.9 us (18%)
  starting transfers between devices  23.7 us (14%)
  waiting for transfers between devices  19.3 us (12%)
    pallas_call x1, Pallas kernels, pair_gradients(): pl.pallas_call(functools.partial(pair_kernel, n_groups, n_mix, len(out_li...  90.1 us
    ppermute x21, starting transfers between devices, swap(): return lax.ppermute(x, axes, [(i, flip(i)) for i in range(size)])  23.7 us
    ppermute x21, waiting for transfers between devices, swap(): return lax.ppermute(x, axes, [(i, flip(i)) for i in range(size)])  19.3 us
    unnamed x43, local copies, waits for them, and re-layouts  14.8 us
    concatenate x1, local copies, waits for them, and re-layouts, pair_gradients(): jnp.concatenate([lax.dynamic_slice_in_dim(own_counts, b, chunk, 1) for b...  7.92 us
  transfers between devices with their start and end apart: 21, of which 9 were waited for; matrix products, arithmetic and copies ran while one was open for 13% of the time, Pallas kernels for 0%

profile of v3, /device:TPU:0, one launch (start us, length us, event | category | flops | bytes accessed | tf_op | source)
XLA Modules:
  0.0 164.4 jit_solution(3406616740564433088)
XLA Ops:
  0.0 1.0 constant_dynamic-slice_fusion.1
  1.5 2.7 %collective-permute-start.2 = (f32[8,3,400]{2,1,0:T(4,128)S(1)}, f32[8,3,400]{2,1,0:T(4,128)S(1)}, u32[]{:S(2)}, u32[]{:S(2)}) collective-permute-start(f32[8,3,400]{2,1,0:T(4,128)S(1)} %copy.39), channel_id=1, source_target_pairs={{0,12},{4,8},{8,4},{12,0},{16,28},{20,24},{24,20},{28,16},{1,13},{... | collective-permute-start | bytes 115208 | tf_op jit(solution)/shard_map/ppermute | solution.py:146
  4.4 3.0 %collective-permute-start.3 = (f32[8,3,400]{2,1,0:T(4,128)S(1)}, f32[8,3,400]{2,1,0:T(4,128)S(1)}, u32[]{:S(2)}, u32[]{:S(2)}) collective-permute-start(f32[8,3,400]{2,1,0:T(4,128)S(1)} %copy.38.rest_0_), channel_id=1, source_target_pairs={{0,16},{4,20},{8,24},{12,28},{16,0},{20,4},{24,8},{28,12},{1,17},{... | collective-permute-start | bytes 115208 | tf_op jit(solution)/shard_map/ppermute | solution.py:146
  8.3 2.4 %fusion = (s32[400,100]{1,0:T(8,128)S(1)}, s32[400,100]{1,0:T(8,128)S(1)}, s32[400,100]{1,0:T(8,128)S(1)}, s32[400,100]{1,0:T(8,128)S(1)}, s32[400,100]{1,0:T(8,...) fusion(s32[800,3200]{1,0:T(8,128)} %param.4, s32[]{:T(128)S(6)} %select_n.97, ...), kind=kLoop, calls=%fused_computation.24 | loop fusion | bytes 2560036 | tf_op jit(solution)/shard_map/dynamic_slice | solution.py:120
  13.2 0.8 copy.33
  16.5 0.8 copy.37
  17.4 2.9 %collective-permute-start.5 = (f32[8,3,400]{2,1,0:T(4,128)S(1)}, f32[8,3,400]{2,1,0:T(4,128)S(1)}, u32[]{:S(2)}, u32[]{:S(2)}) collective-permute-start(f32[8,3,400]{2,1,0:T(4,128)S(1)} %copy.38.rest_0_), channel_id=1, source_target_pairs={{0,24},{4,28},{8,16},{12,20},{16,8},{20,12},{24,0},{28,4},{1,25},{... | collective-permute-start | bytes 115208 | tf_op jit(solution)/shard_map/ppermute | solution.py:146
  22.1 1.6 collective-permute-done.5.rest_6_
  24.4 1.7 %collective-permute-done.6.rest_7_ = f32[8,3,400]{2,1,0:T(4,128)S(1)} collective-permute-done((f32[8,3,400]{2,1,0:T(4,128)S(1)}, f32[8,3,400]{2,1,0:T(4,128)S(1)}, u32[]{:S(2)}, u32[]{:S(2)}) %collective-permute-start.6) | collective-permute-done | bytes 38432 | tf_op jit(solution)/shard_map/ppermute | solution.py:146
  26.8 1.5 collective-permute-start.10
  29.1 2.5 %collective-permute-start.12 = (f32[64,3,100]{2,1,0:T(4,128)S(1)}, f32[64,3,100]{2,1,0:T(4,128)S(1)}, u32[]{:S(2)}, u32[]{:S(2)}) collective-permute-start(f32[64,3,100]{2,1,0:T(4,128)S(1)} %constant_dynamic-update-slice_fusion.rest_8_), channel_id=1, source_target_pairs={{0,3},{1,2},{2,1},{3,0},{4,7},{5,6},{6,5},{7,4},{8,11},{9,10},{10,... | collective-permute-start | bytes 230408 | tf_op jit(solution)/shard_map/ppermute | solution.py:146
  32.2 6.6 %collective-permute-done.10.rest_12_ = f32[64,3,100]{2,1,0:T(4,128)S(1)} collective-permute-done((f32[64,3,100]{2,1,0:T(4,128)S(1)}, f32[64,3,100]{2,1,0:T(4,128)S(1)}, u32[]{:S(2)}, u32[]{:S(2)}) %collective-permute-start.10) | collective-permute-done | bytes 76832 | tf_op jit(solution)/shard_map/ppermute | solution.py:146
  38.8 1.0 collective-permute-start.8
  39.8 1.2 collective-permute-done.11.rest_13_
  41.0 1.2 collective-permute-start.9
  42.2 1.0 fusion.1
  44.2 7.9 %concatenate.17 = s32[400,800]{0,1:T(8,128)S(1)} concatenate(s32[400,100]{0,1:T(8,128)} %copy.30, s32[400,100]{0,1:T(8,128)} %copy.31, s32[400,100]{0,1:T(8,128)} %copy.32, s32[400,100]{0,1:T(8,128)} %copy.33, s32[400,100]{0,1:T(8,128)} %copy.34, s32[400,100]{0,1:T(8,128)} %copy.35, s32[400,100]{0,1:T(8,128)} %copy.36, s32[400,100]{0,1:T(8,128)} %copy.37), dimensions={1} | concatenate | bytes 2560000 | tf_op jit(solution)/shard_map/concatenate | solution.py:120
  52.2 0.8 copy-done.1
  53.0 0.8 copy-done.3
  53.9 0.8 copy-done.5
  54.7 0.8 copy-done.7
  55.6 0.8 copy-done.9
  56.4 0.8 copy-done.11
  57.2 90.1 %pairs.1 = (f32[8,3,400]{2,1,0:T(4,128)S(1)}, f32[8,3,400]{2,1,0:T(4,128)}, f32[8,3,400]{2,1,0:T(4,128)S(1)}, f32[8,3,400]{2,1,0:T(4,128)}, f32[8,3,400]{2,1,0:T...) custom-call(s32[1]{0:T(128)} %bitcast.base_ref, s32[1,400]{1,0:T(1,128)S(1)} %bitcast.4, ...), custom_call_target="tpu_custom_call" | custom-call | tf_op jit(solution)/shard_map/pairs/pallas_call | solution.py:127
  148.7 1.7 %collective-permute-start.15 = (f32[8,3,400]{2,1,0:T(4,128)S(1)}, f32[8,3,400]{2,1,0:T(4,128)S(1)}, u32[]{:S(2)}, u32[]{:S(2)}) collective-permute-start(f32[8,3,400]{2,1,0:T(4,128)S(1)} %get-tuple-element.15), channel_id=1, source_target_pairs={{0,16},{4,20},{8,24},{12,28},{16,0},{20,4},{24,8},{28,12},{1,17},{... | collective-permute-start | bytes 115208 | tf_op jit(solution)/shard_map/ppermute | solution.py:146
  150.4 2.0 %collective-permute-start.16 = (f32[8,3,400]{2,1,0:T(4,128)}, f32[8,3,400]{2,1,0:T(4,128)S(1)}, u32[]{:S(2)}, u32[]{:S(2)}) collective-permute-start(f32[8,3,400]{2,1,0:T(4,128)} %get-tuple-element.16), channel_id=1, source_target_pairs={{0,24},{4,28},{8,16},{12,20},{16,8},{20,12},{24,0},{28,4},{1,25},{... | collective-permute-start | bytes 115208 | tf_op jit(solution)/shard_map/ppermute | solution.py:146
  152.4 2.1 %collective-permute-start.19 = (f32[8,3,400]{2,1,0:T(4,128)}, f32[8,3,400]{2,1,0:T(4,128)S(1)}, u32[]{:S(2)}, u32[]{:S(2)}) collective-permute-start(f32[8,3,400]{2,1,0:T(4,128)} %get-tuple-element.19), channel_id=1, source_target_pairs={{0,20},{4,16},{8,28},{12,24},{16,4},{20,0},{24,12},{28,8},{1,21},{... | collective-permute-start | bytes 115208 | tf_op jit(solution)/shard_map/ppermute | solution.py:146
  154.5 2.5 %collective-permute-done.15 = f32[8,3,400]{2,1,0:T(4,128)S(1)} collective-permute-done((f32[8,3,400]{2,1,0:T(4,128)S(1)}, f32[8,3,400]{2,1,0:T(4,128)S(1)}, u32[]{:S(2)}, u32[]{:S(2)}) %collective-permute-start.15) | collective-permute-done | bytes 38432 | tf_op jit(solution)/shard_map/ppermute | solution.py:146
  157.4 1.0 collective-permute-done.18
  158.4 1.8 %collective-permute-done.19 = f32[8,3,400]{2,1,0:T(4,128)S(1)} collective-permute-done((f32[8,3,400]{2,1,0:T(4,128)}, f32[8,3,400]{2,1,0:T(4,128)S(1)}, u32[]{:S(2)}, u32[]{:S(2)}) %collective-permute-start.19) | collective-permute-done | bytes 38432 | tf_op jit(solution)/shard_map/ppermute | solution.py:146
  160.2 2.5 %collective-permute-done.20 = f32[8,3,400]{2,1,0:T(4,128)S(1)} collective-permute-done((f32[8,3,400]{2,1,0:T(4,128)}, f32[8,3,400]{2,1,0:T(4,128)S(1)}, u32[]{:S(2)}, u32[]{:S(2)}) %collective-permute-start.20) | collective-permute-done | bytes 38432 | tf_op jit(solution)/shard_map/ppermute | solution.py:146
  162.7 0.9 broadcast_select_fusion.1
  (73 shorter events, 14.5 us)
Async XLA Ops:
  1.0 16.3 %collective-permute-start = (f32[8,3,400]{2,1,0:T(4,128)S(1)}, f32[8,3,400]{2,1,0:T(4,128)S(1)}, u32[]{:S(2)}, u32[]{:S(2)}) collective-permute-start(f32[8,3,400]{2,1,0:T(4,128)S(1)} %copy.39), channel_id=1, source_target_pairs={{0,4},{4,0},{8,12},{12,8},{16,20},{20,16},{24,28},{28,24},{1,5},{5... | collective-permute-start | bytes 115208 | tf_op jit(solution)/shard_map/ppermute | solution.py:146
  1.5 19.6 %collective-permute-start.2 = (f32[8,3,400]{2,1,0:T(4,128)S(1)}, f32[8,3,400]{2,1,0:T(4,128)S(1)}, u32[]{:S(2)}, u32[]{:S(2)}) collective-permute-start(f32[8,3,400]{2,1,0:T(4,128)S(1)} %copy.39), channel_id=1, source_target_pairs={{0,12},{4,8},{8,4},{12,0},{16,28},{20,24},{24,20},{28,16},{1,13},{... | collective-permute-start | bytes 115208 | tf_op jit(solution)/shard_map/ppermute | solution.py:146
  4.3 16.1 %collective-permute-start.1 = (f32[8,3,400]{2,1,0:T(4,128)S(1)}, f32[8,3,400]{2,1,0:T(4,128)S(1)}, u32[]{:S(2)}, u32[]{:S(2)}) collective-permute-start(f32[8,3,400]{2,1,0:T(4,128)S(1)} %copy.38.rest_0_), channel_id=1, source_target_pairs={{0,8},{4,12},{8,0},{12,4},{16,24},{20,28},{24,16},{28,20},{1,9},{5... | collective-permute-start | bytes 115208 | tf_op jit(solution)/shard_map/ppermute | solution.py:146
  4.4 16.9 %collective-permute-start.3 = (f32[8,3,400]{2,1,0:T(4,128)S(1)}, f32[8,3,400]{2,1,0:T(4,128)S(1)}, u32[]{:S(2)}, u32[]{:S(2)}) collective-permute-start(f32[8,3,400]{2,1,0:T(4,128)S(1)} %copy.38.rest_0_), channel_id=1, source_target_pairs={{0,16},{4,20},{8,24},{12,28},{16,0},{20,4},{24,8},{28,12},{1,17},{... | collective-permute-start | bytes 115208 | tf_op jit(solution)/shard_map/ppermute | solution.py:146
  7.4 14.0 %collective-permute-start.4 = (f32[8,3,400]{2,1,0:T(4,128)S(1)}, f32[8,3,400]{2,1,0:T(4,128)S(1)}, u32[]{:S(2)}, u32[]{:S(2)}) collective-permute-start(f32[8,3,400]{2,1,0:T(4,128)S(1)} %copy.39), channel_id=1, source_target_pairs={{0,20},{4,16},{8,28},{12,24},{16,4},{20,0},{24,12},{28,8},{1,21},{... | collective-permute-start | bytes 115208 | tf_op jit(solution)/shard_map/ppermute | solution.py:146
  17.4 6.3 %collective-permute-start.5 = (f32[8,3,400]{2,1,0:T(4,128)S(1)}, f32[8,3,400]{2,1,0:T(4,128)S(1)}, u32[]{:S(2)}, u32[]{:S(2)}) collective-permute-start(f32[8,3,400]{2,1,0:T(4,128)S(1)} %copy.38.rest_0_), channel_id=1, source_target_pairs={{0,24},{4,28},{8,16},{12,20},{16,8},{20,12},{24,0},{28,4},{1,25},{... | collective-permute-start | bytes 115208 | tf_op jit(solution)/shard_map/ppermute | solution.py:146
  20.4 5.7 %copy-start.2 = (f32[8,3,400]{2,1,0:T(4,128)}, f32[8,3,400]{2,1,0:T(4,128)S(1)}, u32[]{:S(2)}) copy-start(f32[8,3,400]{2,1,0:T(4,128)S(1)} %collective-permute-done.1.rest_2_) | copy-start | bytes 115204
  20.4 5.7 %collective-permute-start.6 = (f32[8,3,400]{2,1,0:T(4,128)S(1)}, f32[8,3,400]{2,1,0:T(4,128)S(1)}, u32[]{:S(2)}, u32[]{:S(2)}) collective-permute-start(f32[8,3,400]{2,1,0:T(4,128)S(1)} %copy.39), channel_id=1, source_target_pairs={{0,28},{4,24},{8,20},{12,16},{16,12},{20,8},{24,4},{28,0},{1,29},{... | collective-permute-start | bytes 115208 | tf_op jit(solution)/shard_map/ppermute | solution.py:146
  21.1 4.9 %copy-start = (f32[8,3,400]{2,1,0:T(4,128)}, f32[8,3,400]{2,1,0:T(4,128)S(1)}, u32[]{:S(2)}) copy-start(f32[8,3,400]{2,1,0:T(4,128)S(1)} %collective-permute-done.2.rest_3_) | copy-start | bytes 115204
  21.3 4.9 %copy-start.4 = (f32[8,3,400]{2,1,0:T(4,128)}, f32[8,3,400]{2,1,0:T(4,128)S(1)}, u32[]{:S(2)}) copy-start(f32[8,3,400]{2,1,0:T(4,128)S(1)} %collective-permute-done.3.rest_4_) | copy-start | bytes 115204
  26.2 0.6 copy-start.10
  26.8 12.0 %collective-permute-start.10 = (f32[64,3,100]{2,1,0:T(4,128)S(1)}, f32[64,3,100]{2,1,0:T(4,128)S(1)}, u32[]{:S(2)}, u32[]{:S(2)}) collective-permute-start(f32[64,3,100]{2,1,0:T(4,128)S(1)} %constant_dynamic-update-slice_fusion.rest_8_), channel_id=1, source_target_pairs={{0,2},{1,3},{2,0},{3,1},{4,6},{5,7},{6,4},{7,5},{8,10},{9,11},{10,... | collective-permute-start | bytes 230408 | tf_op jit(solution)/shard_map/ppermute | solution.py:146
  28.3 12.7 %collective-permute-start.11 = (f32[64,3,100]{2,1,0:T(4,128)S(1)}, f32[64,3,100]{2,1,0:T(4,128)S(1)}, u32[]{:S(2)}, u32[]{:S(2)}) collective-permute-start(f32[64,3,100]{2,1,0:T(4,128)S(1)} %constant_dynamic-update-slice_fusion.rest_8_), channel_id=1, source_target_pairs={{0,6},{1,7},{2,4},{3,5},{4,2},{5,3},{6,0},{7,1},{8,14},{9,15},{10,... | collective-permute-start | bytes 230408 | tf_op jit(solution)/shard_map/ppermute | solution.py:146
  29.1 23.1 %collective-permute-start.12 = (f32[64,3,100]{2,1,0:T(4,128)S(1)}, f32[64,3,100]{2,1,0:T(4,128)S(1)}, u32[]{:S(2)}, u32[]{:S(2)}) collective-permute-start(f32[64,3,100]{2,1,0:T(4,128)S(1)} %constant_dynamic-update-slice_fusion.rest_8_), channel_id=1, source_target_pairs={{0,3},{1,2},{2,1},{3,0},{4,7},{5,6},{6,5},{7,4},{8,11},{9,10},{10,... | collective-permute-start | bytes 230408 | tf_op jit(solution)/shard_map/ppermute | solution.py:146
  31.5 20.6 %collective-permute-start.13 = (f32[64,3,100]{2,1,0:T(4,128)S(1)}, f32[64,3,100]{2,1,0:T(4,128)S(1)}, u32[]{:S(2)}, u32[]{:S(2)}) collective-permute-start(f32[64,3,100]{2,1,0:T(4,128)S(1)} %constant_dynamic-update-slice_fusion.rest_8_), channel_id=1, source_target_pairs={{0,7},{1,6},{2,5},{3,4},{4,3},{5,2},{6,1},{7,0},{8,15},{9,14},{10,... | collective-permute-start | bytes 230408 | tf_op jit(solution)/shard_map/ppermute | solution.py:146
  31.6 20.6 %collective-permute-start.7 = (f32[64,3,100]{2,1,0:T(4,128)S(1)}, f32[64,3,100]{2,1,0:T(4,128)S(1)}, u32[]{:S(2)}, u32[]{:S(2)}) collective-permute-start(f32[64,3,100]{2,1,0:T(4,128)S(1)} %constant_dynamic-update-slice_fusion.rest_8_), channel_id=1, source_target_pairs={{0,4},{1,5},{2,6},{3,7},{4,0},{5,1},{6,2},{7,3},{8,12},{9,13},{10,... | collective-permute-start | bytes 230408 | tf_op jit(solution)/shard_map/ppermute | solution.py:146
  38.8 13.4 %collective-permute-start.8 = (f32[64,3,100]{2,1,0:T(4,128)S(1)}, f32[64,3,100]{2,1,0:T(4,128)S(1)}, u32[]{:S(2)}, u32[]{:S(2)}) collective-permute-start(f32[64,3,100]{2,1,0:T(4,128)S(1)} %constant_dynamic-update-slice_fusion.rest_8_), channel_id=1, source_target_pairs={{0,1},{1,0},{2,3},{3,2},{4,5},{5,4},{6,7},{7,6},{8,9},{9,8},{10,11... | collective-permute-start | bytes 230408 | tf_op jit(solution)/shard_map/ppermute | solution.py:146
  41.0 11.2 %collective-permute-start.9 = (f32[64,3,100]{2,1,0:T(4,128)S(1)}, f32[64,3,100]{2,1,0:T(4,128)}, u32[]{:S(2)}, u32[]{:S(2)}) collective-permute-start(f32[64,3,100]{2,1,0:T(4,128)S(1)} %constant_dynamic-update-slice_fusion.rest_8_), channel_id=1, source_target_pairs={{0,5},{1,4},{2,7},{3,6},{4,1},{5,0},{6,3},{7,2},{8,13},{9,12},{10,... | collective-permute-start | bytes 230408 | tf_op jit(solution)/shard_map/ppermute | solution.py:146
  52.2 0.8 copy-start.1
  53.0 0.8 copy-start.3
  53.9 0.8 copy-start.5
  54.7 0.8 copy-start.7
  55.5 0.8 copy-start.9
  56.4 0.8 copy-start.11
  147.3 0.6 copy-start.12
  148.0 4.4 %collective-permute-start.14 = (f32[8,3,400]{2,1,0:T(4,128)S(1)}, f32[8,3,400]{2,1,0:T(4,128)S(1)}, u32[]{:S(2)}, u32[]{:S(2)}) collective-permute-start(f32[8,3,400]{2,1,0:T(4,128)S(1)} %get-tuple-element.14), channel_id=1, source_target_pairs={{0,8},{4,12},{8,0},{12,4},{16,24},{20,28},{24,16},{28,20},{1,9},{5... | collective-permute-start | bytes 115208 | tf_op jit(solution)/shard_map/ppermute | solution.py:146
  148.7 8.3 %collective-permute-start.15 = (f32[8,3,400]{2,1,0:T(4,128)S(1)}, f32[8,3,400]{2,1,0:T(4,128)S(1)}, u32[]{:S(2)}, u32[]{:S(2)}) collective-permute-start(f32[8,3,400]{2,1,0:T(4,128)S(1)} %get-tuple-element.15), channel_id=1, source_target_pairs={{0,16},{4,20},{8,24},{12,28},{16,0},{20,4},{24,8},{28,12},{1,17},{... | collective-permute-start | bytes 115208 | tf_op jit(solution)/shard_map/ppermute | solution.py:146
  150.4 7.0 %collective-permute-start.16 = (f32[8,3,400]{2,1,0:T(4,128)}, f32[8,3,400]{2,1,0:T(4,128)S(1)}, u32[]{:S(2)}, u32[]{:S(2)}) collective-permute-start(f32[8,3,400]{2,1,0:T(4,128)} %get-tuple-element.16), channel_id=1, source_target_pairs={{0,24},{4,28},{8,16},{12,20},{16,8},{20,12},{24,0},{28,4},{1,25},{... | collective-permute-start | bytes 115208 | tf_op jit(solution)/shard_map/ppermute | solution.py:146
  152.4 5.0 %collective-permute-start.17 = (f32[8,3,400]{2,1,0:T(4,128)}, f32[8,3,400]{2,1,0:T(4,128)S(1)}, u32[]{:S(2)}, u32[]{:S(2)}) collective-permute-start(f32[8,3,400]{2,1,0:T(4,128)} %get-tuple-element.17), channel_id=1, source_target_pairs={{0,4},{4,0},{8,12},{12,8},{16,20},{20,16},{24,28},{28,24},{1,5},{5... | collective-permute-start | bytes 115208 | tf_op jit(solution)/shard_map/ppermute | solution.py:146
  152.4 6.0 %collective-permute-start.18 = (f32[8,3,400]{2,1,0:T(4,128)}, f32[8,3,400]{2,1,0:T(4,128)S(1)}, u32[]{:S(2)}, u32[]{:S(2)}) collective-permute-start(f32[8,3,400]{2,1,0:T(4,128)} %get-tuple-element.18), channel_id=1, source_target_pairs={{0,12},{4,8},{8,4},{12,0},{16,28},{20,24},{24,20},{28,16},{1,13},{... | collective-permute-start | bytes 115208 | tf_op jit(solution)/shard_map/ppermute | solution.py:146
  152.4 7.8 %collective-permute-start.19 = (f32[8,3,400]{2,1,0:T(4,128)}, f32[8,3,400]{2,1,0:T(4,128)S(1)}, u32[]{:S(2)}, u32[]{:S(2)}) collective-permute-start(f32[8,3,400]{2,1,0:T(4,128)} %get-tuple-element.19), channel_id=1, source_target_pairs={{0,20},{4,16},{8,28},{12,24},{16,4},{20,0},{24,12},{28,8},{1,21},{... | collective-permute-start | bytes 115208 | tf_op jit(solution)/shard_map/ppermute | solution.py:146
  157.0 5.7 %collective-permute-start.20 = (f32[8,3,400]{2,1,0:T(4,128)}, f32[8,3,400]{2,1,0:T(4,128)S(1)}, u32[]{:S(2)}, u32[]{:S(2)}) collective-permute-start(f32[8,3,400]{2,1,0:T(4,128)} %get-tuple-element.20), channel_id=1, source_target_pairs={{0,28},{4,24},{8,20},{12,16},{16,12},{20,8},{24,4},{28,0},{1,29},{... | collective-permute-start | bytes 115208 | tf_op jit(solution)/shard_map/ppermute | solution.py:146
  (2 other events, 1.3 us)

commit v4 on v2

--- a/solution.py
+++ b/solution.py
@@ -26,24 +26,47 @@
     return jnp.where(row == norm_row, norm, jnp.where(row == one_row, 1.0, v8))
 
 
-def pair_kernel(structs, tiles, base_ref, out_xyz_ref, seg_out_ref, seg_par_ref, par_ids_ref, counts_ref, *rest):
-    par_refs = rest[:tiles]
-    grad_ref, lhs_ref, rhs_ref, terms_ref, weight_ref = rest[tiles:]
-    n_out = out_xyz_ref.shape[2]
+def pack_kernel(n_p, n_q, xyz_ref, send_ref):
+    beads = xyz_ref.shape[2]
+    n_rows, piece = beads // n_p, beads // n_q
+    for c in range(3):
+        for q in range(n_q):
+            for p in range(n_p):
+                send_ref[q * n_p + p, c, :, pl.ds(0, piece)] = xyz_ref[c, :, pl.ds(q * piece, piece)]
+                send_ref[q * n_p + p, c, :, pl.ds(piece, n_rows)] = xyz_ref[c, :, pl.ds(p * n_rows, n_rows)]
+
+
+def sum_kernel(n_p, n_q, back_ref, total_ref):
+    n_rows = back_ref.shape[3]
+    for c in range(3):
+        for p in range(n_p):
+            total = back_ref[p, c]
+            for q in range(1, n_q):
+                total += back_ref[q * n_p + p, c]
+            total_ref[c, :, pl.ds(p * n_rows, n_rows)] = total
+
+
+def pair_kernel(structs, tiles, base_ref, seg_out_ref, seg_par_ref, par_ids_ref, counts_ref, both_ref, *rest):
+    par_refs = rest[:tiles - 1]
+    grad_ref, xyz_ref, lhs_ref, rhs_ref, terms_ref, weight_ref = rest[tiles - 1:]
+    n_out = seg_out_ref.shape[1]
+    piece = both_ref.shape[2] - n_out
     n_par = counts_ref.shape[0]
     wide = weight_ref.shape[1]
     deep = terms_ref.shape[2]
     starts = [(a, min(WIDE, n_par - a)) for a in range(0, n_par, WIDE)]
 
     def features(s, carry):
-        par = [ref[s] for ref in par_refs]
+        both = both_ref[s]
+        par = [both[:, :piece]] + [ref[s] for ref in par_refs]
         if deep > n_par:
             par.append(jnp.zeros((3, deep - n_par), jnp.float32))
         hi, mid, lo = split3(augment(jnp.concatenate(par, axis=1), 4, 3))
         left = jnp.concatenate([hi, mid, hi, mid, lo, hi], axis=0)
         lhs_ref[s] = left.T[:n_par].astype(jnp.bfloat16)
         terms_ref[s] = left[0:16].astype(jnp.bfloat16)
-        out = out_xyz_ref[s]
+        out = both[:, piece:]
+        xyz_ref[s] = out
         if wide > n_out:
             out = jnp.concatenate([out, jnp.zeros((3, wide - n_out), jnp.float32)], axis=1)
         hi, mid, lo = split3(augment(out, 3, 4))
@@ -86,7 +109,7 @@
             total += jnp.dot(terms, lo, preferred_element_type=jnp.float32)
         total = total[:, :n_out]
         mixed = total[0:3] + total[8:11]
-        grad_ref[s] = (0.25 / 16) * (mixed - total[3:4] * out_xyz_ref[s])
+        grad_ref[s] = (0.25 / 16) * (mixed - total[3:4] * xyz_ref[s])
         return carry
 
     lax.fori_loop(0, structs, grad_one, 0, unroll=2)
@@ -115,15 +138,17 @@
     tile, ens = lax.axis_index("tile"), lax.axis_index("ens")
     p, q = lax.rem(ens, n_p), lax.div(ens, n_p)
 
-    col_send = jnp.moveaxis(coords.reshape(local_n, 3, n_q, piece), 2, 0)
-    col_send = jnp.broadcast_to(col_send[:, None], (n_q, n_p, local_n, 3, piece)).reshape(n_ens, local_n, 3, piece)
-    row_send = jnp.moveaxis(coords.reshape(local_n, 3, n_p, n_rows), 2, 0)
-    row_send = jnp.broadcast_to(row_send[None], (n_q, n_p, local_n, 3, n_rows)).reshape(n_ens, local_n, 3, n_rows)
-    own = lax.all_to_all(col_send, "ens", 0, 0, tiled=True).reshape(structs, 3, piece)
-    cols = [own]
-    for k in range(1, n_tile):
-        cols.append(lax.ppermute(own, "tile", [(t, (t - k) % n_tile) for t in range(n_tile)]))
-    rows = lax.all_to_all(row_send, "ens", 0, 0, tiled=True).reshape(structs, 3, n_rows)
+    send = pl.pallas_call(
+        functools.partial(pack_kernel, n_p, n_q),
+        out_shape=jax.ShapeDtypeStruct((n_ens, 3, local_n, piece + n_rows), jnp.float32),
+        in_specs=[pl.BlockSpec(memory_space=pltpu.VMEM)],
+        out_specs=pl.BlockSpec(memory_space=pltpu.VMEM),
+        name="pack",
+    )(jnp.swapaxes(coords, 0, 1))
+    both = lax.all_to_all(send, "ens", 0, 0, tiled=True)
+    both = jnp.swapaxes(both, 1, 2).reshape(structs, 3, piece + n_rows)
+    own = both[:, :, :piece]
+    cols = [lax.ppermute(own, "tile", [(t, (t - k) % n_tile) for t in range(n_tile)]) for k in range(1, n_tile)]
 
     row_base = tile * beads + p * n_rows
     col_bases = [lax.rem(tile + k, n_tile) * beads + q * piece for k in range(n_tile)]
@@ -139,9 +164,10 @@
     grad = pl.pallas_call(
         functools.partial(pair_kernel, structs, n_tile),
         out_shape=jax.ShapeDtypeStruct((structs, 3, n_rows), jnp.float32),
-        in_specs=[pl.BlockSpec(memory_space=pltpu.SMEM)] + [vmem] * (5 + n_tile),
+        in_specs=[pl.BlockSpec(memory_space=pltpu.SMEM)] + [vmem] * (4 + n_tile),
         out_specs=vmem,
         scratch_shapes=[
+            pltpu.VMEM((structs, 3, n_rows), jnp.float32),
             pltpu.VMEM((structs, n_cols, 48), jnp.bfloat16),
             pltpu.VMEM((structs, 48, wide), jnp.bfloat16),
             pltpu.VMEM((structs, 16, deep), jnp.bfloat16),
@@ -149,11 +175,18 @@
         ],
         compiler_params=pltpu.CompilerParams(vmem_limit_bytes=48 << 20),
         name="pairs",
-    )(row_base[None], rows, seg_rows, seg_cols, col_ids, block, *cols)
+    )(row_base[None], seg_rows, seg_cols, col_ids, block, both, *cols)
 
-    back = lax.all_to_all(grad.reshape(n_ens, local_n, 3, n_rows), "ens", 0, 0, tiled=True)
-    back = jnp.sum(back.reshape(n_q, n_p, local_n, 3, n_rows), axis=0)
-    return jnp.moveaxis(back, 0, 2).reshape(local_n, 3, beads)
+    back = jnp.swapaxes(grad.reshape(n_ens, local_n, 3, n_rows), 1, 2)
+    back = lax.all_to_all(back, "ens", 0, 0, tiled=True)
+    total = pl.pallas_call(
+        functools.partial(sum_kernel, n_p, n_q),
+        out_shape=jax.ShapeDtypeStruct((3, local_n, beads), jnp.float32),
+        in_specs=[pl.BlockSpec(memory_space=pltpu.VMEM)],
+        out_specs=pl.BlockSpec(memory_space=pltpu.VMEM),
+        name="total",
+    )(back)
+    return jnp.swapaxes(total, 0, 1)
 
 
 def solution(mesh):

time: 150 us -> 146 us (0.973)
  local copies, waits for them, and re-layouts: 13.9 us -> 5.24 us
  waiting for transfers between devices: 14.2 us -> 21.5 us
  starting transfers between devices: 14 us -> 9.92 us
  Pallas kernels: 88.5 us -> 92.4 us
  blocking collectives: 17.1 us -> 15.6 us
    ppermute x3, waiting for transfers between devices: 7.77 us -> 11.9 us  [on_device(): lax.ppermute(own, 'tile', [(t, (t - k) % n_tile) for t in range(n_tile)])]
    all_to_all x2 -> x1, starting transfers between devices: 10.4 us -> 6.33 us  [on_device(): both = lax.all_to_all(send, 'ens', 0, 0, tiled=True)]
    pallas_call x0 -> x2, Pallas kernels: none -> 3.6 us  [the longest x1 1.88 us: on_device(): pl.pallas_call(functools.partial(pack_kernel, n_p, n_q), out_shape=jax.Sh...]
    all_to_all x2 -> x1, waiting for transfers between devices: 6.42 us -> 9.52 us  [on_device(): both = lax.all_to_all(send, 'ens', 0, 0, tiled=True)]
    unnamed x5 -> x4, local copies, waits for them, and re-layouts: 3.83 us -> 0.72 us
    reshape x4 -> x1, local copies, waits for them, and re-layouts: 2.95 us -> 0.13 us  [on_device(): back = jnp.swapaxes(grad.reshape(n_ens, local_n, 3, n_rows), 1, 2)]
  transfers between devices with their start and end apart: 5 -> 4, of which waited for: 4 -> 3; matrix products, arithmetic and copies ran while one was open for 8% -> 4% of each run, Pallas kernels for 0% -> 0%
where the time goes in v4:
time: 146 us; the launch traced here: 145 us
  Pallas kernels  92.4 us (63%)
  waiting for transfers between devices  21.5 us (15%)
  blocking collectives  15.6 us (11%)
  starting transfers between devices  9.92 us (7%)
  local copies, waits for them, and re-layouts  5.24 us (4%)
    pallas_call x1, Pallas kernels, on_device(): pl.pallas_call(functools.partial(pair_kernel, structs, n_tile), out_shape...  88.8 us
    all_to_all x1, blocking collectives, on_device(): back = lax.all_to_all(back, 'ens', 0, 0, tiled=True)  15.6 us
    ppermute x3, waiting for transfers between devices, on_device(): lax.ppermute(own, 'tile', [(t, (t - k) % n_tile) for t in range(n_tile)])  11.9 us
    all_to_all x1, waiting for transfers between devices, on_device(): both = lax.all_to_all(send, 'ens', 0, 0, tiled=True)  9.52 us
    all_to_all x1, starting transfers between devices, on_device(): both = lax.all_to_all(send, 'ens', 0, 0, tiled=True)  6.33 us
    ppermute x3, starting transfers between devices, on_device(): lax.ppermute(own, 'tile', [(t, (t - k) % n_tile) for t in range(n_tile)])  3.6 us
  transfers between devices with their start and end apart: 4, of which 3 were waited for; matrix products, arithmetic and copies ran while one was open for 4% of the time, Pallas kernels for 0%

profile of v4, /device:TPU:0, one launch (start us, length us, event | category | flops | bytes accessed | tf_op | source)
XLA Modules:
  0.0 145.1 jit_solution(3737535355552488274)
XLA Ops:
  0.0 1.9 %pack.1 = f32[8,3,8,600]{3,2,1,0:T(8,128)} custom-call(f32[3,8,800]{2,1,0:T(8,128)} %bitcast.18), custom_call_target="tpu_custom_call" | custom-call | tf_op jit(solution)/shard_map/pack/pallas_call | solution.py:141
  1.9 6.3 %all-to-all-start = ((f32[8,3,8,600]{3,2,1,0:T(8,128)}), f32[8,3,8,600]{3,2,1,0:T(8,128)S(1)}, u32[]{:S(2)}, u32[]{:S(2)}) async-start(f32[8,3,8,600]{3,2,1,0:T(8,128)} %pack.1), calls=%async_computation | async-start | bytes 983040 | tf_op jit(solution)/shard_map/all_to_all | solution.py:148
  8.2 2.2 %fusion = (s32[400,200]{1,0:T(8,128)S(1)}, s32[400,200]{1,0:T(8,128)S(1)}, s32[400,200]{1,0:T(8,128)S(1)}, s32[400,200]{1,0:T(8,128)S(1)}) fusion(s32[800,3200]{1,0:T(8,128)} %param.4, s32[]{:T(128)S(6)} %select_n.38, s32[]{:T(128)S(6)} %select_n.39, s32[]{:T(128)S(6)} %select_n.41, s32[]{:T(128)S(6)} %select_n.40, s32[]{:T(128)S(6)} %select_n.42), kind=kLoop, calls=%fused_computation.8 | loop fusion | bytes 2560020 | tf_op jit(solution)/shard_map/dynamic_slice | solution.py:156
  10.4 0.2 copy.20
  10.6 0.2 copy.21
  10.8 0.2 copy.22
  10.9 0.2 copy.23
  11.2 0.1 pad_add_fusion.1
  11.2 0.2 broadcast_in_dim.17.par_ids_ref
  11.4 0.9 fusion.1
  12.3 0.1 pad_add_fusion
  12.4 0.2 broadcast_in_dim.16.seg_par_ref
  12.6 0.8 dynamic_slice.28
  13.3 9.5 %all-to-all-done = f32[8,3,8,600]{3,2,1,0:T(8,128)S(1)} async-done(((f32[8,3,8,600]{3,2,1,0:T(8,128)}), f32[8,3,8,600]{3,2,1,0:T(8,128)S(1)}, u32[]{:S(2)}, u32[]{:S(2)}) %all-to-all-start) | async-done | bytes 460832 | tf_op jit(solution)/shard_map/all_to_all | solution.py:148
  22.9 0.2 copy.13
  23.1 2.5 %collective-permute-start = (f32[64,3,200]{2,1,0:T(4,128)S(1)}, f32[64,3,200]{2,1,0:T(4,128)S(1)}, u32[]{:S(2)}, u32[]{:S(2)}) collective-permute-start(f32[64,3,200]{2,1,0:T(4,128)S(1)} %slice.4), channel_id=1, source_target_pairs={{0,3},{1,0},{2,1},{3,2},{4,7},{5,4},{6,5},{7,6},{8,11},{9,8},{10,9... | collective-permute-start | bytes 460808 | tf_op jit(solution)/shard_map/ppermute | solution.py:151
  25.6 0.5 collective-permute-start.1
  26.1 0.6 collective-permute-start.2
  26.7 0.1 add_bitcast_fusion.counts_ref
  26.8 5.5 %collective-permute-done.rest_0_ = f32[64,3,200]{2,1,0:T(4,128)S(1)} collective-permute-done((f32[64,3,200]{2,1,0:T(4,128)S(1)}, f32[64,3,200]{2,1,0:T(4,128)S(1)}, u32[]{:S(2)}, u32[]{:S(2)}) %collective-permute-start) | collective-permute-done | bytes 153632 | tf_op jit(solution)/shard_map/ppermute | solution.py:151
  32.4 6.4 %collective-permute-done.1.rest_1_ = f32[64,3,200]{2,1,0:T(4,128)S(1)} collective-permute-done((f32[64,3,200]{2,1,0:T(4,128)S(1)}, f32[64,3,200]{2,1,0:T(4,128)S(1)}, u32[]{:S(2)}, u32[]{:S(2)}) %collective-permute-start.1) | collective-permute-done | bytes 153632 | tf_op jit(solution)/shard_map/ppermute | solution.py:151
  38.8 0.0 collective-permute-done.2.rest_2_
  38.8 88.8 %pairs.1 = f32[64,3,400]{2,1,0:T(4,128)S(1)} custom-call(s32[1]{0:T(128)} %bitcast.base_ref, s32[1,400]{1,0:T(1,128)S(1)} %bitcast.15, s32[800,1]{1,0:T(8,128)S(1)} %broadcast_in_dim.16.seg_par_ref, s32[800,1]{1,0:T(8,128)S(1)} %broadcast_in_dim.17.par_ids_ref, s32[800,400]{1,0:T(8,128)S(1)} %add_bitcast_fusion.counts_ref, f32[64,3,600]{2,1,0:T(4,128)S(1)} %bitcast.13, ...), custom_call_target="tpu_custom_call" | custom-call | tf_op jit(solution)/shard_map/pairs/pallas_call | solution.py:164
  127.6 0.1 copy.25
  127.7 15.6 %all_to_all.10.back_ref = f32[8,3,8,400]{3,2,1,0:T(8,128)} all-to-all(f32[8,3,8,400]{3,2,1,0:T(8,128)S(1)} %bitcast.17), channel_id=1, replica_groups=mesh['ens'=8,'tile'=4] {'ens'}, dimensions={0} | all-to-all | bytes 614400 | tf_op jit(solution)/shard_map/all_to_all | solution.py:181
  143.4 1.7 %total.1 = f32[3,8,800]{2,1,0:T(8,128)} custom-call(f32[8,3,8,400]{3,2,1,0:T(8,128)} %all_to_all.10.back_ref), custom_call_target="tpu_custom_call" | custom-call | tf_op jit(solution)/shard_map/total/pallas_call | solution.py:182
  (3 shorter events, 0.1 us)
Async XLA Ops:
  1.9 21.0 %all-to-all-start = ((f32[8,3,8,600]{3,2,1,0:T(8,128)}), f32[8,3,8,600]{3,2,1,0:T(8,128)S(1)}, u32[]{:S(2)}, u32[]{:S(2)}) async-start(f32[8,3,8,600]{3,2,1,0:T(8,128)} %pack.1), calls=%async_computation | async-start | bytes 983040 | tf_op jit(solution)/shard_map/all_to_all | solution.py:148
  23.1 9.3 %collective-permute-start = (f32[64,3,200]{2,1,0:T(4,128)S(1)}, f32[64,3,200]{2,1,0:T(4,128)S(1)}, u32[]{:S(2)}, u32[]{:S(2)}) collective-permute-start(f32[64,3,200]{2,1,0:T(4,128)S(1)} %slice.4), channel_id=1, source_target_pairs={{0,3},{1,0},{2,1},{3,2},{4,7},{5,4},{6,5},{7,6},{8,11},{9,8},{10,9... | collective-permute-start | bytes 460808 | tf_op jit(solution)/shard_map/ppermute | solution.py:151
  25.6 13.2 %collective-permute-start.1 = (f32[64,3,200]{2,1,0:T(4,128)S(1)}, f32[64,3,200]{2,1,0:T(4,128)S(1)}, u32[]{:S(2)}, u32[]{:S(2)}) collective-permute-start(f32[64,3,200]{2,1,0:T(4,128)S(1)} %slice.4), channel_id=1, source_target_pairs={{0,2},{1,3},{2,0},{3,1},{4,6},{5,7},{6,4},{7,5},{8,10},{9,11},{10,... | collective-permute-start | bytes 460808 | tf_op jit(solution)/shard_map/ppermute | solution.py:151
  26.1 12.7 %collective-permute-start.2 = (f32[64,3,200]{2,1,0:T(4,128)S(1)}, f32[64,3,200]{2,1,0:T(4,128)S(1)}, u32[]{:S(2)}, u32[]{:S(2)}) collective-permute-start(f32[64,3,200]{2,1,0:T(4,128)S(1)} %slice.4), channel_id=1, source_target_pairs={{0,1},{1,2},{2,3},{3,0},{4,5},{5,6},{6,7},{7,4},{8,9},{9,10},{10,1... | collective-permute-start | bytes 460808 | tf_op jit(solution)/shard_map/ppermute | solution.py:151

commit v5 on v4

v5 whole, which is shorter than its diff:
```python
import functools

import jax
import jax.numpy as jnp
from jax import lax
from jax.experimental import pallas as pl
from jax.experimental.pallas import tpu as pltpu
from jax.sharding import PartitionSpec as P

LANES = 128
WIDE = 256
SLOT = 64
NT = (((1,), (1,)), ((), ()))


def up(n, unit):
    return -(-n // unit) * unit


def split3(v):
    hi = v.astype(jnp.bfloat16).astype(jnp.float32)
    rest = v - hi
    mid = rest.astype(jnp.bfloat16).astype(jnp.float32)
    return hi, mid, rest - mid


def pack_kernel(n_p, n_q, xyz_ref, send_ref):
    beads = xyz_ref.shape[2]
    n_rows, piece = beads // n_p, beads // n_q
    for c in range(3):
        for q in range(n_q):
            for p in range(n_p):
                e = q * n_p + p
                send_ref[e, :, pl.ds(c * piece, piece)] = xyz_ref[c, :, pl.ds(q * piece, piece)]
                send_ref[e, :, pl.ds(3 * piece + c * n_rows, n_rows)] = xyz_ref[c, :, pl.ds(p * n_rows, n_rows)]


def sum_kernel(n_p, n_q, back_ref, total_ref):
    n_rows = back_ref.shape[3]
    for c in range(3):
        for p in range(n_p):
            total = back_ref[p, c]
            for q in range(1, n_q):
                total += back_ref[q * n_p + p, c]
            total_ref[c, :, pl.ds(p * n_rows, n_rows)] = total


def put_terms(refs, xyz, norm_row):
    norm = 1.5 - 0.5 * (xyz[0] * xyz[0] + xyz[1] * xyz[1] + xyz[2] * xyz[2])
    n, size = norm.shape
    wide = refs[0].shape[0] * LANES
    for f, v in ((0, xyz[0]), (1, xyz[1]), (2, xyz[2]), (norm_row, norm)):
        if wide > size:
            v = jnp.concatenate([v, jnp.zeros((n, wide - size), jnp.float32)], axis=1)
        for ref, term in zip(refs, split3(v)):
            for k in range(wide // LANES):
                ref[k, pl.ds(f, n, 8), :] = term[:, k * LANES:(k + 1) * LANES]


def get_terms(refs, i):
    return [jnp.concatenate([ref[k, pl.ds(8 * i, 8), :] for k in range(ref.shape[0])], axis=1) for ref in refs]


def pair_kernel(tiles, fold, base_ref, seg_rows_ref, seg_cols_ref, col_ids_ref, counts_ref, both_ref, *rest):
    piece_refs = rest[:tiles - 1]
    (grad_ref, row_terms, col_terms, lhs_ref, lhs_end_ref, rhs_ref, rhs_end_ref, terms_end_ref, weight_ref,
     weight_end_ref) = rest[tiles - 1:]
    groups, per, _ = both_ref.shape
    structs = groups * per
    n_rows, n_cols = counts_ref.shape
    piece = n_cols // tiles
    deep = weight_ref.shape[0]
    full = rhs_ref.shape[2]
    end = n_cols - full
    chunks = [(a, min(WIDE, full - a)) for a in range(0, full, WIDE)]

    for norm_row, one_row, refs in ((3, 4, row_terms), (4, 3, col_terms)):
        for ref in refs:
            ref[...] = jnp.zeros_like(ref)
        for k in range(refs[0].shape[0]):
            refs[0][k, pl.ds(one_row, per, 8), :] = jnp.ones((per, LANES), jnp.float32)
    if end:
        rhs_end_ref[...] = jnp.zeros_like(rhs_end_ref)

    def features(g, carry):
        both = both_ref[g]
        parts = [both] + [ref[g] for ref in piece_refs]
        cols = [jnp.concatenate([v[:, c * piece:(c + 1) * piece] for v in parts], axis=1) for c in range(3)]
        rows = [both[:, 3 * piece + c * n_rows:3 * piece + (c + 1) * n_rows] for c in range(3)]
        put_terms(row_terms, rows, 3)
        put_terms(col_terms, cols, 4)
        for block in range(per // fold):
            lefts = []
            for inside in range(fold):
                i = block * fold + inside
                s = g * per + i
                hi, mid, lo = get_terms(row_terms, i)
                left = jnp.concatenate([hi, hi, mid, mid, hi, lo], axis=0)
                lhs_ref[s] = left.T[:deep].astype(jnp.bfloat16)
                if end:
                    lefts += [left, jnp.zeros((SLOT - 48, left.shape[1]), jnp.float32)]
                hi, mid, lo = get_terms(col_terms, i)
                right = jnp.concatenate([hi, mid, hi, mid, lo, hi], axis=0)
                rhs_ref[s] = right[:, :full].astype(jnp.bfloat16)
                if end:
                    lane = lax.broadcasted_iota(jnp.int32, (48, LANES), 1)
                    last = jnp.where(lane < end, right[:, full:full + LANES], 0.0)
                    if inside:
                        last = pltpu.roll(last, inside * end, 1)
                    last = last.astype(jnp.bfloat16)
                    b = g * (per // fold) + block
                    rhs_end_ref[b, pl.ds(SLOT * inside, 48), :] = last
                    terms_end_ref[b, pl.ds(16 * inside, 16), :] = last[0:16]
            if end:
                lhs_end_ref[g * (per // fold) + block] = jnp.concatenate(lefts, axis=0).T[:deep].astype(jnp.bfloat16)
        return carry

    lax.fori_loop(0, groups, features, 0)
    weight_ref[...] = jnp.zeros_like(weight_ref)
    if end:
        weight_end_ref[...] = jnp.zeros_like(weight_end_ref)

    def tanh_block(s, start, size):
        return jnp.tanh(jnp.dot(lhs_ref[s], rhs_ref[s, :, pl.ds(start, size)], preferred_element_type=jnp.float32))

    def tanh_end(b):
        return jnp.tanh(jnp.dot(lhs_end_ref[b], rhs_end_ref[b], preferred_element_type=jnp.float32))

    def add_some(b, carry):
        for inside in range(fold):
            for start, size in chunks:
                weight_ref[:, pl.ds(start, size)] += tanh_block(b * fold + inside, start, size)
        if end:
            weight_end_ref[...] += tanh_end(b)
        return carry

    lax.fori_loop(0, structs // fold, add_some, 0)

    def mask_and_target(start, size):
        count = counts_ref[:, pl.ds(start, size)].astype(jnp.float32)
        row_ids = base_ref[0] + lax.broadcasted_iota(jnp.int32, (n_rows, size), 0)
        mask = jnp.where(seg_rows_ref[...] == seg_cols_ref[:, pl.ds(start, size)], 1.0, 0.3)
        mask = jnp.where(row_ids == col_ids_ref[:, pl.ds(start, size)], 0.0, mask)
        return mask, mask * (count / (count + 8.0))

    scale = 0.5 / structs
    for start, size in chunks:
        mask, goal = mask_and_target(start, size)
        total = weight_ref[pl.ds(0, n_rows), pl.ds(start, size)]
        weight_ref[pl.ds(0, n_rows), pl.ds(start, size)] = mask * (0.5 + scale * total) - goal
    if deep > n_rows:
        weight_ref[pl.ds(n_rows, deep - n_rows), :] = jnp.zeros((deep - n_rows, full), jnp.float32)
    if end:
        def spread(v):
            v = jnp.concatenate([v, jnp.zeros((n_rows, LANES - end), jnp.float32)], axis=1)
            return sum((pltpu.roll(v, k * end, 1) for k in range(1, fold)), v)

        mask, goal = [spread(v) for v in mask_and_target(full, end)]
        part = weight_end_ref[pl.ds(0, n_rows), :]
        total = sum((pltpu.roll(part, k * end, 1) for k in range(1, fold)), part)
        weight_end_ref[pl.ds(0, n_rows), :] = mask * (0.5 + scale * total) - goal
        if deep > n_rows:
            weight_end_ref[pl.ds(n_rows, deep - n_rows), :] = jnp.zeros((deep - n_rows, LANES), jnp.float32)

    def sums(terms, weight, t):
        g = weight * (1.0 - t * t)
        hi = g.astype(jnp.bfloat16)
        lo = (g - hi.astype(jnp.float32)).astype(jnp.bfloat16)
        return (lax.dot_general(terms, hi, NT, preferred_element_type=jnp.float32)
                + lax.dot_general(terms, lo, NT, preferred_element_type=jnp.float32))

    def grad_some(b, carry):
        if end:
            last = sums(terms_end_ref[b], weight_end_ref[...], tanh_end(b))
        for inside in range(fold):
            s = b * fold + inside
            total = last[16 * inside:16 * inside + 16] if end else jnp.zeros((16, deep), jnp.float32)
            for start, size in chunks:
                total += sums(rhs_ref[s, pl.ds(0, 16), pl.ds(start, size)], weight_ref[:, pl.ds(start, size)],
                              tanh_block(s, start, size))
            total = total[:, :n_rows]
            g, i = lax.div(s, per), lax.rem(s, per)
            both = both_ref[g, pl.ds(i, 1), :]
            for c in range(3):
                xyz = both[:, 3 * piece + c * n_rows:3 * piece + (c + 1) * n_rows]
                grad_ref[g, c, pl.ds(i, 1), :] = (0.25 / 16) * (
                    total[c:c + 1] + total[8 + c:9 + c] - total[3:4] * xyz)
        return carry

    lax.fori_loop(0, structs // fold, grad_some, 0)


def split_ens(n_ens, beads, tiles):
    best = None
    for parts in range(1, n_ens + 1):
        if n_ens % parts or beads % parts or beads % (n_ens // parts):
            continue
        cost = 2 * (beads // parts) + tiles * (beads // (n_ens // parts))
        if best is None or cost < best[0]:
            best = (cost, parts)
    return best[1]


def on_device(coords, counts, segments):
    local_n, _, beads = coords.shape
    n_tile = lax.axis_size("tile")
    n_ens = lax.axis_size("ens")
    structs = local_n * n_ens
    n_p = split_ens(n_ens, beads, n_tile)
    n_q = n_ens // n_p
    n_rows, piece = beads // n_p, beads // n_q
    n_cols = piece * n_tile
    tile, ens = lax.axis_index("tile"), lax.axis_index("ens")
    p, q = lax.rem(ens, n_p), lax.div(ens, n_p)
    vmem = pl.BlockSpec(memory_space=pltpu.VMEM)

    send = pl.pallas_call(
        functools.partial(pack_kernel, n_p, n_q),
        out_shape=jax.ShapeDtypeStruct((n_ens, local_n, 3 * (piece + n_rows)), jnp.float32),
        in_specs=[vmem],
        out_specs=vmem,
        name="pack",
    )(jnp.swapaxes(coords, 0, 1))
    both = lax.all_to_all(send, "ens", 0, 0, tiled=True)
    own = both[:, :, :3 * piece]
    pieces = [lax.ppermute(own, "tile", [(t, (t - k) % n_tile) for t in range(n_tile)]) for k in range(1, n_tile)]

    row_base = tile * beads + p * n_rows
    col_bases = [lax.rem(tile + k, n_tile) * beads + q * piece for k in range(n_tile)]
    own_counts = lax.dynamic_slice_in_dim(counts, p * n_rows, n_rows, 0)
    block = jnp.concatenate([lax.dynamic_slice_in_dim(own_counts, b, piece, 1) for b in col_bases], axis=1)
    seg_cols = jnp.concatenate([lax.dynamic_slice_in_dim(segments, b, piece) for b in col_bases])[None, :]
    col_ids = jnp.concatenate([b + jnp.arange(piece, dtype=jnp.int32) for b in col_bases])[None, :]
    seg_rows = lax.dynamic_slice_in_dim(segments, row_base, n_rows)[:, None]

    full = n_cols // LANES * LANES
    end = n_cols - full
    fold = LANES // end if end and LANES % end == 0 and local_n % (LANES // end) == 0 else 1
    deep = up(n_rows, 16)
    row_wide, col_wide = up(n_rows, LANES), up(n_cols, LANES)
    blocks = structs // fold
    grad = pl.pallas_call(
        functools.partial(pair_kernel, n_tile, fold),
        out_shape=jax.ShapeDtypeStruct((n_ens, 3, local_n, n_rows), jnp.float32),
        in_specs=[pl.BlockSpec(memory_space=pltpu.SMEM)] + [vmem] * (4 + n_tile),
        out_specs=vmem,
        scratch_shapes=[
            [pltpu.VMEM((row_wide // LANES, 8 * local_n, LANES), jnp.float32)] * 3,
            [pltpu.VMEM((col_wide // LANES, 8 * local_n, LANES), jnp.float32)] * 3,
            pltpu.VMEM((structs, deep, 48), jnp.bfloat16),
            pltpu.VMEM((blocks, deep, fold * SLOT), jnp.bfloat16),
            pltpu.VMEM((structs, 48, full), jnp.bfloat16),
            pltpu.VMEM((blocks, fold * SLOT, LANES), jnp.bfloat16),
            pltpu.VMEM((blocks, fold * 16, LANES), jnp.bfloat16),
            pltpu.VMEM((deep, full), jnp.float32),
            pltpu.VMEM((deep, LANES), jnp.float32),
        ],
        compiler_params=pltpu.CompilerParams(vmem_limit_bytes=48 << 20),
        name="pairs",
    )(row_base[None], seg_rows, seg_cols, col_ids, block, both, *pieces)

    back = lax.all_to_all(grad, "ens", 0, 0, tiled=True)
    total = pl.pallas_call(
        functools.partial(sum_kernel, n_p, n_q),
        out_shape=jax.ShapeDtypeStruct((3, local_n, beads), jnp.float32),
        in_specs=[vmem],
        out_specs=vmem,
        name="total",
    )(back)
    return jnp.swapaxes(total, 0, 1)


def solution(mesh):
    return jax.shard_map(
        on_device,
        mesh=mesh,
        in_specs=(P("ens", None, "tile"), P("tile", None), P()),
        out_specs=P("ens", None, "tile"),
        check_vma=False,
    )
```

time: 146 us -> 124 us (0.85)
  Pallas kernels: 92.4 us -> 75.8 us
  waiting for transfers between devices: 21.5 us -> 17.8 us
    pallas_call x1, Pallas kernels: 88.8 us -> 72.2 us  [on_device(): pl.pallas_call(functools.partial(pair_kernel, n_tile, fold), out_shape=ja...]
    ppermute x3, waiting for transfers between devices: 11.9 us -> 6.31 us  [on_device(): lax.ppermute(own, 'tile', [(t, (t - k) % n_tile) for t in range(n_tile)])]
    all_to_all x1, waiting for transfers between devices: 9.52 us -> 11.5 us  [on_device(): both = lax.all_to_all(send, 'ens', 0, 0, tiled=True)]
where the time goes in v5:
time: 124 us
  Pallas kernels  75.8 us (61%)
  waiting for transfers between devices  17.8 us (14%)
  blocking collectives  15.6 us (13%)
  starting transfers between devices  9.92 us (8%)
  local copies, waits for them, and re-layouts  4.01 us (3%)
    pallas_call x1, Pallas kernels, on_device(): pl.pallas_call(functools.partial(pair_kernel, n_tile, fold), out_shape=ja...  72.2 us
    all_to_all x1, blocking collectives, on_device(): back = lax.all_to_all(grad, 'ens', 0, 0, tiled=True)  15.6 us
    all_to_all x1, waiting for transfers between devices, on_device(): both = lax.all_to_all(send, 'ens', 0, 0, tiled=True)  11.5 us
    all_to_all x1, starting transfers between devices, on_device(): both = lax.all_to_all(send, 'ens', 0, 0, tiled=True)  6.33 us
    ppermute x3, waiting for transfers between devices, on_device(): lax.ppermute(own, 'tile', [(t, (t - k) % n_tile) for t in range(n_tile)])  6.31 us
    ppermute x3, starting transfers between devices, on_device(): lax.ppermute(own, 'tile', [(t, (t - k) % n_tile) for t in range(n_tile)])  3.6 us
  transfers between devices with their start and end apart: 4, of which 3 were waited for; matrix products, arithmetic and copies ran while one was open for 4% of the time, Pallas kernels for 0%

profile of v5, /device:TPU:0, one launch (start us, length us, event | category | flops | bytes accessed | tf_op | source)
XLA Modules:
  0.0 123.9 jit_solution(9139110855141986664)
XLA Ops:
  0.0 1.9 %pack.1 = f32[8,8,1800]{2,1,0:T(8,128)} custom-call(f32[3,8,800]{2,1,0:T(8,128)} %bitcast.4), custom_call_target="tpu_custom_call" | custom-call | tf_op jit(solution)/shard_map/pack/pallas_call | solution.py:217
  1.9 6.3 %all-to-all-start = ((f32[8,8,1800]{2,1,0:T(8,128)}), f32[8,8,1800]{2,1,0:T(8,128)S(1)}, u32[]{:S(2)}, u32[]{:S(2)}) async-start(f32[8,8,1800]{2,1,0:T(8,128)} %pack.1), calls=%async_computation | async-start | bytes 983040 | tf_op jit(solution)/shard_map/all_to_all | solution.py:224
  8.2 0.9 fusion.1
  9.1 0.1 pad_add_fusion.2
  9.2 2.2 %fusion = (s32[400,200]{1,0:T(8,128)S(1)}, s32[400,200]{1,0:T(8,128)S(1)}, s32[400,200]{1,0:T(8,128)S(1)}, s32[400,200]{1,0:T(8,128)S(1)}) fusion(s32[800,3200]{1,0:T(8,128)} %param.4, s32[]{:T(128)S(6)} %select_n.38, s32[]{:T(128)S(6)} %select_n.39, s32[]{:T(128)S(6)} %select_n.40, s32[]{:T(128)S(6)} %select_n.42, s32[]{:T(128)S(6)} %select_n.41), kind=kLoop, calls=%fused_computation.7 | loop fusion | bytes 2560020 | tf_op jit(solution)/shard_map/dynamic_slice | solution.py:231
  11.4 11.5 %all-to-all-done.both_ref = f32[8,8,1800]{2,1,0:T(8,128)S(1)} async-done(((f32[8,8,1800]{2,1,0:T(8,128)}), f32[8,8,1800]{2,1,0:T(8,128)S(1)}, u32[]{:S(2)}, u32[]{:S(2)}) %all-to-all-start) | async-done | bytes 460832 | tf_op jit(solution)/shard_map/all_to_all | solution.py:224
  22.9 2.5 %collective-permute-start = (f32[8,8,600]{2,1,0:T(8,128)S(1)}, f32[8,8,600]{2,1,0:T(8,128)S(1)}, u32[]{:S(2)}, u32[]{:S(2)}) collective-permute-start(f32[8,8,600]{2,1,0:T(8,128)S(1)} %slice.4), channel_id=1, source_target_pairs={{0,3},{1,0},{2,1},{3,2},{4,7},{5,4},{6,5},{7,6},{8,11},{9,8},{10,9... | collective-permute-start | bytes 460808 | tf_op jit(solution)/shard_map/ppermute | solution.py:226
  25.4 0.5 collective-permute-start.1
  25.9 0.6 collective-permute-start.2
  26.5 0.1 pad_add_fusion.1
  26.6 0.8 dynamic_slice.28
  27.4 0.1 copy.4.seg_rows_ref
  27.5 0.5 pad_add_fusion.counts_ref
  28.0 2.0 %collective-permute-done.rest_0_ = f32[8,8,600]{2,1,0:T(8,128)S(1)} collective-permute-done((f32[8,8,600]{2,1,0:T(8,128)S(1)}, f32[8,8,600]{2,1,0:T(8,128)S(1)}, u32[]{:S(2)}, u32[]{:S(2)}) %collective-permute-start) | collective-permute-done | bytes 153632 | tf_op jit(solution)/shard_map/ppermute | solution.py:226
  30.0 4.3 %collective-permute-done.1.rest_1_ = f32[8,8,600]{2,1,0:T(8,128)S(1)} collective-permute-done((f32[8,8,600]{2,1,0:T(8,128)S(1)}, f32[8,8,600]{2,1,0:T(8,128)S(1)}, u32[]{:S(2)}, u32[]{:S(2)}) %collective-permute-start.1) | collective-permute-done | bytes 153632 | tf_op jit(solution)/shard_map/ppermute | solution.py:226
  34.4 0.0 collective-permute-done.2.rest_2_
  34.4 72.2 %pairs.1 = f32[8,3,8,400]{3,2,1,0:T(8,128)S(1)} custom-call(s32[1]{0:T(128)} %bitcast.base_ref, s32[400,1]{1,0:T(8,128)S(1)} %copy.4.seg_rows_ref, s32[1,800]{1,0:T(1,128)S(1)} %broadcast_in_dim.14.seg_cols_ref, s32[1,800]{1,0:T(1,128)S(1)} %broadcast_in_dim.15.col_ids_ref, s32[400,800]{1,0:T(8,128)S(1)} %pad_add_fusion.counts_ref, ...), custom_call_target="tpu_custom_call" | custom-call | tf_op jit(solution)/shard_map/pairs/pallas_call | solution.py:242
  106.6 15.6 %all_to_all.10.back_ref = f32[8,3,8,400]{3,2,1,0:T(8,128)} all-to-all(f32[8,3,8,400]{3,2,1,0:T(8,128)S(1)} %pairs.1), channel_id=1, replica_groups=mesh['ens'=8,'tile'=4] {'ens'}, dimensions={0} | all-to-all | bytes 614400 | tf_op jit(solution)/shard_map/all_to_all | solution.py:262
  122.2 1.7 %total.1 = f32[3,8,800]{2,1,0:T(8,128)} custom-call(f32[8,3,8,400]{3,2,1,0:T(8,128)} %all_to_all.10.back_ref), custom_call_target="tpu_custom_call" | custom-call | tf_op jit(solution)/shard_map/total/pallas_call | solution.py:263
  (5 shorter events, 0.0 us)
Async XLA Ops:
  1.9 21.0 %all-to-all-start = ((f32[8,8,1800]{2,1,0:T(8,128)}), f32[8,8,1800]{2,1,0:T(8,128)S(1)}, u32[]{:S(2)}, u32[]{:S(2)}) async-start(f32[8,8,1800]{2,1,0:T(8,128)} %pack.1), calls=%async_computation | async-start | bytes 983040 | tf_op jit(solution)/shard_map/all_to_all | solution.py:224
  22.9 7.1 %collective-permute-start = (f32[8,8,600]{2,1,0:T(8,128)S(1)}, f32[8,8,600]{2,1,0:T(8,128)S(1)}, u32[]{:S(2)}, u32[]{:S(2)}) collective-permute-start(f32[8,8,600]{2,1,0:T(8,128)S(1)} %slice.4), channel_id=1, source_target_pairs={{0,3},{1,0},{2,1},{3,2},{4,7},{5,4},{6,5},{7,6},{8,11},{9,8},{10,9... | collective-permute-start | bytes 460808 | tf_op jit(solution)/shard_map/ppermute | solution.py:226
  25.4 9.0 %collective-permute-start.1 = (f32[8,8,600]{2,1,0:T(8,128)S(1)}, f32[8,8,600]{2,1,0:T(8,128)S(1)}, u32[]{:S(2)}, u32[]{:S(2)}) collective-permute-start(f32[8,8,600]{2,1,0:T(8,128)S(1)} %slice.4), channel_id=1, source_target_pairs={{0,2},{1,3},{2,0},{3,1},{4,6},{5,7},{6,4},{7,5},{8,10},{9,11},{10,... | collective-permute-start | bytes 460808 | tf_op jit(solution)/shard_map/ppermute | solution.py:226
  25.9 8.5 %collective-permute-start.2 = (f32[8,8,600]{2,1,0:T(8,128)S(1)}, f32[8,8,600]{2,1,0:T(8,128)S(1)}, u32[]{:S(2)}, u32[]{:S(2)}) collective-permute-start(f32[8,8,600]{2,1,0:T(8,128)S(1)} %slice.4), channel_id=1, source_target_pairs={{0,1},{1,2},{2,3},{3,0},{4,5},{5,6},{6,7},{7,4},{8,9},{9,10},{10,1... | collective-permute-start | bytes 460808 | tf_op jit(solution)/shard_map/ppermute | solution.py:226

commit v6 on v5

--- a/solution.py
+++ b/solution.py
@@ -61,10 +61,54 @@
     return [jnp.concatenate([ref[k, pl.ds(8 * i, 8), :] for k in range(ref.shape[0])], axis=1) for ref in refs]
 
 
-def pair_kernel(tiles, fold, base_ref, seg_rows_ref, seg_cols_ref, col_ids_ref, counts_ref, both_ref, *rest):
+def init_terms(refs, one_row, per):
+    for ref in refs:
+        ref[...] = jnp.zeros_like(ref)
+    for k in range(refs[0].shape[0]):
+        refs[0][k, pl.ds(one_row, per, 8), :] = jnp.ones((per, LANES), jnp.float32)
+
+
+def tanh_product(left, right):
+    return jnp.tanh(jnp.dot(left, right, preferred_element_type=jnp.float32))
+
+
+def row_kernel(n_rows, piece, fold, both_ref, lhs_ref, lhs_end_ref, first_ref, row_terms, col_terms, rhs_ref):
+    groups, per, _ = both_ref.shape
+    deep = first_ref.shape[0]
+    init_terms(row_terms, 4, per)
+    init_terms(col_terms, 3, per)
+
+    def features(g, carry):
+        both = both_ref[g]
+        put_terms(row_terms, [both[:, 3 * piece + c * n_rows:3 * piece + (c + 1) * n_rows] for c in range(3)], 3)
+        put_terms(col_terms, [both[:, c * piece:c * piece + LANES] for c in range(3)], 4)
+        for block in range(per // fold):
+            lefts = []
+            for inside in range(fold):
+                i = block * fold + inside
+                hi, mid, lo = get_terms(row_terms, i)
+                left = jnp.concatenate([hi, hi, mid, mid, hi, lo], axis=0)
+                lhs_ref[g * per + i] = left.T[:deep].astype(jnp.bfloat16)
+                lefts += [left, jnp.zeros((SLOT - 48, left.shape[1]), jnp.float32)]
+                hi, mid, lo = get_terms(col_terms, i)
+                rhs_ref[g * per + i] = jnp.concatenate([hi, mid, hi, mid, lo, hi], axis=0).astype(jnp.bfloat16)
+            lhs_end_ref[g * (per // fold) + block] = jnp.concatenate(lefts, axis=0).T[:deep].astype(jnp.bfloat16)
+        return carry
+
+    lax.fori_loop(0, groups, features, 0)
+    first_ref[...] = jnp.zeros_like(first_ref)
+
+    def add_one(s, carry):
+        first_ref[...] += tanh_product(lhs_ref[s], rhs_ref[s])
+        return carry
+
+    lax.fori_loop(0, groups * per, add_one, 0, unroll=8)
+
+
+def pair_kernel(tiles, fold, head, base_ref, seg_rows_ref, seg_cols_ref, col_ids_ref, counts_ref, lhs_ref,
+                lhs_end_ref, first_ref, both_ref, *rest):
     piece_refs = rest[:tiles - 1]
-    (grad_ref, row_terms, col_terms, lhs_ref, lhs_end_ref, rhs_ref, rhs_end_ref, terms_end_ref, weight_ref,
-     weight_end_ref) = rest[tiles - 1:]
+    grad_ref, col_terms, rhs_ref, rhs_end_ref, terms_end_ref, weight_ref, weight_end_ref = rest[tiles - 1:]
     groups, per, _ = both_ref.shape
     structs = groups * per
     n_rows, n_cols = counts_ref.shape
@@ -73,12 +117,9 @@
     full = rhs_ref.shape[2]
     end = n_cols - full
     chunks = [(a, min(WIDE, full - a)) for a in range(0, full, WIDE)]
-
-    for norm_row, one_row, refs in ((3, 4, row_terms), (4, 3, col_terms)):
-        for ref in refs:
-            ref[...] = jnp.zeros_like(ref)
-        for k in range(refs[0].shape[0]):
-            refs[0][k, pl.ds(one_row, per, 8), :] = jnp.ones((per, LANES), jnp.float32)
+    tail = [(a, min(WIDE, full - a)) for a in range(head, full, WIDE)]
+
+    init_terms(col_terms, 3, per)
     if end:
         rhs_end_ref[...] = jnp.zeros_like(rhs_end_ref)
 
@@ -86,19 +127,11 @@
         both = both_ref[g]
         parts = [both] + [ref[g] for ref in piece_refs]
         cols = [jnp.concatenate([v[:, c * piece:(c + 1) * piece] for v in parts], axis=1) for c in range(3)]
-        rows = [both[:, 3 * piece + c * n_rows:3 * piece + (c + 1) * n_rows] for c in range(3)]
-        put_terms(row_terms, rows, 3)
         put_terms(col_terms, cols, 4)
         for block in range(per // fold):
-            lefts = []
             for inside in range(fold):
                 i = block * fold + inside
                 s = g * per + i
-                hi, mid, lo = get_terms(row_terms, i)
-                left = jnp.concatenate([hi, hi, mid, mid, hi, lo], axis=0)
-                lhs_ref[s] = left.T[:deep].astype(jnp.bfloat16)
-                if end:
-                    lefts += [left, jnp.zeros((SLOT - 48, left.shape[1]), jnp.float32)]
                 hi, mid, lo = get_terms(col_terms, i)
                 right = jnp.concatenate([hi, mid, hi, mid, lo, hi], axis=0)
                 rhs_ref[s] = right[:, :full].astype(jnp.bfloat16)
@@ -111,24 +144,24 @@
                     b = g * (per // fold) + block
                     rhs_end_ref[b, pl.ds(SLOT * inside, 48), :] = last
                     terms_end_ref[b, pl.ds(16 * inside, 16), :] = last[0:16]
-            if end:
-                lhs_end_ref[g * (per // fold) + block] = jnp.concatenate(lefts, axis=0).T[:deep].astype(jnp.bfloat16)
         return carry
 
     lax.fori_loop(0, groups, features, 0)
     weight_ref[...] = jnp.zeros_like(weight_ref)
+    if head:
+        weight_ref[:, pl.ds(0, head)] = first_ref[...]
     if end:
         weight_end_ref[...] = jnp.zeros_like(weight_end_ref)
 
     def tanh_block(s, start, size):
-        return jnp.tanh(jnp.dot(lhs_ref[s], rhs_ref[s, :, pl.ds(start, size)], preferred_element_type=jnp.float32))
+        return tanh_product(lhs_ref[s], rhs_ref[s, :, pl.ds(start, size)])
 
     def tanh_end(b):
-        return jnp.tanh(jnp.dot(lhs_end_ref[b], rhs_end_ref[b], preferred_element_type=jnp.float32))
+        return tanh_product(lhs_end_ref[b], rhs_end_ref[b])
 
     def add_some(b, carry):
         for inside in range(fold):
-            for start, size in chunks:
+            for start, size in tail:
                 weight_ref[:, pl.ds(start, size)] += tanh_block(b * fold + inside, start, size)
         if end:
             weight_end_ref[...] += tanh_end(b)
@@ -239,25 +272,40 @@
     deep = up(n_rows, 16)
     row_wide, col_wide = up(n_rows, LANES), up(n_cols, LANES)
     blocks = structs // fold
+    head = LANES if piece >= LANES else 0
+    lhs, lhs_end, first = pl.pallas_call(
+        functools.partial(row_kernel, n_rows, piece, fold),
+        out_shape=[
+            jax.ShapeDtypeStruct((structs, deep, 48), jnp.bfloat16),
+            jax.ShapeDtypeStruct((blocks, deep, fold * SLOT), jnp.bfloat16),
+            jax.ShapeDtypeStruct((deep, LANES), jnp.float32),
+        ],
+        in_specs=[vmem],
+        out_specs=[vmem] * 3,
+        scratch_shapes=[
+            [pltpu.VMEM((row_wide // LANES, 8 * local_n, LANES), jnp.float32)] * 3,
+            [pltpu.VMEM((1, 8 * local_n, LANES), jnp.float32)] * 3,
+            pltpu.VMEM((structs, 48, LANES), jnp.bfloat16),
+        ],
+        compiler_params=pltpu.CompilerParams(vmem_limit_bytes=32 << 20),
+        name="rows",
+    )(both)
     grad = pl.pallas_call(
-        functools.partial(pair_kernel, n_tile, fold),
+        functools.partial(pair_kernel, n_tile, fold, head),
         out_shape=jax.ShapeDtypeStruct((n_ens, 3, local_n, n_rows), jnp.float32),
-        in_specs=[pl.BlockSpec(memory_space=pltpu.SMEM)] + [vmem] * (4 + n_tile),
+        in_specs=[pl.BlockSpec(memory_space=pltpu.SMEM)] + [vmem] * (7 + n_tile),
         out_specs=vmem,
         scratch_shapes=[
-            [pltpu.VMEM((row_wide // LANES, 8 * local_n, LANES), jnp.float32)] * 3,
             [pltpu.VMEM((col_wide // LANES, 8 * local_n, LANES), jnp.float32)] * 3,
-            pltpu.VMEM((structs, deep, 48), jnp.bfloat16),
-            pltpu.VMEM((blocks, deep, fold * SLOT), jnp.bfloat16),
             pltpu.VMEM((structs, 48, full), jnp.bfloat16),
             pltpu.VMEM((blocks, fold * SLOT, LANES), jnp.bfloat16),
             pltpu.VMEM((blocks, fold * 16, LANES), jnp.bfloat16),
             pltpu.VMEM((deep, full), jnp.float32),
             pltpu.VMEM((deep, LANES), jnp.float32),
         ],
-        compiler_params=pltpu.CompilerParams(vmem_limit_bytes=48 << 20),
+        compiler_params=pltpu.CompilerParams(vmem_limit_bytes=40 << 20),
         name="pairs",
-    )(row_base[None], seg_rows, seg_cols, col_ids, block, both, *pieces)
+    )(row_base[None], seg_rows, seg_cols, col_ids, block, lhs, lhs_end, first, both, *pieces)
 
     back = lax.all_to_all(grad, "ens", 0, 0, tiled=True)
     total = pl.pallas_call(

time: 124 us -> 125 us (level)
  waiting for transfers between devices: 17.8 us -> 11.5 us
  Pallas kernels: 75.8 us -> 81.9 us
    ppermute x3, waiting for transfers between devices: 6.31 us -> 0.01 us  [on_device(): lax.ppermute(own, 'tile', [(t, (t - k) % n_tile) for t in range(n_tile)])]
    pallas_call x1 -> x2, Pallas kernels: 72.2 us -> 78.3 us  [the longest x1 68.8 us: on_device(): pl.pallas_call(functools.partial(pair_kernel, n_tile, fold, head), out_sh...]
  transfers between devices with their start and end apart: 4 -> 4, of which waited for: 3 -> 1; matrix products, arithmetic and copies ran while one was open for 4% -> 4% of each run, Pallas kernels for 0% -> 8%
where the time goes in v6:
time: 125 us
  Pallas kernels  81.9 us (66%)
  blocking collectives  15.6 us (12%)
  waiting for transfers between devices  11.5 us (9%)
  starting transfers between devices  10.8 us (9%)
  local copies, waits for them, and re-layouts  3.99 us (3%)
    pallas_call x1, Pallas kernels, on_device(): pl.pallas_call(functools.partial(pair_kernel, n_tile, fold, head), out_sh...  68.8 us
    all_to_all x1, blocking collectives, on_device(): back = lax.all_to_all(grad, 'ens', 0, 0, tiled=True)  15.6 us
    all_to_all x1, waiting for transfers between devices, on_device(): both = lax.all_to_all(send, 'ens', 0, 0, tiled=True)  11.5 us
    pallas_call x1, Pallas kernels, on_device(): pl.pallas_call(functools.partial(row_kernel, n_rows, piece, fold), out_sh...  9.51 us
    all_to_all x1, starting transfers between devices, on_device(): both = lax.all_to_all(send, 'ens', 0, 0, tiled=True)  6.33 us
    ppermute x3, starting transfers between devices, on_device(): lax.ppermute(own, 'tile', [(t, (t - k) % n_tile) for t in range(n_tile)])  4.5 us
  transfers between devices with their start and end apart: 4, of which 1 were waited for; matrix products, arithmetic and copies ran while one was open for 4% of the time, Pallas kernels for 8%

profile of v6, /device:TPU:0, one launch (start us, length us, event | category | flops | bytes accessed | tf_op | source)
XLA Modules:
  0.0 124.6 jit_solution(15915991177648887195)
XLA Ops:
  0.0 1.9 %pack.1 = f32[8,8,1800]{2,1,0:T(8,128)} custom-call(f32[3,8,800]{2,1,0:T(8,128)} %bitcast.4), custom_call_target="tpu_custom_call" | custom-call | tf_op jit(solution)/shard_map/pack/pallas_call | solution.py:250
  1.9 6.3 %all-to-all-start = ((f32[8,8,1800]{2,1,0:T(8,128)}), f32[8,8,1800]{2,1,0:T(8,128)S(1)}, u32[]{:S(2)}, u32[]{:S(2)}) async-start(f32[8,8,1800]{2,1,0:T(8,128)} %pack.1), calls=%async_computation | async-start | bytes 983040 | tf_op jit(solution)/shard_map/all_to_all | solution.py:257
  8.2 0.9 fusion.1
  9.1 0.1 pad_add_fusion.2
  9.2 2.2 %fusion = (s32[400,200]{1,0:T(8,128)S(1)}, s32[400,200]{1,0:T(8,128)S(1)}, s32[400,200]{1,0:T(8,128)S(1)}, s32[400,200]{1,0:T(8,128)S(1)}) fusion(s32[800,3200]{1,0:T(8,128)} %param.4, s32[]{:T(128)S(6)} %select_n.38, s32[]{:T(128)S(6)} %select_n.39, s32[]{:T(128)S(6)} %select_n.40, s32[]{:T(128)S(6)} %select_n.42, s32[]{:T(128)S(6)} %select_n.41), kind=kLoop, calls=%fused_computation.7 | loop fusion | bytes 2560020 | tf_op jit(solution)/shard_map/dynamic_slice | solution.py:264
  11.4 11.5 %all-to-all-done.both_ref = f32[8,8,1800]{2,1,0:T(8,128)S(1)} async-done(((f32[8,8,1800]{2,1,0:T(8,128)}), f32[8,8,1800]{2,1,0:T(8,128)S(1)}, u32[]{:S(2)}, u32[]{:S(2)}) %all-to-all-start) | async-done | bytes 460832 | tf_op jit(solution)/shard_map/all_to_all | solution.py:257
  22.9 1.5 %collective-permute-start.2 = (f32[8,8,600]{2,1,0:T(8,128)S(1)}, f32[8,8,600]{2,1,0:T(8,128)S(1)}, u32[]{:S(2)}, u32[]{:S(2)}) collective-permute-start(f32[8,8,600]{2,1,0:T(8,128)S(1)} %slice.4), channel_id=1, source_target_pairs={{0,1},{1,2},{2,3},{3,0},{4,5},{5,6},{6,7},{7,4},{8,9},{9,10},{10,1... | collective-permute-start | bytes 460808 | tf_op jit(solution)/shard_map/ppermute | solution.py:259
  24.4 1.5 %collective-permute-start.1 = (f32[8,8,600]{2,1,0:T(8,128)S(1)}, f32[8,8,600]{2,1,0:T(8,128)S(1)}, u32[]{:S(2)}, u32[]{:S(2)}) collective-permute-start(f32[8,8,600]{2,1,0:T(8,128)S(1)} %slice.4), channel_id=1, source_target_pairs={{0,2},{1,3},{2,0},{3,1},{4,6},{5,7},{6,4},{7,5},{8,10},{9,11},{10,... | collective-permute-start | bytes 460808 | tf_op jit(solution)/shard_map/ppermute | solution.py:259
  25.9 1.4 %collective-permute-start = (f32[8,8,600]{2,1,0:T(8,128)S(1)}, f32[8,8,600]{2,1,0:T(8,128)S(1)}, u32[]{:S(2)}, u32[]{:S(2)}) collective-permute-start(f32[8,8,600]{2,1,0:T(8,128)S(1)} %slice.4), channel_id=1, source_target_pairs={{0,3},{1,0},{2,1},{3,2},{4,7},{5,4},{6,5},{7,6},{8,11},{9,8},{10,9... | collective-permute-start | bytes 460808 | tf_op jit(solution)/shard_map/ppermute | solution.py:259
  27.4 0.1 pad_add_fusion.1
  27.5 0.8 dynamic_slice.28
  28.2 0.1 copy.4.seg_rows_ref
  28.4 0.5 pad_add_fusion.counts_ref
  28.9 9.5 %rows.1 = (bf16[64,400,48]{2,1,0:T(8,128)(2,1)S(1)}, bf16[16,400,256]{2,1,0:T(8,128)(2,1)S(1)}, f32[400,128]{1,0:T(8,128)S(1)}) custom-call(f32[8,8,1800]{2,1,0:T(8,128)S(1)} %all-to-all-done.both_ref), custom_call_target="tpu_custom_call" | custom-call | tf_op jit(solution)/shard_map/rows/pallas_call | solution.py:276
  38.4 0.0 collective-permute-done.2.rest_2_
  38.5 0.0 collective-permute-done.1.rest_1_
  38.5 0.0 collective-permute-done.rest_0_
  38.5 68.8 %pairs.1 = f32[8,3,8,400]{3,2,1,0:T(8,128)S(1)} custom-call(s32[1]{0:T(128)} %bitcast.base_ref, s32[400,1]{1,0:T(8,128)S(1)} %copy.4.seg_rows_ref, s32[1,800]{1,0:T(1,128)S(1)} %broadcast_in_dim.14.seg_cols_ref, s32[1,800]{1,0:T(1,128)S(1)} %broadcast_in_dim.15.col_ids_ref, s32[400,800]{1,0:T(8,128)S(1)} %pad_add_fusion.counts_ref, ...), custom_call_target="tpu_custom_call" | custom-call | tf_op jit(solution)/shard_map/pairs/pallas_call | solution.py:293
  107.3 15.6 %all_to_all.10.back_ref = f32[8,3,8,400]{3,2,1,0:T(8,128)} all-to-all(f32[8,3,8,400]{3,2,1,0:T(8,128)S(1)} %pairs.1), channel_id=1, replica_groups=mesh['ens'=8,'tile'=4] {'ens'}, dimensions={0} | all-to-all | bytes 614400 | tf_op jit(solution)/shard_map/all_to_all | solution.py:310
  122.9 1.7 %total.1 = f32[3,8,800]{2,1,0:T(8,128)} custom-call(f32[8,3,8,400]{3,2,1,0:T(8,128)} %all_to_all.10.back_ref), custom_call_target="tpu_custom_call" | custom-call | tf_op jit(solution)/shard_map/total/pallas_call | solution.py:311
  (5 shorter events, 0.0 us)
Async XLA Ops:
  1.9 21.0 %all-to-all-start = ((f32[8,8,1800]{2,1,0:T(8,128)}), f32[8,8,1800]{2,1,0:T(8,128)S(1)}, u32[]{:S(2)}, u32[]{:S(2)}) async-start(f32[8,8,1800]{2,1,0:T(8,128)} %pack.1), calls=%async_computation | async-start | bytes 983040 | tf_op jit(solution)/shard_map/all_to_all | solution.py:257
  22.9 15.6 %collective-permute-start.2 = (f32[8,8,600]{2,1,0:T(8,128)S(1)}, f32[8,8,600]{2,1,0:T(8,128)S(1)}, u32[]{:S(2)}, u32[]{:S(2)}) collective-permute-start(f32[8,8,600]{2,1,0:T(8,128)S(1)} %slice.4), channel_id=1, source_target_pairs={{0,1},{1,2},{2,3},{3,0},{4,5},{5,6},{6,7},{7,4},{8,9},{9,10},{10,1... | collective-permute-start | bytes 460808 | tf_op jit(solution)/shard_map/ppermute | solution.py:259
  24.4 14.0 %collective-permute-start.1 = (f32[8,8,600]{2,1,0:T(8,128)S(1)}, f32[8,8,600]{2,1,0:T(8,128)S(1)}, u32[]{:S(2)}, u32[]{:S(2)}) collective-permute-start(f32[8,8,600]{2,1,0:T(8,128)S(1)} %slice.4), channel_id=1, source_target_pairs={{0,2},{1,3},{2,0},{3,1},{4,6},{5,7},{6,4},{7,5},{8,10},{9,11},{10,... | collective-permute-start | bytes 460808 | tf_op jit(solution)/shard_map/ppermute | solution.py:259
  25.9 12.5 %collective-permute-start = (f32[8,8,600]{2,1,0:T(8,128)S(1)}, f32[8,8,600]{2,1,0:T(8,128)S(1)}, u32[]{:S(2)}, u32[]{:S(2)}) collective-permute-start(f32[8,8,600]{2,1,0:T(8,128)S(1)} %slice.4), channel_id=1, source_target_pairs={{0,3},{1,0},{2,1},{3,2},{4,7},{5,4},{6,5},{7,6},{8,11},{9,8},{10,9... | collective-permute-start | bytes 460808 | tf_op jit(solution)/shard_map/ppermute | solution.py:259

commit v7 on v5

--- a/solution.py
+++ b/solution.py
@@ -166,18 +166,21 @@
         g = weight * (1.0 - t * t)
         hi = g.astype(jnp.bfloat16)
         lo = (g - hi.astype(jnp.float32)).astype(jnp.bfloat16)
-        return (lax.dot_general(terms, hi, NT, preferred_element_type=jnp.float32)
-                + lax.dot_general(terms, lo, NT, preferred_element_type=jnp.float32))
+        return (lax.dot_general(hi, terms, NT, preferred_element_type=jnp.float32)
+                + lax.dot_general(lo, terms, NT, preferred_element_type=jnp.float32))
 
     def grad_some(b, carry):
         if end:
-            last = sums(terms_end_ref[b], weight_end_ref[...], tanh_end(b))
+            last = sums(terms_end_ref[b], weight_end_ref[...], tanh_end(b)).T
         for inside in range(fold):
             s = b * fold + inside
-            total = last[16 * inside:16 * inside + 16] if end else jnp.zeros((16, deep), jnp.float32)
+            total = jnp.zeros((deep, 16), jnp.float32)
             for start, size in chunks:
                 total += sums(rhs_ref[s, pl.ds(0, 16), pl.ds(start, size)], weight_ref[:, pl.ds(start, size)],
                               tanh_block(s, start, size))
+            total = total.T
+            if end:
+                total += last[16 * inside:16 * inside + 16]
             total = total[:, :n_rows]
             g, i = lax.div(s, per), lax.rem(s, per)
             both = both_ref[g, pl.ds(i, 1), :]

time: 124 us -> 117 us (0.944)
  Pallas kernels: 75.8 us -> 68.2 us
    pallas_call x1, Pallas kernels: 72.2 us -> 64.6 us  [on_device(): pl.pallas_call(functools.partial(pair_kernel, n_tile, fold), out_shape=ja...]
where the time goes in v7:
time: 117 us; the launch traced here: 116 us
  Pallas kernels  68.2 us (58%)
  waiting for transfers between devices  17.8 us (15%)
  blocking collectives  15.6 us (13%)
  starting transfers between devices  9.92 us (8%)
  local copies, waits for them, and re-layouts  4.01 us (3%)
    pallas_call x1, Pallas kernels, on_device(): pl.pallas_call(functools.partial(pair_kernel, n_tile, fold), out_shape=ja...  64.6 us
    all_to_all x1, blocking collectives, on_device(): back = lax.all_to_all(grad, 'ens', 0, 0, tiled=True)  15.6 us
    all_to_all x1, waiting for transfers between devices, on_device(): both = lax.all_to_all(send, 'ens', 0, 0, tiled=True)  11.5 us
    all_to_all x1, starting transfers between devices, on_device(): both = lax.all_to_all(send, 'ens', 0, 0, tiled=True)  6.33 us
    ppermute x3, waiting for transfers between devices, on_device(): lax.ppermute(own, 'tile', [(t, (t - k) % n_tile) for t in range(n_tile)])  6.31 us
    ppermute x3, starting transfers between devices, on_device(): lax.ppermute(own, 'tile', [(t, (t - k) % n_tile) for t in range(n_tile)])  3.6 us
  transfers between devices with their start and end apart: 4, of which 3 were waited for; matrix products, arithmetic and copies ran while one was open for 4% of the time, Pallas kernels for 0%

profile of v7, /device:TPU:0, one launch (start us, length us, event | category | flops | bytes accessed | tf_op | source)
XLA Modules:
  0.0 116.3 jit_solution(3412554729671240417)
XLA Ops:
  0.0 1.9 %pack.1 = f32[8,8,1800]{2,1,0:T(8,128)} custom-call(f32[3,8,800]{2,1,0:T(8,128)} %bitcast.4), custom_call_target="tpu_custom_call" | custom-call | tf_op jit(solution)/shard_map/pack/pallas_call | solution.py:220
  1.9 6.3 %all-to-all-start = ((f32[8,8,1800]{2,1,0:T(8,128)}), f32[8,8,1800]{2,1,0:T(8,128)S(1)}, u32[]{:S(2)}, u32[]{:S(2)}) async-start(f32[8,8,1800]{2,1,0:T(8,128)} %pack.1), calls=%async_computation | async-start | bytes 983040 | tf_op jit(solution)/shard_map/all_to_all | solution.py:227
  8.2 0.9 fusion.1
  9.1 0.1 pad_add_fusion.2
  9.2 2.2 %fusion = (s32[400,200]{1,0:T(8,128)S(1)}, s32[400,200]{1,0:T(8,128)S(1)}, s32[400,200]{1,0:T(8,128)S(1)}, s32[400,200]{1,0:T(8,128)S(1)}) fusion(s32[800,3200]{1,0:T(8,128)} %param.4, s32[]{:T(128)S(6)} %select_n.38, s32[]{:T(128)S(6)} %select_n.39, s32[]{:T(128)S(6)} %select_n.40, s32[]{:T(128)S(6)} %select_n.42, s32[]{:T(128)S(6)} %select_n.41), kind=kLoop, calls=%fused_computation.7 | loop fusion | bytes 2560020 | tf_op jit(solution)/shard_map/dynamic_slice | solution.py:234
  11.4 11.5 %all-to-all-done.both_ref = f32[8,8,1800]{2,1,0:T(8,128)S(1)} async-done(((f32[8,8,1800]{2,1,0:T(8,128)}), f32[8,8,1800]{2,1,0:T(8,128)S(1)}, u32[]{:S(2)}, u32[]{:S(2)}) %all-to-all-start) | async-done | bytes 460832 | tf_op jit(solution)/shard_map/all_to_all | solution.py:227
  22.9 2.5 %collective-permute-start = (f32[8,8,600]{2,1,0:T(8,128)S(1)}, f32[8,8,600]{2,1,0:T(8,128)S(1)}, u32[]{:S(2)}, u32[]{:S(2)}) collective-permute-start(f32[8,8,600]{2,1,0:T(8,128)S(1)} %slice.4), channel_id=1, source_target_pairs={{0,3},{1,0},{2,1},{3,2},{4,7},{5,4},{6,5},{7,6},{8,11},{9,8},{10,9... | collective-permute-start | bytes 460808 | tf_op jit(solution)/shard_map/ppermute | solution.py:229
  25.4 0.5 collective-permute-start.1
  25.9 0.6 collective-permute-start.2
  26.5 0.1 pad_add_fusion.1
  26.6 0.8 dynamic_slice.28
  27.4 0.1 copy.4.seg_rows_ref
  27.5 0.5 pad_add_fusion.counts_ref
  28.0 2.0 %collective-permute-done.rest_0_ = f32[8,8,600]{2,1,0:T(8,128)S(1)} collective-permute-done((f32[8,8,600]{2,1,0:T(8,128)S(1)}, f32[8,8,600]{2,1,0:T(8,128)S(1)}, u32[]{:S(2)}, u32[]{:S(2)}) %collective-permute-start) | collective-permute-done | bytes 153632 | tf_op jit(solution)/shard_map/ppermute | solution.py:229
  30.0 4.3 %collective-permute-done.1.rest_1_ = f32[8,8,600]{2,1,0:T(8,128)S(1)} collective-permute-done((f32[8,8,600]{2,1,0:T(8,128)S(1)}, f32[8,8,600]{2,1,0:T(8,128)S(1)}, u32[]{:S(2)}, u32[]{:S(2)}) %collective-permute-start.1) | collective-permute-done | bytes 153632 | tf_op jit(solution)/shard_map/ppermute | solution.py:229
  34.4 0.0 collective-permute-done.2.rest_2_
  34.4 64.6 %pairs.1 = f32[8,3,8,400]{3,2,1,0:T(8,128)S(1)} custom-call(s32[1]{0:T(128)} %bitcast.base_ref, s32[400,1]{1,0:T(8,128)S(1)} %copy.4.seg_rows_ref, s32[1,800]{1,0:T(1,128)S(1)} %broadcast_in_dim.14.seg_cols_ref, s32[1,800]{1,0:T(1,128)S(1)} %broadcast_in_dim.15.col_ids_ref, s32[400,800]{1,0:T(8,128)S(1)} %pad_add_fusion.counts_ref, ...), custom_call_target="tpu_custom_call" | custom-call | tf_op jit(solution)/shard_map/pairs/pallas_call | solution.py:245
  98.9 15.6 %all_to_all.10.back_ref = f32[8,3,8,400]{3,2,1,0:T(8,128)} all-to-all(f32[8,3,8,400]{3,2,1,0:T(8,128)S(1)} %pairs.1), channel_id=1, replica_groups=mesh['ens'=8,'tile'=4] {'ens'}, dimensions={0} | all-to-all | bytes 614400 | tf_op jit(solution)/shard_map/all_to_all | solution.py:265
  114.6 1.7 %total.1 = f32[3,8,800]{2,1,0:T(8,128)} custom-call(f32[8,3,8,400]{3,2,1,0:T(8,128)} %all_to_all.10.back_ref), custom_call_target="tpu_custom_call" | custom-call | tf_op jit(solution)/shard_map/total/pallas_call | solution.py:266
  (5 shorter events, 0.0 us)
Async XLA Ops:
  1.9 21.0 %all-to-all-start = ((f32[8,8,1800]{2,1,0:T(8,128)}), f32[8,8,1800]{2,1,0:T(8,128)S(1)}, u32[]{:S(2)}, u32[]{:S(2)}) async-start(f32[8,8,1800]{2,1,0:T(8,128)} %pack.1), calls=%async_computation | async-start | bytes 983040 | tf_op jit(solution)/shard_map/all_to_all | solution.py:227
  22.9 7.1 %collective-permute-start = (f32[8,8,600]{2,1,0:T(8,128)S(1)}, f32[8,8,600]{2,1,0:T(8,128)S(1)}, u32[]{:S(2)}, u32[]{:S(2)}) collective-permute-start(f32[8,8,600]{2,1,0:T(8,128)S(1)} %slice.4), channel_id=1, source_target_pairs={{0,3},{1,0},{2,1},{3,2},{4,7},{5,4},{6,5},{7,6},{8,11},{9,8},{10,9... | collective-permute-start | bytes 460808 | tf_op jit(solution)/shard_map/ppermute | solution.py:229
  25.4 9.0 %collective-permute-start.1 = (f32[8,8,600]{2,1,0:T(8,128)S(1)}, f32[8,8,600]{2,1,0:T(8,128)S(1)}, u32[]{:S(2)}, u32[]{:S(2)}) collective-permute-start(f32[8,8,600]{2,1,0:T(8,128)S(1)} %slice.4), channel_id=1, source_target_pairs={{0,2},{1,3},{2,0},{3,1},{4,6},{5,7},{6,4},{7,5},{8,10},{9,11},{10,... | collective-permute-start | bytes 460808 | tf_op jit(solution)/shard_map/ppermute | solution.py:229
  25.9 8.5 %collective-permute-start.2 = (f32[8,8,600]{2,1,0:T(8,128)S(1)}, f32[8,8,600]{2,1,0:T(8,128)S(1)}, u32[]{:S(2)}, u32[]{:S(2)}) collective-permute-start(f32[8,8,600]{2,1,0:T(8,128)S(1)} %slice.4), channel_id=1, source_target_pairs={{0,1},{1,2},{2,3},{3,0},{4,5},{5,6},{6,7},{7,4},{8,9},{9,10},{10,1... | collective-permute-start | bytes 460808 | tf_op jit(solution)/shard_map/ppermute | solution.py:229

commit v8 on v7

--- a/solution.py
+++ b/solution.py
@@ -162,22 +162,25 @@
         if deep > n_rows:
             weight_end_ref[pl.ds(n_rows, deep - n_rows), :] = jnp.zeros((deep - n_rows, LANES), jnp.float32)
 
-    def sums(terms, weight, t):
+    def split2(weight, t):
         g = weight * (1.0 - t * t)
         hi = g.astype(jnp.bfloat16)
-        lo = (g - hi.astype(jnp.float32)).astype(jnp.bfloat16)
-        return (lax.dot_general(hi, terms, NT, preferred_element_type=jnp.float32)
-                + lax.dot_general(lo, terms, NT, preferred_element_type=jnp.float32))
+        return [hi, (g - hi.astype(jnp.float32)).astype(jnp.bfloat16)]
+
+    def sums(terms, parts):
+        return lax.dot_general(jnp.concatenate(parts, axis=1), jnp.concatenate(terms, axis=1), NT,
+                               preferred_element_type=jnp.float32)
 
     def grad_some(b, carry):
         if end:
-            last = sums(terms_end_ref[b], weight_end_ref[...], tanh_end(b)).T
+            last = sums([terms_end_ref[b]] * 2, split2(weight_end_ref[...], tanh_end(b))).T
         for inside in range(fold):
             s = b * fold + inside
-            total = jnp.zeros((deep, 16), jnp.float32)
+            terms, parts = [], []
             for start, size in chunks:
-                total += sums(rhs_ref[s, pl.ds(0, 16), pl.ds(start, size)], weight_ref[:, pl.ds(start, size)],
-                              tanh_block(s, start, size))
+                terms += [rhs_ref[s, pl.ds(0, 16), pl.ds(start, size)]] * 2
+                parts += split2(weight_ref[:, pl.ds(start, size)], tanh_block(s, start, size))
+            total = sums(terms, parts)
             total = total.T
             if end:
                 total += last[16 * inside:16 * inside + 16]

time: 117 us -> 112 us (0.957)
  Pallas kernels: 68.2 us -> 63.2 us
    pallas_call x1, Pallas kernels: 64.6 us -> 59.6 us  [on_device(): pl.pallas_call(functools.partial(pair_kernel, n_tile, fold), out_shape=ja...]
where the time goes in v8:
time: 112 us; the launch traced here: 111 us
  Pallas kernels  63.2 us (56%)
  waiting for transfers between devices  17.8 us (16%)
  blocking collectives  15.6 us (14%)
  starting transfers between devices  9.92 us (9%)
  local copies, waits for them, and re-layouts  4.01 us (4%)
    pallas_call x1, Pallas kernels, on_device(): pl.pallas_call(functools.partial(pair_kernel, n_tile, fold), out_shape=ja...  59.6 us
    all_to_all x1, blocking collectives, on_device(): back = lax.all_to_all(grad, 'ens', 0, 0, tiled=True)  15.6 us
    all_to_all x1, waiting for transfers between devices, on_device(): both = lax.all_to_all(send, 'ens', 0, 0, tiled=True)  11.5 us
    all_to_all x1, starting transfers between devices, on_device(): both = lax.all_to_all(send, 'ens', 0, 0, tiled=True)  6.33 us
    ppermute x3, waiting for transfers between devices, on_device(): lax.ppermute(own, 'tile', [(t, (t - k) % n_tile) for t in range(n_tile)])  6.31 us
    ppermute x3, starting transfers between devices, on_device(): lax.ppermute(own, 'tile', [(t, (t - k) % n_tile) for t in range(n_tile)])  3.6 us
  transfers between devices with their start and end apart: 4, of which 3 were waited for; matrix products, arithmetic and copies ran while one was open for 4% of the time, Pallas kernels for 0%

profile of v8, /device:TPU:0, one launch (start us, length us, event | category | flops | bytes accessed | tf_op | source)
XLA Modules:
  0.0 111.3 jit_solution(3083842078997993592)
XLA Ops:
  0.0 1.9 %pack.1 = f32[8,8,1800]{2,1,0:T(8,128)} custom-call(f32[3,8,800]{2,1,0:T(8,128)} %bitcast.4), custom_call_target="tpu_custom_call" | custom-call | tf_op jit(solution)/shard_map/pack/pallas_call | solution.py:223
  1.9 6.3 %all-to-all-start = ((f32[8,8,1800]{2,1,0:T(8,128)}), f32[8,8,1800]{2,1,0:T(8,128)S(1)}, u32[]{:S(2)}, u32[]{:S(2)}) async-start(f32[8,8,1800]{2,1,0:T(8,128)} %pack.1), calls=%async_computation | async-start | bytes 983040 | tf_op jit(solution)/shard_map/all_to_all | solution.py:230
  8.2 0.9 fusion.1
  9.1 0.1 pad_add_fusion.2
  9.2 2.2 %fusion = (s32[400,200]{1,0:T(8,128)S(1)}, s32[400,200]{1,0:T(8,128)S(1)}, s32[400,200]{1,0:T(8,128)S(1)}, s32[400,200]{1,0:T(8,128)S(1)}) fusion(s32[800,3200]{1,0:T(8,128)} %param.4, s32[]{:T(128)S(6)} %select_n.38, s32[]{:T(128)S(6)} %select_n.39, s32[]{:T(128)S(6)} %select_n.40, s32[]{:T(128)S(6)} %select_n.42, s32[]{:T(128)S(6)} %select_n.41), kind=kLoop, calls=%fused_computation.7 | loop fusion | bytes 2560020 | tf_op jit(solution)/shard_map/dynamic_slice | solution.py:237
  11.4 11.5 %all-to-all-done.both_ref = f32[8,8,1800]{2,1,0:T(8,128)S(1)} async-done(((f32[8,8,1800]{2,1,0:T(8,128)}), f32[8,8,1800]{2,1,0:T(8,128)S(1)}, u32[]{:S(2)}, u32[]{:S(2)}) %all-to-all-start) | async-done | bytes 460832 | tf_op jit(solution)/shard_map/all_to_all | solution.py:230
  22.9 2.5 %collective-permute-start = (f32[8,8,600]{2,1,0:T(8,128)S(1)}, f32[8,8,600]{2,1,0:T(8,128)S(1)}, u32[]{:S(2)}, u32[]{:S(2)}) collective-permute-start(f32[8,8,600]{2,1,0:T(8,128)S(1)} %slice.4), channel_id=1, source_target_pairs={{0,3},{1,0},{2,1},{3,2},{4,7},{5,4},{6,5},{7,6},{8,11},{9,8},{10,9... | collective-permute-start | bytes 460808 | tf_op jit(solution)/shard_map/ppermute | solution.py:232
  25.4 0.5 collective-permute-start.1
  25.9 0.6 collective-permute-start.2
  26.5 0.1 pad_add_fusion.1
  26.6 0.8 dynamic_slice.28
  27.4 0.1 copy.4.seg_rows_ref
  27.5 0.5 pad_add_fusion.counts_ref
  28.0 2.0 %collective-permute-done.rest_0_ = f32[8,8,600]{2,1,0:T(8,128)S(1)} collective-permute-done((f32[8,8,600]{2,1,0:T(8,128)S(1)}, f32[8,8,600]{2,1,0:T(8,128)S(1)}, u32[]{:S(2)}, u32[]{:S(2)}) %collective-permute-start) | collective-permute-done | bytes 153632 | tf_op jit(solution)/shard_map/ppermute | solution.py:232
  30.0 4.3 %collective-permute-done.1.rest_1_ = f32[8,8,600]{2,1,0:T(8,128)S(1)} collective-permute-done((f32[8,8,600]{2,1,0:T(8,128)S(1)}, f32[8,8,600]{2,1,0:T(8,128)S(1)}, u32[]{:S(2)}, u32[]{:S(2)}) %collective-permute-start.1) | collective-permute-done | bytes 153632 | tf_op jit(solution)/shard_map/ppermute | solution.py:232
  34.4 0.0 collective-permute-done.2.rest_2_
  34.4 59.6 %pairs.1 = f32[8,3,8,400]{3,2,1,0:T(8,128)S(1)} custom-call(s32[1]{0:T(128)} %bitcast.base_ref, s32[400,1]{1,0:T(8,128)S(1)} %copy.4.seg_rows_ref, s32[1,800]{1,0:T(1,128)S(1)} %broadcast_in_dim.14.seg_cols_ref, s32[1,800]{1,0:T(1,128)S(1)} %broadcast_in_dim.15.col_ids_ref, s32[400,800]{1,0:T(8,128)S(1)} %pad_add_fusion.counts_ref, ...), custom_call_target="tpu_custom_call" | custom-call | tf_op jit(solution)/shard_map/pairs/pallas_call | solution.py:248
  94.0 15.6 %all_to_all.10.back_ref = f32[8,3,8,400]{3,2,1,0:T(8,128)} all-to-all(f32[8,3,8,400]{3,2,1,0:T(8,128)S(1)} %pairs.1), channel_id=1, replica_groups=mesh['ens'=8,'tile'=4] {'ens'}, dimensions={0} | all-to-all | bytes 614400 | tf_op jit(solution)/shard_map/all_to_all | solution.py:268
  109.6 1.7 %total.1 = f32[3,8,800]{2,1,0:T(8,128)} custom-call(f32[8,3,8,400]{3,2,1,0:T(8,128)} %all_to_all.10.back_ref), custom_call_target="tpu_custom_call" | custom-call | tf_op jit(solution)/shard_map/total/pallas_call | solution.py:269
  (5 shorter events, 0.0 us)
Async XLA Ops:
  1.9 21.0 %all-to-all-start = ((f32[8,8,1800]{2,1,0:T(8,128)}), f32[8,8,1800]{2,1,0:T(8,128)S(1)}, u32[]{:S(2)}, u32[]{:S(2)}) async-start(f32[8,8,1800]{2,1,0:T(8,128)} %pack.1), calls=%async_computation | async-start | bytes 983040 | tf_op jit(solution)/shard_map/all_to_all | solution.py:230
  22.9 7.1 %collective-permute-start = (f32[8,8,600]{2,1,0:T(8,128)S(1)}, f32[8,8,600]{2,1,0:T(8,128)S(1)}, u32[]{:S(2)}, u32[]{:S(2)}) collective-permute-start(f32[8,8,600]{2,1,0:T(8,128)S(1)} %slice.4), channel_id=1, source_target_pairs={{0,3},{1,0},{2,1},{3,2},{4,7},{5,4},{6,5},{7,6},{8,11},{9,8},{10,9... | collective-permute-start | bytes 460808 | tf_op jit(solution)/shard_map/ppermute | solution.py:232
  25.4 9.0 %collective-permute-start.1 = (f32[8,8,600]{2,1,0:T(8,128)S(1)}, f32[8,8,600]{2,1,0:T(8,128)S(1)}, u32[]{:S(2)}, u32[]{:S(2)}) collective-permute-start(f32[8,8,600]{2,1,0:T(8,128)S(1)} %slice.4), channel_id=1, source_target_pairs={{0,2},{1,3},{2,0},{3,1},{4,6},{5,7},{6,4},{7,5},{8,10},{9,11},{10,... | collective-permute-start | bytes 460808 | tf_op jit(solution)/shard_map/ppermute | solution.py:232
  25.9 8.5 %collective-permute-start.2 = (f32[8,8,600]{2,1,0:T(8,128)S(1)}, f32[8,8,600]{2,1,0:T(8,128)S(1)}, u32[]{:S(2)}, u32[]{:S(2)}) collective-permute-start(f32[8,8,600]{2,1,0:T(8,128)S(1)} %slice.4), channel_id=1, source_target_pairs={{0,1},{1,2},{2,3},{3,0},{4,5},{5,6},{6,7},{7,4},{8,9},{9,10},{10,1... | collective-permute-start | bytes 460808 | tf_op jit(solution)/shard_map/ppermute | solution.py:232

commit v9 on v8

--- a/solution.py
+++ b/solution.py
@@ -10,6 +10,7 @@
 LANES = 128
 WIDE = 256
 SLOT = 64
+FINE = 32768.0
 NT = (((1,), (1,)), ((), ()))
 
 
@@ -147,7 +148,7 @@
     for start, size in chunks:
         mask, goal = mask_and_target(start, size)
         total = weight_ref[pl.ds(0, n_rows), pl.ds(start, size)]
-        weight_ref[pl.ds(0, n_rows), pl.ds(start, size)] = mask * (0.5 + scale * total) - goal
+        weight_ref[pl.ds(0, n_rows), pl.ds(start, size)] = FINE * (mask * (0.5 + scale * total) - goal)
     if deep > n_rows:
         weight_ref[pl.ds(n_rows, deep - n_rows), :] = jnp.zeros((deep - n_rows, full), jnp.float32)
     if end:
@@ -158,29 +159,27 @@
         mask, goal = [spread(v) for v in mask_and_target(full, end)]
         part = weight_end_ref[pl.ds(0, n_rows), :]
         total = sum((pltpu.roll(part, k * end, 1) for k in range(1, fold)), part)
-        weight_end_ref[pl.ds(0, n_rows), :] = mask * (0.5 + scale * total) - goal
+        weight_end_ref[pl.ds(0, n_rows), :] = FINE * (mask * (0.5 + scale * total) - goal)
         if deep > n_rows:
             weight_end_ref[pl.ds(n_rows, deep - n_rows), :] = jnp.zeros((deep - n_rows, LANES), jnp.float32)
 
     def split2(weight, t):
         g = weight * (1.0 - t * t)
         hi = g.astype(jnp.bfloat16)
-        return [hi, (g - hi.astype(jnp.float32)).astype(jnp.bfloat16)]
+        return hi, (g - hi.astype(jnp.float32)).astype(jnp.float8_e4m3fn)
 
     def sums(terms, parts):
-        return lax.dot_general(jnp.concatenate(parts, axis=1), jnp.concatenate(terms, axis=1), NT,
-                               preferred_element_type=jnp.float32)
+        hi, lo = [jnp.concatenate(v, axis=1) for v in zip(*parts)]
+        return (lax.dot_general(hi, terms, NT, preferred_element_type=jnp.float32)
+                + lax.dot_general(lo, terms.astype(jnp.float8_e4m3fn), NT, preferred_element_type=jnp.float32))
 
     def grad_some(b, carry):
         if end:
-            last = sums([terms_end_ref[b]] * 2, split2(weight_end_ref[...], tanh_end(b))).T
+            last = sums(terms_end_ref[b], [split2(weight_end_ref[...], tanh_end(b))]).T
         for inside in range(fold):
             s = b * fold + inside
-            terms, parts = [], []
-            for start, size in chunks:
-                terms += [rhs_ref[s, pl.ds(0, 16), pl.ds(start, size)]] * 2
-                parts += split2(weight_ref[:, pl.ds(start, size)], tanh_block(s, start, size))
-            total = sums(terms, parts)
+            total = sums(rhs_ref[s, pl.ds(0, 16), :],
+                         [split2(weight_ref[:, pl.ds(start, size)], tanh_block(s, start, size)) for start, size in chunks])
             total = total.T
             if end:
                 total += last[16 * inside:16 * inside + 16]
@@ -189,7 +188,7 @@
             both = both_ref[g, pl.ds(i, 1), :]
             for c in range(3):
                 xyz = both[:, 3 * piece + c * n_rows:3 * piece + (c + 1) * n_rows]
-                grad_ref[g, c, pl.ds(i, 1), :] = (0.25 / 16) * (
+                grad_ref[g, c, pl.ds(i, 1), :] = (0.25 / 16 / FINE) * (
                     total[c:c + 1] + total[8 + c:9 + c] - total[3:4] * xyz)
         return carry
 

time: 112 us -> 114 us (1.018)
  Pallas kernels: 63.2 us -> 65.9 us
    pallas_call x1, Pallas kernels: 59.6 us -> 62.3 us  [on_device(): pl.pallas_call(functools.partial(pair_kernel, n_tile, fold), out_shape=ja...]
where the time goes in v9:
time: 114 us
  Pallas kernels  65.9 us (58%)
  waiting for transfers between devices  17.8 us (16%)
  blocking collectives  15.6 us (14%)
  starting transfers between devices  9.92 us (9%)
  local copies, waits for them, and re-layouts  4.01 us (4%)
    pallas_call x1, Pallas kernels, on_device(): pl.pallas_call(functools.partial(pair_kernel, n_tile, fold), out_shape=ja...  62.3 us
    all_to_all x1, blocking collectives, on_device(): back = lax.all_to_all(grad, 'ens', 0, 0, tiled=True)  15.6 us
    all_to_all x1, waiting for transfers between devices, on_device(): both = lax.all_to_all(send, 'ens', 0, 0, tiled=True)  11.5 us
    all_to_all x1, starting transfers between devices, on_device(): both = lax.all_to_all(send, 'ens', 0, 0, tiled=True)  6.33 us
    ppermute x3, waiting for transfers between devices, on_device(): lax.ppermute(own, 'tile', [(t, (t - k) % n_tile) for t in range(n_tile)])  6.31 us
    ppermute x3, starting transfers between devices, on_device(): lax.ppermute(own, 'tile', [(t, (t - k) % n_tile) for t in range(n_tile)])  3.6 us
  transfers between devices with their start and end apart: 4, of which 3 were waited for; matrix products, arithmetic and copies ran while one was open for 4% of the time, Pallas kernels for 0%

profile of v9, /device:TPU:0, one launch (start us, length us, event | category | flops | bytes accessed | tf_op | source)
XLA Modules:
  0.0 114.0 jit_solution(10023708236798098775)
XLA Ops:
  0.0 1.9 %pack.1 = f32[8,8,1800]{2,1,0:T(8,128)} custom-call(f32[3,8,800]{2,1,0:T(8,128)} %bitcast.4), custom_call_target="tpu_custom_call" | custom-call | tf_op jit(solution)/shard_map/pack/pallas_call | solution.py:222
  1.9 6.3 %all-to-all-start = ((f32[8,8,1800]{2,1,0:T(8,128)}), f32[8,8,1800]{2,1,0:T(8,128)S(1)}, u32[]{:S(2)}, u32[]{:S(2)}) async-start(f32[8,8,1800]{2,1,0:T(8,128)} %pack.1), calls=%async_computation | async-start | bytes 983040 | tf_op jit(solution)/shard_map/all_to_all | solution.py:229
  8.2 0.9 fusion.1
  9.1 0.1 pad_add_fusion.2
  9.2 2.2 %fusion = (s32[400,200]{1,0:T(8,128)S(1)}, s32[400,200]{1,0:T(8,128)S(1)}, s32[400,200]{1,0:T(8,128)S(1)}, s32[400,200]{1,0:T(8,128)S(1)}) fusion(s32[800,3200]{1,0:T(8,128)} %param.4, s32[]{:T(128)S(6)} %select_n.38, s32[]{:T(128)S(6)} %select_n.39, s32[]{:T(128)S(6)} %select_n.40, s32[]{:T(128)S(6)} %select_n.42, s32[]{:T(128)S(6)} %select_n.41), kind=kLoop, calls=%fused_computation.7 | loop fusion | bytes 2560020 | tf_op jit(solution)/shard_map/dynamic_slice | solution.py:236
  11.4 11.5 %all-to-all-done.both_ref = f32[8,8,1800]{2,1,0:T(8,128)S(1)} async-done(((f32[8,8,1800]{2,1,0:T(8,128)}), f32[8,8,1800]{2,1,0:T(8,128)S(1)}, u32[]{:S(2)}, u32[]{:S(2)}) %all-to-all-start) | async-done | bytes 460832 | tf_op jit(solution)/shard_map/all_to_all | solution.py:229
  22.9 2.5 %collective-permute-start = (f32[8,8,600]{2,1,0:T(8,128)S(1)}, f32[8,8,600]{2,1,0:T(8,128)S(1)}, u32[]{:S(2)}, u32[]{:S(2)}) collective-permute-start(f32[8,8,600]{2,1,0:T(8,128)S(1)} %slice.4), channel_id=1, source_target_pairs={{0,3},{1,0},{2,1},{3,2},{4,7},{5,4},{6,5},{7,6},{8,11},{9,8},{10,9... | collective-permute-start | bytes 460808 | tf_op jit(solution)/shard_map/ppermute | solution.py:231
  25.4 0.5 collective-permute-start.1
  25.9 0.6 collective-permute-start.2
  26.5 0.1 pad_add_fusion.1
  26.6 0.8 dynamic_slice.28
  27.4 0.1 copy.4.seg_rows_ref
  27.5 0.5 pad_add_fusion.counts_ref
  28.0 2.0 %collective-permute-done.rest_0_ = f32[8,8,600]{2,1,0:T(8,128)S(1)} collective-permute-done((f32[8,8,600]{2,1,0:T(8,128)S(1)}, f32[8,8,600]{2,1,0:T(8,128)S(1)}, u32[]{:S(2)}, u32[]{:S(2)}) %collective-permute-start) | collective-permute-done | bytes 153632 | tf_op jit(solution)/shard_map/ppermute | solution.py:231
  30.0 4.3 %collective-permute-done.1.rest_1_ = f32[8,8,600]{2,1,0:T(8,128)S(1)} collective-permute-done((f32[8,8,600]{2,1,0:T(8,128)S(1)}, f32[8,8,600]{2,1,0:T(8,128)S(1)}, u32[]{:S(2)}, u32[]{:S(2)}) %collective-permute-start.1) | collective-permute-done | bytes 153632 | tf_op jit(solution)/shard_map/ppermute | solution.py:231
  34.4 0.0 collective-permute-done.2.rest_2_
  34.4 62.3 %pairs.1 = f32[8,3,8,400]{3,2,1,0:T(8,128)S(1)} custom-call(s32[1]{0:T(128)} %bitcast.base_ref, s32[400,1]{1,0:T(8,128)S(1)} %copy.4.seg_rows_ref, s32[1,800]{1,0:T(1,128)S(1)} %broadcast_in_dim.14.seg_cols_ref, s32[1,800]{1,0:T(1,128)S(1)} %broadcast_in_dim.15.col_ids_ref, s32[400,800]{1,0:T(8,128)S(1)} %pad_add_fusion.counts_ref, ...), custom_call_target="tpu_custom_call" | custom-call | tf_op jit(solution)/shard_map/pairs/pallas_call | solution.py:247
  96.6 15.6 %all_to_all.10.back_ref = f32[8,3,8,400]{3,2,1,0:T(8,128)} all-to-all(f32[8,3,8,400]{3,2,1,0:T(8,128)S(1)} %pairs.1), channel_id=1, replica_groups=mesh['ens'=8,'tile'=4] {'ens'}, dimensions={0} | all-to-all | bytes 614400 | tf_op jit(solution)/shard_map/all_to_all | solution.py:267
  112.2 1.7 %total.1 = f32[3,8,800]{2,1,0:T(8,128)} custom-call(f32[8,3,8,400]{3,2,1,0:T(8,128)} %all_to_all.10.back_ref), custom_call_target="tpu_custom_call" | custom-call | tf_op jit(solution)/shard_map/total/pallas_call | solution.py:268
  (5 shorter events, 0.0 us)
Async XLA Ops:
  1.9 21.0 %all-to-all-start = ((f32[8,8,1800]{2,1,0:T(8,128)}), f32[8,8,1800]{2,1,0:T(8,128)S(1)}, u32[]{:S(2)}, u32[]{:S(2)}) async-start(f32[8,8,1800]{2,1,0:T(8,128)} %pack.1), calls=%async_computation | async-start | bytes 983040 | tf_op jit(solution)/shard_map/all_to_all | solution.py:229
  22.9 7.1 %collective-permute-start = (f32[8,8,600]{2,1,0:T(8,128)S(1)}, f32[8,8,600]{2,1,0:T(8,128)S(1)}, u32[]{:S(2)}, u32[]{:S(2)}) collective-permute-start(f32[8,8,600]{2,1,0:T(8,128)S(1)} %slice.4), channel_id=1, source_target_pairs={{0,3},{1,0},{2,1},{3,2},{4,7},{5,4},{6,5},{7,6},{8,11},{9,8},{10,9... | collective-permute-start | bytes 460808 | tf_op jit(solution)/shard_map/ppermute | solution.py:231
  25.4 9.0 %collective-permute-start.1 = (f32[8,8,600]{2,1,0:T(8,128)S(1)}, f32[8,8,600]{2,1,0:T(8,128)S(1)}, u32[]{:S(2)}, u32[]{:S(2)}) collective-permute-start(f32[8,8,600]{2,1,0:T(8,128)S(1)} %slice.4), channel_id=1, source_target_pairs={{0,2},{1,3},{2,0},{3,1},{4,6},{5,7},{6,4},{7,5},{8,10},{9,11},{10,... | collective-permute-start | bytes 460808 | tf_op jit(solution)/shard_map/ppermute | solution.py:231
  25.9 8.5 %collective-permute-start.2 = (f32[8,8,600]{2,1,0:T(8,128)S(1)}, f32[8,8,600]{2,1,0:T(8,128)S(1)}, u32[]{:S(2)}, u32[]{:S(2)}) collective-permute-start(f32[8,8,600]{2,1,0:T(8,128)S(1)} %slice.4), channel_id=1, source_target_pairs={{0,1},{1,2},{2,3},{3,0},{4,5},{5,6},{6,7},{7,4},{8,9},{9,10},{10,1... | collective-permute-start | bytes 460808 | tf_op jit(solution)/shard_map/ppermute | solution.py:231

commit v10 on v8

--- a/solution.py
+++ b/solution.py
@@ -10,6 +10,7 @@
 LANES = 128
 WIDE = 256
 SLOT = 64
+ROW_BLOCKS = 4
 NT = (((1,), (1,)), ((), ()))
 
 
@@ -73,6 +74,8 @@
     full = rhs_ref.shape[2]
     end = n_cols - full
     chunks = [(a, min(WIDE, full - a)) for a in range(0, full, WIDE)]
+    tall = up(-(-deep // ROW_BLOCKS), 16)
+    row_blocks = [pl.ds(a, min(tall, deep - a)) for a in range(0, deep, tall)]
 
     for norm_row, one_row, refs in ((3, 4, row_terms), (4, 3, col_terms)):
         for ref in refs:
@@ -120,16 +123,17 @@
     if end:
         weight_end_ref[...] = jnp.zeros_like(weight_end_ref)
 
-    def tanh_block(s, start, size):
-        return jnp.tanh(jnp.dot(lhs_ref[s], rhs_ref[s, :, pl.ds(start, size)], preferred_element_type=jnp.float32))
+    def tanh_block(s, rows, start, size):
+        return jnp.tanh(jnp.dot(lhs_ref[s, rows], rhs_ref[s, :, pl.ds(start, size)], preferred_element_type=jnp.float32))
 
     def tanh_end(b):
         return jnp.tanh(jnp.dot(lhs_end_ref[b], rhs_end_ref[b], preferred_element_type=jnp.float32))
 
     def add_some(b, carry):
         for inside in range(fold):
-            for start, size in chunks:
-                weight_ref[:, pl.ds(start, size)] += tanh_block(b * fold + inside, start, size)
+            for rows in row_blocks:
+                for start, size in chunks:
+                    weight_ref[rows, pl.ds(start, size)] += tanh_block(b * fold + inside, rows, start, size)
         if end:
             weight_end_ref[...] += tanh_end(b)
         return carry
@@ -176,11 +180,14 @@
             last = sums([terms_end_ref[b]] * 2, split2(weight_end_ref[...], tanh_end(b))).T
         for inside in range(fold):
             s = b * fold + inside
-            terms, parts = [], []
-            for start, size in chunks:
-                terms += [rhs_ref[s, pl.ds(0, 16), pl.ds(start, size)]] * 2
-                parts += split2(weight_ref[:, pl.ds(start, size)], tanh_block(s, start, size))
-            total = sums(terms, parts)
+            blocks = []
+            for rows in row_blocks:
+                terms, parts = [], []
+                for start, size in chunks:
+                    terms += [rhs_ref[s, pl.ds(0, 16), pl.ds(start, size)]] * 2
+                    parts += split2(weight_ref[rows, pl.ds(start, size)], tanh_block(s, rows, start, size))
+                blocks.append(sums(terms, parts))
+            total = jnp.concatenate(blocks, axis=0)
             total = total.T
             if end:
                 total += last[16 * inside:16 * inside + 16]

time: 112 us -> 119 us (1.062)
  Pallas kernels: 63.2 us -> 70.7 us
    pallas_call x1, Pallas kernels: 59.6 us -> 67.1 us  [on_device(): pl.pallas_call(functools.partial(pair_kernel, n_tile, fold), out_shape=ja...]
where the time goes in v10:
time: 119 us
  Pallas kernels  70.7 us (59%)
  waiting for transfers between devices  17.8 us (15%)
  blocking collectives  15.6 us (13%)
  starting transfers between devices  9.92 us (8%)
  local copies, waits for them, and re-layouts  4.01 us (3%)
    pallas_call x1, Pallas kernels, on_device(): pl.pallas_call(functools.partial(pair_kernel, n_tile, fold), out_shape=ja...  67.1 us
    all_to_all x1, blocking collectives, on_device(): back = lax.all_to_all(grad, 'ens', 0, 0, tiled=True)  15.6 us
    all_to_all x1, waiting for transfers between devices, on_device(): both = lax.all_to_all(send, 'ens', 0, 0, tiled=True)  11.5 us
    all_to_all x1, starting transfers between devices, on_device(): both = lax.all_to_all(send, 'ens', 0, 0, tiled=True)  6.33 us
    ppermute x3, waiting for transfers between devices, on_device(): lax.ppermute(own, 'tile', [(t, (t - k) % n_tile) for t in range(n_tile)])  6.31 us
    ppermute x3, starting transfers between devices, on_device(): lax.ppermute(own, 'tile', [(t, (t - k) % n_tile) for t in range(n_tile)])  3.6 us
  transfers between devices with their start and end apart: 4, of which 3 were waited for; matrix products, arithmetic and copies ran while one was open for 4% of the time, Pallas kernels for 0%

profile of v10, /device:TPU:0, one launch (start us, length us, event | category | flops | bytes accessed | tf_op | source)
XLA Modules:
  0.0 118.8 jit_solution(8779287011059095066)
XLA Ops:
  0.0 1.9 %pack.1 = f32[8,8,1800]{2,1,0:T(8,128)} custom-call(f32[3,8,800]{2,1,0:T(8,128)} %bitcast.4), custom_call_target="tpu_custom_call" | custom-call | tf_op jit(solution)/shard_map/pack/pallas_call | solution.py:230
  1.9 6.3 %all-to-all-start = ((f32[8,8,1800]{2,1,0:T(8,128)}), f32[8,8,1800]{2,1,0:T(8,128)S(1)}, u32[]{:S(2)}, u32[]{:S(2)}) async-start(f32[8,8,1800]{2,1,0:T(8,128)} %pack.1), calls=%async_computation | async-start | bytes 983040 | tf_op jit(solution)/shard_map/all_to_all | solution.py:237
  8.2 0.9 fusion.1
  9.1 0.1 pad_add_fusion.2
  9.2 2.2 %fusion = (s32[400,200]{1,0:T(8,128)S(1)}, s32[400,200]{1,0:T(8,128)S(1)}, s32[400,200]{1,0:T(8,128)S(1)}, s32[400,200]{1,0:T(8,128)S(1)}) fusion(s32[800,3200]{1,0:T(8,128)} %param.4, s32[]{:T(128)S(6)} %select_n.38, s32[]{:T(128)S(6)} %select_n.39, s32[]{:T(128)S(6)} %select_n.40, s32[]{:T(128)S(6)} %select_n.42, s32[]{:T(128)S(6)} %select_n.41), kind=kLoop, calls=%fused_computation.7 | loop fusion | bytes 2560020 | tf_op jit(solution)/shard_map/dynamic_slice | solution.py:244
  11.4 11.5 %all-to-all-done.both_ref = f32[8,8,1800]{2,1,0:T(8,128)S(1)} async-done(((f32[8,8,1800]{2,1,0:T(8,128)}), f32[8,8,1800]{2,1,0:T(8,128)S(1)}, u32[]{:S(2)}, u32[]{:S(2)}) %all-to-all-start) | async-done | bytes 460832 | tf_op jit(solution)/shard_map/all_to_all | solution.py:237
  22.9 2.5 %collective-permute-start = (f32[8,8,600]{2,1,0:T(8,128)S(1)}, f32[8,8,600]{2,1,0:T(8,128)S(1)}, u32[]{:S(2)}, u32[]{:S(2)}) collective-permute-start(f32[8,8,600]{2,1,0:T(8,128)S(1)} %slice.4), channel_id=1, source_target_pairs={{0,3},{1,0},{2,1},{3,2},{4,7},{5,4},{6,5},{7,6},{8,11},{9,8},{10,9... | collective-permute-start | bytes 460808 | tf_op jit(solution)/shard_map/ppermute | solution.py:239
  25.4 0.5 collective-permute-start.1
  25.9 0.6 collective-permute-start.2
  26.5 0.1 pad_add_fusion.1
  26.6 0.8 dynamic_slice.28
  27.4 0.1 copy.4.seg_rows_ref
  27.5 0.5 pad_add_fusion.counts_ref
  28.0 2.0 %collective-permute-done.rest_0_ = f32[8,8,600]{2,1,0:T(8,128)S(1)} collective-permute-done((f32[8,8,600]{2,1,0:T(8,128)S(1)}, f32[8,8,600]{2,1,0:T(8,128)S(1)}, u32[]{:S(2)}, u32[]{:S(2)}) %collective-permute-start) | collective-permute-done | bytes 153632 | tf_op jit(solution)/shard_map/ppermute | solution.py:239
  30.0 4.3 %collective-permute-done.1.rest_1_ = f32[8,8,600]{2,1,0:T(8,128)S(1)} collective-permute-done((f32[8,8,600]{2,1,0:T(8,128)S(1)}, f32[8,8,600]{2,1,0:T(8,128)S(1)}, u32[]{:S(2)}, u32[]{:S(2)}) %collective-permute-start.1) | collective-permute-done | bytes 153632 | tf_op jit(solution)/shard_map/ppermute | solution.py:239
  34.4 0.0 collective-permute-done.2.rest_2_
  34.4 67.1 %pairs.1 = f32[8,3,8,400]{3,2,1,0:T(8,128)S(1)} custom-call(s32[1]{0:T(128)} %bitcast.base_ref, s32[400,1]{1,0:T(8,128)S(1)} %copy.4.seg_rows_ref, s32[1,800]{1,0:T(1,128)S(1)} %broadcast_in_dim.14.seg_cols_ref, s32[1,800]{1,0:T(1,128)S(1)} %broadcast_in_dim.15.col_ids_ref, s32[400,800]{1,0:T(8,128)S(1)} %pad_add_fusion.counts_ref, ...), custom_call_target="tpu_custom_call" | custom-call | tf_op jit(solution)/shard_map/pairs/pallas_call | solution.py:255
  101.5 15.6 %all_to_all.10.back_ref = f32[8,3,8,400]{3,2,1,0:T(8,128)} all-to-all(f32[8,3,8,400]{3,2,1,0:T(8,128)S(1)} %pairs.1), channel_id=1, replica_groups=mesh['ens'=8,'tile'=4] {'ens'}, dimensions={0} | all-to-all | bytes 614400 | tf_op jit(solution)/shard_map/all_to_all | solution.py:275
  117.1 1.7 %total.1 = f32[3,8,800]{2,1,0:T(8,128)} custom-call(f32[8,3,8,400]{3,2,1,0:T(8,128)} %all_to_all.10.back_ref), custom_call_target="tpu_custom_call" | custom-call | tf_op jit(solution)/shard_map/total/pallas_call | solution.py:276
  (5 shorter events, 0.0 us)
Async XLA Ops:
  1.9 21.0 %all-to-all-start = ((f32[8,8,1800]{2,1,0:T(8,128)}), f32[8,8,1800]{2,1,0:T(8,128)S(1)}, u32[]{:S(2)}, u32[]{:S(2)}) async-start(f32[8,8,1800]{2,1,0:T(8,128)} %pack.1), calls=%async_computation | async-start | bytes 983040 | tf_op jit(solution)/shard_map/all_to_all | solution.py:237
  22.9 7.1 %collective-permute-start = (f32[8,8,600]{2,1,0:T(8,128)S(1)}, f32[8,8,600]{2,1,0:T(8,128)S(1)}, u32[]{:S(2)}, u32[]{:S(2)}) collective-permute-start(f32[8,8,600]{2,1,0:T(8,128)S(1)} %slice.4), channel_id=1, source_target_pairs={{0,3},{1,0},{2,1},{3,2},{4,7},{5,4},{6,5},{7,6},{8,11},{9,8},{10,9... | collective-permute-start | bytes 460808 | tf_op jit(solution)/shard_map/ppermute | solution.py:239
  25.4 9.0 %collective-permute-start.1 = (f32[8,8,600]{2,1,0:T(8,128)S(1)}, f32[8,8,600]{2,1,0:T(8,128)S(1)}, u32[]{:S(2)}, u32[]{:S(2)}) collective-permute-start(f32[8,8,600]{2,1,0:T(8,128)S(1)} %slice.4), channel_id=1, source_target_pairs={{0,2},{1,3},{2,0},{3,1},{4,6},{5,7},{6,4},{7,5},{8,10},{9,11},{10,... | collective-permute-start | bytes 460808 | tf_op jit(solution)/shard_map/ppermute | solution.py:239
  25.9 8.5 %collective-permute-start.2 = (f32[8,8,600]{2,1,0:T(8,128)S(1)}, f32[8,8,600]{2,1,0:T(8,128)S(1)}, u32[]{:S(2)}, u32[]{:S(2)}) collective-permute-start(f32[8,8,600]{2,1,0:T(8,128)S(1)} %slice.4), channel_id=1, source_target_pairs={{0,1},{1,2},{2,3},{3,0},{4,5},{5,6},{6,7},{7,4},{8,9},{9,10},{10,1... | collective-permute-start | bytes 460808 | tf_op jit(solution)/shard_map/ppermute | solution.py:239

commit v11 on v8

--- a/solution.py
+++ b/solution.py
@@ -9,8 +9,11 @@
 
 LANES = 128
 WIDE = 256
-SLOT = 64
+SLOT = 32
+KEEP_BYTES = 36 << 20
 NT = (((1,), (1,)), ((), ()))
+ROW_FEATURES = "hhnmmhl1"
+COL_FEATURES = "hm1hmlhn"
 
 
 def up(n, unit):
@@ -36,49 +39,58 @@
 
 
 def sum_kernel(n_p, n_q, back_ref, total_ref):
-    n_rows = back_ref.shape[3]
-    for c in range(3):
-        for p in range(n_p):
-            total = back_ref[p, c]
-            for q in range(1, n_q):
-                total += back_ref[q * n_p + p, c]
-            total_ref[c, :, pl.ds(p * n_rows, n_rows)] = total
-
-
-def put_terms(refs, xyz, norm_row):
+    n_rows = back_ref.shape[2] // 3
+    for p in range(n_p):
+        total = back_ref[p]
+        for q in range(1, n_q):
+            total += back_ref[q * n_p + p]
+        for c in range(3):
+            total_ref[c, :, pl.ds(p * n_rows, n_rows)] = total[:, c * n_rows:(c + 1) * n_rows]
+
+
+def put_terms(ref, xyz, layout):
     norm = 1.5 - 0.5 * (xyz[0] * xyz[0] + xyz[1] * xyz[1] + xyz[2] * xyz[2])
     n, size = norm.shape
-    wide = refs[0].shape[0] * LANES
-    for f, v in ((0, xyz[0]), (1, xyz[1]), (2, xyz[2]), (norm_row, norm)):
-        if wide > size:
-            v = jnp.concatenate([v, jnp.zeros((n, wide - size), jnp.float32)], axis=1)
-        for ref, term in zip(refs, split3(v)):
-            for k in range(wide // LANES):
-                ref[k, pl.ds(f, n, 8), :] = term[:, k * LANES:(k + 1) * LANES]
-
-
-def get_terms(refs, i):
-    return [jnp.concatenate([ref[k, pl.ds(8 * i, 8), :] for k in range(ref.shape[0])], axis=1) for ref in refs]
+    blocks = ref.shape[0]
+    if blocks * LANES > size:
+        pad = jnp.zeros((n, blocks * LANES - size), jnp.float32)
+        xyz, norm = [jnp.concatenate([v, pad], axis=1) for v in xyz], jnp.concatenate([norm, pad], axis=1)
+    terms = dict(zip("hml", zip(*[split3(v) for v in xyz])))
+    terms["n"] = split3(norm)
+    for r, name in enumerate(layout):
+        if name != "1":
+            for c in range(3):
+                for k in range(blocks):
+                    ref[k, pl.ds(3 * r + c, n, SLOT), :] = terms[name][c][:, k * LANES:(k + 1) * LANES]
+
+
+def init_terms(ref, n, layout):
+    ref[...] = jnp.zeros_like(ref)
+    for k in range(ref.shape[0]):
+        for c in range(3):
+            ref[k, pl.ds(3 * layout.index("1") + c, n, SLOT), :] = jnp.ones((n, LANES), jnp.float32)
+
+
+def get_terms(ref, i, n):
+    return jnp.concatenate([ref[k, pl.ds(SLOT * i, SLOT * n), :] for k in range(ref.shape[0])], axis=1)
 
 
 def pair_kernel(tiles, fold, base_ref, seg_rows_ref, seg_cols_ref, col_ids_ref, counts_ref, both_ref, *rest):
     piece_refs = rest[:tiles - 1]
-    (grad_ref, row_terms, col_terms, lhs_ref, lhs_end_ref, rhs_ref, rhs_end_ref, terms_end_ref, weight_ref,
-     weight_end_ref) = rest[tiles - 1:]
+    (grad_ref, row_terms, col_terms, lhs_ref, rhs_ref, rhs_end_ref, terms_end_ref, weight_ref, weight_end_ref, kept_ref,
+     kept_end_ref) = rest[tiles - 1:]
     groups, per, _ = both_ref.shape
     structs = groups * per
     n_rows, n_cols = counts_ref.shape
     piece = n_cols // tiles
-    deep = weight_ref.shape[0]
+    blocks, deep, _ = lhs_ref.shape
+    kept = kept_end_ref.shape[0]
     full = rhs_ref.shape[2]
     end = n_cols - full
     chunks = [(a, min(WIDE, full - a)) for a in range(0, full, WIDE)]
 
-    for norm_row, one_row, refs in ((3, 4, row_terms), (4, 3, col_terms)):
-        for ref in refs:
-            ref[...] = jnp.zeros_like(ref)
-        for k in range(refs[0].shape[0]):
-            refs[0][k, pl.ds(one_row, per, 8), :] = jnp.ones((per, LANES), jnp.float32)
+    init_terms(row_terms, per, ROW_FEATURES)
+    init_terms(col_terms, per, COL_FEATURES)
     if end:
         rhs_end_ref[...] = jnp.zeros_like(rhs_end_ref)
 
@@ -87,32 +99,22 @@
         parts = [both] + [ref[g] for ref in piece_refs]
         cols = [jnp.concatenate([v[:, c * piece:(c + 1) * piece] for v in parts], axis=1) for c in range(3)]
         rows = [both[:, 3 * piece + c * n_rows:3 * piece + (c + 1) * n_rows] for c in range(3)]
-        put_terms(row_terms, rows, 3)
-        put_terms(col_terms, cols, 4)
+        put_terms(row_terms, rows, ROW_FEATURES)
+        put_terms(col_terms, cols, COL_FEATURES)
         for block in range(per // fold):
-            lefts = []
+            b = g * (per // fold) + block
+            lhs_ref[b] = get_terms(row_terms, block * fold, fold).T[:deep].astype(jnp.bfloat16)
             for inside in range(fold):
-                i = block * fold + inside
-                s = g * per + i
-                hi, mid, lo = get_terms(row_terms, i)
-                left = jnp.concatenate([hi, hi, mid, mid, hi, lo], axis=0)
-                lhs_ref[s] = left.T[:deep].astype(jnp.bfloat16)
+                right = get_terms(col_terms, block * fold + inside, 1)
+                rhs_ref[b * fold + inside] = right[:, :full].astype(jnp.bfloat16)
                 if end:
-                    lefts += [left, jnp.zeros((SLOT - 48, left.shape[1]), jnp.float32)]
-                hi, mid, lo = get_terms(col_terms, i)
-                right = jnp.concatenate([hi, mid, hi, mid, lo, hi], axis=0)
-                rhs_ref[s] = right[:, :full].astype(jnp.bfloat16)
-                if end:
-                    lane = lax.broadcasted_iota(jnp.int32, (48, LANES), 1)
+                    lane = lax.broadcasted_iota(jnp.int32, (SLOT, LANES), 1)
                     last = jnp.where(lane < end, right[:, full:full + LANES], 0.0)
                     if inside:
                         last = pltpu.roll(last, inside * end, 1)
                     last = last.astype(jnp.bfloat16)
-                    b = g * (per // fold) + block
-                    rhs_end_ref[b, pl.ds(SLOT * inside, 48), :] = last
+                    rhs_end_ref[b, pl.ds(SLOT * inside, SLOT), :] = last
                     terms_end_ref[b, pl.ds(16 * inside, 16), :] = last[0:16]
-            if end:
-                lhs_end_ref[g * (per // fold) + block] = jnp.concatenate(lefts, axis=0).T[:deep].astype(jnp.bfloat16)
         return carry
 
     lax.fori_loop(0, groups, features, 0)
@@ -120,21 +122,30 @@
     if end:
         weight_end_ref[...] = jnp.zeros_like(weight_end_ref)
 
-    def tanh_block(s, start, size):
-        return jnp.tanh(jnp.dot(lhs_ref[s], rhs_ref[s, :, pl.ds(start, size)], preferred_element_type=jnp.float32))
+    def tanh_block(b, inside, start, size):
+        left = lhs_ref[b, :, pl.ds(SLOT * inside, SLOT)]
+        right = rhs_ref[b * fold + inside, :, pl.ds(start, size)]
+        return jnp.tanh(jnp.dot(left, right, preferred_element_type=jnp.float32))
 
     def tanh_end(b):
-        return jnp.tanh(jnp.dot(lhs_end_ref[b], rhs_end_ref[b], preferred_element_type=jnp.float32))
-
-    def add_some(b, carry):
+        return jnp.tanh(jnp.dot(lhs_ref[b], rhs_end_ref[b], preferred_element_type=jnp.float32))
+
+    def add_some(keep, b, carry):
         for inside in range(fold):
             for start, size in chunks:
-                weight_ref[:, pl.ds(start, size)] += tanh_block(b * fold + inside, start, size)
+                t = tanh_block(b, inside, start, size)
+                if keep:
+                    kept_ref[b * fold + inside, :, pl.ds(start, size)] = t
+                weight_ref[:, pl.ds(start, size)] += t
         if end:
-            weight_end_ref[...] += tanh_end(b)
+            t = tanh_end(b)
+            if keep:
+                kept_end_ref[b] = t
+            weight_end_ref[...] += t
         return carry
 
-    lax.fori_loop(0, structs // fold, add_some, 0)
+    lax.fori_loop(0, kept, functools.partial(add_some, True), 0)
+    lax.fori_loop(kept, blocks, functools.partial(add_some, False), 0)
 
     def mask_and_target(start, size):
         count = counts_ref[:, pl.ds(start, size)].astype(jnp.float32)
@@ -171,29 +182,32 @@
         return lax.dot_general(jnp.concatenate(parts, axis=1), jnp.concatenate(terms, axis=1), NT,
                                preferred_element_type=jnp.float32)
 
-    def grad_some(b, carry):
+    def grad_some(keep, b, carry):
         if end:
-            last = sums([terms_end_ref[b]] * 2, split2(weight_end_ref[...], tanh_end(b))).T
+            t = kept_end_ref[b] if keep else tanh_end(b)
+            last = sums([terms_end_ref[b]] * 2, split2(weight_end_ref[...], t)).T
         for inside in range(fold):
             s = b * fold + inside
             terms, parts = [], []
             for start, size in chunks:
+                t = kept_ref[s, :, pl.ds(start, size)] if keep else tanh_block(b, inside, start, size)
                 terms += [rhs_ref[s, pl.ds(0, 16), pl.ds(start, size)]] * 2
-                parts += split2(weight_ref[:, pl.ds(start, size)], tanh_block(s, start, size))
-            total = sums(terms, parts)
-            total = total.T
+                parts += split2(weight_ref[:, pl.ds(start, size)], t)
+            total = sums(terms, parts).T
             if end:
                 total += last[16 * inside:16 * inside + 16]
             total = total[:, :n_rows]
             g, i = lax.div(s, per), lax.rem(s, per)
             both = both_ref[g, pl.ds(i, 1), :]
+            grad = []
             for c in range(3):
                 xyz = both[:, 3 * piece + c * n_rows:3 * piece + (c + 1) * n_rows]
-                grad_ref[g, c, pl.ds(i, 1), :] = (0.25 / 16) * (
-                    total[c:c + 1] + total[8 + c:9 + c] - total[3:4] * xyz)
+                grad.append((0.25 / 16) * (total[c:c + 1] + total[3 + c:4 + c] - total[6:7] * xyz))
+            grad_ref[g, pl.ds(i, 1), :] = jnp.concatenate(grad, axis=1)
         return carry
 
-    lax.fori_loop(0, structs // fold, grad_some, 0)
+    lax.fori_loop(0, kept, functools.partial(grad_some, True), 0)
+    lax.fori_loop(kept, blocks, functools.partial(grad_some, False), 0)
 
 
 def split_ens(n_ens, beads, tiles):
@@ -245,23 +259,25 @@
     deep = up(n_rows, 16)
     row_wide, col_wide = up(n_rows, LANES), up(n_cols, LANES)
     blocks = structs // fold
+    kept = max(1, min(blocks, KEEP_BYTES // (4 * deep * (fold * full + LANES))))
     grad = pl.pallas_call(
         functools.partial(pair_kernel, n_tile, fold),
-        out_shape=jax.ShapeDtypeStruct((n_ens, 3, local_n, n_rows), jnp.float32),
+        out_shape=jax.ShapeDtypeStruct((n_ens, local_n, 3 * n_rows), jnp.float32),
         in_specs=[pl.BlockSpec(memory_space=pltpu.SMEM)] + [vmem] * (4 + n_tile),
         out_specs=vmem,
         scratch_shapes=[
-            [pltpu.VMEM((row_wide // LANES, 8 * local_n, LANES), jnp.float32)] * 3,
-            [pltpu.VMEM((col_wide // LANES, 8 * local_n, LANES), jnp.float32)] * 3,
-            pltpu.VMEM((structs, deep, 48), jnp.bfloat16),
+            pltpu.VMEM((row_wide // LANES, SLOT * local_n, LANES), jnp.float32),
+            pltpu.VMEM((col_wide // LANES, SLOT * local_n, LANES), jnp.float32),
             pltpu.VMEM((blocks, deep, fold * SLOT), jnp.bfloat16),
-            pltpu.VMEM((structs, 48, full), jnp.bfloat16),
+            pltpu.VMEM((structs, SLOT, full), jnp.bfloat16),
             pltpu.VMEM((blocks, fold * SLOT, LANES), jnp.bfloat16),
             pltpu.VMEM((blocks, fold * 16, LANES), jnp.bfloat16),
             pltpu.VMEM((deep, full), jnp.float32),
             pltpu.VMEM((deep, LANES), jnp.float32),
+            pltpu.VMEM((kept * fold, deep, full), jnp.float32),
+            pltpu.VMEM((kept, deep, LANES), jnp.float32),
         ],
-        compiler_params=pltpu.CompilerParams(vmem_limit_bytes=48 << 20),
+        compiler_params=pltpu.CompilerParams(vmem_limit_bytes=56 << 20),
         name="pairs",
     )(row_base[None], seg_rows, seg_cols, col_ids, block, both, *pieces)
 

time: 112 us -> 114 us (1.018)
  waiting for transfers between devices: 17.8 us -> 14.8 us
  local copies, waits for them, and re-layouts: 4.01 us -> 6.59 us
  Pallas kernels: 63.2 us -> 64.8 us
    ppermute x3, waiting for transfers between devices: 6.31 us -> 3.36 us  [on_device(): lax.ppermute(own, 'tile', [(t, (t - k) % n_tile) for t in range(n_tile)])]
    pallas_call x1, Pallas kernels: 59.6 us -> 61.2 us  [on_device(): pl.pallas_call(functools.partial(pair_kernel, n_tile, fold), out_shape=ja...]
  transfers between devices with their start and end apart: 4 -> 4, of which waited for: 3 -> 2; matrix products, arithmetic and copies ran while one was open for 4% -> 7% of each run, Pallas kernels for 0% -> 0%
where the time goes in v11:
time: 114 us; the launch traced here: 113 us
  Pallas kernels  64.8 us (57%)
  blocking collectives  15.2 us (13%)
  waiting for transfers between devices  14.8 us (13%)
  starting transfers between devices  9.92 us (9%)
  local copies, waits for them, and re-layouts  6.59 us (6%)
  other arithmetic  1.83 us (2%)
    pallas_call x1, Pallas kernels, on_device(): pl.pallas_call(functools.partial(pair_kernel, n_tile, fold), out_shape=ja...  61.2 us
    all_to_all x1, blocking collectives, on_device(): back = lax.all_to_all(grad, 'ens', 0, 0, tiled=True)  15.2 us
    all_to_all x1, waiting for transfers between devices, on_device(): both = lax.all_to_all(send, 'ens', 0, 0, tiled=True)  11.5 us
    all_to_all x1, starting transfers between devices, on_device(): both = lax.all_to_all(send, 'ens', 0, 0, tiled=True)  6.33 us
    ppermute x3, starting transfers between devices, on_device(): lax.ppermute(own, 'tile', [(t, (t - k) % n_tile) for t in range(n_tile)])  3.6 us
    ppermute x3, waiting for transfers between devices, on_device(): lax.ppermute(own, 'tile', [(t, (t - k) % n_tile) for t in range(n_tile)])  3.36 us
  transfers between devices with their start and end apart: 4, of which 2 were waited for; matrix products, arithmetic and copies ran while one was open for 7% of the time, Pallas kernels for 0%

profile of v11, /device:TPU:0, one launch (start us, length us, event | category | flops | bytes accessed | tf_op | source)
XLA Modules:
  0.0 113.3 jit_solution(14354063776959391516)
XLA Ops:
  0.0 1.9 %pack.1 = f32[8,8,1800]{2,1,0:T(8,128)} custom-call(f32[3,8,800]{2,1,0:T(8,128)} %bitcast.4), custom_call_target="tpu_custom_call" | custom-call | tf_op jit(solution)/shard_map/pack/pallas_call | solution.py:237
  1.9 6.3 %all-to-all-start = ((f32[8,8,1800]{2,1,0:T(8,128)}), f32[8,8,1800]{2,1,0:T(8,128)S(1)}, u32[]{:S(2)}, u32[]{:S(2)}) async-start(f32[8,8,1800]{2,1,0:T(8,128)} %pack.1), calls=%async_computation | async-start | bytes 983040 | tf_op jit(solution)/shard_map/all_to_all | solution.py:244
  8.2 0.9 fusion.1
  9.1 0.1 pad_add_fusion.2
  9.2 2.2 %fusion = (s32[400,200]{1,0:T(8,128)S(1)}, s32[400,200]{1,0:T(8,128)S(1)}, s32[400,200]{1,0:T(8,128)S(1)}, s32[400,200]{1,0:T(8,128)S(1)}) fusion(s32[800,3200]{1,0:T(8,128)} %param.4, s32[]{:T(128)S(6)} %select_n.38, s32[]{:T(128)S(6)} %select_n.39, s32[]{:T(128)S(6)} %select_n.40, s32[]{:T(128)S(6)} %select_n.42, s32[]{:T(128)S(6)} %select_n.41), kind=kLoop, calls=%fused_computation.7 | loop fusion | bytes 2560020 | tf_op jit(solution)/shard_map/dynamic_slice | solution.py:251
  11.4 11.5 %all-to-all-done.both_ref = f32[8,8,1800]{2,1,0:T(8,128)S(1)} async-done(((f32[8,8,1800]{2,1,0:T(8,128)}), f32[8,8,1800]{2,1,0:T(8,128)S(1)}, u32[]{:S(2)}, u32[]{:S(2)}) %all-to-all-start) | async-done | bytes 460832 | tf_op jit(solution)/shard_map/all_to_all | solution.py:244
  22.9 0.0 copy-start
  22.9 2.5 %collective-permute-start = (f32[8,8,600]{2,1,0:T(8,128)S(1)}, f32[8,8,600]{2,1,0:T(8,128)S(1)}, u32[]{:S(2)}, u32[]{:S(2)}) collective-permute-start(f32[8,8,600]{2,1,0:T(8,128)S(1)} %slice.4), channel_id=1, source_target_pairs={{0,3},{1,0},{2,1},{3,2},{4,7},{5,4},{6,5},{7,6},{8,11},{9,8},{10,9... | collective-permute-start | bytes 460808 | tf_op jit(solution)/shard_map/ppermute | solution.py:246
  25.4 0.5 collective-permute-start.1
  25.9 0.6 collective-permute-start.2
  26.5 0.1 pad_add_fusion.1
  26.6 0.6 broadcast_in_dim.15.col_ids_ref
  27.2 0.6 broadcast_in_dim.14.seg_cols_ref
  27.7 0.8 dynamic_slice.28
  28.5 0.8 copy.4.seg_rows_ref
  29.3 1.7 %pad_add_fusion.counts_ref = s32[400,800]{1,0:T(8,128)} fusion(s32[400,200]{1,0:T(8,128)S(1)} %get-tuple-element.7, s32[400,200]{1,0:T(8,128)S(1)} %get-tuple-element.8, s32[400,200]{1,0:T(8,128)S(1)} %get-tuple-element.6, s32[400,200]{1,0:T(8,128)S(1)} %get-tuple-element.5), kind=kLoop, calls=%fused_computation | loop fusion | flops 960000 | bytes 2560000 | tf_op jit(solution)/shard_map/concatenate | solution.py:251
  31.0 0.0 copy-done
  31.0 0.0 collective-permute-done.rest_0_
  31.0 0.0 copy-start.1
  31.0 3.4 %collective-permute-done.1.rest_1_ = f32[8,8,600]{2,1,0:T(8,128)S(1)} collective-permute-done((f32[8,8,600]{2,1,0:T(8,128)S(1)}, f32[8,8,600]{2,1,0:T(8,128)S(1)}, u32[]{:S(2)}, u32[]{:S(2)}) %collective-permute-start.1) | collective-permute-done | bytes 153632 | tf_op jit(solution)/shard_map/ppermute | solution.py:246
  34.4 0.0 copy-start.2
  34.4 0.0 collective-permute-done.2.rest_2_
  34.4 0.0 copy-start.3
  34.4 0.0 copy-done.1
  34.4 0.6 copy-done.2
  35.0 0.1 copy-done.3
  35.1 61.2 %pairs.1 = f32[8,8,1200]{2,1,0:T(8,128)} custom-call(s32[1]{0:T(128)} %bitcast.base_ref, s32[400,1]{1,0:T(8,128)} %copy.4.seg_rows_ref, s32[1,800]{1,0:T(1,128)} %broadcast_in_dim.14.seg_cols_ref, s32[1,800]{1,0:T(1,128)} %broadcast_in_dim.15.col_ids_ref, s32[400,800]{1,0:T(8,128)} %pad_add_fusion.counts_ref, f32[8,8,1800]{2,1,0:T(8,128)} %copy-done, ...), custom_call_target="tpu_custom_call" | custom-call | tf_op jit(solution)/shard_map/pairs/pallas_call | solution.py:263
  96.4 15.2 %all_to_all.10.back_ref = f32[8,8,1200]{2,1,0:T(8,128)} all-to-all(f32[8,8,1200]{2,1,0:T(8,128)} %pairs.1), channel_id=1, replica_groups=mesh['ens'=8,'tile'=4] {'ens'}, dimensions={0} | all-to-all | bytes 614400 | tf_op jit(solution)/shard_map/all_to_all | solution.py:284
  111.6 1.7 %total.1 = f32[3,8,800]{2,1,0:T(8,128)} custom-call(f32[8,8,1200]{2,1,0:T(8,128)} %all_to_all.10.back_ref), custom_call_target="tpu_custom_call" | custom-call | tf_op jit(solution)/shard_map/total/pallas_call | solution.py:285
  (3 shorter events, 0.0 us)
Async XLA Ops:
  1.9 21.0 %all-to-all-start = ((f32[8,8,1800]{2,1,0:T(8,128)}), f32[8,8,1800]{2,1,0:T(8,128)S(1)}, u32[]{:S(2)}, u32[]{:S(2)}) async-start(f32[8,8,1800]{2,1,0:T(8,128)} %pack.1), calls=%async_computation | async-start | bytes 983040 | tf_op jit(solution)/shard_map/all_to_all | solution.py:244
  22.9 8.1 %copy-start = (f32[8,8,1800]{2,1,0:T(8,128)}, f32[8,8,1800]{2,1,0:T(8,128)S(1)}, u32[]{:S(2)}) copy-start(f32[8,8,1800]{2,1,0:T(8,128)S(1)} %all-to-all-done.both_ref) | copy-start | bytes 1382404
  22.9 8.1 %collective-permute-start = (f32[8,8,600]{2,1,0:T(8,128)S(1)}, f32[8,8,600]{2,1,0:T(8,128)S(1)}, u32[]{:S(2)}, u32[]{:S(2)}) collective-permute-start(f32[8,8,600]{2,1,0:T(8,128)S(1)} %slice.4), channel_id=1, source_target_pairs={{0,3},{1,0},{2,1},{3,2},{4,7},{5,4},{6,5},{7,6},{8,11},{9,8},{10,9... | collective-permute-start | bytes 460808 | tf_op jit(solution)/shard_map/ppermute | solution.py:246
  25.4 9.0 %collective-permute-start.1 = (f32[8,8,600]{2,1,0:T(8,128)S(1)}, f32[8,8,600]{2,1,0:T(8,128)S(1)}, u32[]{:S(2)}, u32[]{:S(2)}) collective-permute-start(f32[8,8,600]{2,1,0:T(8,128)S(1)} %slice.4), channel_id=1, source_target_pairs={{0,2},{1,3},{2,0},{3,1},{4,6},{5,7},{6,4},{7,5},{8,10},{9,11},{10,... | collective-permute-start | bytes 460808 | tf_op jit(solution)/shard_map/ppermute | solution.py:246
  25.9 8.5 %collective-permute-start.2 = (f32[8,8,600]{2,1,0:T(8,128)S(1)}, f32[8,8,600]{2,1,0:T(8,128)S(1)}, u32[]{:S(2)}, u32[]{:S(2)}) collective-permute-start(f32[8,8,600]{2,1,0:T(8,128)S(1)} %slice.4), channel_id=1, source_target_pairs={{0,1},{1,2},{2,3},{3,0},{4,5},{5,6},{6,7},{7,4},{8,9},{9,10},{10,1... | collective-permute-start | bytes 460808 | tf_op jit(solution)/shard_map/ppermute | solution.py:246
  31.0 3.4 %copy-start.1 = (f32[8,8,600]{2,1,0:T(8,128)}, f32[8,8,600]{2,1,0:T(8,128)S(1)}, u32[]{:S(2)}) copy-start(f32[8,8,600]{2,1,0:T(8,128)S(1)} %collective-permute-done.rest_0_) | copy-start | bytes 460804
  34.4 0.7 copy-start.2
  34.4 0.7 copy-start.3

commit v12 on v11

--- a/solution.py
+++ b/solution.py
@@ -10,7 +10,6 @@
 LANES = 128
 WIDE = 256
 SLOT = 32
-KEEP_BYTES = 36 << 20
 NT = (((1,), (1,)), ((), ()))
 ROW_FEATURES = "hhnmmhl1"
 COL_FEATURES = "hm1hmlhn"
@@ -77,14 +76,13 @@
 
 def pair_kernel(tiles, fold, base_ref, seg_rows_ref, seg_cols_ref, col_ids_ref, counts_ref, both_ref, *rest):
     piece_refs = rest[:tiles - 1]
-    (grad_ref, row_terms, col_terms, lhs_ref, rhs_ref, rhs_end_ref, terms_end_ref, weight_ref, weight_end_ref, kept_ref,
-     kept_end_ref) = rest[tiles - 1:]
+    (grad_ref, row_terms, col_terms, lhs_ref, lhs_end_ref, rhs_ref, rhs_end_ref, terms_end_ref, weight_ref,
+     weight_end_ref) = rest[tiles - 1:]
     groups, per, _ = both_ref.shape
     structs = groups * per
     n_rows, n_cols = counts_ref.shape
     piece = n_cols // tiles
-    blocks, deep, _ = lhs_ref.shape
-    kept = kept_end_ref.shape[0]
+    blocks, deep, _ = lhs_end_ref.shape
     full = rhs_ref.shape[2]
     end = n_cols - full
     chunks = [(a, min(WIDE, full - a)) for a in range(0, full, WIDE)]
@@ -103,8 +101,10 @@
         put_terms(col_terms, cols, COL_FEATURES)
         for block in range(per // fold):
             b = g * (per // fold) + block
-            lhs_ref[b] = get_terms(row_terms, block * fold, fold).T[:deep].astype(jnp.bfloat16)
+            left = get_terms(row_terms, block * fold, fold).T[:deep].astype(jnp.bfloat16)
+            lhs_end_ref[b] = left
             for inside in range(fold):
+                lhs_ref[b * fold + inside] = left[:, SLOT * inside:SLOT * (inside + 1)]
                 right = get_terms(col_terms, block * fold + inside, 1)
                 rhs_ref[b * fold + inside] = right[:, :full].astype(jnp.bfloat16)
                 if end:
@@ -122,30 +122,21 @@
     if end:
         weight_end_ref[...] = jnp.zeros_like(weight_end_ref)
 
-    def tanh_block(b, inside, start, size):
-        left = lhs_ref[b, :, pl.ds(SLOT * inside, SLOT)]
-        right = rhs_ref[b * fold + inside, :, pl.ds(start, size)]
-        return jnp.tanh(jnp.dot(left, right, preferred_element_type=jnp.float32))
+    def tanh_block(s, start, size):
+        return jnp.tanh(jnp.dot(lhs_ref[s], rhs_ref[s, :, pl.ds(start, size)], preferred_element_type=jnp.float32))
 
     def tanh_end(b):
-        return jnp.tanh(jnp.dot(lhs_ref[b], rhs_end_ref[b], preferred_element_type=jnp.float32))
-
-    def add_some(keep, b, carry):
-        for inside in range(fold):
-            for start, size in chunks:
-                t = tanh_block(b, inside, start, size)
-                if keep:
-                    kept_ref[b * fold + inside, :, pl.ds(start, size)] = t
-                weight_ref[:, pl.ds(start, size)] += t
+        return jnp.tanh(jnp.dot(lhs_end_ref[b], rhs_end_ref[b], preferred_element_type=jnp.float32))
+
+    def add_some(b, carry):
+        for start, size in chunks:
+            some = [tanh_block(b * fold + inside, start, size) for inside in range(fold)]
+            weight_ref[:, pl.ds(start, size)] += functools.reduce(jnp.add, some)
         if end:
-            t = tanh_end(b)
-            if keep:
-                kept_end_ref[b] = t
-            weight_end_ref[...] += t
+            weight_end_ref[...] += tanh_end(b)
         return carry
 
-    lax.fori_loop(0, kept, functools.partial(add_some, True), 0)
-    lax.fori_loop(kept, blocks, functools.partial(add_some, False), 0)
+    lax.fori_loop(0, blocks, add_some, 0)
 
     def mask_and_target(start, size):
         count = counts_ref[:, pl.ds(start, size)].astype(jnp.float32)
@@ -182,17 +173,15 @@
         return lax.dot_general(jnp.concatenate(parts, axis=1), jnp.concatenate(terms, axis=1), NT,
                                preferred_element_type=jnp.float32)
 
-    def grad_some(keep, b, carry):
+    def grad_some(b, carry):
         if end:
-            t = kept_end_ref[b] if keep else tanh_end(b)
-            last = sums([terms_end_ref[b]] * 2, split2(weight_end_ref[...], t)).T
+            last = sums([terms_end_ref[b]] * 2, split2(weight_end_ref[...], tanh_end(b))).T
         for inside in range(fold):
             s = b * fold + inside
             terms, parts = [], []
             for start, size in chunks:
-                t = kept_ref[s, :, pl.ds(start, size)] if keep else tanh_block(b, inside, start, size)
                 terms += [rhs_ref[s, pl.ds(0, 16), pl.ds(start, size)]] * 2
-                parts += split2(weight_ref[:, pl.ds(start, size)], t)
+                parts += split2(weight_ref[:, pl.ds(start, size)], tanh_block(s, start, size))
             total = sums(terms, parts).T
             if end:
                 total += last[16 * inside:16 * inside + 16]
@@ -206,8 +195,7 @@
             grad_ref[g, pl.ds(i, 1), :] = jnp.concatenate(grad, axis=1)
         return carry
 
-    lax.fori_loop(0, kept, functools.partial(grad_some, True), 0)
-    lax.fori_loop(kept, blocks, functools.partial(grad_some, False), 0)
+    lax.fori_loop(0, blocks, grad_some, 0)
 
 
 def split_ens(n_ens, beads, tiles):
@@ -259,7 +247,6 @@
     deep = up(n_rows, 16)
     row_wide, col_wide = up(n_rows, LANES), up(n_cols, LANES)
     blocks = structs // fold
-    kept = max(1, min(blocks, KEEP_BYTES // (4 * deep * (fold * full + LANES))))
     grad = pl.pallas_call(
         functools.partial(pair_kernel, n_tile, fold),
         out_shape=jax.ShapeDtypeStruct((n_ens, local_n, 3 * n_rows), jnp.float32),
@@ -268,16 +255,15 @@
         scratch_shapes=[
             pltpu.VMEM((row_wide // LANES, SLOT * local_n, LANES), jnp.float32),
             pltpu.VMEM((col_wide // LANES, SLOT * local_n, LANES), jnp.float32),
+            pltpu.VMEM((structs, deep, SLOT), jnp.bfloat16),
             pltpu.VMEM((blocks, deep, fold * SLOT), jnp.bfloat16),
             pltpu.VMEM((structs, SLOT, full), jnp.bfloat16),
             pltpu.VMEM((blocks, fold * SLOT, LANES), jnp.bfloat16),
             pltpu.VMEM((blocks, fold * 16, LANES), jnp.bfloat16),
             pltpu.VMEM((deep, full), jnp.float32),
             pltpu.VMEM((deep, LANES), jnp.float32),
-            pltpu.VMEM((kept * fold, deep, full), jnp.float32),
-            pltpu.VMEM((kept, deep, LANES), jnp.float32),
         ],
-        compiler_params=pltpu.CompilerParams(vmem_limit_bytes=56 << 20),
+        compiler_params=pltpu.CompilerParams(vmem_limit_bytes=48 << 20),
         name="pairs",
     )(row_base[None], seg_rows, seg_cols, col_ids, block, both, *pieces)
 

time: 114 us -> 117 us (1.026)
  Pallas kernels: 64.8 us -> 69.4 us
  waiting for transfers between devices: 14.8 us -> 17.8 us
  local copies, waits for them, and re-layouts: 6.59 us -> 4.01 us
    pallas_call x1, Pallas kernels: 61.2 us -> 65.8 us  [on_device(): pl.pallas_call(functools.partial(pair_kernel, n_tile, fold), out_shape=ja...]
    ppermute x3, waiting for transfers between devices: 3.36 us -> 6.31 us  [on_device(): lax.ppermute(own, 'tile', [(t, (t - k) % n_tile) for t in range(n_tile)])]
  transfers between devices with their start and end apart: 4 -> 4, of which waited for: 2 -> 3; matrix products, arithmetic and copies ran while one was open for 7% -> 4% of each run, Pallas kernels for 0% -> 0%
where the time goes in v12:
time: 117 us; the launch traced here: 116 us
  Pallas kernels  69.4 us (59%)
  waiting for transfers between devices  17.8 us (15%)
  blocking collectives  14.2 us (12%)
  starting transfers between devices  9.92 us (8%)
  local copies, waits for them, and re-layouts  4.01 us (3%)
    pallas_call x1, Pallas kernels, on_device(): pl.pallas_call(functools.partial(pair_kernel, n_tile, fold), out_shape=ja...  65.8 us
    all_to_all x1, blocking collectives, on_device(): back = lax.all_to_all(grad, 'ens', 0, 0, tiled=True)  14.2 us
    all_to_all x1, waiting for transfers between devices, on_device(): both = lax.all_to_all(send, 'ens', 0, 0, tiled=True)  11.5 us
    all_to_all x1, starting transfers between devices, on_device(): both = lax.all_to_all(send, 'ens', 0, 0, tiled=True)  6.33 us
    ppermute x3, waiting for transfers between devices, on_device(): lax.ppermute(own, 'tile', [(t, (t - k) % n_tile) for t in range(n_tile)])  6.31 us
    ppermute x3, starting transfers between devices, on_device(): lax.ppermute(own, 'tile', [(t, (t - k) % n_tile) for t in range(n_tile)])  3.6 us
  transfers between devices with their start and end apart: 4, of which 3 were waited for; matrix products, arithmetic and copies ran while one was open for 4% of the time, Pallas kernels for 0%

profile of v12, /device:TPU:0, one launch (start us, length us, event | category | flops | bytes accessed | tf_op | source)
XLA Modules:
  0.0 116.1 jit_solution(8794313501570490441)
XLA Ops:
  0.0 1.9 %pack.1 = f32[8,8,1800]{2,1,0:T(8,128)} custom-call(f32[3,8,800]{2,1,0:T(8,128)} %bitcast.4), custom_call_target="tpu_custom_call" | custom-call | tf_op jit(solution)/shard_map/pack/pallas_call | solution.py:225
  1.9 6.3 %all-to-all-start = ((f32[8,8,1800]{2,1,0:T(8,128)}), f32[8,8,1800]{2,1,0:T(8,128)S(1)}, u32[]{:S(2)}, u32[]{:S(2)}) async-start(f32[8,8,1800]{2,1,0:T(8,128)} %pack.1), calls=%async_computation | async-start | bytes 983040 | tf_op jit(solution)/shard_map/all_to_all | solution.py:232
  8.2 0.9 fusion.1
  9.1 0.1 pad_add_fusion.2
  9.2 2.2 %fusion = (s32[400,200]{1,0:T(8,128)S(1)}, s32[400,200]{1,0:T(8,128)S(1)}, s32[400,200]{1,0:T(8,128)S(1)}, s32[400,200]{1,0:T(8,128)S(1)}) fusion(s32[800,3200]{1,0:T(8,128)} %param.4, s32[]{:T(128)S(6)} %select_n.38, s32[]{:T(128)S(6)} %select_n.39, s32[]{:T(128)S(6)} %select_n.40, s32[]{:T(128)S(6)} %select_n.42, s32[]{:T(128)S(6)} %select_n.41), kind=kLoop, calls=%fused_computation.7 | loop fusion | bytes 2560020 | tf_op jit(solution)/shard_map/dynamic_slice | solution.py:239
  11.4 11.5 %all-to-all-done.both_ref = f32[8,8,1800]{2,1,0:T(8,128)S(1)} async-done(((f32[8,8,1800]{2,1,0:T(8,128)}), f32[8,8,1800]{2,1,0:T(8,128)S(1)}, u32[]{:S(2)}, u32[]{:S(2)}) %all-to-all-start) | async-done | bytes 460832 | tf_op jit(solution)/shard_map/all_to_all | solution.py:232
  22.9 2.5 %collective-permute-start = (f32[8,8,600]{2,1,0:T(8,128)S(1)}, f32[8,8,600]{2,1,0:T(8,128)S(1)}, u32[]{:S(2)}, u32[]{:S(2)}) collective-permute-start(f32[8,8,600]{2,1,0:T(8,128)S(1)} %slice.4), channel_id=1, source_target_pairs={{0,3},{1,0},{2,1},{3,2},{4,7},{5,4},{6,5},{7,6},{8,11},{9,8},{10,9... | collective-permute-start | bytes 460808 | tf_op jit(solution)/shard_map/ppermute | solution.py:234
  25.4 0.5 collective-permute-start.1
  25.9 0.6 collective-permute-start.2
  26.5 0.1 pad_add_fusion.1
  26.6 0.8 dynamic_slice.28
  27.4 0.1 copy.4.seg_rows_ref
  27.5 0.5 pad_add_fusion.counts_ref
  28.0 2.0 %collective-permute-done.rest_0_ = f32[8,8,600]{2,1,0:T(8,128)S(1)} collective-permute-done((f32[8,8,600]{2,1,0:T(8,128)S(1)}, f32[8,8,600]{2,1,0:T(8,128)S(1)}, u32[]{:S(2)}, u32[]{:S(2)}) %collective-permute-start) | collective-permute-done | bytes 153632 | tf_op jit(solution)/shard_map/ppermute | solution.py:234
  30.0 4.3 %collective-permute-done.1.rest_1_ = f32[8,8,600]{2,1,0:T(8,128)S(1)} collective-permute-done((f32[8,8,600]{2,1,0:T(8,128)S(1)}, f32[8,8,600]{2,1,0:T(8,128)S(1)}, u32[]{:S(2)}, u32[]{:S(2)}) %collective-permute-start.1) | collective-permute-done | bytes 153632 | tf_op jit(solution)/shard_map/ppermute | solution.py:234
  34.4 0.0 collective-permute-done.2.rest_2_
  34.4 65.8 %pairs.1 = f32[8,8,1200]{2,1,0:T(8,128)S(1)} custom-call(s32[1]{0:T(128)} %bitcast.base_ref, s32[400,1]{1,0:T(8,128)S(1)} %copy.4.seg_rows_ref, s32[1,800]{1,0:T(1,128)S(1)} %broadcast_in_dim.14.seg_cols_ref, s32[1,800]{1,0:T(1,128)S(1)} %broadcast_in_dim.15.col_ids_ref, s32[400,800]{1,0:T(8,128)S(1)} %pad_add_fusion.counts_ref, ...), custom_call_target="tpu_custom_call" | custom-call | tf_op jit(solution)/shard_map/pairs/pallas_call | solution.py:250
  100.2 14.2 %all_to_all.10.back_ref = f32[8,8,1200]{2,1,0:T(8,128)} all-to-all(f32[8,8,1200]{2,1,0:T(8,128)S(1)} %pairs.1), channel_id=1, replica_groups=mesh['ens'=8,'tile'=4] {'ens'}, dimensions={0} | all-to-all | bytes 614400 | tf_op jit(solution)/shard_map/all_to_all | solution.py:270
  114.4 1.7 %total.1 = f32[3,8,800]{2,1,0:T(8,128)} custom-call(f32[8,8,1200]{2,1,0:T(8,128)} %all_to_all.10.back_ref), custom_call_target="tpu_custom_call" | custom-call | tf_op jit(solution)/shard_map/total/pallas_call | solution.py:271
  (5 shorter events, 0.0 us)
Async XLA Ops:
  1.9 21.0 %all-to-all-start = ((f32[8,8,1800]{2,1,0:T(8,128)}), f32[8,8,1800]{2,1,0:T(8,128)S(1)}, u32[]{:S(2)}, u32[]{:S(2)}) async-start(f32[8,8,1800]{2,1,0:T(8,128)} %pack.1), calls=%async_computation | async-start | bytes 983040 | tf_op jit(solution)/shard_map/all_to_all | solution.py:232
  22.9 7.1 %collective-permute-start = (f32[8,8,600]{2,1,0:T(8,128)S(1)}, f32[8,8,600]{2,1,0:T(8,128)S(1)}, u32[]{:S(2)}, u32[]{:S(2)}) collective-permute-start(f32[8,8,600]{2,1,0:T(8,128)S(1)} %slice.4), channel_id=1, source_target_pairs={{0,3},{1,0},{2,1},{3,2},{4,7},{5,4},{6,5},{7,6},{8,11},{9,8},{10,9... | collective-permute-start | bytes 460808 | tf_op jit(solution)/shard_map/ppermute | solution.py:234
  25.4 9.0 %collective-permute-start.1 = (f32[8,8,600]{2,1,0:T(8,128)S(1)}, f32[8,8,600]{2,1,0:T(8,128)S(1)}, u32[]{:S(2)}, u32[]{:S(2)}) collective-permute-start(f32[8,8,600]{2,1,0:T(8,128)S(1)} %slice.4), channel_id=1, source_target_pairs={{0,2},{1,3},{2,0},{3,1},{4,6},{5,7},{6,4},{7,5},{8,10},{9,11},{10,... | collective-permute-start | bytes 460808 | tf_op jit(solution)/shard_map/ppermute | solution.py:234
  25.9 8.5 %collective-permute-start.2 = (f32[8,8,600]{2,1,0:T(8,128)S(1)}, f32[8,8,600]{2,1,0:T(8,128)S(1)}, u32[]{:S(2)}, u32[]{:S(2)}) collective-permute-start(f32[8,8,600]{2,1,0:T(8,128)S(1)} %slice.4), channel_id=1, source_target_pairs={{0,1},{1,2},{2,3},{3,0},{4,5},{5,6},{6,7},{7,4},{8,9},{9,10},{10,1... | collective-permute-start | bytes 460808 | tf_op jit(solution)/shard_map/ppermute | solution.py:234

commit v13 on v8

--- a/solution.py
+++ b/solution.py
@@ -10,6 +10,7 @@
 LANES = 128
 WIDE = 256
 SLOT = 64
+SLICE = 16
 NT = (((1,), (1,)), ((), ()))
 
 
@@ -73,6 +74,7 @@
     full = rhs_ref.shape[2]
     end = n_cols - full
     chunks = [(a, min(WIDE, full - a)) for a in range(0, full, WIDE)]
+    slices = [(a, min(SLICE, deep - a)) for a in range(0, deep, SLICE)]
 
     for norm_row, one_row, refs in ((3, 4, row_terms), (4, 3, col_terms)):
         for ref in refs:
@@ -120,18 +122,22 @@
     if end:
         weight_end_ref[...] = jnp.zeros_like(weight_end_ref)
 
-    def tanh_block(s, start, size):
-        return jnp.tanh(jnp.dot(lhs_ref[s], rhs_ref[s, :, pl.ds(start, size)], preferred_element_type=jnp.float32))
-
-    def tanh_end(b):
-        return jnp.tanh(jnp.dot(lhs_end_ref[b], rhs_end_ref[b], preferred_element_type=jnp.float32))
+    def half_block(s, start, size):
+        return jnp.dot(lhs_ref[s], rhs_ref[s, :, pl.ds(start, size)], preferred_element_type=jnp.float32)
+
+    def half_end(b):
+        return jnp.dot(lhs_end_ref[b], rhs_end_ref[b], preferred_element_type=jnp.float32)
 
     def add_some(b, carry):
         for inside in range(fold):
             for start, size in chunks:
-                weight_ref[:, pl.ds(start, size)] += tanh_block(b * fold + inside, start, size)
+                half = half_block(b * fold + inside, start, size)
+                for a, n in slices:
+                    weight_ref[pl.ds(a, n), pl.ds(start, size)] += jnp.tanh(half[a:a + n])
         if end:
-            weight_end_ref[...] += tanh_end(b)
+            half = half_end(b)
+            for a, n in slices:
+                weight_end_ref[pl.ds(a, n), :] += jnp.tanh(half[a:a + n])
         return carry
 
     lax.fori_loop(0, structs // fold, add_some, 0)
@@ -162,10 +168,15 @@
         if deep > n_rows:
             weight_end_ref[pl.ds(n_rows, deep - n_rows), :] = jnp.zeros((deep - n_rows, LANES), jnp.float32)
 
-    def split2(weight, t):
-        g = weight * (1.0 - t * t)
-        hi = g.astype(jnp.bfloat16)
-        return [hi, (g - hi.astype(jnp.float32)).astype(jnp.bfloat16)]
+    def split2(ref, start, size, half):
+        his, los = [], []
+        for a, n in slices:
+            t = jnp.tanh(half[a:a + n])
+            g = ref[pl.ds(a, n), pl.ds(start, size)] * (1.0 - t * t)
+            hi = g.astype(jnp.bfloat16)
+            his.append(hi)
+            los.append((g - hi.astype(jnp.float32)).astype(jnp.bfloat16))
+        return [jnp.concatenate(his, axis=0), jnp.concatenate(los, axis=0)]
 
     def sums(terms, parts):
         return lax.dot_general(jnp.concatenate(parts, axis=1), jnp.concatenate(terms, axis=1), NT,
@@ -173,13 +184,13 @@
 
     def grad_some(b, carry):
         if end:
-            last = sums([terms_end_ref[b]] * 2, split2(weight_end_ref[...], tanh_end(b))).T
+            last = sums([terms_end_ref[b]] * 2, split2(weight_end_ref, 0, LANES, half_end(b))).T
         for inside in range(fold):
             s = b * fold + inside
             terms, parts = [], []
             for start, size in chunks:
                 terms += [rhs_ref[s, pl.ds(0, 16), pl.ds(start, size)]] * 2
-                parts += split2(weight_ref[:, pl.ds(start, size)], tanh_block(s, start, size))
+                parts += split2(weight_ref, start, size, half_block(s, start, size))
             total = sums(terms, parts)
             total = total.T
             if end:

time: 112 us -> 112 us (level)
  no operation moved by 1% of the time
where the time goes in v13:
time: 112 us; the launch traced here: 111 us
  Pallas kernels  63.2 us (56%)
  waiting for transfers between devices  17.8 us (16%)
  blocking collectives  15.6 us (14%)
  starting transfers between devices  9.92 us (9%)
  local copies, waits for them, and re-layouts  4.01 us (4%)
    pallas_call x1, Pallas kernels, on_device(): pl.pallas_call(functools.partial(pair_kernel, n_tile, fold), out_shape=ja...  59.6 us
    all_to_all x1, blocking collectives, on_device(): back = lax.all_to_all(grad, 'ens', 0, 0, tiled=True)  15.6 us
    all_to_all x1, waiting for transfers between devices, on_device(): both = lax.all_to_all(send, 'ens', 0, 0, tiled=True)  11.5 us
    all_to_all x1, starting transfers between devices, on_device(): both = lax.all_to_all(send, 'ens', 0, 0, tiled=True)  6.33 us
    ppermute x3, waiting for transfers between devices, on_device(): lax.ppermute(own, 'tile', [(t, (t - k) % n_tile) for t in range(n_tile)])  6.31 us
    ppermute x3, starting transfers between devices, on_device(): lax.ppermute(own, 'tile', [(t, (t - k) % n_tile) for t in range(n_tile)])  3.6 us
  transfers between devices with their start and end apart: 4, of which 3 were waited for; matrix products, arithmetic and copies ran while one was open for 4% of the time, Pallas kernels for 0%

profile of v13, /device:TPU:0, one launch (start us, length us, event | category | flops | bytes accessed | tf_op | source)
XLA Modules:
  0.0 111.3 jit_solution(3083842078997993592)
XLA Ops:
  0.0 1.9 %pack.1 = f32[8,8,1800]{2,1,0:T(8,128)} custom-call(f32[3,8,800]{2,1,0:T(8,128)} %bitcast.4), custom_call_target="tpu_custom_call" | custom-call | tf_op jit(solution)/shard_map/pack/pallas_call | solution.py:234
  1.9 6.3 %all-to-all-start = ((f32[8,8,1800]{2,1,0:T(8,128)}), f32[8,8,1800]{2,1,0:T(8,128)S(1)}, u32[]{:S(2)}, u32[]{:S(2)}) async-start(f32[8,8,1800]{2,1,0:T(8,128)} %pack.1), calls=%async_computation | async-start | bytes 983040 | tf_op jit(solution)/shard_map/all_to_all | solution.py:241
  8.2 0.9 fusion.1
  9.1 0.1 pad_add_fusion.2
  9.2 2.2 %fusion = (s32[400,200]{1,0:T(8,128)S(1)}, s32[400,200]{1,0:T(8,128)S(1)}, s32[400,200]{1,0:T(8,128)S(1)}, s32[400,200]{1,0:T(8,128)S(1)}) fusion(s32[800,3200]{1,0:T(8,128)} %param.4, s32[]{:T(128)S(6)} %select_n.38, s32[]{:T(128)S(6)} %select_n.39, s32[]{:T(128)S(6)} %select_n.40, s32[]{:T(128)S(6)} %select_n.42, s32[]{:T(128)S(6)} %select_n.41), kind=kLoop, calls=%fused_computation.7 | loop fusion | bytes 2560020 | tf_op jit(solution)/shard_map/dynamic_slice | solution.py:248
  11.4 11.5 %all-to-all-done.both_ref = f32[8,8,1800]{2,1,0:T(8,128)S(1)} async-done(((f32[8,8,1800]{2,1,0:T(8,128)}), f32[8,8,1800]{2,1,0:T(8,128)S(1)}, u32[]{:S(2)}, u32[]{:S(2)}) %all-to-all-start) | async-done | bytes 460832 | tf_op jit(solution)/shard_map/all_to_all | solution.py:241
  22.9 2.5 %collective-permute-start = (f32[8,8,600]{2,1,0:T(8,128)S(1)}, f32[8,8,600]{2,1,0:T(8,128)S(1)}, u32[]{:S(2)}, u32[]{:S(2)}) collective-permute-start(f32[8,8,600]{2,1,0:T(8,128)S(1)} %slice.4), channel_id=1, source_target_pairs={{0,3},{1,0},{2,1},{3,2},{4,7},{5,4},{6,5},{7,6},{8,11},{9,8},{10,9... | collective-permute-start | bytes 460808 | tf_op jit(solution)/shard_map/ppermute | solution.py:243
  25.4 0.5 collective-permute-start.1
  25.9 0.6 collective-permute-start.2
  26.5 0.1 pad_add_fusion.1
  26.6 0.8 dynamic_slice.28
  27.4 0.1 copy.4.seg_rows_ref
  27.5 0.5 pad_add_fusion.counts_ref
  28.0 2.0 %collective-permute-done.rest_0_ = f32[8,8,600]{2,1,0:T(8,128)S(1)} collective-permute-done((f32[8,8,600]{2,1,0:T(8,128)S(1)}, f32[8,8,600]{2,1,0:T(8,128)S(1)}, u32[]{:S(2)}, u32[]{:S(2)}) %collective-permute-start) | collective-permute-done | bytes 153632 | tf_op jit(solution)/shard_map/ppermute | solution.py:243
  30.0 4.3 %collective-permute-done.1.rest_1_ = f32[8,8,600]{2,1,0:T(8,128)S(1)} collective-permute-done((f32[8,8,600]{2,1,0:T(8,128)S(1)}, f32[8,8,600]{2,1,0:T(8,128)S(1)}, u32[]{:S(2)}, u32[]{:S(2)}) %collective-permute-start.1) | collective-permute-done | bytes 153632 | tf_op jit(solution)/shard_map/ppermute | solution.py:243
  34.4 0.0 collective-permute-done.2.rest_2_
  34.4 59.6 %pairs.1 = f32[8,3,8,400]{3,2,1,0:T(8,128)S(1)} custom-call(s32[1]{0:T(128)} %bitcast.base_ref, s32[400,1]{1,0:T(8,128)S(1)} %copy.4.seg_rows_ref, s32[1,800]{1,0:T(1,128)S(1)} %broadcast_in_dim.14.seg_cols_ref, s32[1,800]{1,0:T(1,128)S(1)} %broadcast_in_dim.15.col_ids_ref, s32[400,800]{1,0:T(8,128)S(1)} %pad_add_fusion.counts_ref, ...), custom_call_target="tpu_custom_call" | custom-call | tf_op jit(solution)/shard_map/pairs/pallas_call | solution.py:259
  94.0 15.6 %all_to_all.10.back_ref = f32[8,3,8,400]{3,2,1,0:T(8,128)} all-to-all(f32[8,3,8,400]{3,2,1,0:T(8,128)S(1)} %pairs.1), channel_id=1, replica_groups=mesh['ens'=8,'tile'=4] {'ens'}, dimensions={0} | all-to-all | bytes 614400 | tf_op jit(solution)/shard_map/all_to_all | solution.py:279
  109.6 1.7 %total.1 = f32[3,8,800]{2,1,0:T(8,128)} custom-call(f32[8,3,8,400]{3,2,1,0:T(8,128)} %all_to_all.10.back_ref), custom_call_target="tpu_custom_call" | custom-call | tf_op jit(solution)/shard_map/total/pallas_call | solution.py:280
  (5 shorter events, 0.0 us)
Async XLA Ops:
  1.9 21.0 %all-to-all-start = ((f32[8,8,1800]{2,1,0:T(8,128)}), f32[8,8,1800]{2,1,0:T(8,128)S(1)}, u32[]{:S(2)}, u32[]{:S(2)}) async-start(f32[8,8,1800]{2,1,0:T(8,128)} %pack.1), calls=%async_computation | async-start | bytes 983040 | tf_op jit(solution)/shard_map/all_to_all | solution.py:241
  22.9 7.1 %collective-permute-start = (f32[8,8,600]{2,1,0:T(8,128)S(1)}, f32[8,8,600]{2,1,0:T(8,128)S(1)}, u32[]{:S(2)}, u32[]{:S(2)}) collective-permute-start(f32[8,8,600]{2,1,0:T(8,128)S(1)} %slice.4), channel_id=1, source_target_pairs={{0,3},{1,0},{2,1},{3,2},{4,7},{5,4},{6,5},{7,6},{8,11},{9,8},{10,9... | collective-permute-start | bytes 460808 | tf_op jit(solution)/shard_map/ppermute | solution.py:243
  25.4 9.0 %collective-permute-start.1 = (f32[8,8,600]{2,1,0:T(8,128)S(1)}, f32[8,8,600]{2,1,0:T(8,128)S(1)}, u32[]{:S(2)}, u32[]{:S(2)}) collective-permute-start(f32[8,8,600]{2,1,0:T(8,128)S(1)} %slice.4), channel_id=1, source_target_pairs={{0,2},{1,3},{2,0},{3,1},{4,6},{5,7},{6,4},{7,5},{8,10},{9,11},{10,... | collective-permute-start | bytes 460808 | tf_op jit(solution)/shard_map/ppermute | solution.py:243
  25.9 8.5 %collective-permute-start.2 = (f32[8,8,600]{2,1,0:T(8,128)S(1)}, f32[8,8,600]{2,1,0:T(8,128)S(1)}, u32[]{:S(2)}, u32[]{:S(2)}) collective-permute-start(f32[8,8,600]{2,1,0:T(8,128)S(1)} %slice.4), channel_id=1, source_target_pairs={{0,1},{1,2},{2,3},{3,0},{4,5},{5,6},{6,7},{7,4},{8,9},{9,10},{10,1... | collective-permute-start | bytes 460808 | tf_op jit(solution)/shard_map/ppermute | solution.py:243

commit v14 on v8

--- a/solution.py
+++ b/solution.py
@@ -10,6 +10,7 @@
 LANES = 128
 WIDE = 256
 SLOT = 64
+UNROLL = 2
 NT = (((1,), (1,)), ((), ()))
 
 
@@ -61,10 +62,40 @@
     return [jnp.concatenate([ref[k, pl.ds(8 * i, 8), :] for k in range(ref.shape[0])], axis=1) for ref in refs]
 
 
-def pair_kernel(tiles, fold, base_ref, seg_rows_ref, seg_cols_ref, col_ids_ref, counts_ref, both_ref, *rest):
+def init_terms(refs, one_row, per):
+    for ref in refs:
+        ref[...] = jnp.zeros_like(ref)
+    for k in range(refs[0].shape[0]):
+        refs[0][k, pl.ds(one_row, per, 8), :] = jnp.ones((per, LANES), jnp.float32)
+
+
+def row_kernel(n_rows, fold, both_ref, lhs_ref, lhs_end_ref, row_terms):
+    groups, per, width = both_ref.shape
+    deep = lhs_ref.shape[1]
+    first = width - 3 * n_rows
+    init_terms(row_terms, 4, per)
+
+    def features(g, carry):
+        both = both_ref[g]
+        put_terms(row_terms, [both[:, first + c * n_rows:first + (c + 1) * n_rows] for c in range(3)], 3)
+        for block in range(per // fold):
+            lefts = []
+            for inside in range(fold):
+                i = block * fold + inside
+                hi, mid, lo = get_terms(row_terms, i)
+                left = jnp.concatenate([hi, hi, mid, mid, hi, lo], axis=0)
+                lhs_ref[g * per + i] = left.T[:deep].astype(jnp.bfloat16)
+                lefts += [left, jnp.zeros((SLOT - 48, left.shape[1]), jnp.float32)]
+            lhs_end_ref[g * (per // fold) + block] = jnp.concatenate(lefts, axis=0).T[:deep].astype(jnp.bfloat16)
+        return carry
+
+    lax.fori_loop(0, groups, features, 0)
+
+
+def pair_kernel(tiles, fold, base_ref, seg_rows_ref, seg_cols_ref, col_ids_ref, counts_ref, lhs_ref, lhs_end_ref,
+                both_ref, *rest):
     piece_refs = rest[:tiles - 1]
-    (grad_ref, row_terms, col_terms, lhs_ref, lhs_end_ref, rhs_ref, rhs_end_ref, terms_end_ref, weight_ref,
-     weight_end_ref) = rest[tiles - 1:]
+    grad_ref, col_terms, rhs_ref, rhs_end_ref, terms_end_ref, weight_ref, weight_end_ref = rest[tiles - 1:]
     groups, per, _ = both_ref.shape
     structs = groups * per
     n_rows, n_cols = counts_ref.shape
@@ -74,11 +105,7 @@
     end = n_cols - full
     chunks = [(a, min(WIDE, full - a)) for a in range(0, full, WIDE)]
 
-    for norm_row, one_row, refs in ((3, 4, row_terms), (4, 3, col_terms)):
-        for ref in refs:
-            ref[...] = jnp.zeros_like(ref)
-        for k in range(refs[0].shape[0]):
-            refs[0][k, pl.ds(one_row, per, 8), :] = jnp.ones((per, LANES), jnp.float32)
+    init_terms(col_terms, 3, per)
     if end:
         rhs_end_ref[...] = jnp.zeros_like(rhs_end_ref)
 
@@ -86,19 +113,11 @@
         both = both_ref[g]
         parts = [both] + [ref[g] for ref in piece_refs]
         cols = [jnp.concatenate([v[:, c * piece:(c + 1) * piece] for v in parts], axis=1) for c in range(3)]
-        rows = [both[:, 3 * piece + c * n_rows:3 * piece + (c + 1) * n_rows] for c in range(3)]
-        put_terms(row_terms, rows, 3)
         put_terms(col_terms, cols, 4)
         for block in range(per // fold):
-            lefts = []
             for inside in range(fold):
                 i = block * fold + inside
                 s = g * per + i
-                hi, mid, lo = get_terms(row_terms, i)
-                left = jnp.concatenate([hi, hi, mid, mid, hi, lo], axis=0)
-                lhs_ref[s] = left.T[:deep].astype(jnp.bfloat16)
-                if end:
-                    lefts += [left, jnp.zeros((SLOT - 48, left.shape[1]), jnp.float32)]
                 hi, mid, lo = get_terms(col_terms, i)
                 right = jnp.concatenate([hi, mid, hi, mid, lo, hi], axis=0)
                 rhs_ref[s] = right[:, :full].astype(jnp.bfloat16)
@@ -111,8 +130,6 @@
                     b = g * (per // fold) + block
                     rhs_end_ref[b, pl.ds(SLOT * inside, 48), :] = last
                     terms_end_ref[b, pl.ds(16 * inside, 16), :] = last[0:16]
-            if end:
-                lhs_end_ref[g * (per // fold) + block] = jnp.concatenate(lefts, axis=0).T[:deep].astype(jnp.bfloat16)
         return carry
 
     lax.fori_loop(0, groups, features, 0)
@@ -134,7 +151,7 @@
             weight_end_ref[...] += tanh_end(b)
         return carry
 
-    lax.fori_loop(0, structs // fold, add_some, 0)
+    lax.fori_loop(0, structs // fold, add_some, 0, unroll=UNROLL)
 
     def mask_and_target(start, size):
         count = counts_ref[:, pl.ds(start, size)].astype(jnp.float32)
@@ -193,7 +210,7 @@
                     total[c:c + 1] + total[8 + c:9 + c] - total[3:4] * xyz)
         return carry
 
-    lax.fori_loop(0, structs // fold, grad_some, 0)
+    lax.fori_loop(0, structs // fold, grad_some, 0, unroll=UNROLL)
 
 
 def split_ens(n_ens, beads, tiles):
@@ -245,25 +262,34 @@
     deep = up(n_rows, 16)
     row_wide, col_wide = up(n_rows, LANES), up(n_cols, LANES)
     blocks = structs // fold
+    lhs, lhs_end = pl.pallas_call(
+        functools.partial(row_kernel, n_rows, fold),
+        out_shape=[
+            jax.ShapeDtypeStruct((structs, deep, 48), jnp.bfloat16),
+            jax.ShapeDtypeStruct((blocks, deep, fold * SLOT), jnp.bfloat16),
+        ],
+        in_specs=[vmem],
+        out_specs=[vmem] * 2,
+        scratch_shapes=[[pltpu.VMEM((row_wide // LANES, 8 * local_n, LANES), jnp.float32)] * 3],
+        compiler_params=pltpu.CompilerParams(vmem_limit_bytes=32 << 20),
+        name="rows",
+    )(both)
     grad = pl.pallas_call(
         functools.partial(pair_kernel, n_tile, fold),
         out_shape=jax.ShapeDtypeStruct((n_ens, 3, local_n, n_rows), jnp.float32),
-        in_specs=[pl.BlockSpec(memory_space=pltpu.SMEM)] + [vmem] * (4 + n_tile),
+        in_specs=[pl.BlockSpec(memory_space=pltpu.SMEM)] + [vmem] * (6 + n_tile),
         out_specs=vmem,
         scratch_shapes=[
-            [pltpu.VMEM((row_wide // LANES, 8 * local_n, LANES), jnp.float32)] * 3,
             [pltpu.VMEM((col_wide // LANES, 8 * local_n, LANES), jnp.float32)] * 3,
-            pltpu.VMEM((structs, deep, 48), jnp.bfloat16),
-            pltpu.VMEM((blocks, deep, fold * SLOT), jnp.bfloat16),
             pltpu.VMEM((structs, 48, full), jnp.bfloat16),
             pltpu.VMEM((blocks, fold * SLOT, LANES), jnp.bfloat16),
             pltpu.VMEM((blocks, fold * 16, LANES), jnp.bfloat16),
             pltpu.VMEM((deep, full), jnp.float32),
             pltpu.VMEM((deep, LANES), jnp.float32),
         ],
-        compiler_params=pltpu.CompilerParams(vmem_limit_bytes=48 << 20),
+        compiler_params=pltpu.CompilerParams(vmem_limit_bytes=40 << 20),
         name="pairs",
-    )(row_base[None], seg_rows, seg_cols, col_ids, block, both, *pieces)
+    )(row_base[None], seg_rows, seg_cols, col_ids, block, lhs, lhs_end, both, *pieces)
 
     back = lax.all_to_all(grad, "ens", 0, 0, tiled=True)
     total = pl.pallas_call(

time: 112 us -> 105 us (0.938)
  waiting for transfers between devices: 17.8 us -> 11.5 us
    ppermute x3, waiting for transfers between devices: 6.31 us -> 0.01 us  [on_device(): lax.ppermute(own, 'tile', [(t, (t - k) % n_tile) for t in range(n_tile)])]
    pallas_call x1, Pallas kernels: 59.6 us -> 53.6 us  [on_device(): pl.pallas_call(functools.partial(pair_kernel, n_tile, fold), out_shape=ja...]
    pallas_call x0 -> x1, Pallas kernels: none -> 4.99 us  [on_device(): pl.pallas_call(functools.partial(row_kernel, n_rows, fold), out_shape=[ja...]
  transfers between devices with their start and end apart: 4 -> 4, of which waited for: 3 -> 1; matrix products, arithmetic and copies ran while one was open for 4% -> 4% of each run, Pallas kernels for 0% -> 5%
where the time goes in v14:
time: 105 us
  Pallas kernels  62.2 us (59%)
  blocking collectives  15.6 us (15%)
  waiting for transfers between devices  11.5 us (11%)
  starting transfers between devices  10.8 us (10%)
  local copies, waits for them, and re-layouts  3.99 us (4%)
    pallas_call x1, Pallas kernels, on_device(): pl.pallas_call(functools.partial(pair_kernel, n_tile, fold), out_shape=ja...  53.6 us
    all_to_all x1, blocking collectives, on_device(): back = lax.all_to_all(grad, 'ens', 0, 0, tiled=True)  15.6 us
    all_to_all x1, waiting for transfers between devices, on_device(): both = lax.all_to_all(send, 'ens', 0, 0, tiled=True)  11.5 us
    all_to_all x1, starting transfers between devices, on_device(): both = lax.all_to_all(send, 'ens', 0, 0, tiled=True)  6.33 us
    pallas_call x1, Pallas kernels, on_device(): pl.pallas_call(functools.partial(row_kernel, n_rows, fold), out_shape=[ja...  4.99 us
    ppermute x3, starting transfers between devices, on_device(): lax.ppermute(own, 'tile', [(t, (t - k) % n_tile) for t in range(n_tile)])  4.5 us
    dynamic_slice x1, local copies, waits for them, and re-layouts, on_device(): lax.dynamic_slice_in_dim(own_counts, b, piece, 1)  2.17 us
  transfers between devices with their start and end apart: 4, of which 1 were waited for; matrix products, arithmetic and copies ran while one was open for 4% of the time, Pallas kernels for 5%

profile of v14, /device:TPU:0, one launch (start us, length us, event | category | flops | bytes accessed | tf_op | source)
XLA Modules:
  0.0 104.9 jit_solution(14006931056736498194)
XLA Ops:
  0.0 1.9 %pack.1 = f32[8,8,1800]{2,1,0:T(8,128)} custom-call(f32[3,8,800]{2,1,0:T(8,128)} %bitcast.4), custom_call_target="tpu_custom_call" | custom-call | tf_op jit(solution)/shard_map/pack/pallas_call | solution.py:240
  1.9 6.3 %all-to-all-start = ((f32[8,8,1800]{2,1,0:T(8,128)}), f32[8,8,1800]{2,1,0:T(8,128)S(1)}, u32[]{:S(2)}, u32[]{:S(2)}) async-start(f32[8,8,1800]{2,1,0:T(8,128)} %pack.1), calls=%async_computation | async-start | bytes 983040 | tf_op jit(solution)/shard_map/all_to_all | solution.py:247
  8.2 0.9 fusion.1
  9.1 0.1 pad_add_fusion.2
  9.2 2.2 %fusion = (s32[400,200]{1,0:T(8,128)S(1)}, s32[400,200]{1,0:T(8,128)S(1)}, s32[400,200]{1,0:T(8,128)S(1)}, s32[400,200]{1,0:T(8,128)S(1)}) fusion(s32[800,3200]{1,0:T(8,128)} %param.4, s32[]{:T(128)S(6)} %select_n.38, s32[]{:T(128)S(6)} %select_n.39, s32[]{:T(128)S(6)} %select_n.40, s32[]{:T(128)S(6)} %select_n.42, s32[]{:T(128)S(6)} %select_n.41), kind=kLoop, calls=%fused_computation.7 | loop fusion | bytes 2560020 | tf_op jit(solution)/shard_map/dynamic_slice | solution.py:254
  11.4 11.5 %all-to-all-done.both_ref = f32[8,8,1800]{2,1,0:T(8,128)S(1)} async-done(((f32[8,8,1800]{2,1,0:T(8,128)}), f32[8,8,1800]{2,1,0:T(8,128)S(1)}, u32[]{:S(2)}, u32[]{:S(2)}) %all-to-all-start) | async-done | bytes 460832 | tf_op jit(solution)/shard_map/all_to_all | solution.py:247
  22.9 1.5 %collective-permute-start.2 = (f32[8,8,600]{2,1,0:T(8,128)S(1)}, f32[8,8,600]{2,1,0:T(8,128)S(1)}, u32[]{:S(2)}, u32[]{:S(2)}) collective-permute-start(f32[8,8,600]{2,1,0:T(8,128)S(1)} %slice.4), channel_id=1, source_target_pairs={{0,1},{1,2},{2,3},{3,0},{4,5},{5,6},{6,7},{7,4},{8,9},{9,10},{10,1... | collective-permute-start | bytes 460808 | tf_op jit(solution)/shard_map/ppermute | solution.py:249
  24.4 1.5 %collective-permute-start.1 = (f32[8,8,600]{2,1,0:T(8,128)S(1)}, f32[8,8,600]{2,1,0:T(8,128)S(1)}, u32[]{:S(2)}, u32[]{:S(2)}) collective-permute-start(f32[8,8,600]{2,1,0:T(8,128)S(1)} %slice.4), channel_id=1, source_target_pairs={{0,2},{1,3},{2,0},{3,1},{4,6},{5,7},{6,4},{7,5},{8,10},{9,11},{10,... | collective-permute-start | bytes 460808 | tf_op jit(solution)/shard_map/ppermute | solution.py:249
  25.9 1.4 %collective-permute-start = (f32[8,8,600]{2,1,0:T(8,128)S(1)}, f32[8,8,600]{2,1,0:T(8,128)S(1)}, u32[]{:S(2)}, u32[]{:S(2)}) collective-permute-start(f32[8,8,600]{2,1,0:T(8,128)S(1)} %slice.4), channel_id=1, source_target_pairs={{0,3},{1,0},{2,1},{3,2},{4,7},{5,4},{6,5},{7,6},{8,11},{9,8},{10,9... | collective-permute-start | bytes 460808 | tf_op jit(solution)/shard_map/ppermute | solution.py:249
  27.4 0.1 pad_add_fusion.1
  27.5 0.8 dynamic_slice.28
  28.2 0.1 copy.4.seg_rows_ref
  28.4 0.5 pad_add_fusion.counts_ref
  28.9 5.0 %rows.1 = (bf16[64,400,48]{2,1,0:T(8,128)(2,1)S(1)}, bf16[16,400,256]{2,1,0:T(8,128)(2,1)S(1)}) custom-call(f32[8,8,1800]{2,1,0:T(8,128)S(1)} %all-to-all-done.both_ref), custom_call_target="tpu_custom_call" | custom-call | tf_op jit(solution)/shard_map/rows/pallas_call | solution.py:265
  33.9 0.0 collective-permute-done.2.rest_2_
  33.9 0.0 collective-permute-done.1.rest_1_
  33.9 0.0 collective-permute-done.rest_0_
  34.0 53.6 %pairs.1 = f32[8,3,8,400]{3,2,1,0:T(8,128)S(1)} custom-call(s32[1]{0:T(128)} %bitcast.base_ref, s32[400,1]{1,0:T(8,128)S(1)} %copy.4.seg_rows_ref, s32[1,800]{1,0:T(1,128)S(1)} %broadcast_in_dim.14.seg_cols_ref, s32[1,800]{1,0:T(1,128)S(1)} %broadcast_in_dim.15.col_ids_ref, s32[400,800]{1,0:T(8,128)S(1)} %pad_add_fusion.counts_ref, ...), custom_call_target="tpu_custom_call" | custom-call | tf_op jit(solution)/shard_map/pairs/pallas_call | solution.py:277
  87.6 15.6 %all_to_all.10.back_ref = f32[8,3,8,400]{3,2,1,0:T(8,128)} all-to-all(f32[8,3,8,400]{3,2,1,0:T(8,128)S(1)} %pairs.1), channel_id=1, replica_groups=mesh['ens'=8,'tile'=4] {'ens'}, dimensions={0} | all-to-all | bytes 614400 | tf_op jit(solution)/shard_map/all_to_all | solution.py:294
  103.2 1.7 %total.1 = f32[3,8,800]{2,1,0:T(8,128)} custom-call(f32[8,3,8,400]{3,2,1,0:T(8,128)} %all_to_all.10.back_ref), custom_call_target="tpu_custom_call" | custom-call | tf_op jit(solution)/shard_map/total/pallas_call | solution.py:295
  (5 shorter events, 0.0 us)
Async XLA Ops:
  1.9 21.0 %all-to-all-start = ((f32[8,8,1800]{2,1,0:T(8,128)}), f32[8,8,1800]{2,1,0:T(8,128)S(1)}, u32[]{:S(2)}, u32[]{:S(2)}) async-start(f32[8,8,1800]{2,1,0:T(8,128)} %pack.1), calls=%async_computation | async-start | bytes 983040 | tf_op jit(solution)/shard_map/all_to_all | solution.py:247
  22.9 11.0 %collective-permute-start.2 = (f32[8,8,600]{2,1,0:T(8,128)S(1)}, f32[8,8,600]{2,1,0:T(8,128)S(1)}, u32[]{:S(2)}, u32[]{:S(2)}) collective-permute-start(f32[8,8,600]{2,1,0:T(8,128)S(1)} %slice.4), channel_id=1, source_target_pairs={{0,1},{1,2},{2,3},{3,0},{4,5},{5,6},{6,7},{7,4},{8,9},{9,10},{10,1... | collective-permute-start | bytes 460808 | tf_op jit(solution)/shard_map/ppermute | solution.py:249
  24.4 9.5 %collective-permute-start.1 = (f32[8,8,600]{2,1,0:T(8,128)S(1)}, f32[8,8,600]{2,1,0:T(8,128)S(1)}, u32[]{:S(2)}, u32[]{:S(2)}) collective-permute-start(f32[8,8,600]{2,1,0:T(8,128)S(1)} %slice.4), channel_id=1, source_target_pairs={{0,2},{1,3},{2,0},{3,1},{4,6},{5,7},{6,4},{7,5},{8,10},{9,11},{10,... | collective-permute-start | bytes 460808 | tf_op jit(solution)/shard_map/ppermute | solution.py:249
  25.9 8.0 %collective-permute-start = (f32[8,8,600]{2,1,0:T(8,128)S(1)}, f32[8,8,600]{2,1,0:T(8,128)S(1)}, u32[]{:S(2)}, u32[]{:S(2)}) collective-permute-start(f32[8,8,600]{2,1,0:T(8,128)S(1)} %slice.4), channel_id=1, source_target_pairs={{0,3},{1,0},{2,1},{3,2},{4,7},{5,4},{6,5},{7,6},{8,11},{9,8},{10,9... | collective-permute-start | bytes 460808 | tf_op jit(solution)/shard_map/ppermute | solution.py:249

commit v15 on v14

--- a/solution.py
+++ b/solution.py
@@ -10,7 +10,7 @@
 LANES = 128
 WIDE = 256
 SLOT = 64
-UNROLL = 2
+UNROLL = 4
 NT = (((1,), (1,)), ((), ()))
 
 
@@ -92,13 +92,39 @@
     lax.fori_loop(0, groups, features, 0)
 
 
-def pair_kernel(tiles, fold, base_ref, seg_rows_ref, seg_cols_ref, col_ids_ref, counts_ref, lhs_ref, lhs_end_ref,
+def mask_kernel(fold, base_ref, seg_rows_ref, seg_cols_ref, col_ids_ref, counts_ref, mask_ref, goal_ref, mask_end_ref,
+                goal_end_ref):
+    n_rows, n_cols = counts_ref.shape
+    deep, full = mask_ref.shape
+    end = n_cols - full
+    for ref in (mask_ref, goal_ref, mask_end_ref, goal_end_ref):
+        if deep > n_rows:
+            ref[pl.ds(n_rows, deep - n_rows), :] = jnp.zeros((deep - n_rows, ref.shape[1]), jnp.float32)
+
+    def mask_and_goal(start, size):
+        count = counts_ref[:, pl.ds(start, size)].astype(jnp.float32)
+        row_ids = base_ref[0] + lax.broadcasted_iota(jnp.int32, (n_rows, size), 0)
+        mask = jnp.where(seg_rows_ref[...] == seg_cols_ref[:, pl.ds(start, size)], 1.0, 0.3)
+        mask = jnp.where(row_ids == col_ids_ref[:, pl.ds(start, size)], 0.0, mask)
+        return mask, mask * (count / (count + 8.0))
+
+    rows = pl.ds(0, n_rows)
+    for start in range(0, full, LANES):
+        mask_ref[rows, pl.ds(start, LANES)], goal_ref[rows, pl.ds(start, LANES)] = mask_and_goal(start, LANES)
+    if end:
+        def spread(v):
+            v = jnp.concatenate([v, jnp.zeros((n_rows, LANES - end), jnp.float32)], axis=1)
+            return sum((pltpu.roll(v, k * end, 1) for k in range(1, fold)), v)
+
+        mask_end_ref[rows, :], goal_end_ref[rows, :] = [spread(v) for v in mask_and_goal(full, end)]
+
+
+def pair_kernel(tiles, fold, n_rows, n_cols, mask_ref, goal_ref, mask_end_ref, goal_end_ref, lhs_ref, lhs_end_ref,
                 both_ref, *rest):
     piece_refs = rest[:tiles - 1]
     grad_ref, col_terms, rhs_ref, rhs_end_ref, terms_end_ref, weight_ref, weight_end_ref = rest[tiles - 1:]
     groups, per, _ = both_ref.shape
     structs = groups * per
-    n_rows, n_cols = counts_ref.shape
     piece = n_cols // tiles
     deep = weight_ref.shape[0]
     full = rhs_ref.shape[2]
@@ -153,31 +179,14 @@
 
     lax.fori_loop(0, structs // fold, add_some, 0, unroll=UNROLL)
 
-    def mask_and_target(start, size):
-        count = counts_ref[:, pl.ds(start, size)].astype(jnp.float32)
-        row_ids = base_ref[0] + lax.broadcasted_iota(jnp.int32, (n_rows, size), 0)
-        mask = jnp.where(seg_rows_ref[...] == seg_cols_ref[:, pl.ds(start, size)], 1.0, 0.3)
-        mask = jnp.where(row_ids == col_ids_ref[:, pl.ds(start, size)], 0.0, mask)
-        return mask, mask * (count / (count + 8.0))
-
     scale = 0.5 / structs
     for start, size in chunks:
-        mask, goal = mask_and_target(start, size)
-        total = weight_ref[pl.ds(0, n_rows), pl.ds(start, size)]
-        weight_ref[pl.ds(0, n_rows), pl.ds(start, size)] = mask * (0.5 + scale * total) - goal
-    if deep > n_rows:
-        weight_ref[pl.ds(n_rows, deep - n_rows), :] = jnp.zeros((deep - n_rows, full), jnp.float32)
+        cut = pl.ds(start, size)
+        weight_ref[:, cut] = mask_ref[:, cut] * (0.5 + scale * weight_ref[:, cut]) - goal_ref[:, cut]
     if end:
-        def spread(v):
-            v = jnp.concatenate([v, jnp.zeros((n_rows, LANES - end), jnp.float32)], axis=1)
-            return sum((pltpu.roll(v, k * end, 1) for k in range(1, fold)), v)
-
-        mask, goal = [spread(v) for v in mask_and_target(full, end)]
-        part = weight_end_ref[pl.ds(0, n_rows), :]
+        part = weight_end_ref[...]
         total = sum((pltpu.roll(part, k * end, 1) for k in range(1, fold)), part)
-        weight_end_ref[pl.ds(0, n_rows), :] = mask * (0.5 + scale * total) - goal
-        if deep > n_rows:
-            weight_end_ref[pl.ds(n_rows, deep - n_rows), :] = jnp.zeros((deep - n_rows, LANES), jnp.float32)
+        weight_end_ref[...] = mask_end_ref[...] * (0.5 + scale * total) - goal_end_ref[...]
 
     def split2(weight, t):
         g = weight * (1.0 - t * t)
@@ -245,8 +254,6 @@
         name="pack",
     )(jnp.swapaxes(coords, 0, 1))
     both = lax.all_to_all(send, "ens", 0, 0, tiled=True)
-    own = both[:, :, :3 * piece]
-    pieces = [lax.ppermute(own, "tile", [(t, (t - k) % n_tile) for t in range(n_tile)]) for k in range(1, n_tile)]
 
     row_base = tile * beads + p * n_rows
     col_bases = [lax.rem(tile + k, n_tile) * beads + q * piece for k in range(n_tile)]
@@ -262,6 +269,18 @@
     deep = up(n_rows, 16)
     row_wide, col_wide = up(n_rows, LANES), up(n_cols, LANES)
     blocks = structs // fold
+    masks = pl.pallas_call(
+        functools.partial(mask_kernel, fold),
+        out_shape=[jax.ShapeDtypeStruct((deep, width), jnp.float32) for width in (full, full, LANES, LANES)],
+        in_specs=[pl.BlockSpec(memory_space=pltpu.SMEM)] + [vmem] * 4,
+        out_specs=[vmem] * 4,
+        compiler_params=pltpu.CompilerParams(vmem_limit_bytes=32 << 20),
+        name="masks",
+    )(row_base[None], seg_rows, seg_cols, col_ids, block)
+    both, masks = lax.optimization_barrier((both, masks))
+    own = both[:, :, :3 * piece]
+    pieces = [lax.ppermute(own, "tile", [(t, (t - k) % n_tile) for t in range(n_tile)]) for k in range(1, n_tile)]
+
     lhs, lhs_end = pl.pallas_call(
         functools.partial(row_kernel, n_rows, fold),
         out_shape=[
@@ -275,9 +294,9 @@
         name="rows",
     )(both)
     grad = pl.pallas_call(
-        functools.partial(pair_kernel, n_tile, fold),
+        functools.partial(pair_kernel, n_tile, fold, n_rows, n_cols),
         out_shape=jax.ShapeDtypeStruct((n_ens, 3, local_n, n_rows), jnp.float32),
-        in_specs=[pl.BlockSpec(memory_space=pltpu.SMEM)] + [vmem] * (6 + n_tile),
+        in_specs=[vmem] * (6 + n_tile),
         out_specs=vmem,
         scratch_shapes=[
             [pltpu.VMEM((col_wide // LANES, 8 * local_n, LANES), jnp.float32)] * 3,
@@ -289,7 +308,7 @@
         ],
         compiler_params=pltpu.CompilerParams(vmem_limit_bytes=40 << 20),
         name="pairs",
-    )(row_base[None], seg_rows, seg_cols, col_ids, block, lhs, lhs_end, both, *pieces)
+    )(*masks, lhs, lhs_end, both, *pieces)
 
     back = lax.all_to_all(grad, "ens", 0, 0, tiled=True)
     total = pl.pallas_call(

time: 105 us -> 102 us (0.971)
  Pallas kernels: 62.2 us -> 59.8 us
  waiting for transfers between devices: 11.5 us -> 9.14 us
  local copies, waits for them, and re-layouts: 3.99 us -> 5.61 us
    all_to_all x1, waiting for transfers between devices: 11.5 us -> 8.34 us  [on_device(): both = lax.all_to_all(send, 'ens', 0, 0, tiled=True)]
    pallas_call x1 -> x2, Pallas kernels: 53.6 us -> 51.2 us  [the longest x1 50.3 us: on_device(): pl.pallas_call(functools.partial(pair_kernel, n_tile, fold, n_rows, n_col...]
    unnamed x0 -> x4, local copies, waits for them, and re-layouts: none -> 1.6 us
  transfers between devices with their start and end apart: 4 -> 4, of which waited for: 1 -> 3; matrix products, arithmetic and copies ran while one was open for 4% -> 5% of each run, Pallas kernels for 5% -> 6%
where the time goes in v15:
time: 102 us
  Pallas kernels  59.8 us (59%)
  blocking collectives  15.6 us (15%)
  starting transfers between devices  10.8 us (11%)
  waiting for transfers between devices  9.14 us (9%)
  local copies, waits for them, and re-layouts  5.61 us (6%)
    pallas_call x1, Pallas kernels, on_device(): pl.pallas_call(functools.partial(pair_kernel, n_tile, fold, n_rows, n_col...  50.3 us
    all_to_all x1, blocking collectives, on_device(): back = lax.all_to_all(grad, 'ens', 0, 0, tiled=True)  15.6 us
    all_to_all x1, waiting for transfers between devices, on_device(): both = lax.all_to_all(send, 'ens', 0, 0, tiled=True)  8.34 us
    all_to_all x1, starting transfers between devices, on_device(): both = lax.all_to_all(send, 'ens', 0, 0, tiled=True)  6.33 us
    pallas_call x1, Pallas kernels, on_device(): pl.pallas_call(functools.partial(row_kernel, n_rows, fold), out_shape=[ja...  4.98 us
    ppermute x3, starting transfers between devices, on_device(): lax.ppermute(own, 'tile', [(t, (t - k) % n_tile) for t in range(n_tile)])  4.5 us
    dynamic_slice x1, local copies, waits for them, and re-layouts, on_device(): lax.dynamic_slice_in_dim(own_counts, b, piece, 1)  2.19 us
  transfers between devices with their start and end apart: 4, of which 3 were waited for; matrix products, arithmetic and copies ran while one was open for 5% of the time, Pallas kernels for 6%

profile of v15, /device:TPU:0, one launch (start us, length us, event | category | flops | bytes accessed | tf_op | source)
XLA Modules:
  0.0 101.8 jit_solution(4446010706171898117)
XLA Ops:
  0.0 1.9 %pack.1 = f32[8,8,1800]{2,1,0:T(8,128)} custom-call(f32[3,8,800]{2,1,0:T(8,128)} %bitcast.4), custom_call_target="tpu_custom_call" | custom-call | tf_op jit(solution)/shard_map/pack/pallas_call | solution.py:249
  1.9 6.3 %all-to-all-start = ((f32[8,8,1800]{2,1,0:T(8,128)}), f32[8,8,1800]{2,1,0:T(8,128)S(1)}, u32[]{:S(2)}, u32[]{:S(2)}) async-start(f32[8,8,1800]{2,1,0:T(8,128)} %pack.1), calls=%async_computation | async-start | bytes 983040 | tf_op jit(solution)/shard_map/all_to_all | solution.py:256
  8.3 0.1 pad_add_fusion.2
  8.4 0.8 dynamic_slice.28
  9.2 0.9 fusion.1
  10.0 0.1 pad_add_fusion.1
  10.1 0.1 copy.4.seg_rows_ref
  10.3 2.2 %fusion = (s32[400,200]{1,0:T(8,128)S(1)}, s32[400,200]{1,0:T(8,128)S(1)}, s32[400,200]{1,0:T(8,128)S(1)}, s32[400,200]{1,0:T(8,128)S(1)}) fusion(s32[800,3200]{1,0:T(8,128)} %param.4, s32[]{:T(128)S(6)} %select_n.38, s32[]{:T(128)S(6)} %select_n.39, s32[]{:T(128)S(6)} %select_n.40, s32[]{:T(128)S(6)} %select_n.42, s32[]{:T(128)S(6)} %select_n.41), kind=kLoop, calls=%fused_computation.7 | loop fusion | bytes 2560020 | tf_op jit(solution)/shard_map/dynamic_slice | solution.py:261
  12.5 0.5 pad_add_fusion.counts_ref
  13.0 0.8 masks.1
  13.9 0.0 copy-start
  13.9 0.7 copy-done
  14.5 8.3 %all-to-all-done.both_ref = f32[8,8,1800]{2,1,0:T(8,128)S(1)} async-done(((f32[8,8,1800]{2,1,0:T(8,128)}), f32[8,8,1800]{2,1,0:T(8,128)S(1)}, u32[]{:S(2)}, u32[]{:S(2)}) %all-to-all-start) | async-done | bytes 460832 | tf_op jit(solution)/shard_map/all_to_all | solution.py:256
  22.9 1.5 %collective-permute-start.2 = (f32[8,8,600]{2,1,0:T(8,128)S(1)}, f32[8,8,600]{2,1,0:T(8,128)S(1)}, u32[]{:S(2)}, u32[]{:S(2)}) collective-permute-start(f32[8,8,600]{2,1,0:T(8,128)S(1)} %slice.3), channel_id=1, source_target_pairs={{0,1},{1,2},{2,3},{3,0},{4,5},{5,6},{6,7},{7,4},{8,9},{9,10},{10,1... | collective-permute-start | bytes 460808 | tf_op jit(solution)/shard_map/ppermute | solution.py:282
  24.4 1.5 %collective-permute-start.1 = (f32[8,8,600]{2,1,0:T(8,128)S(1)}, f32[8,8,600]{2,1,0:T(8,128)S(1)}, u32[]{:S(2)}, u32[]{:S(2)}) collective-permute-start(f32[8,8,600]{2,1,0:T(8,128)S(1)} %slice.3), channel_id=1, source_target_pairs={{0,2},{1,3},{2,0},{3,1},{4,6},{5,7},{6,4},{7,5},{8,10},{9,11},{10,... | collective-permute-start | bytes 460808 | tf_op jit(solution)/shard_map/ppermute | solution.py:282
  26.0 1.4 %collective-permute-start = (f32[8,8,600]{2,1,0:T(8,128)S(1)}, f32[8,8,600]{2,1,0:T(8,128)S(1)}, u32[]{:S(2)}, u32[]{:S(2)}) collective-permute-start(f32[8,8,600]{2,1,0:T(8,128)S(1)} %slice.3), channel_id=1, source_target_pairs={{0,3},{1,0},{2,1},{3,2},{4,7},{5,4},{6,5},{7,6},{8,11},{9,8},{10,9... | collective-permute-start | bytes 460808 | tf_op jit(solution)/shard_map/ppermute | solution.py:282
  27.4 5.0 %rows.1 = (bf16[64,400,48]{2,1,0:T(8,128)(2,1)S(1)}, bf16[16,400,256]{2,1,0:T(8,128)(2,1)S(1)}) custom-call(f32[8,8,1800]{2,1,0:T(8,128)S(1)} %all-to-all-done.both_ref), custom_call_target="tpu_custom_call" | custom-call | tf_op jit(solution)/shard_map/rows/pallas_call | solution.py:284
  32.4 0.0 collective-permute-done.2.rest_2_
  32.4 0.7 collective-permute-done.1.rest_1_
  33.1 0.1 collective-permute-done.rest_0_
  33.2 0.0 copy-start.1
  33.2 0.9 copy-done.1
  34.1 50.3 %pairs.1 = f32[8,3,8,400]{3,2,1,0:T(8,128)S(1)} custom-call(f32[400,768]{1,0:T(8,128)S(1)} %get-tuple-element.20.mask_ref, f32[400,768]{1,0:T(8,128)S(1)} %get-tuple-element.21.goal_ref, f32[400,128]{1,0:T(8,128)S(1)} %get-tuple-element.22.mask_end_ref, f32[400,128]{1,0:T(8,128)S(1)} %copy-done.1, bf16[64,400,48]{2,1,0:T(8,128)(2,1)S(1)} %get-tuple-element.25.lhs_ref, ...), custom_call_target="tpu_custom_call" | custom-call | tf_op jit(solution)/shard_map/pairs/pallas_call | solution.py:296
  84.5 15.6 %all_to_all.10.back_ref = f32[8,3,8,400]{3,2,1,0:T(8,128)} all-to-all(f32[8,3,8,400]{3,2,1,0:T(8,128)S(1)} %pairs.1), channel_id=1, replica_groups=mesh['ens'=8,'tile'=4] {'ens'}, dimensions={0} | all-to-all | bytes 614400 | tf_op jit(solution)/shard_map/all_to_all | solution.py:313
  100.1 1.7 %total.1 = f32[3,8,800]{2,1,0:T(8,128)} custom-call(f32[8,3,8,400]{3,2,1,0:T(8,128)} %all_to_all.10.back_ref), custom_call_target="tpu_custom_call" | custom-call | tf_op jit(solution)/shard_map/total/pallas_call | solution.py:314
  (5 shorter events, 0.0 us)
Async XLA Ops:
  1.9 21.0 %all-to-all-start = ((f32[8,8,1800]{2,1,0:T(8,128)}), f32[8,8,1800]{2,1,0:T(8,128)S(1)}, u32[]{:S(2)}, u32[]{:S(2)}) async-start(f32[8,8,1800]{2,1,0:T(8,128)} %pack.1), calls=%async_computation | async-start | bytes 983040 | tf_op jit(solution)/shard_map/all_to_all | solution.py:256
  13.9 0.7 copy-start
  22.9 9.5 %collective-permute-start.2 = (f32[8,8,600]{2,1,0:T(8,128)S(1)}, f32[8,8,600]{2,1,0:T(8,128)S(1)}, u32[]{:S(2)}, u32[]{:S(2)}) collective-permute-start(f32[8,8,600]{2,1,0:T(8,128)S(1)} %slice.3), channel_id=1, source_target_pairs={{0,1},{1,2},{2,3},{3,0},{4,5},{5,6},{6,7},{7,4},{8,9},{9,10},{10,1... | collective-permute-start | bytes 460808 | tf_op jit(solution)/shard_map/ppermute | solution.py:282
  24.4 8.7 %collective-permute-start.1 = (f32[8,8,600]{2,1,0:T(8,128)S(1)}, f32[8,8,600]{2,1,0:T(8,128)S(1)}, u32[]{:S(2)}, u32[]{:S(2)}) collective-permute-start(f32[8,8,600]{2,1,0:T(8,128)S(1)} %slice.3), channel_id=1, source_target_pairs={{0,2},{1,3},{2,0},{3,1},{4,6},{5,7},{6,4},{7,5},{8,10},{9,11},{10,... | collective-permute-start | bytes 460808 | tf_op jit(solution)/shard_map/ppermute | solution.py:282
  26.0 7.2 %collective-permute-start = (f32[8,8,600]{2,1,0:T(8,128)S(1)}, f32[8,8,600]{2,1,0:T(8,128)S(1)}, u32[]{:S(2)}, u32[]{:S(2)}) collective-permute-start(f32[8,8,600]{2,1,0:T(8,128)S(1)} %slice.3), channel_id=1, source_target_pairs={{0,3},{1,0},{2,1},{3,2},{4,7},{5,4},{6,5},{7,6},{8,11},{9,8},{10,9... | collective-permute-start | bytes 460808 | tf_op jit(solution)/shard_map/ppermute | solution.py:282
  33.2 0.9 copy-start.1

commit v16 on v15

--- a/solution.py
+++ b/solution.py
@@ -194,20 +194,17 @@
         return [hi, (g - hi.astype(jnp.float32)).astype(jnp.bfloat16)]
 
     def sums(terms, parts):
-        return lax.dot_general(jnp.concatenate(parts, axis=1), jnp.concatenate(terms, axis=1), NT,
-                               preferred_element_type=jnp.float32)
+        hi, lo = [jnp.concatenate(v, axis=1) for v in zip(*parts)]
+        return (lax.dot_general(hi, terms, NT, preferred_element_type=jnp.float32).T
+                + lax.dot_general(terms, lo, NT, preferred_element_type=jnp.float32))
 
     def grad_some(b, carry):
         if end:
-            last = sums([terms_end_ref[b]] * 2, split2(weight_end_ref[...], tanh_end(b))).T
+            last = sums(terms_end_ref[b], [split2(weight_end_ref[...], tanh_end(b))])
         for inside in range(fold):
             s = b * fold + inside
-            terms, parts = [], []
-            for start, size in chunks:
-                terms += [rhs_ref[s, pl.ds(0, 16), pl.ds(start, size)]] * 2
-                parts += split2(weight_ref[:, pl.ds(start, size)], tanh_block(s, start, size))
-            total = sums(terms, parts)
-            total = total.T
+            parts = [split2(weight_ref[:, pl.ds(start, size)], tanh_block(s, start, size)) for start, size in chunks]
+            total = sums(rhs_ref[s, pl.ds(0, 16), :], parts)
             if end:
                 total += last[16 * inside:16 * inside + 16]
             total = total[:, :n_rows]

time: 102 us -> 101 us (level)
  Pallas kernels: 59.8 us -> 58.1 us
    pallas_call x1, Pallas kernels: 50.3 us -> 48.6 us  [on_device(): pl.pallas_call(functools.partial(pair_kernel, n_tile, fold, n_rows, n_col...]
where the time goes in v16:
time: 101 us; the launch traced here: 100 us
  Pallas kernels  58.1 us (58%)
  blocking collectives  15.6 us (15%)
  starting transfers between devices  10.8 us (11%)
  waiting for transfers between devices  9.14 us (9%)
  local copies, waits for them, and re-layouts  5.61 us (6%)
    pallas_call x1, Pallas kernels, on_device(): pl.pallas_call(functools.partial(pair_kernel, n_tile, fold, n_rows, n_col...  48.6 us
    all_to_all x1, blocking collectives, on_device(): back = lax.all_to_all(grad, 'ens', 0, 0, tiled=True)  15.6 us
    all_to_all x1, waiting for transfers between devices, on_device(): both = lax.all_to_all(send, 'ens', 0, 0, tiled=True)  8.34 us
    all_to_all x1, starting transfers between devices, on_device(): both = lax.all_to_all(send, 'ens', 0, 0, tiled=True)  6.33 us
    pallas_call x1, Pallas kernels, on_device(): pl.pallas_call(functools.partial(row_kernel, n_rows, fold), out_shape=[ja...  4.98 us
    ppermute x3, starting transfers between devices, on_device(): lax.ppermute(own, 'tile', [(t, (t - k) % n_tile) for t in range(n_tile)])  4.5 us
    dynamic_slice x1, local copies, waits for them, and re-layouts, on_device(): lax.dynamic_slice_in_dim(own_counts, b, piece, 1)  2.19 us
  transfers between devices with their start and end apart: 4, of which 3 were waited for; matrix products, arithmetic and copies ran while one was open for 5% of the time, Pallas kernels for 6%

profile of v16, /device:TPU:0, one launch (start us, length us, event | category | flops | bytes accessed | tf_op | source)
XLA Modules:
  0.0 100.1 jit_solution(3828871740402820235)
XLA Ops:
  0.0 1.9 %pack.1 = f32[8,8,1800]{2,1,0:T(8,128)} custom-call(f32[3,8,800]{2,1,0:T(8,128)} %bitcast.4), custom_call_target="tpu_custom_call" | custom-call | tf_op jit(solution)/shard_map/pack/pallas_call | solution.py:246
  1.9 6.3 %all-to-all-start = ((f32[8,8,1800]{2,1,0:T(8,128)}), f32[8,8,1800]{2,1,0:T(8,128)S(1)}, u32[]{:S(2)}, u32[]{:S(2)}) async-start(f32[8,8,1800]{2,1,0:T(8,128)} %pack.1), calls=%async_computation | async-start | bytes 983040 | tf_op jit(solution)/shard_map/all_to_all | solution.py:253
  8.3 0.1 pad_add_fusion.2
  8.4 0.8 dynamic_slice.28
  9.2 0.9 fusion.1
  10.0 0.1 pad_add_fusion.1
  10.1 0.1 copy.4.seg_rows_ref
  10.3 2.2 %fusion = (s32[400,200]{1,0:T(8,128)S(1)}, s32[400,200]{1,0:T(8,128)S(1)}, s32[400,200]{1,0:T(8,128)S(1)}, s32[400,200]{1,0:T(8,128)S(1)}) fusion(s32[800,3200]{1,0:T(8,128)} %param.4, s32[]{:T(128)S(6)} %select_n.38, s32[]{:T(128)S(6)} %select_n.39, s32[]{:T(128)S(6)} %select_n.40, s32[]{:T(128)S(6)} %select_n.42, s32[]{:T(128)S(6)} %select_n.41), kind=kLoop, calls=%fused_computation.7 | loop fusion | bytes 2560020 | tf_op jit(solution)/shard_map/dynamic_slice | solution.py:258
  12.5 0.5 pad_add_fusion.counts_ref
  13.0 0.8 masks.1
  13.9 0.0 copy-start
  13.9 0.7 copy-done
  14.5 8.3 %all-to-all-done.both_ref = f32[8,8,1800]{2,1,0:T(8,128)S(1)} async-done(((f32[8,8,1800]{2,1,0:T(8,128)}), f32[8,8,1800]{2,1,0:T(8,128)S(1)}, u32[]{:S(2)}, u32[]{:S(2)}) %all-to-all-start) | async-done | bytes 460832 | tf_op jit(solution)/shard_map/all_to_all | solution.py:253
  22.9 1.5 %collective-permute-start.2 = (f32[8,8,600]{2,1,0:T(8,128)S(1)}, f32[8,8,600]{2,1,0:T(8,128)S(1)}, u32[]{:S(2)}, u32[]{:S(2)}) collective-permute-start(f32[8,8,600]{2,1,0:T(8,128)S(1)} %slice.3), channel_id=1, source_target_pairs={{0,1},{1,2},{2,3},{3,0},{4,5},{5,6},{6,7},{7,4},{8,9},{9,10},{10,1... | collective-permute-start | bytes 460808 | tf_op jit(solution)/shard_map/ppermute | solution.py:279
  24.4 1.5 %collective-permute-start.1 = (f32[8,8,600]{2,1,0:T(8,128)S(1)}, f32[8,8,600]{2,1,0:T(8,128)S(1)}, u32[]{:S(2)}, u32[]{:S(2)}) collective-permute-start(f32[8,8,600]{2,1,0:T(8,128)S(1)} %slice.3), channel_id=1, source_target_pairs={{0,2},{1,3},{2,0},{3,1},{4,6},{5,7},{6,4},{7,5},{8,10},{9,11},{10,... | collective-permute-start | bytes 460808 | tf_op jit(solution)/shard_map/ppermute | solution.py:279
  26.0 1.4 %collective-permute-start = (f32[8,8,600]{2,1,0:T(8,128)S(1)}, f32[8,8,600]{2,1,0:T(8,128)S(1)}, u32[]{:S(2)}, u32[]{:S(2)}) collective-permute-start(f32[8,8,600]{2,1,0:T(8,128)S(1)} %slice.3), channel_id=1, source_target_pairs={{0,3},{1,0},{2,1},{3,2},{4,7},{5,4},{6,5},{7,6},{8,11},{9,8},{10,9... | collective-permute-start | bytes 460808 | tf_op jit(solution)/shard_map/ppermute | solution.py:279
  27.4 5.0 %rows.1 = (bf16[64,400,48]{2,1,0:T(8,128)(2,1)S(1)}, bf16[16,400,256]{2,1,0:T(8,128)(2,1)S(1)}) custom-call(f32[8,8,1800]{2,1,0:T(8,128)S(1)} %all-to-all-done.both_ref), custom_call_target="tpu_custom_call" | custom-call | tf_op jit(solution)/shard_map/rows/pallas_call | solution.py:281
  32.4 0.0 collective-permute-done.2.rest_2_
  32.4 0.7 collective-permute-done.1.rest_1_
  33.1 0.1 collective-permute-done.rest_0_
  33.2 0.0 copy-start.1
  33.2 0.9 copy-done.1
  34.1 48.6 %pairs.1 = f32[8,3,8,400]{3,2,1,0:T(8,128)S(1)} custom-call(f32[400,768]{1,0:T(8,128)S(1)} %get-tuple-element.20.mask_ref, f32[400,768]{1,0:T(8,128)S(1)} %get-tuple-element.21.goal_ref, f32[400,128]{1,0:T(8,128)S(1)} %get-tuple-element.22.mask_end_ref, f32[400,128]{1,0:T(8,128)S(1)} %copy-done.1, bf16[64,400,48]{2,1,0:T(8,128)(2,1)S(1)} %get-tuple-element.25.lhs_ref, ...), custom_call_target="tpu_custom_call" | custom-call | tf_op jit(solution)/shard_map/pairs/pallas_call | solution.py:293
  82.8 15.6 %all_to_all.10.back_ref = f32[8,3,8,400]{3,2,1,0:T(8,128)} all-to-all(f32[8,3,8,400]{3,2,1,0:T(8,128)S(1)} %pairs.1), channel_id=1, replica_groups=mesh['ens'=8,'tile'=4] {'ens'}, dimensions={0} | all-to-all | bytes 614400 | tf_op jit(solution)/shard_map/all_to_all | solution.py:310
  98.4 1.7 %total.1 = f32[3,8,800]{2,1,0:T(8,128)} custom-call(f32[8,3,8,400]{3,2,1,0:T(8,128)} %all_to_all.10.back_ref), custom_call_target="tpu_custom_call" | custom-call | tf_op jit(solution)/shard_map/total/pallas_call | solution.py:311
  (5 shorter events, 0.0 us)
Async XLA Ops:
  1.9 21.0 %all-to-all-start = ((f32[8,8,1800]{2,1,0:T(8,128)}), f32[8,8,1800]{2,1,0:T(8,128)S(1)}, u32[]{:S(2)}, u32[]{:S(2)}) async-start(f32[8,8,1800]{2,1,0:T(8,128)} %pack.1), calls=%async_computation | async-start | bytes 983040 | tf_op jit(solution)/shard_map/all_to_all | solution.py:253
  13.9 0.7 copy-start
  22.9 9.5 %collective-permute-start.2 = (f32[8,8,600]{2,1,0:T(8,128)S(1)}, f32[8,8,600]{2,1,0:T(8,128)S(1)}, u32[]{:S(2)}, u32[]{:S(2)}) collective-permute-start(f32[8,8,600]{2,1,0:T(8,128)S(1)} %slice.3), channel_id=1, source_target_pairs={{0,1},{1,2},{2,3},{3,0},{4,5},{5,6},{6,7},{7,4},{8,9},{9,10},{10,1... | collective-permute-start | bytes 460808 | tf_op jit(solution)/shard_map/ppermute | solution.py:279
  24.4 8.7 %collective-permute-start.1 = (f32[8,8,600]{2,1,0:T(8,128)S(1)}, f32[8,8,600]{2,1,0:T(8,128)S(1)}, u32[]{:S(2)}, u32[]{:S(2)}) collective-permute-start(f32[8,8,600]{2,1,0:T(8,128)S(1)} %slice.3), channel_id=1, source_target_pairs={{0,2},{1,3},{2,0},{3,1},{4,6},{5,7},{6,4},{7,5},{8,10},{9,11},{10,... | collective-permute-start | bytes 460808 | tf_op jit(solution)/shard_map/ppermute | solution.py:279
  26.0 7.2 %collective-permute-start = (f32[8,8,600]{2,1,0:T(8,128)S(1)}, f32[8,8,600]{2,1,0:T(8,128)S(1)}, u32[]{:S(2)}, u32[]{:S(2)}) collective-permute-start(f32[8,8,600]{2,1,0:T(8,128)S(1)} %slice.3), channel_id=1, source_target_pairs={{0,3},{1,0},{2,1},{3,2},{4,7},{5,4},{6,5},{7,6},{8,11},{9,8},{10,9... | collective-permute-start | bytes 460808 | tf_op jit(solution)/shard_map/ppermute | solution.py:279
  33.2 0.9 copy-start.1

commit v17 on v16

--- a/solution.py
+++ b/solution.py
@@ -135,7 +135,7 @@
     if end:
         rhs_end_ref[...] = jnp.zeros_like(rhs_end_ref)
 
-    def features(g, carry):
+    def features(g):
         both = both_ref[g]
         parts = [both] + [ref[g] for ref in piece_refs]
         cols = [jnp.concatenate([v[:, c * piece:(c + 1) * piece] for v in parts], axis=1) for c in range(3)]
@@ -156,9 +156,7 @@
                     b = g * (per // fold) + block
                     rhs_end_ref[b, pl.ds(SLOT * inside, 48), :] = last
                     terms_end_ref[b, pl.ds(16 * inside, 16), :] = last[0:16]
-        return carry
-
-    lax.fori_loop(0, groups, features, 0)
+
     weight_ref[...] = jnp.zeros_like(weight_ref)
     if end:
         weight_end_ref[...] = jnp.zeros_like(weight_end_ref)
@@ -169,15 +167,23 @@
     def tanh_end(b):
         return jnp.tanh(jnp.dot(lhs_end_ref[b], rhs_end_ref[b], preferred_element_type=jnp.float32))
 
-    def add_some(b, carry):
+    def add_some(b):
         for inside in range(fold):
             for start, size in chunks:
                 weight_ref[:, pl.ds(start, size)] += tanh_block(b * fold + inside, start, size)
         if end:
             weight_end_ref[...] += tanh_end(b)
+
+    together = 2 if groups % 2 == 0 else 1
+
+    def add_groups(step, carry):
+        for j in range(together):
+            features(step * together + j)
+        for j in range(together * (per // fold)):
+            add_some(step * (together * (per // fold)) + j)
         return carry
 
-    lax.fori_loop(0, structs // fold, add_some, 0, unroll=UNROLL)
+    lax.fori_loop(0, groups // together, add_groups, 0)
 
     scale = 0.5 / structs
     for start, size in chunks:

time: 101 us -> 100 us (0.990)
  no operation moved by 1% of the time
where the time goes in v17:
time: 100 us; the launch traced here: 99.5 us
  Pallas kernels  57.5 us (58%)
  blocking collectives  15.6 us (16%)
  starting transfers between devices  10.8 us (11%)
  waiting for transfers between devices  9.14 us (9%)
  local copies, waits for them, and re-layouts  5.61 us (6%)
    pallas_call x1, Pallas kernels, on_device(): pl.pallas_call(functools.partial(pair_kernel, n_tile, fold, n_rows, n_col...  48.1 us
    all_to_all x1, blocking collectives, on_device(): back = lax.all_to_all(grad, 'ens', 0, 0, tiled=True)  15.6 us
    all_to_all x1, waiting for transfers between devices, on_device(): both = lax.all_to_all(send, 'ens', 0, 0, tiled=True)  8.34 us
    all_to_all x1, starting transfers between devices, on_device(): both = lax.all_to_all(send, 'ens', 0, 0, tiled=True)  6.33 us
    pallas_call x1, Pallas kernels, on_device(): pl.pallas_call(functools.partial(row_kernel, n_rows, fold), out_shape=[ja...  4.98 us
    ppermute x3, starting transfers between devices, on_device(): lax.ppermute(own, 'tile', [(t, (t - k) % n_tile) for t in range(n_tile)])  4.5 us
    dynamic_slice x1, local copies, waits for them, and re-layouts, on_device(): lax.dynamic_slice_in_dim(own_counts, b, piece, 1)  2.19 us
  transfers between devices with their start and end apart: 4, of which 3 were waited for; matrix products, arithmetic and copies ran while one was open for 5% of the time, Pallas kernels for 6%

profile of v17, /device:TPU:0, one launch (start us, length us, event | category | flops | bytes accessed | tf_op | source)
XLA Modules:
  0.0 99.5 jit_solution(10308630277757874869)
XLA Ops:
  0.0 1.9 %pack.1 = f32[8,8,1800]{2,1,0:T(8,128)} custom-call(f32[3,8,800]{2,1,0:T(8,128)} %bitcast.4), custom_call_target="tpu_custom_call" | custom-call | tf_op jit(solution)/shard_map/pack/pallas_call | solution.py:252
  1.9 6.3 %all-to-all-start = ((f32[8,8,1800]{2,1,0:T(8,128)}), f32[8,8,1800]{2,1,0:T(8,128)S(1)}, u32[]{:S(2)}, u32[]{:S(2)}) async-start(f32[8,8,1800]{2,1,0:T(8,128)} %pack.1), calls=%async_computation | async-start | bytes 983040 | tf_op jit(solution)/shard_map/all_to_all | solution.py:259
  8.3 0.1 pad_add_fusion.2
  8.4 0.8 dynamic_slice.28
  9.2 0.9 fusion.1
  10.0 0.1 pad_add_fusion.1
  10.1 0.1 copy.4.seg_rows_ref
  10.3 2.2 %fusion = (s32[400,200]{1,0:T(8,128)S(1)}, s32[400,200]{1,0:T(8,128)S(1)}, s32[400,200]{1,0:T(8,128)S(1)}, s32[400,200]{1,0:T(8,128)S(1)}) fusion(s32[800,3200]{1,0:T(8,128)} %param.4, s32[]{:T(128)S(6)} %select_n.38, s32[]{:T(128)S(6)} %select_n.39, s32[]{:T(128)S(6)} %select_n.40, s32[]{:T(128)S(6)} %select_n.42, s32[]{:T(128)S(6)} %select_n.41), kind=kLoop, calls=%fused_computation.7 | loop fusion | bytes 2560020 | tf_op jit(solution)/shard_map/dynamic_slice | solution.py:264
  12.5 0.5 pad_add_fusion.counts_ref
  13.0 0.8 masks.1
  13.9 0.0 copy-start
  13.9 0.7 copy-done
  14.5 8.3 %all-to-all-done.both_ref = f32[8,8,1800]{2,1,0:T(8,128)S(1)} async-done(((f32[8,8,1800]{2,1,0:T(8,128)}), f32[8,8,1800]{2,1,0:T(8,128)S(1)}, u32[]{:S(2)}, u32[]{:S(2)}) %all-to-all-start) | async-done | bytes 460832 | tf_op jit(solution)/shard_map/all_to_all | solution.py:259
  22.9 1.5 %collective-permute-start.2 = (f32[8,8,600]{2,1,0:T(8,128)S(1)}, f32[8,8,600]{2,1,0:T(8,128)S(1)}, u32[]{:S(2)}, u32[]{:S(2)}) collective-permute-start(f32[8,8,600]{2,1,0:T(8,128)S(1)} %slice.3), channel_id=1, source_target_pairs={{0,1},{1,2},{2,3},{3,0},{4,5},{5,6},{6,7},{7,4},{8,9},{9,10},{10,1... | collective-permute-start | bytes 460808 | tf_op jit(solution)/shard_map/ppermute | solution.py:285
  24.4 1.5 %collective-permute-start.1 = (f32[8,8,600]{2,1,0:T(8,128)S(1)}, f32[8,8,600]{2,1,0:T(8,128)S(1)}, u32[]{:S(2)}, u32[]{:S(2)}) collective-permute-start(f32[8,8,600]{2,1,0:T(8,128)S(1)} %slice.3), channel_id=1, source_target_pairs={{0,2},{1,3},{2,0},{3,1},{4,6},{5,7},{6,4},{7,5},{8,10},{9,11},{10,... | collective-permute-start | bytes 460808 | tf_op jit(solution)/shard_map/ppermute | solution.py:285
  26.0 1.4 %collective-permute-start = (f32[8,8,600]{2,1,0:T(8,128)S(1)}, f32[8,8,600]{2,1,0:T(8,128)S(1)}, u32[]{:S(2)}, u32[]{:S(2)}) collective-permute-start(f32[8,8,600]{2,1,0:T(8,128)S(1)} %slice.3), channel_id=1, source_target_pairs={{0,3},{1,0},{2,1},{3,2},{4,7},{5,4},{6,5},{7,6},{8,11},{9,8},{10,9... | collective-permute-start | bytes 460808 | tf_op jit(solution)/shard_map/ppermute | solution.py:285
  27.4 5.0 %rows.1 = (bf16[64,400,48]{2,1,0:T(8,128)(2,1)S(1)}, bf16[16,400,256]{2,1,0:T(8,128)(2,1)S(1)}) custom-call(f32[8,8,1800]{2,1,0:T(8,128)S(1)} %all-to-all-done.both_ref), custom_call_target="tpu_custom_call" | custom-call | tf_op jit(solution)/shard_map/rows/pallas_call | solution.py:287
  32.4 0.0 collective-permute-done.2.rest_2_
  32.4 0.7 collective-permute-done.1.rest_1_
  33.1 0.1 collective-permute-done.rest_0_
  33.2 0.0 copy-start.1
  33.2 0.9 copy-done.1
  34.1 48.1 %pairs.1 = f32[8,3,8,400]{3,2,1,0:T(8,128)S(1)} custom-call(f32[400,768]{1,0:T(8,128)S(1)} %get-tuple-element.20.mask_ref, f32[400,768]{1,0:T(8,128)S(1)} %get-tuple-element.21.goal_ref, f32[400,128]{1,0:T(8,128)S(1)} %get-tuple-element.22.mask_end_ref, f32[400,128]{1,0:T(8,128)S(1)} %copy-done.1, bf16[64,400,48]{2,1,0:T(8,128)(2,1)S(1)} %get-tuple-element.25.lhs_ref, ...), custom_call_target="tpu_custom_call" | custom-call | tf_op jit(solution)/shard_map/pairs/pallas_call | solution.py:299
  82.2 15.6 %all_to_all.10.back_ref = f32[8,3,8,400]{3,2,1,0:T(8,128)} all-to-all(f32[8,3,8,400]{3,2,1,0:T(8,128)S(1)} %pairs.1), channel_id=1, replica_groups=mesh['ens'=8,'tile'=4] {'ens'}, dimensions={0} | all-to-all | bytes 614400 | tf_op jit(solution)/shard_map/all_to_all | solution.py:316
  97.8 1.7 %total.1 = f32[3,8,800]{2,1,0:T(8,128)} custom-call(f32[8,3,8,400]{3,2,1,0:T(8,128)} %all_to_all.10.back_ref), custom_call_target="tpu_custom_call" | custom-call | tf_op jit(solution)/shard_map/total/pallas_call | solution.py:317
  (5 shorter events, 0.0 us)
Async XLA Ops:
  1.9 21.0 %all-to-all-start = ((f32[8,8,1800]{2,1,0:T(8,128)}), f32[8,8,1800]{2,1,0:T(8,128)S(1)}, u32[]{:S(2)}, u32[]{:S(2)}) async-start(f32[8,8,1800]{2,1,0:T(8,128)} %pack.1), calls=%async_computation | async-start | bytes 983040 | tf_op jit(solution)/shard_map/all_to_all | solution.py:259
  13.9 0.7 copy-start
  22.9 9.5 %collective-permute-start.2 = (f32[8,8,600]{2,1,0:T(8,128)S(1)}, f32[8,8,600]{2,1,0:T(8,128)S(1)}, u32[]{:S(2)}, u32[]{:S(2)}) collective-permute-start(f32[8,8,600]{2,1,0:T(8,128)S(1)} %slice.3), channel_id=1, source_target_pairs={{0,1},{1,2},{2,3},{3,0},{4,5},{5,6},{6,7},{7,4},{8,9},{9,10},{10,1... | collective-permute-start | bytes 460808 | tf_op jit(solution)/shard_map/ppermute | solution.py:285
  24.4 8.7 %collective-permute-start.1 = (f32[8,8,600]{2,1,0:T(8,128)S(1)}, f32[8,8,600]{2,1,0:T(8,128)S(1)}, u32[]{:S(2)}, u32[]{:S(2)}) collective-permute-start(f32[8,8,600]{2,1,0:T(8,128)S(1)} %slice.3), channel_id=1, source_target_pairs={{0,2},{1,3},{2,0},{3,1},{4,6},{5,7},{6,4},{7,5},{8,10},{9,11},{10,... | collective-permute-start | bytes 460808 | tf_op jit(solution)/shard_map/ppermute | solution.py:285
  26.0 7.2 %collective-permute-start = (f32[8,8,600]{2,1,0:T(8,128)S(1)}, f32[8,8,600]{2,1,0:T(8,128)S(1)}, u32[]{:S(2)}, u32[]{:S(2)}) collective-permute-start(f32[8,8,600]{2,1,0:T(8,128)S(1)} %slice.3), channel_id=1, source_target_pairs={{0,3},{1,0},{2,1},{3,2},{4,7},{5,4},{6,5},{7,6},{8,11},{9,8},{10,9... | collective-permute-start | bytes 460808 | tf_op jit(solution)/shard_map/ppermute | solution.py:285
  33.2 0.9 copy-start.1

commit v18 on v17

--- a/solution.py
+++ b/solution.py
@@ -8,7 +8,7 @@
 from jax.sharding import PartitionSpec as P
 
 LANES = 128
-WIDE = 256
+WIDE = 1024
 SLOT = 64
 UNROLL = 4
 NT = (((1,), (1,)), ((), ()))

time: 100 us -> 100 us (level)
  no operation moved by 1% of the time
where the time goes in v18:
time: 100 us; the launch traced here: 99.6 us
  Pallas kernels  57.6 us (58%)
  blocking collectives  15.6 us (16%)
  starting transfers between devices  10.8 us (11%)
  waiting for transfers between devices  9.14 us (9%)
  local copies, waits for them, and re-layouts  5.61 us (6%)
    pallas_call x1, Pallas kernels, on_device(): pl.pallas_call(functools.partial(pair_kernel, n_tile, fold, n_rows, n_col...  48.2 us
    all_to_all x1, blocking collectives, on_device(): back = lax.all_to_all(grad, 'ens', 0, 0, tiled=True)  15.6 us
    all_to_all x1, waiting for transfers between devices, on_device(): both = lax.all_to_all(send, 'ens', 0, 0, tiled=True)  8.34 us
    all_to_all x1, starting transfers between devices, on_device(): both = lax.all_to_all(send, 'ens', 0, 0, tiled=True)  6.33 us
    pallas_call x1, Pallas kernels, on_device(): pl.pallas_call(functools.partial(row_kernel, n_rows, fold), out_shape=[ja...  4.98 us
    ppermute x3, starting transfers between devices, on_device(): lax.ppermute(own, 'tile', [(t, (t - k) % n_tile) for t in range(n_tile)])  4.5 us
    dynamic_slice x1, local copies, waits for them, and re-layouts, on_device(): lax.dynamic_slice_in_dim(own_counts, b, piece, 1)  2.19 us
  transfers between devices with their start and end apart: 4, of which 3 were waited for; matrix products, arithmetic and copies ran while one was open for 5% of the time, Pallas kernels for 6%

profile of v18, /device:TPU:0, one launch (start us, length us, event | category | flops | bytes accessed | tf_op | source)
XLA Modules:
  0.0 99.6 jit_solution(15414507927318384350)
XLA Ops:
  0.0 1.9 %pack.1 = f32[8,8,1800]{2,1,0:T(8,128)} custom-call(f32[3,8,800]{2,1,0:T(8,128)} %bitcast.4), custom_call_target="tpu_custom_call" | custom-call | tf_op jit(solution)/shard_map/pack/pallas_call | solution.py:252
  1.9 6.3 %all-to-all-start = ((f32[8,8,1800]{2,1,0:T(8,128)}), f32[8,8,1800]{2,1,0:T(8,128)S(1)}, u32[]{:S(2)}, u32[]{:S(2)}) async-start(f32[8,8,1800]{2,1,0:T(8,128)} %pack.1), calls=%async_computation | async-start | bytes 983040 | tf_op jit(solution)/shard_map/all_to_all | solution.py:259
  8.3 0.1 pad_add_fusion.2
  8.4 0.8 dynamic_slice.28
  9.2 0.9 fusion.1
  10.0 0.1 pad_add_fusion.1
  10.1 0.1 copy.4.seg_rows_ref
  10.3 2.2 %fusion = (s32[400,200]{1,0:T(8,128)S(1)}, s32[400,200]{1,0:T(8,128)S(1)}, s32[400,200]{1,0:T(8,128)S(1)}, s32[400,200]{1,0:T(8,128)S(1)}) fusion(s32[800,3200]{1,0:T(8,128)} %param.4, s32[]{:T(128)S(6)} %select_n.38, s32[]{:T(128)S(6)} %select_n.39, s32[]{:T(128)S(6)} %select_n.40, s32[]{:T(128)S(6)} %select_n.42, s32[]{:T(128)S(6)} %select_n.41), kind=kLoop, calls=%fused_computation.7 | loop fusion | bytes 2560020 | tf_op jit(solution)/shard_map/dynamic_slice | solution.py:264
  12.5 0.5 pad_add_fusion.counts_ref
  13.0 0.8 masks.1
  13.9 0.0 copy-start
  13.9 0.7 copy-done
  14.5 8.3 %all-to-all-done.both_ref = f32[8,8,1800]{2,1,0:T(8,128)S(1)} async-done(((f32[8,8,1800]{2,1,0:T(8,128)}), f32[8,8,1800]{2,1,0:T(8,128)S(1)}, u32[]{:S(2)}, u32[]{:S(2)}) %all-to-all-start) | async-done | bytes 460832 | tf_op jit(solution)/shard_map/all_to_all | solution.py:259
  22.9 1.5 %collective-permute-start.2 = (f32[8,8,600]{2,1,0:T(8,128)S(1)}, f32[8,8,600]{2,1,0:T(8,128)S(1)}, u32[]{:S(2)}, u32[]{:S(2)}) collective-permute-start(f32[8,8,600]{2,1,0:T(8,128)S(1)} %slice.3), channel_id=1, source_target_pairs={{0,1},{1,2},{2,3},{3,0},{4,5},{5,6},{6,7},{7,4},{8,9},{9,10},{10,1... | collective-permute-start | bytes 460808 | tf_op jit(solution)/shard_map/ppermute | solution.py:285
  24.4 1.5 %collective-permute-start.1 = (f32[8,8,600]{2,1,0:T(8,128)S(1)}, f32[8,8,600]{2,1,0:T(8,128)S(1)}, u32[]{:S(2)}, u32[]{:S(2)}) collective-permute-start(f32[8,8,600]{2,1,0:T(8,128)S(1)} %slice.3), channel_id=1, source_target_pairs={{0,2},{1,3},{2,0},{3,1},{4,6},{5,7},{6,4},{7,5},{8,10},{9,11},{10,... | collective-permute-start | bytes 460808 | tf_op jit(solution)/shard_map/ppermute | solution.py:285
  26.0 1.4 %collective-permute-start = (f32[8,8,600]{2,1,0:T(8,128)S(1)}, f32[8,8,600]{2,1,0:T(8,128)S(1)}, u32[]{:S(2)}, u32[]{:S(2)}) collective-permute-start(f32[8,8,600]{2,1,0:T(8,128)S(1)} %slice.3), channel_id=1, source_target_pairs={{0,3},{1,0},{2,1},{3,2},{4,7},{5,4},{6,5},{7,6},{8,11},{9,8},{10,9... | collective-permute-start | bytes 460808 | tf_op jit(solution)/shard_map/ppermute | solution.py:285
  27.4 5.0 %rows.1 = (bf16[64,400,48]{2,1,0:T(8,128)(2,1)S(1)}, bf16[16,400,256]{2,1,0:T(8,128)(2,1)S(1)}) custom-call(f32[8,8,1800]{2,1,0:T(8,128)S(1)} %all-to-all-done.both_ref), custom_call_target="tpu_custom_call" | custom-call | tf_op jit(solution)/shard_map/rows/pallas_call | solution.py:287
  32.4 0.0 collective-permute-done.2.rest_2_
  32.4 0.7 collective-permute-done.1.rest_1_
  33.1 0.1 collective-permute-done.rest_0_
  33.2 0.0 copy-start.1
  33.2 0.9 copy-done.1
  34.1 48.2 %pairs.1 = f32[8,3,8,400]{3,2,1,0:T(8,128)S(1)} custom-call(f32[400,768]{1,0:T(8,128)S(1)} %get-tuple-element.20.mask_ref, f32[400,768]{1,0:T(8,128)S(1)} %get-tuple-element.21.goal_ref, f32[400,128]{1,0:T(8,128)S(1)} %get-tuple-element.22.mask_end_ref, f32[400,128]{1,0:T(8,128)S(1)} %copy-done.1, bf16[64,400,48]{2,1,0:T(8,128)(2,1)S(1)} %get-tuple-element.25.lhs_ref, ...), custom_call_target="tpu_custom_call" | custom-call | tf_op jit(solution)/shard_map/pairs/pallas_call | solution.py:299
  82.3 15.6 %all_to_all.10.back_ref = f32[8,3,8,400]{3,2,1,0:T(8,128)} all-to-all(f32[8,3,8,400]{3,2,1,0:T(8,128)S(1)} %pairs.1), channel_id=1, replica_groups=mesh['ens'=8,'tile'=4] {'ens'}, dimensions={0} | all-to-all | bytes 614400 | tf_op jit(solution)/shard_map/all_to_all | solution.py:316
  97.9 1.7 %total.1 = f32[3,8,800]{2,1,0:T(8,128)} custom-call(f32[8,3,8,400]{3,2,1,0:T(8,128)} %all_to_all.10.back_ref), custom_call_target="tpu_custom_call" | custom-call | tf_op jit(solution)/shard_map/total/pallas_call | solution.py:317
  (5 shorter events, 0.0 us)
Async XLA Ops:
  1.9 21.0 %all-to-all-start = ((f32[8,8,1800]{2,1,0:T(8,128)}), f32[8,8,1800]{2,1,0:T(8,128)S(1)}, u32[]{:S(2)}, u32[]{:S(2)}) async-start(f32[8,8,1800]{2,1,0:T(8,128)} %pack.1), calls=%async_computation | async-start | bytes 983040 | tf_op jit(solution)/shard_map/all_to_all | solution.py:259
  13.9 0.7 copy-start
  22.9 9.5 %collective-permute-start.2 = (f32[8,8,600]{2,1,0:T(8,128)S(1)}, f32[8,8,600]{2,1,0:T(8,128)S(1)}, u32[]{:S(2)}, u32[]{:S(2)}) collective-permute-start(f32[8,8,600]{2,1,0:T(8,128)S(1)} %slice.3), channel_id=1, source_target_pairs={{0,1},{1,2},{2,3},{3,0},{4,5},{5,6},{6,7},{7,4},{8,9},{9,10},{10,1... | collective-permute-start | bytes 460808 | tf_op jit(solution)/shard_map/ppermute | solution.py:285
  24.4 8.7 %collective-permute-start.1 = (f32[8,8,600]{2,1,0:T(8,128)S(1)}, f32[8,8,600]{2,1,0:T(8,128)S(1)}, u32[]{:S(2)}, u32[]{:S(2)}) collective-permute-start(f32[8,8,600]{2,1,0:T(8,128)S(1)} %slice.3), channel_id=1, source_target_pairs={{0,2},{1,3},{2,0},{3,1},{4,6},{5,7},{6,4},{7,5},{8,10},{9,11},{10,... | collective-permute-start | bytes 460808 | tf_op jit(solution)/shard_map/ppermute | solution.py:285
  26.0 7.2 %collective-permute-start = (f32[8,8,600]{2,1,0:T(8,128)S(1)}, f32[8,8,600]{2,1,0:T(8,128)S(1)}, u32[]{:S(2)}, u32[]{:S(2)}) collective-permute-start(f32[8,8,600]{2,1,0:T(8,128)S(1)} %slice.3), channel_id=1, source_target_pairs={{0,3},{1,0},{2,1},{3,2},{4,7},{5,4},{6,5},{7,6},{8,11},{9,8},{10,9... | collective-permute-start | bytes 460808 | tf_op jit(solution)/shard_map/ppermute | solution.py:285
  33.2 0.9 copy-start.1

commit v19 on v17

--- a/solution.py
+++ b/solution.py
@@ -92,13 +92,14 @@
     lax.fori_loop(0, groups, features, 0)
 
 
-def mask_kernel(fold, base_ref, seg_rows_ref, seg_cols_ref, col_ids_ref, counts_ref, mask_ref, goal_ref, mask_end_ref,
-                goal_end_ref):
+def mask_kernel(fold, base_ref, seg_rows_ref, seg_cols_ref, col_ids_ref, counts_ref, mask_ref, goal_ref):
     n_rows, n_cols = counts_ref.shape
-    deep, full = mask_ref.shape
+    deep = mask_ref.shape[0]
+    full = n_cols // LANES * LANES
     end = n_cols - full
-    for ref in (mask_ref, goal_ref, mask_end_ref, goal_end_ref):
-        if deep > n_rows:
+    rows = pl.ds(0, n_rows)
+    if deep > n_rows:
+        for ref in (mask_ref, goal_ref):
             ref[pl.ds(n_rows, deep - n_rows), :] = jnp.zeros((deep - n_rows, ref.shape[1]), jnp.float32)
 
     def mask_and_goal(start, size):
@@ -108,7 +109,6 @@
         mask = jnp.where(row_ids == col_ids_ref[:, pl.ds(start, size)], 0.0, mask)
         return mask, mask * (count / (count + 8.0))
 
-    rows = pl.ds(0, n_rows)
     for start in range(0, full, LANES):
         mask_ref[rows, pl.ds(start, LANES)], goal_ref[rows, pl.ds(start, LANES)] = mask_and_goal(start, LANES)
     if end:
@@ -116,11 +116,11 @@
             v = jnp.concatenate([v, jnp.zeros((n_rows, LANES - end), jnp.float32)], axis=1)
             return sum((pltpu.roll(v, k * end, 1) for k in range(1, fold)), v)
 
-        mask_end_ref[rows, :], goal_end_ref[rows, :] = [spread(v) for v in mask_and_goal(full, end)]
-
-
-def pair_kernel(tiles, fold, n_rows, n_cols, mask_ref, goal_ref, mask_end_ref, goal_end_ref, lhs_ref, lhs_end_ref,
-                both_ref, *rest):
+        last = pl.ds(full, LANES)
+        mask_ref[rows, last], goal_ref[rows, last] = [spread(v) for v in mask_and_goal(full, end)]
+
+
+def pair_kernel(tiles, fold, n_rows, n_cols, mask_ref, goal_ref, lhs_ref, lhs_end_ref, both_ref, *rest):
     piece_refs = rest[:tiles - 1]
     grad_ref, col_terms, rhs_ref, rhs_end_ref, terms_end_ref, weight_ref, weight_end_ref = rest[tiles - 1:]
     groups, per, _ = both_ref.shape
@@ -168,9 +168,10 @@
         return jnp.tanh(jnp.dot(lhs_end_ref[b], rhs_end_ref[b], preferred_element_type=jnp.float32))
 
     def add_some(b):
-        for inside in range(fold):
+        for inside in range(0, fold, 2):
             for start, size in chunks:
-                weight_ref[:, pl.ds(start, size)] += tanh_block(b * fold + inside, start, size)
+                t = [tanh_block(b * fold + i, start, size) for i in range(inside, min(inside + 2, fold))]
+                weight_ref[:, pl.ds(start, size)] += functools.reduce(jnp.add, t)
         if end:
             weight_end_ref[...] += tanh_end(b)
 
@@ -192,7 +193,8 @@
     if end:
         part = weight_end_ref[...]
         total = sum((pltpu.roll(part, k * end, 1) for k in range(1, fold)), part)
-        weight_end_ref[...] = mask_end_ref[...] * (0.5 + scale * total) - goal_end_ref[...]
+        last = pl.ds(full, LANES)
+        weight_end_ref[...] = mask_ref[:, last] * (0.5 + scale * total) - goal_ref[:, last]
 
     def split2(weight, t):
         g = weight * (1.0 - t * t)
@@ -274,9 +276,9 @@
     blocks = structs // fold
     masks = pl.pallas_call(
         functools.partial(mask_kernel, fold),
-        out_shape=[jax.ShapeDtypeStruct((deep, width), jnp.float32) for width in (full, full, LANES, LANES)],
+        out_shape=[jax.ShapeDtypeStruct((deep, col_wide), jnp.float32)] * 2,
         in_specs=[pl.BlockSpec(memory_space=pltpu.SMEM)] + [vmem] * 4,
-        out_specs=[vmem] * 4,
+        out_specs=[vmem] * 2,
         compiler_params=pltpu.CompilerParams(vmem_limit_bytes=32 << 20),
         name="masks",
     )(row_base[None], seg_rows, seg_cols, col_ids, block)
@@ -299,7 +301,7 @@
     grad = pl.pallas_call(
         functools.partial(pair_kernel, n_tile, fold, n_rows, n_cols),
         out_shape=jax.ShapeDtypeStruct((n_ens, 3, local_n, n_rows), jnp.float32),
-        in_specs=[vmem] * (6 + n_tile),
+        in_specs=[vmem] * (4 + n_tile),
         out_specs=vmem,
         scratch_shapes=[
             [pltpu.VMEM((col_wide // LANES, 8 * local_n, LANES), jnp.float32)] * 3,

time: 100 us -> 98.9 us (0.989)
    unnamed x4 -> x2, local copies, waits for them, and re-layouts: 1.6 us -> 0.38 us
where the time goes in v19:
time: 98.9 us; the launch traced here: 98.5 us
  Pallas kernels  57.4 us (58%)
  blocking collectives  15.6 us (16%)
  starting transfers between devices  10.8 us (11%)
  waiting for transfers between devices  8.75 us (9%)
  local copies, waits for them, and re-layouts  5.06 us (5%)
    pallas_call x1, Pallas kernels, on_device(): pl.pallas_call(functools.partial(pair_kernel, n_tile, fold, n_rows, n_col...  47.9 us
    all_to_all x1, blocking collectives, on_device(): back = lax.all_to_all(grad, 'ens', 0, 0, tiled=True)  15.6 us
    all_to_all x1, waiting for transfers between devices, on_device(): both = lax.all_to_all(send, 'ens', 0, 0, tiled=True)  7.94 us
    all_to_all x1, starting transfers between devices, on_device(): both = lax.all_to_all(send, 'ens', 0, 0, tiled=True)  6.33 us
    pallas_call x1, Pallas kernels, on_device(): pl.pallas_call(functools.partial(row_kernel, n_rows, fold), out_shape=[ja...  4.98 us
    ppermute x3, starting transfers between devices, on_device(): lax.ppermute(own, 'tile', [(t, (t - k) % n_tile) for t in range(n_tile)])  4.5 us
    dynamic_slice x1, local copies, waits for them, and re-layouts, on_device(): lax.dynamic_slice_in_dim(own_counts, b, piece, 1)  2.17 us
  transfers between devices with their start and end apart: 4, of which 3 were waited for; matrix products, arithmetic and copies ran while one was open for 5% of the time, Pallas kernels for 6%

profile of v19, /device:TPU:0, one launch (start us, length us, event | category | flops | bytes accessed | tf_op | source)
XLA Modules:
  0.0 98.5 jit_solution(4315910195088885866)
XLA Ops:
  0.0 1.9 %pack.1 = f32[8,8,1800]{2,1,0:T(8,128)} custom-call(f32[3,8,800]{2,1,0:T(8,128)} %bitcast.4), custom_call_target="tpu_custom_call" | custom-call | tf_op jit(solution)/shard_map/pack/pallas_call | solution.py:254
  1.9 6.3 %all-to-all-start = ((f32[8,8,1800]{2,1,0:T(8,128)}), f32[8,8,1800]{2,1,0:T(8,128)S(1)}, u32[]{:S(2)}, u32[]{:S(2)}) async-start(f32[8,8,1800]{2,1,0:T(8,128)} %pack.1), calls=%async_computation | async-start | bytes 983040 | tf_op jit(solution)/shard_map/all_to_all | solution.py:261
  8.3 0.1 pad_add_fusion.2
  8.4 0.8 dynamic_slice.28
  9.2 0.9 fusion.1
  10.0 0.1 pad_add_fusion.1
  10.1 0.8 copy.4.seg_rows_ref
  11.0 2.2 %fusion = (s32[400,200]{1,0:T(8,128)S(1)}, s32[400,200]{1,0:T(8,128)S(1)}, s32[400,200]{1,0:T(8,128)S(1)}, s32[400,200]{1,0:T(8,128)S(1)}) fusion(s32[800,3200]{1,0:T(8,128)} %param.4, s32[]{:T(128)S(6)} %select_n.38, s32[]{:T(128)S(6)} %select_n.39, s32[]{:T(128)S(6)} %select_n.40, s32[]{:T(128)S(6)} %select_n.42, s32[]{:T(128)S(6)} %select_n.41), kind=kLoop, calls=%fused_computation.7 | loop fusion | bytes 2560020 | tf_op jit(solution)/shard_map/dynamic_slice | solution.py:266
  13.1 0.0 copy-start
  13.1 0.5 pad_add_fusion.counts_ref
  13.7 0.4 copy-done
  14.1 0.9 masks.1
  14.9 7.9 %all-to-all-done.both_ref = f32[8,8,1800]{2,1,0:T(8,128)S(1)} async-done(((f32[8,8,1800]{2,1,0:T(8,128)}), f32[8,8,1800]{2,1,0:T(8,128)S(1)}, u32[]{:S(2)}, u32[]{:S(2)}) %all-to-all-start) | async-done | bytes 460832 | tf_op jit(solution)/shard_map/all_to_all | solution.py:261
  22.9 1.5 %collective-permute-start.2 = (f32[8,8,600]{2,1,0:T(8,128)S(1)}, f32[8,8,600]{2,1,0:T(8,128)S(1)}, u32[]{:S(2)}, u32[]{:S(2)}) collective-permute-start(f32[8,8,600]{2,1,0:T(8,128)S(1)} %slice.3), channel_id=1, source_target_pairs={{0,1},{1,2},{2,3},{3,0},{4,5},{5,6},{6,7},{7,4},{8,9},{9,10},{10,1... | collective-permute-start | bytes 460808 | tf_op jit(solution)/shard_map/ppermute | solution.py:287
  24.4 1.5 %collective-permute-start.1 = (f32[8,8,600]{2,1,0:T(8,128)S(1)}, f32[8,8,600]{2,1,0:T(8,128)S(1)}, u32[]{:S(2)}, u32[]{:S(2)}) collective-permute-start(f32[8,8,600]{2,1,0:T(8,128)S(1)} %slice.3), channel_id=1, source_target_pairs={{0,2},{1,3},{2,0},{3,1},{4,6},{5,7},{6,4},{7,5},{8,10},{9,11},{10,... | collective-permute-start | bytes 460808 | tf_op jit(solution)/shard_map/ppermute | solution.py:287
  26.0 1.4 %collective-permute-start = (f32[8,8,600]{2,1,0:T(8,128)S(1)}, f32[8,8,600]{2,1,0:T(8,128)S(1)}, u32[]{:S(2)}, u32[]{:S(2)}) collective-permute-start(f32[8,8,600]{2,1,0:T(8,128)S(1)} %slice.3), channel_id=1, source_target_pairs={{0,3},{1,0},{2,1},{3,2},{4,7},{5,4},{6,5},{7,6},{8,11},{9,8},{10,9... | collective-permute-start | bytes 460808 | tf_op jit(solution)/shard_map/ppermute | solution.py:287
  27.4 5.0 %rows.1 = (bf16[64,400,48]{2,1,0:T(8,128)(2,1)S(1)}, bf16[16,400,256]{2,1,0:T(8,128)(2,1)S(1)}) custom-call(f32[8,8,1800]{2,1,0:T(8,128)S(1)} %all-to-all-done.both_ref), custom_call_target="tpu_custom_call" | custom-call | tf_op jit(solution)/shard_map/rows/pallas_call | solution.py:289
  32.4 0.0 collective-permute-done.2.rest_2_
  32.4 0.7 collective-permute-done.1.rest_1_
  33.1 0.1 collective-permute-done.rest_0_
  33.2 47.9 %pairs.1 = f32[8,3,8,400]{3,2,1,0:T(8,128)S(1)} custom-call(f32[400,896]{1,0:T(8,128)S(1)} %get-tuple-element.14.mask_ref, f32[400,896]{1,0:T(8,128)S(1)} %get-tuple-element.15.goal_ref, bf16[64,400,48]{2,1,0:T(8,128)(2,1)S(1)} %get-tuple-element.17.lhs_ref, bf16[16,400,256]{2,1,0:T(8,128)(2,1)S(1)} %get-tuple-element.18.lhs_end_ref, ...), custom_call_target="tpu_custom_call" | custom-call | tf_op jit(solution)/shard_map/pairs/pallas_call | solution.py:301
  81.1 15.6 %all_to_all.10.back_ref = f32[8,3,8,400]{3,2,1,0:T(8,128)} all-to-all(f32[8,3,8,400]{3,2,1,0:T(8,128)S(1)} %pairs.1), channel_id=1, replica_groups=mesh['ens'=8,'tile'=4] {'ens'}, dimensions={0} | all-to-all | bytes 614400 | tf_op jit(solution)/shard_map/all_to_all | solution.py:318
  96.8 1.7 %total.1 = f32[3,8,800]{2,1,0:T(8,128)} custom-call(f32[8,3,8,400]{3,2,1,0:T(8,128)} %all_to_all.10.back_ref), custom_call_target="tpu_custom_call" | custom-call | tf_op jit(solution)/shard_map/total/pallas_call | solution.py:319
  (5 shorter events, 0.0 us)
Async XLA Ops:
  1.9 21.0 %all-to-all-start = ((f32[8,8,1800]{2,1,0:T(8,128)}), f32[8,8,1800]{2,1,0:T(8,128)S(1)}, u32[]{:S(2)}, u32[]{:S(2)}) async-start(f32[8,8,1800]{2,1,0:T(8,128)} %pack.1), calls=%async_computation | async-start | bytes 983040 | tf_op jit(solution)/shard_map/all_to_all | solution.py:261
  13.1 0.9 copy-start
  22.9 9.5 %collective-permute-start.2 = (f32[8,8,600]{2,1,0:T(8,128)S(1)}, f32[8,8,600]{2,1,0:T(8,128)S(1)}, u32[]{:S(2)}, u32[]{:S(2)}) collective-permute-start(f32[8,8,600]{2,1,0:T(8,128)S(1)} %slice.3), channel_id=1, source_target_pairs={{0,1},{1,2},{2,3},{3,0},{4,5},{5,6},{6,7},{7,4},{8,9},{9,10},{10,1... | collective-permute-start | bytes 460808 | tf_op jit(solution)/shard_map/ppermute | solution.py:287
  24.4 8.7 %collective-permute-start.1 = (f32[8,8,600]{2,1,0:T(8,128)S(1)}, f32[8,8,600]{2,1,0:T(8,128)S(1)}, u32[]{:S(2)}, u32[]{:S(2)}) collective-permute-start(f32[8,8,600]{2,1,0:T(8,128)S(1)} %slice.3), channel_id=1, source_target_pairs={{0,2},{1,3},{2,0},{3,1},{4,6},{5,7},{6,4},{7,5},{8,10},{9,11},{10,... | collective-permute-start | bytes 460808 | tf_op jit(solution)/shard_map/ppermute | solution.py:287
  26.0 7.2 %collective-permute-start = (f32[8,8,600]{2,1,0:T(8,128)S(1)}, f32[8,8,600]{2,1,0:T(8,128)S(1)}, u32[]{:S(2)}, u32[]{:S(2)}) collective-permute-start(f32[8,8,600]{2,1,0:T(8,128)S(1)} %slice.3), channel_id=1, source_target_pairs={{0,3},{1,0},{2,1},{3,2},{4,7},{5,4},{6,5},{7,6},{8,11},{9,8},{10,9... | collective-permute-start | bytes 460808 | tf_op jit(solution)/shard_map/ppermute | solution.py:287

commit v20 on v19

--- a/solution.py
+++ b/solution.py
@@ -10,7 +10,7 @@
 LANES = 128
 WIDE = 256
 SLOT = 64
-UNROLL = 4
+KEEP_BYTES = 24 << 20
 NT = (((1,), (1,)), ((), ()))
 
 
@@ -122,7 +122,8 @@
 
 def pair_kernel(tiles, fold, n_rows, n_cols, mask_ref, goal_ref, lhs_ref, lhs_end_ref, both_ref, *rest):
     piece_refs = rest[:tiles - 1]
-    grad_ref, col_terms, rhs_ref, rhs_end_ref, terms_end_ref, weight_ref, weight_end_ref = rest[tiles - 1:]
+    (grad_ref, col_terms, rhs_ref, rhs_end_ref, terms_end_ref, weight_ref, weight_end_ref, kept_ref,
+     kept_end_ref) = rest[tiles - 1:]
     groups, per, _ = both_ref.shape
     structs = groups * per
     piece = n_cols // tiles
@@ -167,24 +168,34 @@
     def tanh_end(b):
         return jnp.tanh(jnp.dot(lhs_end_ref[b], rhs_end_ref[b], preferred_element_type=jnp.float32))
 
-    def add_some(b):
+    def add_some(b, keep):
         for inside in range(0, fold, 2):
             for start, size in chunks:
-                t = [tanh_block(b * fold + i, start, size) for i in range(inside, min(inside + 2, fold))]
+                t = []
+                for i in range(inside, min(inside + 2, fold)):
+                    t.append(tanh_block(b * fold + i, start, size))
+                    if keep:
+                        kept_ref[b * fold + i, :, pl.ds(start, size)] = t[-1]
                 weight_ref[:, pl.ds(start, size)] += functools.reduce(jnp.add, t)
         if end:
-            weight_end_ref[...] += tanh_end(b)
+            t = tanh_end(b)
+            if keep:
+                kept_end_ref[b] = t
+            weight_end_ref[...] += t
 
     together = 2 if groups % 2 == 0 else 1
-
-    def add_groups(step, carry):
+    per_step = together * (per // fold)
+    kept = kept_ref.shape[0] // (per_step * fold)
+
+    def add_groups(keep, step, carry):
         for j in range(together):
             features(step * together + j)
-        for j in range(together * (per // fold)):
-            add_some(step * (together * (per // fold)) + j)
+        for j in range(per_step):
+            add_some(step * per_step + j, keep)
         return carry
 
-    lax.fori_loop(0, groups // together, add_groups, 0)
+    lax.fori_loop(0, kept, functools.partial(add_groups, True), 0)
+    lax.fori_loop(kept, groups // together, functools.partial(add_groups, False), 0)
 
     scale = 0.5 / structs
     for start, size in chunks:
@@ -206,12 +217,16 @@
         return (lax.dot_general(hi, terms, NT, preferred_element_type=jnp.float32).T
                 + lax.dot_general(terms, lo, NT, preferred_element_type=jnp.float32))
 
-    def grad_some(b, carry):
+    def grad_some(b, keep):
         if end:
-            last = sums(terms_end_ref[b], [split2(weight_end_ref[...], tanh_end(b))])
+            t = kept_end_ref[b] if keep else tanh_end(b)
+            last = sums(terms_end_ref[b], [split2(weight_end_ref[...], t)])
         for inside in range(fold):
             s = b * fold + inside
-            parts = [split2(weight_ref[:, pl.ds(start, size)], tanh_block(s, start, size)) for start, size in chunks]
+            parts = []
+            for start, size in chunks:
+                cut = pl.ds(start, size)
+                parts.append(split2(weight_ref[:, cut], kept_ref[s, :, cut] if keep else tanh_block(s, start, size)))
             total = sums(rhs_ref[s, pl.ds(0, 16), :], parts)
             if end:
                 total += last[16 * inside:16 * inside + 16]
@@ -222,9 +237,14 @@
                 xyz = both[:, 3 * piece + c * n_rows:3 * piece + (c + 1) * n_rows]
                 grad_ref[g, c, pl.ds(i, 1), :] = (0.25 / 16) * (
                     total[c:c + 1] + total[8 + c:9 + c] - total[3:4] * xyz)
+
+    def grad_groups(keep, step, carry):
+        for j in range(per_step):
+            grad_some(step * per_step + j, keep)
         return carry
 
-    lax.fori_loop(0, structs // fold, grad_some, 0, unroll=UNROLL)
+    lax.fori_loop(0, kept, functools.partial(grad_groups, True), 0)
+    lax.fori_loop(kept, groups // together, functools.partial(grad_groups, False), 0)
 
 
 def split_ens(n_ens, beads, tiles):
@@ -274,6 +294,9 @@
     deep = up(n_rows, 16)
     row_wide, col_wide = up(n_rows, LANES), up(n_cols, LANES)
     blocks = structs // fold
+    kept = min(structs, local_n * (2 if n_ens % 2 == 0 else 1))
+    if 4 * kept * deep * (full + LANES) > KEEP_BYTES:
+        kept = 0
     masks = pl.pallas_call(
         functools.partial(mask_kernel, fold),
         out_shape=[jax.ShapeDtypeStruct((deep, col_wide), jnp.float32)] * 2,
@@ -310,8 +333,10 @@
             pltpu.VMEM((blocks, fold * 16, LANES), jnp.bfloat16),
             pltpu.VMEM((deep, full), jnp.float32),
             pltpu.VMEM((deep, LANES), jnp.float32),
+            pltpu.VMEM((max(kept, 1), deep, full), jnp.float32),
+            pltpu.VMEM((max(kept // fold, 1), deep, LANES), jnp.float32),
         ],
-        compiler_params=pltpu.CompilerParams(vmem_limit_bytes=40 << 20),
+        compiler_params=pltpu.CompilerParams(vmem_limit_bytes=44 << 20),
         name="pairs",
     )(*masks, lhs, lhs_end, both, *pieces)
 

time: 98.9 us -> 101 us (1.021)
  local copies, waits for them, and re-layouts: 5.06 us -> 7.77 us
    unnamed x2 -> x4, local copies, waits for them, and re-layouts: 0.38 us -> 3.1 us
  transfers between devices with their start and end apart: 4 -> 4, of which waited for: 3 -> 1; matrix products, arithmetic and copies ran while one was open for 5% -> 5% of each run, Pallas kernels for 6% -> 6%
where the time goes in v20:
time: 101 us; the launch traced here: 100 us
  Pallas kernels  57.3 us (57%)
  blocking collectives  15.6 us (15%)
  starting transfers between devices  10.8 us (11%)
  waiting for transfers between devices  7.96 us (8%)
  local copies, waits for them, and re-layouts  7.77 us (8%)
    pallas_call x1, Pallas kernels, on_device(): pl.pallas_call(functools.partial(pair_kernel, n_tile, fold, n_rows, n_col...  47.8 us
    all_to_all x1, blocking collectives, on_device(): back = lax.all_to_all(grad, 'ens', 0, 0, tiled=True)  15.6 us
    all_to_all x1, waiting for transfers between devices, on_device(): both = lax.all_to_all(send, 'ens', 0, 0, tiled=True)  7.95 us
    all_to_all x1, starting transfers between devices, on_device(): both = lax.all_to_all(send, 'ens', 0, 0, tiled=True)  6.33 us
    pallas_call x1, Pallas kernels, on_device(): pl.pallas_call(functools.partial(row_kernel, n_rows, fold), out_shape=[ja...  4.98 us
    ppermute x3, starting transfers between devices, on_device(): lax.ppermute(own, 'tile', [(t, (t - k) % n_tile) for t in range(n_tile)])  4.5 us
    unnamed x4, local copies, waits for them, and re-layouts  3.1 us
    dynamic_slice x1, local copies, waits for them, and re-layouts, on_device(): lax.dynamic_slice_in_dim(own_counts, b, piece, 1)  2.17 us
  transfers between devices with their start and end apart: 4, of which 1 were waited for; matrix products, arithmetic and copies ran while one was open for 5% of the time, Pallas kernels for 6%

profile of v20, /device:TPU:0, one launch (start us, length us, event | category | flops | bytes accessed | tf_op | source)
XLA Modules:
  0.0 100.3 jit_solution(7282805549783624358)
XLA Ops:
  0.0 1.9 %pack.1 = f32[8,8,1800]{2,1,0:T(8,128)} custom-call(f32[3,8,800]{2,1,0:T(8,128)} %bitcast.4), custom_call_target="tpu_custom_call" | custom-call | tf_op jit(solution)/shard_map/pack/pallas_call | solution.py:274
  1.9 6.3 %all-to-all-start = ((f32[8,8,1800]{2,1,0:T(8,128)}), f32[8,8,1800]{2,1,0:T(8,128)S(1)}, u32[]{:S(2)}, u32[]{:S(2)}) async-start(f32[8,8,1800]{2,1,0:T(8,128)} %pack.1), calls=%async_computation | async-start | bytes 983040 | tf_op jit(solution)/shard_map/all_to_all | solution.py:281
  8.3 0.1 pad_add_fusion.2
  8.4 0.8 dynamic_slice.28
  9.2 0.9 fusion.1
  10.0 0.1 pad_add_fusion.1
  10.1 0.8 copy.4.seg_rows_ref
  11.0 2.2 %fusion = (s32[400,200]{1,0:T(8,128)S(1)}, s32[400,200]{1,0:T(8,128)S(1)}, s32[400,200]{1,0:T(8,128)S(1)}, s32[400,200]{1,0:T(8,128)S(1)}) fusion(s32[800,3200]{1,0:T(8,128)} %param.4, s32[]{:T(128)S(6)} %select_n.38, s32[]{:T(128)S(6)} %select_n.39, s32[]{:T(128)S(6)} %select_n.40, s32[]{:T(128)S(6)} %select_n.42, s32[]{:T(128)S(6)} %select_n.41), kind=kLoop, calls=%fused_computation.7 | loop fusion | bytes 2560020 | tf_op jit(solution)/shard_map/dynamic_slice | solution.py:286
  13.1 0.0 copy-start.1
  13.1 0.5 pad_add_fusion.counts_ref
  13.7 0.4 copy-done.1
  14.1 0.9 masks.1
  14.9 7.9 %all-to-all-done.both_ref = f32[8,8,1800]{2,1,0:T(8,128)S(1)} async-done(((f32[8,8,1800]{2,1,0:T(8,128)}), f32[8,8,1800]{2,1,0:T(8,128)S(1)}, u32[]{:S(2)}, u32[]{:S(2)}) %all-to-all-start) | async-done | bytes 460832 | tf_op jit(solution)/shard_map/all_to_all | solution.py:281
  22.9 1.5 %collective-permute-start.2 = (f32[8,8,600]{2,1,0:T(8,128)S(1)}, f32[8,8,600]{2,1,0:T(8,128)S(1)}, u32[]{:S(2)}, u32[]{:S(2)}) collective-permute-start(f32[8,8,600]{2,1,0:T(8,128)S(1)} %slice.3), channel_id=1, source_target_pairs={{0,1},{1,2},{2,3},{3,0},{4,5},{5,6},{6,7},{7,4},{8,9},{9,10},{10,1... | collective-permute-start | bytes 460808 | tf_op jit(solution)/shard_map/ppermute | solution.py:310
  24.4 1.5 %collective-permute-start.1 = (f32[8,8,600]{2,1,0:T(8,128)S(1)}, f32[8,8,600]{2,1,0:T(8,128)S(1)}, u32[]{:S(2)}, u32[]{:S(2)}) collective-permute-start(f32[8,8,600]{2,1,0:T(8,128)S(1)} %slice.3), channel_id=1, source_target_pairs={{0,2},{1,3},{2,0},{3,1},{4,6},{5,7},{6,4},{7,5},{8,10},{9,11},{10,... | collective-permute-start | bytes 460808 | tf_op jit(solution)/shard_map/ppermute | solution.py:310
  26.0 1.4 %collective-permute-start = (f32[8,8,600]{2,1,0:T(8,128)S(1)}, f32[8,8,600]{2,1,0:T(8,128)S(1)}, u32[]{:S(2)}, u32[]{:S(2)}) collective-permute-start(f32[8,8,600]{2,1,0:T(8,128)S(1)} %slice.3), channel_id=1, source_target_pairs={{0,3},{1,0},{2,1},{3,2},{4,7},{5,4},{6,5},{7,6},{8,11},{9,8},{10,9... | collective-permute-start | bytes 460808 | tf_op jit(solution)/shard_map/ppermute | solution.py:310
  27.4 5.0 %rows.1 = (bf16[64,400,48]{2,1,0:T(8,128)(2,1)S(1)}, bf16[16,400,256]{2,1,0:T(8,128)(2,1)S(1)}) custom-call(f32[8,8,1800]{2,1,0:T(8,128)S(1)} %all-to-all-done.both_ref), custom_call_target="tpu_custom_call" | custom-call | tf_op jit(solution)/shard_map/rows/pallas_call | solution.py:312
  32.4 0.0 copy-start
  32.4 2.7 %copy-done = bf16[64,400,48]{2,1,0:T(8,128)(2,1)} copy-done((bf16[64,400,48]{2,1,0:T(8,128)(2,1)}, bf16[64,400,48]{2,1,0:T(8,128)(2,1)S(1)}, u32[]{:S(2)}) %copy-start) | copy-done | bytes 2457624
  35.1 0.0 collective-permute-done.2.rest_2_
  35.1 0.0 collective-permute-done.1.rest_1_
  35.1 0.0 collective-permute-done.rest_0_
  35.1 47.8 %pairs.1 = f32[8,3,8,400]{3,2,1,0:T(8,128)S(1)} custom-call(f32[400,896]{1,0:T(8,128)S(1)} %get-tuple-element.14.mask_ref, f32[400,896]{1,0:T(8,128)S(1)} %get-tuple-element.15.goal_ref, bf16[64,400,48]{2,1,0:T(8,128)(2,1)} %copy-done, bf16[16,400,256]{2,1,0:T(8,128)(2,1)S(1)} %get-tuple-element.18.lhs_end_ref, f32[8,8,1800]{2,1,0:T(8,128)S(1)} %all-to-all-done.both_ref, ...), custom_call_target="tpu_custom_call" | custom-call | tf_op jit(solution)/shard_map/pairs/pallas_call | solution.py:324
  82.9 15.6 %all_to_all.10.back_ref = f32[8,3,8,400]{3,2,1,0:T(8,128)} all-to-all(f32[8,3,8,400]{3,2,1,0:T(8,128)S(1)} %pairs.1), channel_id=1, replica_groups=mesh['ens'=8,'tile'=4] {'ens'}, dimensions={0} | all-to-all | bytes 614400 | tf_op jit(solution)/shard_map/all_to_all | solution.py:343
  98.6 1.7 %total.1 = f32[3,8,800]{2,1,0:T(8,128)} custom-call(f32[8,3,8,400]{3,2,1,0:T(8,128)} %all_to_all.10.back_ref), custom_call_target="tpu_custom_call" | custom-call | tf_op jit(solution)/shard_map/total/pallas_call | solution.py:344
  (5 shorter events, 0.0 us)
Async XLA Ops:
  1.9 21.0 %all-to-all-start = ((f32[8,8,1800]{2,1,0:T(8,128)}), f32[8,8,1800]{2,1,0:T(8,128)S(1)}, u32[]{:S(2)}, u32[]{:S(2)}) async-start(f32[8,8,1800]{2,1,0:T(8,128)} %pack.1), calls=%async_computation | async-start | bytes 983040 | tf_op jit(solution)/shard_map/all_to_all | solution.py:281
  13.1 0.9 copy-start.1
  22.9 12.2 %collective-permute-start.2 = (f32[8,8,600]{2,1,0:T(8,128)S(1)}, f32[8,8,600]{2,1,0:T(8,128)S(1)}, u32[]{:S(2)}, u32[]{:S(2)}) collective-permute-start(f32[8,8,600]{2,1,0:T(8,128)S(1)} %slice.3), channel_id=1, source_target_pairs={{0,1},{1,2},{2,3},{3,0},{4,5},{5,6},{6,7},{7,4},{8,9},{9,10},{10,1... | collective-permute-start | bytes 460808 | tf_op jit(solution)/shard_map/ppermute | solution.py:310
  24.4 10.7 %collective-permute-start.1 = (f32[8,8,600]{2,1,0:T(8,128)S(1)}, f32[8,8,600]{2,1,0:T(8,128)S(1)}, u32[]{:S(2)}, u32[]{:S(2)}) collective-permute-start(f32[8,8,600]{2,1,0:T(8,128)S(1)} %slice.3), channel_id=1, source_target_pairs={{0,2},{1,3},{2,0},{3,1},{4,6},{5,7},{6,4},{7,5},{8,10},{9,11},{10,... | collective-permute-start | bytes 460808 | tf_op jit(solution)/shard_map/ppermute | solution.py:310
  26.0 9.2 %collective-permute-start = (f32[8,8,600]{2,1,0:T(8,128)S(1)}, f32[8,8,600]{2,1,0:T(8,128)S(1)}, u32[]{:S(2)}, u32[]{:S(2)}) collective-permute-start(f32[8,8,600]{2,1,0:T(8,128)S(1)} %slice.3), channel_id=1, source_target_pairs={{0,3},{1,0},{2,1},{3,2},{4,7},{5,4},{6,5},{7,6},{8,11},{9,8},{10,9... | collective-permute-start | bytes 460808 | tf_op jit(solution)/shard_map/ppermute | solution.py:310
  32.4 2.7 %copy-start = (bf16[64,400,48]{2,1,0:T(8,128)(2,1)}, bf16[64,400,48]{2,1,0:T(8,128)(2,1)S(1)}, u32[]{:S(2)}) copy-start(bf16[64,400,48]{2,1,0:T(8,128)(2,1)S(1)} %get-tuple-element.17.lhs_ref) | copy-start | bytes 7372804

commit v21 on v19

--- a/solution.py
+++ b/solution.py
@@ -10,7 +10,7 @@
 LANES = 128
 WIDE = 256
 SLOT = 64
-UNROLL = 4
+TOGETHER = 4
 NT = (((1,), (1,)), ((), ()))
 
 
@@ -122,7 +122,7 @@
 
 def pair_kernel(tiles, fold, n_rows, n_cols, mask_ref, goal_ref, lhs_ref, lhs_end_ref, both_ref, *rest):
     piece_refs = rest[:tiles - 1]
-    grad_ref, col_terms, rhs_ref, rhs_end_ref, terms_end_ref, weight_ref, weight_end_ref = rest[tiles - 1:]
+    grad_ref, col_terms, rhs_ref, rhs_end_ref, terms_end_ref, weight_ref, weight_end_ref, sums_ref = rest[tiles - 1:]
     groups, per, _ = both_ref.shape
     structs = groups * per
     piece = n_cols // tiles
@@ -175,7 +175,7 @@
         if end:
             weight_end_ref[...] += tanh_end(b)
 
-    together = 2 if groups % 2 == 0 else 1
+    together = TOGETHER if groups % TOGETHER == 0 else 1
 
     def add_groups(step, carry):
         for j in range(together):
@@ -206,25 +206,34 @@
         return (lax.dot_general(hi, terms, NT, preferred_element_type=jnp.float32).T
                 + lax.dot_general(terms, lo, NT, preferred_element_type=jnp.float32))
 
-    def grad_some(b, carry):
-        if end:
-            last = sums(terms_end_ref[b], [split2(weight_end_ref[...], tanh_end(b))])
-        for inside in range(fold):
-            s = b * fold + inside
-            parts = [split2(weight_ref[:, pl.ds(start, size)], tanh_block(s, start, size)) for start, size in chunks]
-            total = sums(rhs_ref[s, pl.ds(0, 16), :], parts)
+    def grad_group(g):
+        for block in range(per // fold):
+            b = g * (per // fold) + block
             if end:
-                total += last[16 * inside:16 * inside + 16]
-            total = total[:, :n_rows]
-            g, i = lax.div(s, per), lax.rem(s, per)
-            both = both_ref[g, pl.ds(i, 1), :]
-            for c in range(3):
-                xyz = both[:, 3 * piece + c * n_rows:3 * piece + (c + 1) * n_rows]
-                grad_ref[g, c, pl.ds(i, 1), :] = (0.25 / 16) * (
-                    total[c:c + 1] + total[8 + c:9 + c] - total[3:4] * xyz)
+                last = sums(terms_end_ref[b], [split2(weight_end_ref[...], tanh_end(b))])
+            for inside in range(fold):
+                s = b * fold + inside
+                parts = [split2(weight_ref[:, pl.ds(start, size)], tanh_block(s, start, size)) for start, size in chunks]
+                total = sums(rhs_ref[s, pl.ds(0, 16), :], parts)
+                if end:
+                    total += last[16 * inside:16 * inside + 16]
+                total = total[:, :n_rows]
+                mixed = total[0:3] + total[8:11]
+                i = block * fold + inside
+                for c in range(3):
+                    sums_ref[c, pl.ds(i, 1), :] = mixed[c:c + 1]
+                sums_ref[3, pl.ds(i, 1), :] = total[3:4]
+        both = both_ref[g]
+        for c in range(3):
+            xyz = both[:, 3 * piece + c * n_rows:3 * piece + (c + 1) * n_rows]
+            grad_ref[g, c] = (0.25 / 16) * (sums_ref[c] - sums_ref[3] * xyz)
+
+    def grad_groups(step, carry):
+        for j in range(together):
+            grad_group(step * together + j)
         return carry
 
-    lax.fori_loop(0, structs // fold, grad_some, 0, unroll=UNROLL)
+    lax.fori_loop(0, groups // together, grad_groups, 0)
 
 
 def split_ens(n_ens, beads, tiles):
@@ -310,6 +319,7 @@
             pltpu.VMEM((blocks, fold * 16, LANES), jnp.bfloat16),
             pltpu.VMEM((deep, full), jnp.float32),
             pltpu.VMEM((deep, LANES), jnp.float32),
+            pltpu.VMEM((4, local_n, n_rows), jnp.float32),
         ],
         compiler_params=pltpu.CompilerParams(vmem_limit_bytes=40 << 20),
         name="pairs",

time: 98.9 us -> 98.3 us (level)
  no operation moved by 1% of the time
where the time goes in v21:
time: 98.3 us; the launch traced here: 97.8 us
  Pallas kernels  56.7 us (58%)
  blocking collectives  15.6 us (16%)
  starting transfers between devices  10.8 us (11%)
  waiting for transfers between devices  8.75 us (9%)
  local copies, waits for them, and re-layouts  5.06 us (5%)
    pallas_call x1, Pallas kernels, on_device(): pl.pallas_call(functools.partial(pair_kernel, n_tile, fold, n_rows, n_col...  47.3 us
    all_to_all x1, blocking collectives, on_device(): back = lax.all_to_all(grad, 'ens', 0, 0, tiled=True)  15.6 us
    all_to_all x1, waiting for transfers between devices, on_device(): both = lax.all_to_all(send, 'ens', 0, 0, tiled=True)  7.94 us
    all_to_all x1, starting transfers between devices, on_device(): both = lax.all_to_all(send, 'ens', 0, 0, tiled=True)  6.33 us
    pallas_call x1, Pallas kernels, on_device(): pl.pallas_call(functools.partial(row_kernel, n_rows, fold), out_shape=[ja...  4.98 us
    ppermute x3, starting transfers between devices, on_device(): lax.ppermute(own, 'tile', [(t, (t - k) % n_tile) for t in range(n_tile)])  4.5 us
    dynamic_slice x1, local copies, waits for them, and re-layouts, on_device(): lax.dynamic_slice_in_dim(own_counts, b, piece, 1)  2.17 us
  transfers between devices with their start and end apart: 4, of which 3 were waited for; matrix products, arithmetic and copies ran while one was open for 5% of the time, Pallas kernels for 6%

profile of v21, /device:TPU:0, one launch (start us, length us, event | category | flops | bytes accessed | tf_op | source)
XLA Modules:
  0.0 97.8 jit_solution(14459844419488145213)
XLA Ops:
  0.0 1.9 %pack.1 = f32[8,8,1800]{2,1,0:T(8,128)} custom-call(f32[3,8,800]{2,1,0:T(8,128)} %bitcast.4), custom_call_target="tpu_custom_call" | custom-call | tf_op jit(solution)/shard_map/pack/pallas_call | solution.py:263
  1.9 6.3 %all-to-all-start = ((f32[8,8,1800]{2,1,0:T(8,128)}), f32[8,8,1800]{2,1,0:T(8,128)S(1)}, u32[]{:S(2)}, u32[]{:S(2)}) async-start(f32[8,8,1800]{2,1,0:T(8,128)} %pack.1), calls=%async_computation | async-start | bytes 983040 | tf_op jit(solution)/shard_map/all_to_all | solution.py:270
  8.3 0.1 pad_add_fusion.2
  8.4 0.8 dynamic_slice.28
  9.2 0.9 fusion.1
  10.0 0.1 pad_add_fusion.1
  10.1 0.8 copy.4.seg_rows_ref
  11.0 2.2 %fusion = (s32[400,200]{1,0:T(8,128)S(1)}, s32[400,200]{1,0:T(8,128)S(1)}, s32[400,200]{1,0:T(8,128)S(1)}, s32[400,200]{1,0:T(8,128)S(1)}) fusion(s32[800,3200]{1,0:T(8,128)} %param.4, s32[]{:T(128)S(6)} %select_n.38, s32[]{:T(128)S(6)} %select_n.39, s32[]{:T(128)S(6)} %select_n.40, s32[]{:T(128)S(6)} %select_n.42, s32[]{:T(128)S(6)} %select_n.41), kind=kLoop, calls=%fused_computation.7 | loop fusion | bytes 2560020 | tf_op jit(solution)/shard_map/dynamic_slice | solution.py:275
  13.1 0.0 copy-start
  13.1 0.5 pad_add_fusion.counts_ref
  13.7 0.4 copy-done
  14.1 0.9 masks.1
  14.9 7.9 %all-to-all-done.both_ref = f32[8,8,1800]{2,1,0:T(8,128)S(1)} async-done(((f32[8,8,1800]{2,1,0:T(8,128)}), f32[8,8,1800]{2,1,0:T(8,128)S(1)}, u32[]{:S(2)}, u32[]{:S(2)}) %all-to-all-start) | async-done | bytes 460832 | tf_op jit(solution)/shard_map/all_to_all | solution.py:270
  22.9 1.5 %collective-permute-start.2 = (f32[8,8,600]{2,1,0:T(8,128)S(1)}, f32[8,8,600]{2,1,0:T(8,128)S(1)}, u32[]{:S(2)}, u32[]{:S(2)}) collective-permute-start(f32[8,8,600]{2,1,0:T(8,128)S(1)} %slice.3), channel_id=1, source_target_pairs={{0,1},{1,2},{2,3},{3,0},{4,5},{5,6},{6,7},{7,4},{8,9},{9,10},{10,1... | collective-permute-start | bytes 460808 | tf_op jit(solution)/shard_map/ppermute | solution.py:296
  24.4 1.5 %collective-permute-start.1 = (f32[8,8,600]{2,1,0:T(8,128)S(1)}, f32[8,8,600]{2,1,0:T(8,128)S(1)}, u32[]{:S(2)}, u32[]{:S(2)}) collective-permute-start(f32[8,8,600]{2,1,0:T(8,128)S(1)} %slice.3), channel_id=1, source_target_pairs={{0,2},{1,3},{2,0},{3,1},{4,6},{5,7},{6,4},{7,5},{8,10},{9,11},{10,... | collective-permute-start | bytes 460808 | tf_op jit(solution)/shard_map/ppermute | solution.py:296
  26.0 1.4 %collective-permute-start = (f32[8,8,600]{2,1,0:T(8,128)S(1)}, f32[8,8,600]{2,1,0:T(8,128)S(1)}, u32[]{:S(2)}, u32[]{:S(2)}) collective-permute-start(f32[8,8,600]{2,1,0:T(8,128)S(1)} %slice.3), channel_id=1, source_target_pairs={{0,3},{1,0},{2,1},{3,2},{4,7},{5,4},{6,5},{7,6},{8,11},{9,8},{10,9... | collective-permute-start | bytes 460808 | tf_op jit(solution)/shard_map/ppermute | solution.py:296
  27.4 5.0 %rows.1 = (bf16[64,400,48]{2,1,0:T(8,128)(2,1)S(1)}, bf16[16,400,256]{2,1,0:T(8,128)(2,1)S(1)}) custom-call(f32[8,8,1800]{2,1,0:T(8,128)S(1)} %all-to-all-done.both_ref), custom_call_target="tpu_custom_call" | custom-call | tf_op jit(solution)/shard_map/rows/pallas_call | solution.py:298
  32.4 0.0 collective-permute-done.2.rest_2_
  32.4 0.7 collective-permute-done.1.rest_1_
  33.1 0.1 collective-permute-done.rest_0_
  33.2 47.3 %pairs.1 = f32[8,3,8,400]{3,2,1,0:T(8,128)S(1)} custom-call(f32[400,896]{1,0:T(8,128)S(1)} %get-tuple-element.14.mask_ref, f32[400,896]{1,0:T(8,128)S(1)} %get-tuple-element.15.goal_ref, bf16[64,400,48]{2,1,0:T(8,128)(2,1)S(1)} %get-tuple-element.17.lhs_ref, bf16[16,400,256]{2,1,0:T(8,128)(2,1)S(1)} %get-tuple-element.18.lhs_end_ref, ...), custom_call_target="tpu_custom_call" | custom-call | tf_op jit(solution)/shard_map/pairs/pallas_call | solution.py:310
  80.5 15.6 %all_to_all.10.back_ref = f32[8,3,8,400]{3,2,1,0:T(8,128)} all-to-all(f32[8,3,8,400]{3,2,1,0:T(8,128)S(1)} %pairs.1), channel_id=1, replica_groups=mesh['ens'=8,'tile'=4] {'ens'}, dimensions={0} | all-to-all | bytes 614400 | tf_op jit(solution)/shard_map/all_to_all | solution.py:328
  96.1 1.7 %total.1 = f32[3,8,800]{2,1,0:T(8,128)} custom-call(f32[8,3,8,400]{3,2,1,0:T(8,128)} %all_to_all.10.back_ref), custom_call_target="tpu_custom_call" | custom-call | tf_op jit(solution)/shard_map/total/pallas_call | solution.py:329
  (5 shorter events, 0.0 us)
Async XLA Ops:
  1.9 21.0 %all-to-all-start = ((f32[8,8,1800]{2,1,0:T(8,128)}), f32[8,8,1800]{2,1,0:T(8,128)S(1)}, u32[]{:S(2)}, u32[]{:S(2)}) async-start(f32[8,8,1800]{2,1,0:T(8,128)} %pack.1), calls=%async_computation | async-start | bytes 983040 | tf_op jit(solution)/shard_map/all_to_all | solution.py:270
  13.1 0.9 copy-start
  22.9 9.5 %collective-permute-start.2 = (f32[8,8,600]{2,1,0:T(8,128)S(1)}, f32[8,8,600]{2,1,0:T(8,128)S(1)}, u32[]{:S(2)}, u32[]{:S(2)}) collective-permute-start(f32[8,8,600]{2,1,0:T(8,128)S(1)} %slice.3), channel_id=1, source_target_pairs={{0,1},{1,2},{2,3},{3,0},{4,5},{5,6},{6,7},{7,4},{8,9},{9,10},{10,1... | collective-permute-start | bytes 460808 | tf_op jit(solution)/shard_map/ppermute | solution.py:296
  24.4 8.7 %collective-permute-start.1 = (f32[8,8,600]{2,1,0:T(8,128)S(1)}, f32[8,8,600]{2,1,0:T(8,128)S(1)}, u32[]{:S(2)}, u32[]{:S(2)}) collective-permute-start(f32[8,8,600]{2,1,0:T(8,128)S(1)} %slice.3), channel_id=1, source_target_pairs={{0,2},{1,3},{2,0},{3,1},{4,6},{5,7},{6,4},{7,5},{8,10},{9,11},{10,... | collective-permute-start | bytes 460808 | tf_op jit(solution)/shard_map/ppermute | solution.py:296
  26.0 7.2 %collective-permute-start = (f32[8,8,600]{2,1,0:T(8,128)S(1)}, f32[8,8,600]{2,1,0:T(8,128)S(1)}, u32[]{:S(2)}, u32[]{:S(2)}) collective-permute-start(f32[8,8,600]{2,1,0:T(8,128)S(1)} %slice.3), channel_id=1, source_target_pairs={{0,3},{1,0},{2,1},{3,2},{4,7},{5,4},{6,5},{7,6},{8,11},{9,8},{10,9... | collective-permute-start | bytes 460808 | tf_op jit(solution)/shard_map/ppermute | solution.py:296

commit v22 on v21

--- a/solution.py
+++ b/solution.py
@@ -10,7 +10,8 @@
 LANES = 128
 WIDE = 256
 SLOT = 64
-TOGETHER = 4
+TOGETHER = 2
+KEEP_BYTES = 24 << 20
 NT = (((1,), (1,)), ((), ()))
 
 
@@ -122,7 +123,8 @@
 
 def pair_kernel(tiles, fold, n_rows, n_cols, mask_ref, goal_ref, lhs_ref, lhs_end_ref, both_ref, *rest):
     piece_refs = rest[:tiles - 1]
-    grad_ref, col_terms, rhs_ref, rhs_end_ref, terms_end_ref, weight_ref, weight_end_ref, sums_ref = rest[tiles - 1:]
+    (grad_ref, col_terms, rhs_ref, rhs_end_ref, terms_end_ref, weight_ref, weight_end_ref, sums_ref,
+     kept_ref, kept_end_ref) = rest[tiles - 1:]
     groups, per, _ = both_ref.shape
     structs = groups * per
     piece = n_cols // tiles
@@ -167,24 +169,34 @@
     def tanh_end(b):
         return jnp.tanh(jnp.dot(lhs_end_ref[b], rhs_end_ref[b], preferred_element_type=jnp.float32))
 
-    def add_some(b):
+    def add_some(b, keep):
         for inside in range(0, fold, 2):
             for start, size in chunks:
-                t = [tanh_block(b * fold + i, start, size) for i in range(inside, min(inside + 2, fold))]
+                t = []
+                for i in range(inside, min(inside + 2, fold)):
+                    t.append(tanh_block(b * fold + i, start, size))
+                    if keep:
+                        kept_ref[b * fold + i, :, pl.ds(start, size)] = 1.0 - t[-1] * t[-1]
                 weight_ref[:, pl.ds(start, size)] += functools.reduce(jnp.add, t)
         if end:
-            weight_end_ref[...] += tanh_end(b)
+            t = tanh_end(b)
+            if keep:
+                kept_end_ref[b] = 1.0 - t * t
+            weight_end_ref[...] += t
 
     together = TOGETHER if groups % TOGETHER == 0 else 1
-
-    def add_groups(step, carry):
+    per_step = together * (per // fold)
+    kept = kept_ref.shape[0] // (per_step * fold)
+
+    def add_groups(keep, step, carry):
         for j in range(together):
             features(step * together + j)
-        for j in range(together * (per // fold)):
-            add_some(step * (together * (per // fold)) + j)
+        for j in range(per_step):
+            add_some(step * per_step + j, keep)
         return carry
 
-    lax.fori_loop(0, groups // together, add_groups, 0)
+    lax.fori_loop(0, kept, functools.partial(add_groups, True), 0)
+    lax.fori_loop(kept, groups // together, functools.partial(add_groups, False), 0)
 
     scale = 0.5 / structs
     for start, size in chunks:
@@ -196,8 +208,11 @@
         last = pl.ds(full, LANES)
         weight_end_ref[...] = mask_ref[:, last] * (0.5 + scale * total) - goal_ref[:, last]
 
-    def split2(weight, t):
-        g = weight * (1.0 - t * t)
+    def slope(t):
+        return 1.0 - t * t
+
+    def split2(weight, slopes):
+        g = weight * slopes
         hi = g.astype(jnp.bfloat16)
         return [hi, (g - hi.astype(jnp.float32)).astype(jnp.bfloat16)]
 
@@ -206,14 +221,19 @@
         return (lax.dot_general(hi, terms, NT, preferred_element_type=jnp.float32).T
                 + lax.dot_general(terms, lo, NT, preferred_element_type=jnp.float32))
 
-    def grad_group(g):
+    def grad_group(g, keep):
         for block in range(per // fold):
             b = g * (per // fold) + block
             if end:
-                last = sums(terms_end_ref[b], [split2(weight_end_ref[...], tanh_end(b))])
+                slopes = kept_end_ref[b] if keep else slope(tanh_end(b))
+                last = sums(terms_end_ref[b], [split2(weight_end_ref[...], slopes)])
             for inside in range(fold):
                 s = b * fold + inside
-                parts = [split2(weight_ref[:, pl.ds(start, size)], tanh_block(s, start, size)) for start, size in chunks]
+                parts = []
+                for start, size in chunks:
+                    cut = pl.ds(start, size)
+                    slopes = kept_ref[s, :, cut] if keep else slope(tanh_block(s, start, size))
+                    parts.append(split2(weight_ref[:, cut], slopes))
                 total = sums(rhs_ref[s, pl.ds(0, 16), :], parts)
                 if end:
                     total += last[16 * inside:16 * inside + 16]
@@ -228,12 +248,13 @@
             xyz = both[:, 3 * piece + c * n_rows:3 * piece + (c + 1) * n_rows]
             grad_ref[g, c] = (0.25 / 16) * (sums_ref[c] - sums_ref[3] * xyz)
 
-    def grad_groups(step, carry):
+    def grad_groups(keep, step, carry):
         for j in range(together):
-            grad_group(step * together + j)
+            grad_group(step * together + j, keep)
         return carry
 
-    lax.fori_loop(0, groups // together, grad_groups, 0)
+    lax.fori_loop(0, kept, functools.partial(grad_groups, True), 0)
+    lax.fori_loop(kept, groups // together, functools.partial(grad_groups, False), 0)
 
 
 def split_ens(n_ens, beads, tiles):
@@ -283,6 +304,9 @@
     deep = up(n_rows, 16)
     row_wide, col_wide = up(n_rows, LANES), up(n_cols, LANES)
     blocks = structs // fold
+    kept = local_n * (TOGETHER if n_ens % TOGETHER == 0 else 1)
+    if 4 * kept * deep * (full + LANES) > KEEP_BYTES:
+        kept = 0
     masks = pl.pallas_call(
         functools.partial(mask_kernel, fold),
         out_shape=[jax.ShapeDtypeStruct((deep, col_wide), jnp.float32)] * 2,
@@ -320,6 +344,8 @@
             pltpu.VMEM((deep, full), jnp.float32),
             pltpu.VMEM((deep, LANES), jnp.float32),
             pltpu.VMEM((4, local_n, n_rows), jnp.float32),
+            pltpu.VMEM((max(kept, 1), deep, full), jnp.float32),
+            pltpu.VMEM((max(kept // fold, 1), deep, LANES), jnp.float32),
         ],
         compiler_params=pltpu.CompilerParams(vmem_limit_bytes=40 << 20),
         name="pairs",

time: 98.3 us -> 96 us (0.977)
  Pallas kernels: 56.7 us -> 54.4 us
    pallas_call x1, Pallas kernels: 47.3 us -> 45 us  [on_device(): pl.pallas_call(functools.partial(pair_kernel, n_tile, fold, n_rows, n_col...]
  transfers between devices with their start and end apart: 4 -> 4, of which waited for: 3 -> 3; matrix products, arithmetic and copies ran while one was open for 5% -> 6% of each run, Pallas kernels for 6% -> 6%
where the time goes in v22:
time: 96 us; the launch traced here: 95.5 us
  Pallas kernels  54.4 us (57%)
  blocking collectives  15.6 us (16%)
  starting transfers between devices  10.8 us (11%)
  waiting for transfers between devices  8.75 us (9%)
  local copies, waits for them, and re-layouts  5.06 us (5%)
    pallas_call x1, Pallas kernels, on_device(): pl.pallas_call(functools.partial(pair_kernel, n_tile, fold, n_rows, n_col...  45 us
    all_to_all x1, blocking collectives, on_device(): back = lax.all_to_all(grad, 'ens', 0, 0, tiled=True)  15.6 us
    all_to_all x1, waiting for transfers between devices, on_device(): both = lax.all_to_all(send, 'ens', 0, 0, tiled=True)  7.94 us
    all_to_all x1, starting transfers between devices, on_device(): both = lax.all_to_all(send, 'ens', 0, 0, tiled=True)  6.33 us
    pallas_call x1, Pallas kernels, on_device(): pl.pallas_call(functools.partial(row_kernel, n_rows, fold), out_shape=[ja...  4.98 us
    ppermute x3, starting transfers between devices, on_device(): lax.ppermute(own, 'tile', [(t, (t - k) % n_tile) for t in range(n_tile)])  4.5 us
    dynamic_slice x1, local copies, waits for them, and re-layouts, on_device(): lax.dynamic_slice_in_dim(own_counts, b, piece, 1)  2.17 us
  transfers between devices with their start and end apart: 4, of which 3 were waited for; matrix products, arithmetic and copies ran while one was open for 6% of the time, Pallas kernels for 6%

profile of v22, /device:TPU:0, one launch (start us, length us, event | category | flops | bytes accessed | tf_op | source)
XLA Modules:
  0.0 95.5 jit_solution(16641234415401434715)
XLA Ops:
  0.0 1.9 %pack.1 = f32[8,8,1800]{2,1,0:T(8,128)} custom-call(f32[3,8,800]{2,1,0:T(8,128)} %bitcast.4), custom_call_target="tpu_custom_call" | custom-call | tf_op jit(solution)/shard_map/pack/pallas_call | solution.py:284
  1.9 6.3 %all-to-all-start = ((f32[8,8,1800]{2,1,0:T(8,128)}), f32[8,8,1800]{2,1,0:T(8,128)S(1)}, u32[]{:S(2)}, u32[]{:S(2)}) async-start(f32[8,8,1800]{2,1,0:T(8,128)} %pack.1), calls=%async_computation | async-start | bytes 983040 | tf_op jit(solution)/shard_map/all_to_all | solution.py:291
  8.3 0.1 pad_add_fusion.2
  8.4 0.8 dynamic_slice.28
  9.2 0.9 fusion.1
  10.0 0.1 pad_add_fusion.1
  10.1 0.8 copy.4.seg_rows_ref
  11.0 2.2 %fusion = (s32[400,200]{1,0:T(8,128)S(1)}, s32[400,200]{1,0:T(8,128)S(1)}, s32[400,200]{1,0:T(8,128)S(1)}, s32[400,200]{1,0:T(8,128)S(1)}) fusion(s32[800,3200]{1,0:T(8,128)} %param.4, s32[]{:T(128)S(6)} %select_n.38, s32[]{:T(128)S(6)} %select_n.39, s32[]{:T(128)S(6)} %select_n.40, s32[]{:T(128)S(6)} %select_n.42, s32[]{:T(128)S(6)} %select_n.41), kind=kLoop, calls=%fused_computation.7 | loop fusion | bytes 2560020 | tf_op jit(solution)/shard_map/dynamic_slice | solution.py:296
  13.1 0.0 copy-start
  13.1 0.5 pad_add_fusion.counts_ref
  13.7 0.4 copy-done
  14.1 0.9 masks.1
  14.9 7.9 %all-to-all-done.both_ref = f32[8,8,1800]{2,1,0:T(8,128)S(1)} async-done(((f32[8,8,1800]{2,1,0:T(8,128)}), f32[8,8,1800]{2,1,0:T(8,128)S(1)}, u32[]{:S(2)}, u32[]{:S(2)}) %all-to-all-start) | async-done | bytes 460832 | tf_op jit(solution)/shard_map/all_to_all | solution.py:291
  22.9 1.5 %collective-permute-start.2 = (f32[8,8,600]{2,1,0:T(8,128)S(1)}, f32[8,8,600]{2,1,0:T(8,128)S(1)}, u32[]{:S(2)}, u32[]{:S(2)}) collective-permute-start(f32[8,8,600]{2,1,0:T(8,128)S(1)} %slice.3), channel_id=1, source_target_pairs={{0,1},{1,2},{2,3},{3,0},{4,5},{5,6},{6,7},{7,4},{8,9},{9,10},{10,1... | collective-permute-start | bytes 460808 | tf_op jit(solution)/shard_map/ppermute | solution.py:320
  24.4 1.5 %collective-permute-start.1 = (f32[8,8,600]{2,1,0:T(8,128)S(1)}, f32[8,8,600]{2,1,0:T(8,128)S(1)}, u32[]{:S(2)}, u32[]{:S(2)}) collective-permute-start(f32[8,8,600]{2,1,0:T(8,128)S(1)} %slice.3), channel_id=1, source_target_pairs={{0,2},{1,3},{2,0},{3,1},{4,6},{5,7},{6,4},{7,5},{8,10},{9,11},{10,... | collective-permute-start | bytes 460808 | tf_op jit(solution)/shard_map/ppermute | solution.py:320
  26.0 1.4 %collective-permute-start = (f32[8,8,600]{2,1,0:T(8,128)S(1)}, f32[8,8,600]{2,1,0:T(8,128)S(1)}, u32[]{:S(2)}, u32[]{:S(2)}) collective-permute-start(f32[8,8,600]{2,1,0:T(8,128)S(1)} %slice.3), channel_id=1, source_target_pairs={{0,3},{1,0},{2,1},{3,2},{4,7},{5,4},{6,5},{7,6},{8,11},{9,8},{10,9... | collective-permute-start | bytes 460808 | tf_op jit(solution)/shard_map/ppermute | solution.py:320
  27.4 5.0 %rows.1 = (bf16[64,400,48]{2,1,0:T(8,128)(2,1)S(1)}, bf16[16,400,256]{2,1,0:T(8,128)(2,1)S(1)}) custom-call(f32[8,8,1800]{2,1,0:T(8,128)S(1)} %all-to-all-done.both_ref), custom_call_target="tpu_custom_call" | custom-call | tf_op jit(solution)/shard_map/rows/pallas_call | solution.py:322
  32.4 0.0 collective-permute-done.2.rest_2_
  32.4 0.7 collective-permute-done.1.rest_1_
  33.1 0.1 collective-permute-done.rest_0_
  33.2 45.0 %pairs.1 = f32[8,3,8,400]{3,2,1,0:T(8,128)S(1)} custom-call(f32[400,896]{1,0:T(8,128)S(1)} %get-tuple-element.14.mask_ref, f32[400,896]{1,0:T(8,128)S(1)} %get-tuple-element.15.goal_ref, bf16[64,400,48]{2,1,0:T(8,128)(2,1)S(1)} %get-tuple-element.17.lhs_ref, bf16[16,400,256]{2,1,0:T(8,128)(2,1)S(1)} %get-tuple-element.18.lhs_end_ref, ...), custom_call_target="tpu_custom_call" | custom-call | tf_op jit(solution)/shard_map/pairs/pallas_call | solution.py:334
  78.2 15.6 %all_to_all.10.back_ref = f32[8,3,8,400]{3,2,1,0:T(8,128)} all-to-all(f32[8,3,8,400]{3,2,1,0:T(8,128)S(1)} %pairs.1), channel_id=1, replica_groups=mesh['ens'=8,'tile'=4] {'ens'}, dimensions={0} | all-to-all | bytes 614400 | tf_op jit(solution)/shard_map/all_to_all | solution.py:354
  93.8 1.7 %total.1 = f32[3,8,800]{2,1,0:T(8,128)} custom-call(f32[8,3,8,400]{3,2,1,0:T(8,128)} %all_to_all.10.back_ref), custom_call_target="tpu_custom_call" | custom-call | tf_op jit(solution)/shard_map/total/pallas_call | solution.py:355
  (5 shorter events, 0.0 us)
Async XLA Ops:
  1.9 21.0 %all-to-all-start = ((f32[8,8,1800]{2,1,0:T(8,128)}), f32[8,8,1800]{2,1,0:T(8,128)S(1)}, u32[]{:S(2)}, u32[]{:S(2)}) async-start(f32[8,8,1800]{2,1,0:T(8,128)} %pack.1), calls=%async_computation | async-start | bytes 983040 | tf_op jit(solution)/shard_map/all_to_all | solution.py:291
  13.1 0.9 copy-start
  22.9 9.5 %collective-permute-start.2 = (f32[8,8,600]{2,1,0:T(8,128)S(1)}, f32[8,8,600]{2,1,0:T(8,128)S(1)}, u32[]{:S(2)}, u32[]{:S(2)}) collective-permute-start(f32[8,8,600]{2,1,0:T(8,128)S(1)} %slice.3), channel_id=1, source_target_pairs={{0,1},{1,2},{2,3},{3,0},{4,5},{5,6},{6,7},{7,4},{8,9},{9,10},{10,1... | collective-permute-start | bytes 460808 | tf_op jit(solution)/shard_map/ppermute | solution.py:320
  24.4 8.7 %collective-permute-start.1 = (f32[8,8,600]{2,1,0:T(8,128)S(1)}, f32[8,8,600]{2,1,0:T(8,128)S(1)}, u32[]{:S(2)}, u32[]{:S(2)}) collective-permute-start(f32[8,8,600]{2,1,0:T(8,128)S(1)} %slice.3), channel_id=1, source_target_pairs={{0,2},{1,3},{2,0},{3,1},{4,6},{5,7},{6,4},{7,5},{8,10},{9,11},{10,... | collective-permute-start | bytes 460808 | tf_op jit(solution)/shard_map/ppermute | solution.py:320
  26.0 7.2 %collective-permute-start = (f32[8,8,600]{2,1,0:T(8,128)S(1)}, f32[8,8,600]{2,1,0:T(8,128)S(1)}, u32[]{:S(2)}, u32[]{:S(2)}) collective-permute-start(f32[8,8,600]{2,1,0:T(8,128)S(1)} %slice.3), channel_id=1, source_target_pairs={{0,3},{1,0},{2,1},{3,2},{4,7},{5,4},{6,5},{7,6},{8,11},{9,8},{10,9... | collective-permute-start | bytes 460808 | tf_op jit(solution)/shard_map/ppermute | solution.py:320

commit v23 on v22

--- a/solution.py
+++ b/solution.py
@@ -11,6 +11,7 @@
 WIDE = 256
 SLOT = 64
 TOGETHER = 2
+WIDE_STEP = 3
 KEEP_BYTES = 24 << 20
 NT = (((1,), (1,)), ((), ()))
 
@@ -188,15 +189,18 @@
     per_step = together * (per // fold)
     kept = kept_ref.shape[0] // (per_step * fold)
 
-    def add_groups(keep, step, carry):
-        for j in range(together):
-            features(step * together + j)
-        for j in range(per_step):
-            add_some(step * per_step + j, keep)
+    first = kept * together
+    wide_step = WIDE_STEP if (groups - first) % WIDE_STEP == 0 else together
+
+    def add_groups(keep, start, n, step, carry):
+        for j in range(n):
+            features(start + step * n + j)
+        for j in range(n * (per // fold)):
+            add_some((start + step * n) * (per // fold) + j, keep)
         return carry
 
-    lax.fori_loop(0, kept, functools.partial(add_groups, True), 0)
-    lax.fori_loop(kept, groups // together, functools.partial(add_groups, False), 0)
+    lax.fori_loop(0, kept, functools.partial(add_groups, True, 0, together), 0)
+    lax.fori_loop(0, (groups - first) // wide_step, functools.partial(add_groups, False, first, wide_step), 0)
 
     scale = 0.5 / structs
     for start, size in chunks:
@@ -248,13 +252,13 @@
             xyz = both[:, 3 * piece + c * n_rows:3 * piece + (c + 1) * n_rows]
             grad_ref[g, c] = (0.25 / 16) * (sums_ref[c] - sums_ref[3] * xyz)
 
-    def grad_groups(keep, step, carry):
-        for j in range(together):
-            grad_group(step * together + j, keep)
+    def grad_groups(keep, start, n, step, carry):
+        for j in range(n):
+            grad_group(start + step * n + j, keep)
         return carry
 
-    lax.fori_loop(0, kept, functools.partial(grad_groups, True), 0)
-    lax.fori_loop(kept, groups // together, functools.partial(grad_groups, False), 0)
+    lax.fori_loop(0, kept, functools.partial(grad_groups, True, 0, together), 0)
+    lax.fori_loop(0, (groups - first) // wide_step, functools.partial(grad_groups, False, first, wide_step), 0)
 
 
 def split_ens(n_ens, beads, tiles):

time: 96 us -> 95.4 us (level)
  no operation moved by 1% of the time
where the time goes in v23:
time: 95.4 us; the launch traced here: 94.9 us
  Pallas kernels  53.8 us (56%)
  blocking collectives  15.6 us (16%)
  starting transfers between devices  10.8 us (11%)
  waiting for transfers between devices  8.75 us (9%)
  local copies, waits for them, and re-layouts  5.06 us (5%)
    pallas_call x1, Pallas kernels, on_device(): pl.pallas_call(functools.partial(pair_kernel, n_tile, fold, n_rows, n_col...  44.4 us
    all_to_all x1, blocking collectives, on_device(): back = lax.all_to_all(grad, 'ens', 0, 0, tiled=True)  15.6 us
    all_to_all x1, waiting for transfers between devices, on_device(): both = lax.all_to_all(send, 'ens', 0, 0, tiled=True)  7.94 us
    all_to_all x1, starting transfers between devices, on_device(): both = lax.all_to_all(send, 'ens', 0, 0, tiled=True)  6.33 us
    pallas_call x1, Pallas kernels, on_device(): pl.pallas_call(functools.partial(row_kernel, n_rows, fold), out_shape=[ja...  4.98 us
    ppermute x3, starting transfers between devices, on_device(): lax.ppermute(own, 'tile', [(t, (t - k) % n_tile) for t in range(n_tile)])  4.5 us
    dynamic_slice x1, local copies, waits for them, and re-layouts, on_device(): lax.dynamic_slice_in_dim(own_counts, b, piece, 1)  2.17 us
  transfers between devices with their start and end apart: 4, of which 3 were waited for; matrix products, arithmetic and copies ran while one was open for 6% of the time, Pallas kernels for 6%

profile of v23, /device:TPU:0, one launch (start us, length us, event | category | flops | bytes accessed | tf_op | source)
XLA Modules:
  0.0 94.9 jit_solution(9891945763901102752)
XLA Ops:
  0.0 1.9 %pack.1 = f32[8,8,1800]{2,1,0:T(8,128)} custom-call(f32[3,8,800]{2,1,0:T(8,128)} %bitcast.4), custom_call_target="tpu_custom_call" | custom-call | tf_op jit(solution)/shard_map/pack/pallas_call | solution.py:288
  1.9 6.3 %all-to-all-start = ((f32[8,8,1800]{2,1,0:T(8,128)}), f32[8,8,1800]{2,1,0:T(8,128)S(1)}, u32[]{:S(2)}, u32[]{:S(2)}) async-start(f32[8,8,1800]{2,1,0:T(8,128)} %pack.1), calls=%async_computation | async-start | bytes 983040 | tf_op jit(solution)/shard_map/all_to_all | solution.py:295
  8.3 0.1 pad_add_fusion.2
  8.4 0.8 dynamic_slice.28
  9.2 0.9 fusion.1
  10.0 0.1 pad_add_fusion.1
  10.1 0.8 copy.4.seg_rows_ref
  11.0 2.2 %fusion = (s32[400,200]{1,0:T(8,128)S(1)}, s32[400,200]{1,0:T(8,128)S(1)}, s32[400,200]{1,0:T(8,128)S(1)}, s32[400,200]{1,0:T(8,128)S(1)}) fusion(s32[800,3200]{1,0:T(8,128)} %param.4, s32[]{:T(128)S(6)} %select_n.38, s32[]{:T(128)S(6)} %select_n.39, s32[]{:T(128)S(6)} %select_n.40, s32[]{:T(128)S(6)} %select_n.42, s32[]{:T(128)S(6)} %select_n.41), kind=kLoop, calls=%fused_computation.7 | loop fusion | bytes 2560020 | tf_op jit(solution)/shard_map/dynamic_slice | solution.py:300
  13.1 0.0 copy-start
  13.1 0.5 pad_add_fusion.counts_ref
  13.7 0.4 copy-done
  14.1 0.9 masks.1
  14.9 7.9 %all-to-all-done.both_ref = f32[8,8,1800]{2,1,0:T(8,128)S(1)} async-done(((f32[8,8,1800]{2,1,0:T(8,128)}), f32[8,8,1800]{2,1,0:T(8,128)S(1)}, u32[]{:S(2)}, u32[]{:S(2)}) %all-to-all-start) | async-done | bytes 460832 | tf_op jit(solution)/shard_map/all_to_all | solution.py:295
  22.9 1.5 %collective-permute-start.2 = (f32[8,8,600]{2,1,0:T(8,128)S(1)}, f32[8,8,600]{2,1,0:T(8,128)S(1)}, u32[]{:S(2)}, u32[]{:S(2)}) collective-permute-start(f32[8,8,600]{2,1,0:T(8,128)S(1)} %slice.3), channel_id=1, source_target_pairs={{0,1},{1,2},{2,3},{3,0},{4,5},{5,6},{6,7},{7,4},{8,9},{9,10},{10,1... | collective-permute-start | bytes 460808 | tf_op jit(solution)/shard_map/ppermute | solution.py:324
  24.4 1.5 %collective-permute-start.1 = (f32[8,8,600]{2,1,0:T(8,128)S(1)}, f32[8,8,600]{2,1,0:T(8,128)S(1)}, u32[]{:S(2)}, u32[]{:S(2)}) collective-permute-start(f32[8,8,600]{2,1,0:T(8,128)S(1)} %slice.3), channel_id=1, source_target_pairs={{0,2},{1,3},{2,0},{3,1},{4,6},{5,7},{6,4},{7,5},{8,10},{9,11},{10,... | collective-permute-start | bytes 460808 | tf_op jit(solution)/shard_map/ppermute | solution.py:324
  26.0 1.4 %collective-permute-start = (f32[8,8,600]{2,1,0:T(8,128)S(1)}, f32[8,8,600]{2,1,0:T(8,128)S(1)}, u32[]{:S(2)}, u32[]{:S(2)}) collective-permute-start(f32[8,8,600]{2,1,0:T(8,128)S(1)} %slice.3), channel_id=1, source_target_pairs={{0,3},{1,0},{2,1},{3,2},{4,7},{5,4},{6,5},{7,6},{8,11},{9,8},{10,9... | collective-permute-start | bytes 460808 | tf_op jit(solution)/shard_map/ppermute | solution.py:324
  27.4 5.0 %rows.1 = (bf16[64,400,48]{2,1,0:T(8,128)(2,1)S(1)}, bf16[16,400,256]{2,1,0:T(8,128)(2,1)S(1)}) custom-call(f32[8,8,1800]{2,1,0:T(8,128)S(1)} %all-to-all-done.both_ref), custom_call_target="tpu_custom_call" | custom-call | tf_op jit(solution)/shard_map/rows/pallas_call | solution.py:326
  32.4 0.0 collective-permute-done.2.rest_2_
  32.4 0.7 collective-permute-done.1.rest_1_
  33.1 0.1 collective-permute-done.rest_0_
  33.2 44.4 %pairs.1 = f32[8,3,8,400]{3,2,1,0:T(8,128)S(1)} custom-call(f32[400,896]{1,0:T(8,128)S(1)} %get-tuple-element.14.mask_ref, f32[400,896]{1,0:T(8,128)S(1)} %get-tuple-element.15.goal_ref, bf16[64,400,48]{2,1,0:T(8,128)(2,1)S(1)} %get-tuple-element.17.lhs_ref, bf16[16,400,256]{2,1,0:T(8,128)(2,1)S(1)} %get-tuple-element.18.lhs_end_ref, ...), custom_call_target="tpu_custom_call" | custom-call | tf_op jit(solution)/shard_map/pairs/pallas_call | solution.py:338
  77.6 15.6 %all_to_all.10.back_ref = f32[8,3,8,400]{3,2,1,0:T(8,128)} all-to-all(f32[8,3,8,400]{3,2,1,0:T(8,128)S(1)} %pairs.1), channel_id=1, replica_groups=mesh['ens'=8,'tile'=4] {'ens'}, dimensions={0} | all-to-all | bytes 614400 | tf_op jit(solution)/shard_map/all_to_all | solution.py:358
  93.2 1.7 %total.1 = f32[3,8,800]{2,1,0:T(8,128)} custom-call(f32[8,3,8,400]{3,2,1,0:T(8,128)} %all_to_all.10.back_ref), custom_call_target="tpu_custom_call" | custom-call | tf_op jit(solution)/shard_map/total/pallas_call | solution.py:359
  (5 shorter events, 0.0 us)
Async XLA Ops:
  1.9 21.0 %all-to-all-start = ((f32[8,8,1800]{2,1,0:T(8,128)}), f32[8,8,1800]{2,1,0:T(8,128)S(1)}, u32[]{:S(2)}, u32[]{:S(2)}) async-start(f32[8,8,1800]{2,1,0:T(8,128)} %pack.1), calls=%async_computation | async-start | bytes 983040 | tf_op jit(solution)/shard_map/all_to_all | solution.py:295
  13.1 0.9 copy-start
  22.9 9.5 %collective-permute-start.2 = (f32[8,8,600]{2,1,0:T(8,128)S(1)}, f32[8,8,600]{2,1,0:T(8,128)S(1)}, u32[]{:S(2)}, u32[]{:S(2)}) collective-permute-start(f32[8,8,600]{2,1,0:T(8,128)S(1)} %slice.3), channel_id=1, source_target_pairs={{0,1},{1,2},{2,3},{3,0},{4,5},{5,6},{6,7},{7,4},{8,9},{9,10},{10,1... | collective-permute-start | bytes 460808 | tf_op jit(solution)/shard_map/ppermute | solution.py:324
  24.4 8.7 %collective-permute-start.1 = (f32[8,8,600]{2,1,0:T(8,128)S(1)}, f32[8,8,600]{2,1,0:T(8,128)S(1)}, u32[]{:S(2)}, u32[]{:S(2)}) collective-permute-start(f32[8,8,600]{2,1,0:T(8,128)S(1)} %slice.3), channel_id=1, source_target_pairs={{0,2},{1,3},{2,0},{3,1},{4,6},{5,7},{6,4},{7,5},{8,10},{9,11},{10,... | collective-permute-start | bytes 460808 | tf_op jit(solution)/shard_map/ppermute | solution.py:324
  26.0 7.2 %collective-permute-start = (f32[8,8,600]{2,1,0:T(8,128)S(1)}, f32[8,8,600]{2,1,0:T(8,128)S(1)}, u32[]{:S(2)}, u32[]{:S(2)}) collective-permute-start(f32[8,8,600]{2,1,0:T(8,128)S(1)} %slice.3), channel_id=1, source_target_pairs={{0,3},{1,0},{2,1},{3,2},{4,7},{5,4},{6,5},{7,6},{8,11},{9,8},{10,9... | collective-permute-start | bytes 460808 | tf_op jit(solution)/shard_map/ppermute | solution.py:324
